TPU v7x, 32 devices: a whole 2x2x4 slice. The times are simulated.
32 devices in a mesh: vocab: 4 (over y, x), ctx: 8 (over z, core).
Axes of the slice: x: 2, y: 2, z: 4, core: 2. Of those that a mesh axis runs over, the one named last changes fastest.
Arguments:
- hidden: bfloat16 [1024, 8192], P('ctx', 'vocab'), may hold values from -20 to 20
- norm_gain: float32 [8192], replicated, may hold values from 0.5 to 1.5
- head_weight: bfloat16 [152064, 8192], P(('vocab', 'ctx')), may hold values from -16 to 16
- targets: int32 [64], replicated, may hold values from 0 to 152063
- loss_rows: int32 [64], replicated, may hold values from 0 to 127, as said below
- stretch_of_slot: int32 [16], replicated, may hold values from 0 to 15, as said below
- queries: bfloat16 [1024, 8192], P('ctx', 'vocab'), may hold values from -20 to 20
- key_states: bfloat16 [1024, 1024], P('ctx', 'vocab'), may hold values from -20 to 20
- attention_values: bfloat16 [1024, 1024], P('ctx', 'vocab'), may hold values from -6 to 6
- output_weight: bfloat16 [8192, 8192], P('vocab', 'ctx'), may hold values from -0.0625 to 0.0625
Outputs:
- mean_loss: float32 [], replicated
- query_grad: bfloat16 [64, 8192], P('ctx', 'vocab')
- key_gradient: bfloat16 [1024, 1024], P('ctx', 'vocab')
- value_gradient: bfloat16 [1024, 1024], P('ctx', 'vocab')
- resid_grad: bfloat16 [8192, 64], P('ctx')
Inputs may be any that keep to these rules, and one draw needn't show every extreme that they name: `loss_rows`: within each block of 8 entries, entry j lies in rows j * 16 to (j + 1) * 16 - 1. `stretch_of_slot`: A permutation of the stretches in which slots 2c and 2c+1 hold stretches that sum to 15.
All inputs are finite; a program needn't handle non-finite values.
Results may differ from a plain program's by a relative error of at most 0.023.
Values may be sent and summed in bfloat16 or wider, within the bound.
No kernel may reach another device: no remote copies, remote signals or barrier semaphores. Data moves between devices by JAX's collectives and lax.ppermute only.
A program may use at most 128 MiB of HBM per device.

v0:
```python
import jax
import jax.numpy as jnp
from jax import lax
from jax.sharding import PartitionSpec as P

HEAD_SIZE = 128


norm_eps = 1e-06
grad_weight = 16.0
masked_fill = -1e30


def joined(value, axis, combine):
    everything = jax.tree.map(lambda part: lax.all_gather(part, axis), value)
    leading = jax.tree.map(lambda part: part[0], everything)

    def lap(k, so_far):
        return combine(so_far, jax.tree.map(lambda part: part[k], everything))

    return lax.fori_loop(1, lax.axis_size(axis), lap, leading)


def lookup_small(indices, table):
    span = table.shape[0]
    match = indices[:, None] == lax.broadcasted_iota(jnp.int32, (1, span), 1)
    return jnp.sum(jnp.where(match, table[None, :], 0), axis=1)


def merge_vocab(earlier, latter):
    top_both = jnp.maximum(earlier[0], latter[0])
    left_factor = jnp.exp(earlier[0] - top_both)
    right_factor = jnp.exp(latter[0] - top_both)
    return (top_both, earlier[1] * left_factor + latter[1] * right_factor, earlier[2] + latter[2])


def head_scores(query_heads, key_heads, query_pos, key_pos, score_scale):
    scores = (
        jnp.einsum("tjgd,sjd->jgts", query_heads, key_heads, preferred_element_type=jnp.float32)
        * score_scale
    )
    visible = key_pos[None, None, None, :] <= query_pos[None, None, :, None]
    return (jnp.where(visible, scores, masked_fill), visible)


def score_backward(prob_full, output, value_heads, grad_heads):
    row_delta = jnp.sum(
        output * jnp.transpose(grad_heads, (1, 2, 0, 3)).astype(jnp.float32), axis=3
    )
    prob_grad = jnp.einsum(
        "tjgd,sjd->jgts", grad_heads, value_heads, preferred_element_type=jnp.float32
    )
    score_grad = (prob_full * (prob_grad - row_delta[..., None])).astype(jnp.bfloat16)
    return (prob_full.astype(jnp.bfloat16), score_grad)


def per_device(
    hidden,
    norm_gain,
    head_weight,
    targets,
    loss_rows,
    stretch_of_slot,
    queries,
    key_states,
    attention_values,
    output_weight,
):
    ctx_count = lax.axis_size("ctx")
    ctx_index = lax.axis_index("ctx")
    vocab_index = lax.axis_index("vocab")
    device_rows = hidden.shape[0]
    stretch_len = device_rows // 2
    loss_total = loss_rows.shape[0]
    loss_per_device = loss_total // ctx_count
    model_width = norm_gain.shape[0]
    voc_rows = head_weight.shape[0]
    head_dim = HEAD_SIZE
    query_width = queries.shape[1]
    key_width = key_states.shape[1]
    key_head_count = key_width // head_dim
    query_group_size = query_width // key_width
    score_scale = head_dim ** (-0.5)
    cols_ctx = model_width // ctx_count
    own_rows = lax.dynamic_slice_in_dim(loss_rows, ctx_index * loss_per_device, loss_per_device)
    picked = jnp.take(hidden, own_rows, axis=0)
    wide_rows = lax.all_gather(picked, "vocab", axis=1, tiled=True)
    rows_all = lax.all_gather(wide_rows, "ctx", axis=0, tiled=True)
    rows_float = rows_all.astype(jnp.float32)
    inv_rms = lax.rsqrt(jnp.mean(rows_float * rows_float, axis=1) + norm_eps)
    normed = (rows_float * inv_rms[:, None] * norm_gain[None, :]).astype(jnp.bfloat16)
    logit_rows = lax.dot_general(
        head_weight, normed, (((1,), (1,)), ((), ())), preferred_element_type=jnp.float32
    )
    first_vocab = (vocab_index * ctx_count + ctx_index) * voc_rows
    vocab_ids = first_vocab + lax.broadcasted_iota(jnp.int32, (voc_rows, 1), 0)
    is_target = vocab_ids == targets[None, :]
    local_top = jnp.max(logit_rows, axis=0)
    target_part = jnp.sum(jnp.where(is_target, logit_rows, 0.0), axis=0)
    local_total = jnp.sum(jnp.exp(logit_rows - local_top[None, :]), axis=0)
    top_score, row_total, target_logit = joined(
        (local_top, local_total, target_part), ("vocab", "ctx"), merge_vocab
    )
    log_total = top_score + jnp.log(row_total)
    mean_loss = jnp.mean(log_total - target_logit)
    logit_grad = (
        grad_weight * (jnp.exp(logit_rows - log_total[None, :]) - is_target.astype(jnp.float32))
    ).astype(jnp.bfloat16)
    partial_rows = lax.psum_scatter(
        lax.dot_general(
            head_weight, logit_grad, (((0,), (0,)), ((), ())), preferred_element_type=jnp.float32
        ),
        "ctx",
        scatter_dimension=0,
        tiled=True,
    )
    normed_grad = lax.psum(partial_rows, "vocab")
    col_start = ctx_index * cols_ctx
    gain_part = lax.dynamic_slice_in_dim(norm_gain, col_start, cols_ctx)
    unit_rows = (lax.dynamic_slice_in_dim(rows_float, col_start, cols_ctx, 1) * inv_rms[:, None]).T
    scaled = normed_grad * gain_part[:, None]
    inner = lax.psum(jnp.sum(scaled * unit_rows, axis=0), "ctx")
    resid_grad = (inv_rms[None, :] * (scaled - unit_rows * (inner / model_width)[None, :])).astype(
        jnp.bfloat16
    )
    own_stretches = lax.dynamic_slice_in_dim(stretch_of_slot, 2 * ctx_index, 2)
    stretch_iota = lax.broadcasted_iota(jnp.int32, (1, stretch_len), 1)
    own_pos = (own_stretches[:, None] * stretch_len + stretch_iota).reshape(device_rows)
    query_mine = jnp.take(queries, own_rows, axis=0)
    attn_grad = lax.psum_scatter(
        lax.dot_general(
            resid_grad, output_weight, (((0,), (1,)), ((), ())), preferred_element_type=jnp.float32
        ),
        "ctx",
        scatter_dimension=0,
        tiled=True,
    ).astype(jnp.bfloat16)
    keys_all, value_rows_full = (
        lax.all_gather(key_states, "ctx", axis=0, tiled=True),
        lax.all_gather(attention_values, "ctx", axis=0, tiled=True),
    )
    query_heads = query_mine.reshape(loss_per_device, key_head_count, query_group_size, head_dim)
    grad_heads = attn_grad.reshape(loss_per_device, key_head_count, query_group_size, head_dim)
    key_heads = keys_all.reshape(-1, key_head_count, head_dim)
    value_heads = value_rows_full.reshape(-1, key_head_count, head_dim)
    key_pos = (stretch_of_slot[:, None] * stretch_len + stretch_iota).reshape(-1)
    query_pos = lookup_small(own_rows, own_pos)
    masked, visible = head_scores(query_heads, key_heads, query_pos, key_pos, score_scale)
    top_row = jnp.max(masked, axis=3)
    raw_weights = jnp.where(visible, jnp.exp(masked - top_row[..., None]), 0.0)
    prob_full = raw_weights / jnp.sum(raw_weights, axis=3)[..., None]
    output = jnp.einsum(
        "jgts,sjd->jgtd",
        prob_full,
        value_heads.astype(jnp.float32),
        precision=lax.Precision.HIGHEST,
    )
    prob_half, score_grad = score_backward(prob_full, output, value_heads, grad_heads)
    query_grad = (
        jnp.einsum("jgts,sjd->tjgd", score_grad, key_heads, preferred_element_type=jnp.float32)
        * score_scale
    )
    query_grad = query_grad.reshape(loss_per_device, query_width).astype(jnp.bfloat16)
    value_term = jnp.einsum(
        "jgts,tjgd->sjd", prob_half, grad_heads, preferred_element_type=jnp.float32
    )
    key_term = (
        jnp.einsum("jgts,tjgd->sjd", score_grad, query_heads, preferred_element_type=jnp.float32)
        * score_scale
    )
    key_value_sum = lax.psum_scatter(
        jnp.concatenate(
            [
                key_term.reshape(device_rows * lax.axis_size("ctx"), key_width),
                value_term.reshape(device_rows * lax.axis_size("ctx"), key_width),
            ],
            axis=1,
        ),
        "ctx",
        scatter_dimension=0,
        tiled=True,
    )
    key_gradient = key_value_sum[:, :key_width].astype(jnp.bfloat16)
    value_gradient = key_value_sum[:, key_width:].astype(jnp.bfloat16)
    return (mean_loss, query_grad, key_gradient, value_gradient, resid_grad)


def solution(mesh):
    placed = (
        P("ctx", "vocab"),
        P(),
        P(("vocab", "ctx"), None),
        P(),
        P(),
        P(),
        P("ctx", "vocab"),
        P("ctx", "vocab"),
        P("ctx", "vocab"),
        P("vocab", "ctx"),
    )
    return jax.shard_map(
        per_device,
        mesh=mesh,
        in_specs=placed,
        out_specs=(P(), P("ctx", "vocab"), P("ctx", "vocab"), P("ctx", "vocab"), P("ctx", None)),
        check_vma=False,
    )
```

profile of v0, /device:TPU:3, one launch (start us, length us, event | category | flops | bytes accessed | tf_op | source)
XLA Modules:
  0.0 332.0 jit_solution(8804714415934763447)
XLA Ops:
  7.2 0.8 compare_and_fusion
  8.2 0.6 gather_fusion.1
  8.8 1.7 gather_fusion
  10.6 7.1 %all_gather.30 = bf16[8,8192]{1,0:T(8,128)(2,1)} all-gather(bf16[8,2048]{1,0:T(8,128)(2,1)S(1)} %get-tuple-element.216), channel_id=1, replica_groups=mesh['vocab'=4,'ctx'=8] {'vocab'}, dimensions={1}, use_global_device_ids=true | all-gather | bytes 163840 | tf_op jit(solution)/shard_map/all_gather | solution.py:87
  17.8 24.9 %all-gather.5.cloned.1.call-done = bf16[64,8192]{1,0:T(8,128)(2,1)} async-done(((bf16[8,8192]{1,0:T(8,128)(2,1)}), bf16[64,8192]{1,0:T(8,128)(2,1)}) %all-gather.5.cloned.1.call-update) | async-done | bytes 1048592 | tf_op jit(solution)/shard_map/all_gather | solution.py:88
  42.7 1.5 multiply_reduce_fusion
  44.2 35.2 %fusion.49 = (f32[64]{0:T(128)S(1)}, f32[64,4752]{1,0:T(8,128)S(1)}) fusion(bf16[4752,8192]{1,0:T(8,128)(2,1)} %param.16, f32[8192]{0:T(1024)S(1)} %copy-done.7, f32[64]{0:T(128)S(1)} %add_rsqrt_fusion, bf16[64,8192]{1,0:T(8,128)(2,1)} %all-gather.5.cloned.1.call-done), kind=kOutput, calls=%fused_computation.88 | convolution fusion | flops 4985234432 | bytes 80155136 | tf_op jit(solution)/shard_map/dot_general | solution.py:92
  79.8 0.5 fusion.10
  80.8 39.3 %all-reduce.3 = (f32[2048]{0:T(1024)S(1)}, f32[2048]{0:T(1024)S(1)}, f32[2048]{0:T(1024)S(1)}) all-reduce(f32[2048]{0:T(1024)S(1)} %dynamic-update-slice, f32[2048]{0:T(1024)S(1)} %dynamic-update-slice.1, f32[2048]{0:T(1024)S(1)} %dynamic-update-slice.2), channel_id=2, replica_groups=mesh['vocab'=4,'ctx'=8] {'vocab','ctx'}, use_global_device_ids=true, to_apply=%add | all-reduce | flops 6144 | bytes 49152
  120.4 1.4 while.19
  121.8 0.6 subtract_reduce_fusion
  122.4 28.6 %convolution_bitcast_fusion = f32[8192,64]{0,1:T(8,128)} fusion(bf16[4752,8192]{1,0:T(8,128)(2,1)} %param.16, f32[64,4752]{1,0:T(8,128)S(1)} %get-tuple-element.218, f32[64]{0:T(128)S(1)} %get-tuple-element.209, s32[4752]{0:T(1024)S(1)} %iota_add_fusion, s32[64]{0:T(128)S(1)} %copy-done.8), kind=kOutput, calls=%fused_computation.13 | convolution fusion | flops 4984657920 | bytes 81189952 | tf_op jit(solution)/shard_map/dot_general | solution.py:110
  151.1 0.6 copy-done.9
  151.9 32.5 %reduce-scatter.4.cloned.1.call-done = f32[1024,64]{0,1:T(8,128)} async-done(((f32[8192,64]{0,1:T(8,128)}), f32[1024,64]{0,1:T(8,128)}) %reduce-scatter.4.cloned.1.call-update) | async-done | bytes 262160 | tf_op jit(solution)/shard_map/reduce_scatter | solution.py:109
  184.8 1.5 convert_element_type.42
  186.3 44.8 %all-reduce.6.cloned.1.call-done = f32[1024,64]{0,1:T(8,128)} async-done(((f32[1024,64]{0,1:T(8,128)}), f32[1024,64]{0,1:T(8,128)}) %all-reduce.6.cloned.1.call-update) | async-done | bytes 262160 | tf_op jit(solution)/shard_map/psum | solution.py:117
  231.0 1.2 fusion.36
  232.3 14.1 %psum.15 = f32[64]{0:T(128)S(1)} all-reduce(f32[64]{0:T(128)S(1)} %fusion.36), channel_id=1, replica_groups=mesh['vocab'=4,'ctx'=8] {'ctx'}, use_global_device_ids=true, to_apply=%region_13.15 | all-reduce | flops 64 | bytes 512 | tf_op jit(solution)/shard_map/psum | solution.py:122
  246.3 1.1 fusion.39
  247.5 4.5 %fusion.53 = f32[64,2048]{1,0:T(8,128)} fusion(bf16[1024,64]{0,1:T(8,128)(2,1)S(1)} %fusion.39, bf16[2048,1024]{1,0:T(8,128)(2,1)} %param.23), kind=kOutput, calls=%fused_computation.90 | convolution fusion | flops 268435456 | bytes 4849664 | tf_op jit(solution)/shard_map/dot_general | solution.py:131
  252.4 17.0 %all_gather.39 = bf16[1024,256]{0,1:T(8,128)(2,1)S(1)} all-gather(bf16[128,256]{0,1:T(8,128)(2,1)S(1)} %copy.71), channel_id=1, replica_groups=mesh['vocab'=4,'ctx'=8] {'ctx'}, dimensions={0}, use_global_device_ids=true | all-gather | bytes 589824 | tf_op jit(solution)/shard_map/all_gather | solution.py:140
  269.4 15.1 %all_gather.38 = bf16[1024,256]{0,1:T(8,128)(2,1)S(1)} all-gather(bf16[128,256]{0,1:T(8,128)(2,1)S(1)} %copy.68), channel_id=1, replica_groups=mesh['vocab'=4,'ctx'=8] {'ctx'}, dimensions={0}, use_global_device_ids=true | all-gather | bytes 589824 | tf_op jit(solution)/shard_map/all_gather | solution.py:139
  284.5 0.4 fusion.50
  285.0 0.8 convert_element_type.47
  285.9 0.8 fusion.25
  286.9 0.3 fusion.40
  288.0 1.3 copy.82
  289.4 2.9 pad_maximum_fusion
  293.2 0.6 copy.113
  293.9 28.9 %reduce-scatter.8.cloned.1.call-done = f32[128,512]{1,0:T(8,128)} async-done(((f32[1024,512]{1,0:T(8,128)}), f32[128,512]{1,0:T(8,128)}) %reduce-scatter.8.cloned.1.call-update) | async-done | bytes 262160 | tf_op jit(solution)/shard_map/reduce_scatter | solution.py:171
  322.7 1.0 convert.5
  323.7 0.7 fusion.48
  (96 shorter events, 4.8 us)
Async XLA Ops:
  7.2 1.1 copy-start
  7.2 37.0 %copy-start.7 = (f32[8192]{0:T(1024)S(1)}, f32[8192]{0:T(1024)}, u32[]{:S(2)}) copy-start(f32[8192]{0:T(1024)} %param.15) | copy-start | bytes 98308
  7.2 35.5 %all-gather.5.cloned.1.call-start = ((), (), s32[]{:S(2)}) async-start(), calls=%async_computation.3 | async-start | bytes 1179648 | tf_op jit(solution)/shard_map/all_gather | solution.py:88
  10.6 273.9 %copy-start.3 = (bf16[8,2048]{1,0:T(8,128)(2,1)}, bf16[8,2048]{1,0:T(8,128)(2,1)S(1)}, u32[]{:S(2)}) copy-start(bf16[8,2048]{1,0:T(8,128)(2,1)S(1)} %get-tuple-element.215) | copy-start | bytes 98308
  17.7 166.6 %reduce-scatter.4.cloned.1.call-start = ((), (), s32[]{:S(2)}) async-start(), calls=%async_computation.4 | async-start | bytes 2359296 | tf_op jit(solution)/shard_map/reduce_scatter | solution.py:109
  44.2 35.5 %copy-start.8 = (s32[64]{0:T(128)S(1)}, s32[64]{0:T(128)}, u32[]{:S(2)}) copy-start(s32[64]{0:T(128)} %param.17) | copy-start | bytes 772
  151.0 0.7 copy-start.9
  151.0 33.8 %copy-start.1 = (bf16[64,8192]{1,0:T(8,128)(2,1)S(1)}, bf16[64,8192]{1,0:T(8,128)(2,1)}, u32[]{:S(2)}) copy-start(bf16[64,8192]{1,0:T(8,128)(2,1)} %all-gather.5.cloned.1.call-done) | copy-start | bytes 3145732
  151.0 80.0 %all-reduce.6.cloned.1.call-start = ((), (), s32[]{:S(2)}) async-start(), calls=%async_computation.5 | async-start | bytes 524288 | tf_op jit(solution)/shard_map/psum | solution.py:117
  184.4 100.7 %reduce-scatter.6.cloned.1.call-start = ((), (), s32[]{:S(2)}) async-start(), calls=%async_computation.6 | async-start | bytes 589824 | tf_op jit(solution)/shard_map/reduce_scatter | solution.py:130
  247.5 4.5 %copy-start.2 = (bf16[1024,64]{0,1:T(8,128)(2,1)}, bf16[1024,64]{0,1:T(8,128)(2,1)S(1)}, u32[]{:S(2)}) copy-start(bf16[1024,64]{0,1:T(8,128)(2,1)S(1)} %fusion.39) | copy-start | bytes 393220
  247.5 4.6 %copy-start.5 = (bf16[128,256]{1,0:T(8,128)(2,1)S(1)}, bf16[128,256]{1,0:T(8,128)(2,1)}, u32[]{:S(2)}) copy-start(bf16[128,256]{1,0:T(8,128)(2,1)} %param.22) | copy-start | bytes 196612
  247.5 4.7 %copy-start.6 = (bf16[128,256]{1,0:T(8,128)(2,1)S(1)}, bf16[128,256]{1,0:T(8,128)(2,1)}, u32[]{:S(2)}) copy-start(bf16[128,256]{1,0:T(8,128)(2,1)} %param.21) | copy-start | bytes 196612
  252.0 70.7 %reduce-scatter.8.cloned.1.call-start = ((), (), s32[]{:S(2)}) async-start(), calls=%async_computation.7 | async-start | bytes 2359296 | tf_op jit(solution)/shard_map/reduce_scatter | solution.py:171
  286.9 0.8 copy-start.4
Sparse Core Ops, SparseCore 0:
  17.8 24.7 all-gather.4
  151.1 33.1 reduce-scatter.3
  187.3 43.6 all-reduce.5
  252.1 28.5 reduce-scatter.5
  292.4 30.3 reduce-scatter.7
where the time goes:
time: 337 us; the launch traced here: 332 us
  waiting for transfers between devices  131 us (39%)
  blocking collectives  92.6 us (27%)
  matrix products  70.7 us (21%)
  between operations  15.8 us (5%)
  other arithmetic  13.5 us (4%)
  local copies, waits for them, and re-layouts  7.51 us (2%)
    psum x1, waiting for transfers between devices, per_device(): normed_grad = lax.psum(partial_rows, 'vocab')  44.8 us
    unnamed x1, blocking collectives  39.3 us
    dot_general x1, matrix products, per_device(): lax.dot_general(head_weight, normed, (((1,), (1,)), ((), ())), preferred_...  35.2 us
    reduce_scatter x1, waiting for transfers between devices, per_device(): lax.psum_scatter(lax.dot_general(head_weight, logit_grad, (((0,), (0,)),...  32.5 us
    reduce_scatter x1, waiting for transfers between devices, per_device(): lax.psum_scatter(jnp.concatenate([key_term.reshape(device_rows * lax.axis...  28.9 us
    dot_general x1, matrix products, per_device(): lax.dot_general(head_weight, logit_grad, (((0,), (0,)), ((), ())), prefer...  28.6 us
    all_gather x1, waiting for transfers between devices, per_device(): rows_all = lax.all_gather(wide_rows, 'ctx', axis=0, tiled=True)  24.9 us
    all_gather x1, blocking collectives, per_device(): lax.all_gather(attention_values, 'ctx', axis=0, tiled=True)  17 us
  transfers between devices with their start and end apart: 5, of which 4 were waited for; matrix products, arithmetic and copies ran while one was open for 1% of the time, Pallas kernels for 0%

commit v1 on v0

v1 whole, which is shorter than its diff:
```python
import functools

import jax
import jax.numpy as jnp
from jax import lax
from jax.experimental import pallas as pl
from jax.experimental.pallas import tpu as pltpu
from jax.sharding import PartitionSpec as P

HEAD_SIZE = 128
CORES = 2
CHUNK = 512
SLOTS = 3
LANES = 128

norm_eps = 1e-06
grad_weight = 16.0
masked_fill = -1e30

f32 = jnp.float32
bf16 = jnp.bfloat16

NT = (((1,), (1,)), ((), ()))
NN = (((1,), (0,)), ((), ()))
TN = (((0,), (0,)), ((), ()))


def dot(a, b, dims):
    return lax.dot_general(a, b, dims, preferred_element_type=f32)


def smem():
    return pl.BlockSpec(memory_space=pltpu.SMEM)


def vmem():
    return pl.BlockSpec(memory_space=pltpu.VMEM)


def shape(dims, dtype):
    return jax.ShapeDtypeStruct(dims, dtype)


def call(body, outs, ins, scratch=(), limit=48, flops=0, moved=0, exps=0):
    return pl.pallas_call(
        body,
        out_shape=outs,
        in_specs=ins,
        out_specs=jax.tree.map(lambda _: vmem(), outs),
        scratch_shapes=list(scratch),
        compiler_params=pltpu.CompilerParams(vmem_limit_bytes=limit * 2**20),
        cost_estimate=pl.CostEstimate(flops=flops, bytes_accessed=moved, transcendentals=exps),
    )


def shifted(value, axis, step, inner=1, ring=None):
    size = lax.axis_size(axis)
    outer = size // inner
    pairs = [(i, ((i // inner + step) % outer) * inner + i % inner) for i in range(size)]
    return lax.ppermute(value, axis, pairs)


def swapped(value):
    size = lax.axis_size("ctx")
    return lax.ppermute(value, "ctx", [(i, i ^ 1) for i in range(size)])


def pick_body(loss_per, place, rows, hidden, queries, keys, values, picked, packed):
    base = place[3] * loss_per
    tokens, width = hidden.shape
    row_iota = lax.broadcasted_iota(jnp.int32, (loss_per, tokens), 0)
    col_iota = lax.broadcasted_iota(jnp.int32, (loss_per, tokens), 1)
    sel = jnp.zeros((loss_per, tokens), f32)
    for j in range(loss_per):
        sel = jnp.where((row_iota == j) & (col_iota == rows[base + j]), 1.0, sel)
    sel = sel.astype(bf16)
    mine = dot(sel, hidden[...], NN)
    half = width // 2
    picked[...] = jnp.concatenate([mine[:, :half], mine[:, half:]], axis=0).astype(bf16)
    mine = dot(sel, queries[...], NN)
    key_width = keys.shape[1]
    packed[0:tokens, 0:key_width] = keys[...]
    packed[0:tokens, key_width : 2 * key_width] = values[...]
    parts = queries.shape[1] // (2 * key_width)
    stacked = [mine[:, b * 2 * key_width : (b + 1) * 2 * key_width] for b in range(parts)]
    packed[tokens : tokens + parts * loss_per, :] = jnp.concatenate(stacked, axis=0).astype(bf16)


def flash_body(
    first,
    place,
    own,
    other,
    gain,
    targets,
    weight,
    keep,
    send,
    stats,
    unit,
    normed,
    raw,
    acc,
    probs,
    state,
    head_buf,
    buf,
    head_sem,
    sems,
):
    vocab_at, z_at, core_at, ctx_at, first_id = (place[k] for k in range(5))
    nv, nz = own.shape[0], own.shape[1]
    loss, width = normed.shape
    half = own.shape[3]
    total_rows = weight.shape[0]
    chunks = (total_rows - first) // CHUNK
    blocks = acc.shape[0]
    block_width = width // blocks

    def head_copy():
        return pltpu.make_async_copy(weight.at[pl.ds(0, first), :], head_buf, head_sem)

    def body_copy(c):
        slot = lax.rem(c, SLOTS)
        start = pl.multiple_of(first + c * CHUNK, 16)
        return pltpu.make_async_copy(
            weight.at[pl.ds(start, CHUNK), :], buf.at[slot], sems.at[slot]
        )

    head_copy().start()
    for c in range(min(SLOTS, chunks)):
        body_copy(c).start()

    is_even = core_at == 0
    for zr in range(nz):
        z_src = lax.rem(z_at - zr + nz, nz)
        square_own = jnp.zeros((8, 1), f32)
        square_other = jnp.zeros((8, 1), f32)
        for vr in range(nv):
            a = own[vr, zr].astype(f32)
            b = other[vr, zr].astype(f32)
            square_a = jnp.sum(a * a, axis=1, keepdims=True)
            square_b = jnp.sum(b * b, axis=1, keepdims=True)
            square_own += square_a[:8] + square_a[8:]
            square_other += square_b[:8] + square_b[8:]
        square = jnp.concatenate(
            [
                jnp.where(is_even, square_own, square_other),
                jnp.where(is_even, square_other, square_own),
            ],
            axis=0,
        )
        inv = lax.rsqrt(square / width + norm_eps)
        row_at = pl.multiple_of(z_src * 16, 16)
        state[pl.ds(row_at, 16), :] = jnp.broadcast_to(inv, (16, LANES))
        for vr in range(nv):
            v_src = lax.rem(vocab_at - vr + nv, nv)
            a = own[vr, zr].astype(f32)
            b = other[vr, zr].astype(f32)
            low = jnp.where(is_even, a, b)
            high = jnp.where(is_even, b, a)
            for k in range(2):
                x = jnp.concatenate([low[8 * k : 8 * k + 8], high[8 * k : 8 * k + 8]], axis=0)
                lane_at = pl.multiple_of((v_src * 2 + k) * half, half)
                raw[pl.ds(row_at, 16), pl.ds(lane_at, half)] = x.astype(bf16)
                normed[pl.ds(row_at, 16), pl.ds(lane_at, half)] = (
                    x * inv * gain[:, pl.ds(lane_at, half)]
                ).astype(bf16)

    per_vocab = loss // nv
    mine_at = pl.multiple_of(vocab_at * per_vocab, per_vocab)
    feature_at = pl.multiple_of(ctx_at * block_width, block_width)
    unit[...] = (
        raw[pl.ds(mine_at, per_vocab), pl.ds(feature_at, block_width)].astype(f32)
        * state[pl.ds(mine_at, per_vocab), 0:1]
    )

    target_col = targets[...]

    def softmax(scores, base, before):
        cols = scores.shape[1]
        ids = base + lax.broadcasted_iota(jnp.int32, (loss, cols), 1)
        hit = ids == target_col
        top = jnp.max(scores, axis=1, keepdims=True)
        if before is not None:
            top = jnp.maximum(top, before[0])
        shifted_scores = scores - top
        weights = jnp.exp(shifted_scores)
        total = jnp.sum(weights, axis=1, keepdims=True)
        moment = jnp.sum(weights * shifted_scores, axis=1, keepdims=True)
        logit = jnp.sum(jnp.where(hit, scores, 0.0), axis=1, keepdims=True)
        scale = None
        if before is not None:
            gap = before[0] - top
            scale = jnp.exp(gap)
            total = total + before[1] * scale
            moment = moment + scale * (before[2] + gap * before[1])
            logit = logit + before[3]
        masked = jnp.where(hit, 0.0, weights).astype(bf16)
        return masked, scale, (top, total, moment, logit)

    def scores_of(block):
        return dot(normed[...], block, NT)

    def add_product(p, scale, read):
        for b in range(blocks):
            part = dot(p, read(b * block_width, block_width), NN)
            if scale is None:
                acc[b] = part
            else:
                acc[b] = acc[b] * scale + part

    head_copy().wait()
    p, _, run = softmax(scores_of(head_buf[...]), first_id, None)
    add_product(p, None, lambda at, n: head_buf[:, at : at + n])
    if chunks:
        body_copy(0).wait()
        p, scale, run = softmax(scores_of(buf[0]), first_id + first, run)
        probs[...] = p

        def step(c, carry):
            scale, run = carry
            body_copy(c).wait()
            here = lax.rem(c, SLOTS)
            there = lax.rem(c - 1, SLOTS)
            scores = scores_of(buf[here])
            add_product(probs[...], scale, lambda at, n: buf[there, :, at : at + n])

            @pl.when(c + SLOTS - 1 < chunks)
            def _():
                body_copy(c + SLOTS - 1).start()

            p, scale, run = softmax(scores, first_id + first + c * CHUNK, run)
            probs[...] = p
            return scale, run

        scale, run = lax.fori_loop(1, chunks, step, (scale, run))
        last = (chunks - 1) % SLOTS
        add_product(probs[...], scale, lambda at, n: buf[last, :, at : at + n])

    for z in range(nz):
        keep[z] = acc[CORES * z + core_at]
        send[z] = acc[CORES * z + 1 - core_at].astype(bf16)
    lane = lax.broadcasted_iota(jnp.int32, (loss, LANES), 1)
    table = state[...]
    for k in range(4):
        table = jnp.where(lane == k, run[k], table)
    stats[...] = table


def merge_stats(tables):
    columns = [[t[:, k : k + 1] for k in range(4)] for t in tables]
    top = functools.reduce(jnp.maximum, [c[0] for c in columns])
    gaps = [c[0] - top for c in columns]
    scales = [jnp.exp(g) for g in gaps]
    total = sum(s * c[1] for s, c in zip(scales, columns))
    moment = sum(s * (c[2] + g * c[1]) for s, g, c in zip(scales, gaps, columns))
    logit = sum(c[3] for c in columns)
    return scales, (top, total, moment, logit)


def with_stats(table, merged):
    lane = lax.broadcasted_iota(jnp.int32, table.shape, 1)
    for k in range(4):
        table = jnp.where(lane == k, merged[k], table)
    return table


def core_body(count, place, keep, got, mine, theirs, new_stats, new_keep, *sends_and_scratch):
    sends, (total,) = sends_and_scratch[:count], sends_and_scratch[count:]
    scales, merged = merge_stats([mine[...], theirs[...]])
    new_stats[...] = with_stats(mine[...], merged)
    nz, loss, _ = keep.shape
    per = loss // (count + 1)
    for z in range(nz):
        total[z] = keep[z] * scales[0] + got[z].astype(f32) * scales[1]
    new_keep[...] = total[:, pl.ds(pl.multiple_of(place[0] * per, per), per), :]
    for s in range(count):
        to = lax.rem(place[0] + s + 1, count + 1)
        sends[s][...] = total[:, pl.ds(pl.multiple_of(to * per, per), per), :].astype(bf16)


def plane_body(count, nz, place, keep, *refs):
    got, refs = refs[:count], refs[count:]
    tables, refs = refs[: count + 1], refs[count + 1 :]
    new_stats, new_keep = refs[:2]
    sends, (scale_ref, total) = refs[2 : 1 + nz], refs[1 + nz :]
    scales, merged = merge_stats([t[...] for t in tables])
    new_stats[...] = with_stats(tables[0][...], merged)
    per = keep.shape[1]
    at = pl.multiple_of(place[0] * per, per)
    for k in range(count + 1):
        scale_ref[k] = jnp.broadcast_to(scales[k], scale_ref.shape[1:])
    factors = [scale_ref[k, pl.ds(at, per), 0:1] for k in range(count + 1)]
    for z in range(nz):
        value = keep[z] * factors[0]
        for k in range(count):
            value = value + got[k][z].astype(f32) * factors[k + 1]
        total[z] = value
    new_keep[...] = total[place[1]]
    for s in range(nz - 1):
        sends[s][...] = total[lax.rem(place[1] + s + 1, nz)].astype(bf16)


def line_body(nz, width, place, keep, *refs):
    got, refs = refs[: nz - 1], refs[nz - 1 :]
    tables, refs = refs[:nz], refs[nz:]
    target_rows, unit, gain, resid, loss_out, scale_ref, final = refs
    scales, merged = merge_stats([t[...] for t in tables])
    top, total, moment, logit = merged
    log_total = top + jnp.log(total)
    loss_out[...] = jnp.broadcast_to(
        jnp.mean(log_total - logit, axis=0, keepdims=True), loss_out.shape
    )
    per, block_width = keep.shape
    at = pl.multiple_of(place[0] * per, per)
    for k in range(nz):
        scale_ref[k] = jnp.broadcast_to(scales[k] / total, scale_ref.shape[1:])
    value = keep[...] * scale_ref[0, pl.ds(at, per), 0:1]
    for k in range(nz - 1):
        value = value + got[k][...].astype(f32) * scale_ref[k + 1, pl.ds(at, per), 0:1]
    inner_all = grad_weight * (moment / total + (top - logit)) / width
    short_all = jnp.exp(logit - log_total) - 1.0
    lane = lax.broadcasted_iota(jnp.int32, final.shape, 1)
    final[...] = jnp.where(
        lane == 0, inner_all, jnp.where(lane == 1, short_all, tables[0][...])
    )
    inner = final[pl.ds(at, per), 0:1]
    short = final[pl.ds(at, per), 1:2]
    inv = final[pl.ds(at, per), 4:5]
    grad = grad_weight * (value + short * target_rows[...].astype(f32))
    gain_at = pl.multiple_of(place[3] * block_width, block_width)
    scaled = grad * gain[:, pl.ds(gain_at, block_width)]
    resid[...] = (inv * (scaled - unit[...] * inner)).astype(bf16)


def project_body(nv, nc, place, *refs):
    pieces, refs = refs[:nv], refs[nv:]
    weight, resid, keep = refs[:3]
    sends, (whole, partial) = refs[3 : 2 + nc], refs[2 + nc :]
    per = pieces[0].shape[0]
    for s in range(nv):
        src = lax.rem(place[0] - s + nv, nv)
        whole[pl.ds(pl.multiple_of(src * per, per), per), :] = pieces[s][...]
    resid[...] = whole[...]
    partial[...] = dot(whole[...], weight[...], NT)
    rows, cols = keep.shape
    for s in range(nc):
        to = lax.rem(place[3] + s, nc)
        row_at = pl.multiple_of(lax.div(to, CORES) * rows, rows)
        col_at = pl.multiple_of(lax.rem(to, CORES) * cols, cols)
        value = partial[pl.ds(row_at, rows), pl.ds(col_at, cols)]
        if s == 0:
            keep[...] = value
        else:
            sends[s - 1][...] = value.astype(bf16)


def sum_body(keep, *refs):
    value = keep[...]
    for ref in refs[:-1]:
        value = value + ref[...].astype(f32)
    refs[-1][...] = value.astype(bf16)


def forward_body(
    loss_per, heads, group, heads_at_once, place, key_pos, query_pos, packed, p_own, p_rows, out, scratch
):
    nc = packed.shape[0]
    tokens = p_own.shape[2]
    loss = loss_per * nc
    key_width = heads * HEAD_SIZE
    score_scale = HEAD_SIZE ** (-0.5)
    ctx_at = place[3]
    own_at = pl.multiple_of(ctx_at * tokens, tokens)
    row_at = pl.multiple_of(ctx_at * loss_per, loss_per)
    for j in range(heads):
        key = jnp.concatenate(
            [packed[c, 0:tokens, j * HEAD_SIZE : (j + 1) * HEAD_SIZE] for c in range(nc)], axis=0
        )
        at = key_width + j * HEAD_SIZE
        value = jnp.concatenate(
            [packed[c, 0:tokens, at : at + HEAD_SIZE] for c in range(nc)], axis=0
        )
        for g0 in range(0, group, heads_at_once):
            stacked = []
            for g in range(g0, g0 + heads_at_once):
                stacked.append(query_of(packed, j * group + g, tokens, loss_per, key_width))
            query = jnp.concatenate(stacked, axis=0).astype(bf16)
            where_at = jnp.concatenate([query_pos[...]] * heads_at_once, axis=0)
            visible = key_pos[...] <= where_at
            scores = jnp.where(visible, dot(query, key, NT) * score_scale, masked_fill)
            top = jnp.max(scores, axis=1, keepdims=True)
            raw = jnp.where(visible, jnp.exp(scores - top), 0.0)
            prob = raw / jnp.sum(raw, axis=1, keepdims=True)
            scratch[...] = prob
            coarse = prob.astype(bf16)
            fine = (prob - coarse.astype(f32)).astype(bf16)
            first = g0 * loss
            n = heads_at_once * loss
            out[j, first : first + n, :] = dot(coarse, value, NN) + dot(fine, value, NN)
            p_own[j, first : first + n, :] = scratch[:, pl.ds(own_at, tokens)]
            for k in range(heads_at_once):
                p_rows[j, (g0 + k) * loss_per : (g0 + k + 1) * loss_per, :] = scratch[
                    pl.ds(pl.multiple_of(k * loss + row_at, loss_per), loss_per), :
                ]


def query_of(packed, head, tokens, loss_per, key_width):
    lane = head * HEAD_SIZE
    b, at = lane // (2 * key_width), lane % (2 * key_width)
    parts = []
    for c in range(packed.shape[0]):
        block = packed[c, tokens:, at : at + HEAD_SIZE].astype(f32)
        parts.append(block[b * loss_per : (b + 1) * loss_per])
    return jnp.concatenate(parts, axis=0)


def backward_body(loss_per, heads, group, nc, place, *refs):
    pieces, refs = refs[:nc], refs[nc:]
    packed, p_own, p_rows, out, query_grad, key_grad, value_grad, grad = refs
    tokens = p_own.shape[2]
    loss = loss_per * nc
    key_width = heads * HEAD_SIZE
    score_scale = HEAD_SIZE ** (-0.5)
    ctx_at = place[3]
    rows, cols = pieces[0].shape
    for s in range(nc):
        src = lax.rem(ctx_at - s + nc, nc)
        row_at = pl.multiple_of(lax.div(src, CORES) * rows, rows)
        col_at = pl.multiple_of(lax.rem(src, CORES) * cols, cols)
        grad[pl.ds(row_at, rows), pl.ds(col_at, cols)] = pieces[s][...].astype(f32)
    mine_at = pl.multiple_of(ctx_at * loss_per, loss_per)
    for j in range(heads):
        lanes = [slice((j * group + g) * HEAD_SIZE, (j * group + g + 1) * HEAD_SIZE) for g in range(group)]
        d_out = jnp.concatenate([grad[:, s] for s in lanes], axis=0)
        d_half = d_out.astype(bf16)
        delta = jnp.sum(d_out * out[j], axis=1, keepdims=True)
        query = jnp.concatenate(
            [query_of(packed, j * group + g, tokens, loss_per, key_width) for g in range(group)], axis=0
        ).astype(bf16)
        at = key_width + j * HEAD_SIZE
        own_value = packed[ctx_at, 0:tokens, at : at + HEAD_SIZE]
        prob = p_own[j]
        score_grad = (prob * (dot(d_half, own_value, NT) - delta)).astype(bf16)
        k_lanes = slice(j * HEAD_SIZE, (j + 1) * HEAD_SIZE)
        key_grad[:, k_lanes] = (dot(score_grad, query, TN) * score_scale).astype(bf16)
        value_grad[:, k_lanes] = dot(prob.astype(bf16), d_half, TN).astype(bf16)
        key = jnp.concatenate([packed[c, 0:tokens, k_lanes] for c in range(nc)], axis=0)
        value = jnp.concatenate([packed[c, 0:tokens, at : at + HEAD_SIZE] for c in range(nc)], axis=0)
        d_mine = jnp.concatenate([grad[pl.ds(mine_at, loss_per), s] for s in lanes], axis=0)
        out_mine = jnp.concatenate(
            [
                out[j, pl.ds(pl.multiple_of(g * loss + mine_at, loss_per), loss_per), :]
                for g in range(group)
            ],
            axis=0,
        )
        delta = jnp.sum(d_mine * out_mine, axis=1, keepdims=True)
        d_prob = dot(d_mine.astype(bf16), value, NT)
        score_grad = (p_rows[j] * (d_prob - delta)).astype(bf16)
        result = dot(score_grad, key, NN) * score_scale
        for g in range(group):
            query_grad[:, lanes[g]] = result[g * loss_per : (g + 1) * loss_per].astype(bf16)


def per_device(
    hidden,
    norm_gain,
    head_weight,
    targets,
    loss_rows,
    stretch_of_slot,
    queries,
    key_states,
    attention_values,
    output_weight,
):
    nc = lax.axis_size("ctx")
    nv = lax.axis_size("vocab")
    nz = nc // CORES
    ctx_at = lax.axis_index("ctx")
    vocab_at = lax.axis_index("vocab")
    tokens = hidden.shape[0]
    stretch_len = tokens // 2
    loss = loss_rows.shape[0]
    loss_per = loss // nc
    width = norm_gain.shape[0]
    voc_rows = head_weight.shape[0]
    part_width = hidden.shape[1]
    query_width = queries.shape[1]
    key_width = key_states.shape[1]
    heads = key_width // HEAD_SIZE
    group = query_width // key_width
    block_width = width // nc
    per_vocab = loss // nv
    all_tokens = tokens * nc

    first_id = (vocab_at * nc + ctx_at) * voc_rows
    place = jnp.stack([vocab_at, ctx_at // CORES, ctx_at % CORES, ctx_at, first_id]).astype(jnp.int32)

    slots = stretch_of_slot.shape[0]
    owner = lax.broadcasted_iota(jnp.int32, (loss, 1), 0) // loss_per
    slot = 2 * owner + loss_rows[:, None] // stretch_len
    slot_iota = lax.broadcasted_iota(jnp.int32, (1, slots), 1)
    stretch = jnp.sum(jnp.where(slot == slot_iota, stretch_of_slot[None, :], 0), axis=1, keepdims=True)
    query_pos = stretch * stretch_len + loss_rows[:, None] % stretch_len
    key_pos = (
        stretch_of_slot[:, None] * stretch_len
        + lax.broadcasted_iota(jnp.int32, (1, stretch_len), 1)
    ).reshape(1, all_tokens)
    local = targets - first_id
    is_local = (local >= 0) & (local < voc_rows)
    target_rows = head_weight.at[jnp.clip(local, 0, voc_rows - 1)].get(mode="promise_in_bounds")
    target_rows = jnp.where(is_local[:, None], target_rows, jnp.zeros((), bf16))

    extra = (query_width // (2 * key_width)) * loss_per
    picked, packed = call(
        functools.partial(pick_body, loss_per),
        (
            shape((2 * loss_per, part_width // 2), bf16),
            shape((tokens + extra, 2 * key_width), bf16),
        ),
        [smem(), smem()] + [vmem()] * 4,
    )(place, loss_rows, hidden, queries, key_states, attention_values)
    by_z = jnp.stack([picked] + [shifted(picked, "ctx", s, CORES) for s in range(1, nz)])
    by_plane = jnp.stack([by_z] + [shifted(by_z, "vocab", s) for s in range(1, nv)])
    other = swapped(by_plane)

    target_blocks = (
        target_rows.reshape(nv, per_vocab, nc, block_width)
        .transpose(2, 0, 1, 3)
        .reshape(nc * nv * per_vocab, block_width)
    )
    other, packed, target_blocks = lax.optimization_barrier((other, packed, target_blocks))
    packed_all = lax.all_gather(packed, "ctx")
    target_mine = lax.psum_scatter(
        target_blocks, ("ctx", "vocab"), scatter_dimension=0, tiled=True
    )

    first = voc_rows % CHUNK
    if voc_rows < SLOTS * CHUNK or first % 16 or not first:
        first = voc_rows if voc_rows < SLOTS * CHUNK else CHUNK
    chunks = (voc_rows - first) // CHUNK
    gain = norm_gain.reshape(1, width)
    keep, send, stats, unit = pl.pallas_call(
        functools.partial(flash_body, first),
        out_shape=(
            shape((nz, loss, block_width), f32),
            shape((nz, loss, block_width), bf16),
            shape((loss, LANES), f32),
            shape((per_vocab, block_width), f32),
        ),
        in_specs=[smem()] + [vmem()] * 4 + [pl.BlockSpec(memory_space=pl.ANY)],
        out_specs=[vmem()] * 4,
        scratch_shapes=[
            pltpu.VMEM((loss, width), bf16),
            pltpu.VMEM((loss, width), bf16),
            pltpu.VMEM((nc, loss, block_width), f32),
            pltpu.VMEM((loss, CHUNK), bf16),
            pltpu.VMEM((loss, LANES), f32),
            pltpu.VMEM((first, width), bf16),
            pltpu.VMEM((SLOTS if chunks else 1, CHUNK if chunks else 16, width), bf16),
            pltpu.SemaphoreType.DMA,
            pltpu.SemaphoreType.DMA((SLOTS,)),
        ],
        compiler_params=pltpu.CompilerParams(vmem_limit_bytes=50 * 2**20),
        cost_estimate=pl.CostEstimate(
            flops=4 * loss * width * voc_rows,
            bytes_accessed=2 * width * voc_rows,
            transcendentals=loss * voc_rows,
        ),
    )(place, by_plane, other, gain, targets.reshape(loss, 1), head_weight)

    at_once = max(1, min(group, (4 * 2**20) // (loss * all_tokens * 4)))
    p_own, p_rows, out = call(
        functools.partial(forward_body, loss_per, heads, group, at_once),
        (
            shape((heads, group * loss, tokens), f32),
            shape((heads, group * loss_per, all_tokens), f32),
            shape((heads, group * loss, HEAD_SIZE), f32),
        ),
        [smem()] + [vmem()] * 3,
        [pltpu.VMEM((at_once * loss, all_tokens), f32)],
        flops=6 * heads * group * loss * all_tokens * HEAD_SIZE,
        moved=2 * packed_all.size,
        exps=heads * group * loss * all_tokens,
    )(place, key_pos, query_pos, packed_all)

    got, got_stats = swapped(send), swapped(stats)
    stats, keep, *sends = call(
        functools.partial(core_body, nv - 1),
        (
            shape((loss, LANES), f32),
            shape((nz, per_vocab, block_width), f32),
        )
        + (shape((nz, per_vocab, block_width), bf16),) * (nv - 1),
        [smem()] + [vmem()] * 4,
        [pltpu.VMEM((nz, loss, block_width), f32)],
    )(place, keep, got, stats, got_stats)
    got = [shifted(sends[s - 1], "vocab", s) for s in range(1, nv)]
    tables = [stats] + [shifted(stats, "vocab", s) for s in range(1, nv)]
    stats, keep, *sends = call(
        functools.partial(plane_body, nv - 1, nz),
        (shape((loss, LANES), f32), shape((per_vocab, block_width), f32))
        + (shape((per_vocab, block_width), bf16),) * (nz - 1),
        [smem()] + [vmem()] * (1 + (nv - 1) + nv),
        [
            pltpu.VMEM((nv, loss, LANES), f32),
            pltpu.VMEM((nz, per_vocab, block_width), f32),
        ],
    )(place, keep, *got, *tables)
    got = [shifted(sends[s - 1], "ctx", s, CORES) for s in range(1, nz)]
    tables = [stats] + [shifted(stats, "ctx", s, CORES) for s in range(1, nz)]
    resid, mean_loss = call(
        functools.partial(line_body, nz, width),
        (shape((per_vocab, block_width), bf16), shape((8, LANES), f32)),
        [smem()] + [vmem()] * (1 + (nz - 1) + nz + 3),
        [pltpu.VMEM((nz, loss, LANES), f32), pltpu.VMEM((loss, LANES), f32)],
    )(place, keep, *got, *tables, target_mine, unit, gain)

    pieces = [resid] + [shifted(resid, "vocab", s) for s in range(1, nv)]
    rows, cols = loss // nz, query_width // CORES
    resid_rows, keep, *sends = call(
        functools.partial(project_body, nv, nc),
        (shape((loss, block_width), bf16), shape((rows, cols), f32))
        + (shape((rows, cols), bf16),) * (nc - 1),
        [smem()] + [vmem()] * (nv + 1),
        [pltpu.VMEM((loss, block_width), bf16), pltpu.VMEM((loss, query_width), f32)],
    )(place, *pieces, output_weight)
    got = [shifted(sends[s - 1], "ctx", s) for s in range(1, nc)]
    piece = call(sum_body, shape((rows, cols), bf16), [vmem()] * nc)(keep, *got)
    pieces = [piece] + [shifted(piece, "ctx", s) for s in range(1, nc)]
    query_grad, key_grad, value_grad = call(
        functools.partial(backward_body, loss_per, heads, group, nc),
        (
            shape((loss_per, query_width), bf16),
            shape((tokens, key_width), bf16),
            shape((tokens, key_width), bf16),
        ),
        [smem()] + [vmem()] * (nc + 4),
        [pltpu.VMEM((loss, query_width), f32)],
    )(place, *pieces, packed_all, p_own, p_rows, out)
    return (mean_loss[0, 0], query_grad, key_grad, value_grad, resid_rows.T)


def solution(mesh):
    placed = (
        P("ctx", "vocab"),
        P(),
        P(("vocab", "ctx"), None),
        P(),
        P(),
        P(),
        P("ctx", "vocab"),
        P("ctx", "vocab"),
        P("ctx", "vocab"),
        P("vocab", "ctx"),
    )
    return jax.shard_map(
        per_device,
        mesh=mesh,
        in_specs=placed,
        out_specs=(P(), P("ctx", "vocab"), P("ctx", "vocab"), P("ctx", "vocab"), P("ctx", None)),
        check_vma=False,
    )
```

time: 337 us -> 229 us (0.68); the launches traced: 332 us -> 228 us
  blocking collectives: 92.6 us -> 0 us
  matrix products: 70.7 us -> 0 us
  Pallas kernels: 0 us -> 61.1 us
  waiting for transfers between devices: 131 us -> 77.8 us
  starting transfers between devices: 0.2 us -> 50.1 us
  local copies, waits for them, and re-layouts: 7.51 us -> 19.4 us
  other arithmetic: 13.5 us -> 3.8 us
    dot_general x8 -> x0, matrix products: 70.3 us -> none  [the longest x1 35.2 us: per_device(): lax.dot_general(head_weight, normed, (((1,), (1,)), ((), ())), preferred_...]
    pallas_call x0 -> x9, Pallas kernels: none -> 61.1 us  [the longest x1 47.7 us: per_device(): pl.pallas_call(functools.partial(flash_body, first), out_shape=(shape((nz...]
    ppermute x0 -> x38, starting transfers between devices: none -> 49.9 us  [the longest x35 45.9 us: shifted(): return lax.ppermute(value, axis, pairs)]
    psum x1 -> x0, waiting for transfers between devices: 44.8 us -> none  [per_device(): normed_grad = lax.psum(partial_rows, 'vocab')]
    unnamed x1 -> x0, blocking collectives: 39.3 us -> none
    all_gather x3 -> x0, blocking collectives: 39.2 us -> none  [the longest x1 17 us: per_device(): lax.all_gather(attention_values, 'ctx', axis=0, tiled=True)]
    ppermute x0 -> x38, waiting for transfers between devices: none -> 25.5 us  [the longest x35 24 us: shifted(): return lax.ppermute(value, axis, pairs)]
    all_gather x1, waiting for transfers between devices: 24.9 us -> 0.01 us  [per_device(): packed_all = lax.all_gather(packed, 'ctx')]
  transfers between devices with their start and end apart: 5 -> 40, of which waited for: 4 -> 15; matrix products, arithmetic and copies ran while one was open for 1% -> 5% of each run, Pallas kernels for 0% -> 25%
where the time goes in v1:
time: 229 us; the launch traced here: 228 us
  waiting for transfers between devices  77.8 us (34%)
  Pallas kernels  61.1 us (27%)
  starting transfers between devices  50.1 us (22%)
  local copies, waits for them, and re-layouts  19.4 us (8%)
  between operations  15.7 us (7%)
  other arithmetic  3.8 us (2%)
    reduce_scatter x1, waiting for transfers between devices, per_device(): lax.psum_scatter(target_blocks, ('ctx', 'vocab'), scatter_dimension=0, ti...  52.3 us
    pallas_call x1, Pallas kernels, per_device(): pl.pallas_call(functools.partial(flash_body, first), out_shape=(shape((nz...  47.7 us
    ppermute x35, starting transfers between devices, shifted(): return lax.ppermute(value, axis, pairs)  45.9 us
    ppermute x35, waiting for transfers between devices, shifted(): return lax.ppermute(value, axis, pairs)  24 us
    unnamed x27, local copies, waits for them, and re-layouts  11.4 us
    gather x1, local copies, waits for them, and re-layouts, per_device(): head_weight.at[jnp.clip(local, 0, voc_rows - 1)]  6.46 us
  transfers between devices with their start and end apart: 40, of which 15 were waited for; matrix products, arithmetic and copies ran while one was open for 5% of the time, Pallas kernels for 25%

profile of v1, /device:TPU:3, one launch (start us, length us, event | category | flops | bytes accessed | tf_op | source)
XLA Modules:
  0.0 227.9 jit_solution(5103234579188210810)
XLA Ops:
  12.6 1.5 shard_map.137
  15.4 2.3 %collective-permute-start.1 = (bf16[16,1024]{1,0:T(8,128)(2,1)S(1)}, bf16[16,1024]{1,0:T(8,128)(2,1)S(1)}, u32[]{:S(2)}, u32[]{:S(2)}) collective-permute-start(bf16[16,1024]{1,0:T(8,128)(2,1)S(1)} %get-tuple-element.41), channel_id=1, source_target_pairs={{0,4},{1,5},{2,6},{3,7},{4,0},{5,1},{6,2},{7,3},{8,12},{9,13},{10,... | collective-permute-start | bytes 98312 | tf_op jit(solution)/shard_map/ppermute | solution.py:60
  19.0 2.0 collective-permute-done.2
  24.9 2.7 %collective-permute-done.4 = bf16[4,16,1024]{2,1,0:T(8,128)(2,1)S(1)} collective-permute-done((bf16[4,16,1024]{2,1,0:T(8,128)(2,1)S(1)}, bf16[4,16,1024]{2,1,0:T(8,128)(2,1)S(1)}, u32[]{:S(2)}, u32[]{:S(2)}) %collective-permute-start.4) | collective-permute-done | bytes 131104 | tf_op jit(solution)/shard_map/ppermute | solution.py:60
  27.8 3.3 %collective-permute-start.6 = (bf16[4,4,16,1024]{3,2,1,0:T(8,128)(2,1)S(1)}, bf16[4,4,16,1024]{3,2,1,0:T(8,128)(2,1)S(1)}, u32[]{:S(2)}, u32[]{:S(2)}) collective-permute-start(bf16[4,4,16,1024]{3,2,1,0:T(8,128)(2,1)S(1)} %pad_maximum_fusion.own), channel_id=1, source_target_pairs={{0,1},{1,0},{2,3},{3,2},{4,5},{5,4},{6,7},{7,6},{8,9},{9,8},{10,11... | collective-permute-start | bytes 1572872 | tf_op jit(solution)/shard_map/ppermute | solution.py:65
  31.2 6.5 %gather_fusion = bf16[64,8192]{1,0:T(8,128)(2,1)S(1)} fusion(bf16[4752,8192]{1,0:T(8,128)(2,1)} %weight.1, s32[1024]{0:T(1024)S(1)} %pad_clamp_fusion), kind=kCustom, calls=%fused_computation | custom fusion | bytes 2097408 | tf_op jit(solution)/shard_map/gather | solution.py:514
  39.0 2.2 copy_select_fusion
  43.0 47.7 %shard_map.138 = (f32[4,64,1024]{2,1,0:T(8,128)S(1)}, bf16[4,64,1024]{2,1,0:T(8,128)(2,1)S(1)}, f32[64,128]{1,0:T(8,128)S(1)}, f32[16,1024]{1,0:T(8,128)S(1)}) custom-call(s32[5]{0:T(128)S(1)} %stack.53.place, bf16[4,4,16,1024]{3,2,1,0:T(8,128)(2,1)S(1)} %pad_maximum_fusion.own, bf16[4,4,16,1024]{3,2,1,0:T(8,128)(2,1)S(1)} %collective-permute-done.6.other, ...), custom_call_target="tpu_custom_call" | custom-call | flops 9965666304 | bytes 77856768 | tf_op jit(solution)/shard_map/pallas_call | solution.py:546
  91.3 1.4 collective-permute-done.8.theirs
  93.8 1.4 collective-permute-start.10
  95.1 2.4 %collective-permute-start.9 = (bf16[4,16,1024]{2,1,0:T(8,128)(2,1)S(1)}, bf16[4,16,1024]{2,1,0:T(8,128)(2,1)S(1)}, u32[]{:S(2)}, u32[]{:S(2)}) collective-permute-start(bf16[4,16,1024]{2,1,0:T(8,128)(2,1)S(1)} %get-tuple-element.48), channel_id=1, source_target_pairs={{0,8},{8,16},{16,24},{24,0},{1,9},{9,17},{17,25},{25,1},{2,10},{10... | collective-permute-start | bytes 393224 | tf_op jit(solution)/shard_map/ppermute | solution.py:60
  97.8 6.4 %collective-permute-done.12.refs_4_ = f32[64,128]{1,0:T(8,128)S(1)} collective-permute-done((f32[64,128]{1,0:T(8,128)S(1)}, f32[64,128]{1,0:T(8,128)S(1)}, u32[]{:S(2)}, u32[]{:S(2)}) %collective-permute-start.12) | collective-permute-done | bytes 32800 | tf_op jit(solution)/shard_map/ppermute | solution.py:60
  104.2 1.4 collective-permute-start.14
  105.5 2.8 %collective-permute-done.14.refs_6_ = f32[64,128]{1,0:T(8,128)S(1)} collective-permute-done((f32[64,128]{1,0:T(8,128)S(1)}, f32[64,128]{1,0:T(8,128)S(1)}, u32[]{:S(2)}, u32[]{:S(2)}) %collective-permute-start.14) | collective-permute-done | bytes 32800 | tf_op jit(solution)/shard_map/ppermute | solution.py:60
  110.7 2.3 %collective-permute-start.19 = (f32[64,128]{1,0:T(8,128)S(1)}, f32[64,128]{1,0:T(8,128)S(1)}, u32[]{:S(2)}, u32[]{:S(2)}) collective-permute-start(f32[64,128]{1,0:T(8,128)S(1)} %get-tuple-element.56.refs_3_), channel_id=1, source_target_pairs={{0,4},{1,5},{2,6},{3,7},{4,0},{5,1},{6,2},{7,3},{8,12},{9,13},{10,... | collective-permute-start | bytes 98312 | tf_op jit(solution)/shard_map/ppermute | solution.py:60
  113.0 2.1 collective-permute-start.20
  115.1 1.4 collective-permute-start.17
  116.5 2.2 collective-permute-done.16.refs_1_
  118.8 52.3 %reduce-scatter.2.cloned.1.call-done.refs_7_ = bf16[16,1024]{1,0:T(8,128)(2,1)} async-done(((bf16[512,1024]{1,0:T(8,128)(2,1)}), bf16[16,1024]{1,0:T(8,128)(2,1)}) %reduce-scatter.2.cloned.1.call-update) | async-done | bytes 32784 | tf_op jit(solution)/shard_map/reduce_scatter | solution.py:537
  173.6 4.5 %collective-permute-start.22 = (bf16[16,1024]{1,0:T(8,128)(2,1)S(1)}, bf16[16,1024]{1,0:T(8,128)(2,1)S(1)}, u32[]{:S(2)}, u32[]{:S(2)}) collective-permute-start(bf16[16,1024]{1,0:T(8,128)(2,1)S(1)} %get-tuple-element.60.refs_0_), channel_id=1, source_target_pairs={{0,16},{8,24},{16,0},{24,8},{1,17},{9,25},{17,1},{25,9},{2,18},{10... | collective-permute-start | bytes 98312 | tf_op jit(solution)/shard_map/ppermute | solution.py:60
  179.5 2.6 %collective-permute-done.23.refs_3_ = bf16[16,1024]{1,0:T(8,128)(2,1)S(1)} collective-permute-done((bf16[16,1024]{1,0:T(8,128)(2,1)S(1)}, bf16[16,1024]{1,0:T(8,128)(2,1)S(1)}, u32[]{:S(2)}, u32[]{:S(2)}) %collective-permute-start.23) | collective-permute-done | bytes 32800 | tf_op jit(solution)/shard_map/ppermute | solution.py:60
  182.1 2.2 copy-done
  184.2 2.4 %shard_map.142 = (bf16[64,1024]{1,0:T(8,128)(2,1)}, f32[16,1024]{1,0:T(8,128)S(1)}, bf16[16,1024]{1,0:T(8,128)(2,1)S(1)}, bf16[16,1024]{1,0:T(8,128)(2,1)S(1)}, ...) custom-call(s32[5]{0:T(128)S(1)} %stack.53.place, ...), custom_call_target="tpu_custom_call" | custom-call | tf_op jit(solution)/shard_map/pallas_call | solution.py:624
  186.7 4.6 %collective-permute-start.26 = (bf16[16,1024]{1,0:T(8,128)(2,1)S(1)}, bf16[16,1024]{1,0:T(8,128)(2,1)S(1)}, u32[]{:S(2)}, u32[]{:S(2)}) collective-permute-start(bf16[16,1024]{1,0:T(8,128)(2,1)S(1)} %get-tuple-element.64), channel_id=1, source_target_pairs={{0,3},{1,4},{2,5},{3,6},{4,7},{5,0},{6,1},{7,2},{8,11},{9,12},{10,... | collective-permute-start | bytes 98312 | tf_op jit(solution)/shard_map/ppermute | solution.py:60
  191.3 5.7 %collective-permute-start.27 = (bf16[16,1024]{1,0:T(8,128)(2,1)S(1)}, bf16[16,1024]{1,0:T(8,128)(2,1)S(1)}, u32[]{:S(2)}, u32[]{:S(2)}) collective-permute-start(bf16[16,1024]{1,0:T(8,128)(2,1)S(1)} %get-tuple-element.65), channel_id=1, source_target_pairs={{0,4},{1,5},{2,6},{3,7},{4,0},{5,1},{6,2},{7,3},{8,12},{9,13},{10,... | collective-permute-start | bytes 98312 | tf_op jit(solution)/shard_map/ppermute | solution.py:60
  197.0 2.8 %collective-permute-start.28 = (bf16[16,1024]{1,0:T(8,128)(2,1)S(1)}, bf16[16,1024]{1,0:T(8,128)(2,1)S(1)}, u32[]{:S(2)}, u32[]{:S(2)}) collective-permute-start(bf16[16,1024]{1,0:T(8,128)(2,1)S(1)} %get-tuple-element.66), channel_id=1, source_target_pairs={{0,5},{1,6},{2,7},{3,0},{4,1},{5,2},{6,3},{7,4},{8,13},{9,14},{10,... | collective-permute-start | bytes 98312 | tf_op jit(solution)/shard_map/ppermute | solution.py:60
  200.4 2.0 collective-permute-done.28.refs_4_
  205.5 1.7 collective-permute-start.33
  209.7 1.5 collective-permute-start.36
  211.3 1.3 copy-done.1
  212.6 4.1 %shard_map.144 = (f32[2,512,128]{2,1,0:T(8,128)S(1)}, f32[2,64,1024]{2,1,0:T(8,128)S(1)}, f32[2,512,128]{2,1,0:T(8,128)S(1)}) custom-call(s32[5]{0:T(128)S(1)} %stack.53.place, s32[1,1024]{1,0:T(1,128)S(1)} %add.62.key_pos, s32[64,1]{1,0:T(8,128)S(1)} %copy.20.query_pos, bf16[8,160,512]{2,1,0:T(8,128)(2,1)S(1)} %bitcast.27), custom_call_target="tpu_custom_call" | custom-call | flops 805306368 | bytes 1310720 | tf_op jit(solution)/shard_map/pallas_call | solution.py:576
  218.1 2.4 %shard_map.145 = (bf16[8,2048]{1,0:T(8,128)(2,1)}, bf16[128,256]{1,0:T(8,128)(2,1)}, bf16[128,256]{1,0:T(8,128)(2,1)}) custom-call(s32[5]{0:T(128)S(1)} %stack.53.place, bf16[16,1024]{1,0:T(8,128)(2,1)S(1)} %shard_map.143.refs_0_, bf16[16,1024]{1,0:T(8,128)(2,1)S(1)} %collective-permute-done.31.refs_1_, ...), custom_call_target="tpu_custom_call" | custom-call | tf_op jit(solution)/shard_map/pallas_call | solution.py:634
  (104 shorter events, 30.2 us)
Async XLA Ops:
  8.0 163.0 %reduce-scatter.2.cloned.1.call-start = ((), (), s32[]{:S(2)}) async-start(), calls=%async_computation.1 | async-start | bytes 1081344 | tf_op jit(solution)/shard_map/reduce_scatter | solution.py:537
  14.1 4.7 %collective-permute-start = (bf16[16,1024]{1,0:T(8,128)(2,1)S(1)}, bf16[16,1024]{1,0:T(8,128)(2,1)S(1)}, u32[]{:S(2)}, u32[]{:S(2)}) collective-permute-start(bf16[16,1024]{1,0:T(8,128)(2,1)S(1)} %get-tuple-element.41), channel_id=1, source_target_pairs={{0,2},{1,3},{2,4},{3,5},{4,6},{5,7},{6,0},{7,1},{8,10},{9,11},{10,... | collective-permute-start | bytes 98312 | tf_op jit(solution)/shard_map/ppermute | solution.py:60
  21.1 3.9 %collective-permute-start.3 = (bf16[4,16,1024]{2,1,0:T(8,128)(2,1)S(1)}, bf16[4,16,1024]{2,1,0:T(8,128)(2,1)S(1)}, u32[]{:S(2)}, u32[]{:S(2)}) collective-permute-start(bf16[4,16,1024]{2,1,0:T(8,128)(2,1)S(1)} %get-tuple-element.78), channel_id=1, source_target_pairs={{0,8},{8,16},{16,24},{24,0},{1,9},{9,17},{17,25},{25,1},{2,10},{10... | collective-permute-start | bytes 393224 | tf_op jit(solution)/shard_map/ppermute | solution.py:60
  22.3 5.3 %collective-permute-start.4 = (bf16[4,16,1024]{2,1,0:T(8,128)(2,1)S(1)}, bf16[4,16,1024]{2,1,0:T(8,128)(2,1)S(1)}, u32[]{:S(2)}, u32[]{:S(2)}) collective-permute-start(bf16[4,16,1024]{2,1,0:T(8,128)(2,1)S(1)} %get-tuple-element.78), channel_id=1, source_target_pairs={{0,16},{8,24},{16,0},{24,8},{1,17},{9,25},{17,1},{25,9},{2,18},{10... | collective-permute-start | bytes 393224 | tf_op jit(solution)/shard_map/ppermute | solution.py:60
  22.6 5.2 %collective-permute-start.5 = (bf16[4,16,1024]{2,1,0:T(8,128)(2,1)S(1)}, bf16[4,16,1024]{2,1,0:T(8,128)(2,1)S(1)}, u32[]{:S(2)}, u32[]{:S(2)}) collective-permute-start(bf16[4,16,1024]{2,1,0:T(8,128)(2,1)S(1)} %get-tuple-element.78), channel_id=1, source_target_pairs={{0,24},{8,0},{16,8},{24,16},{1,25},{9,1},{17,9},{25,17},{2,26},{10... | collective-permute-start | bytes 393224 | tf_op jit(solution)/shard_map/ppermute | solution.py:60
  27.8 13.4 %collective-permute-start.6 = (bf16[4,4,16,1024]{3,2,1,0:T(8,128)(2,1)S(1)}, bf16[4,4,16,1024]{3,2,1,0:T(8,128)(2,1)S(1)}, u32[]{:S(2)}, u32[]{:S(2)}) collective-permute-start(bf16[4,4,16,1024]{3,2,1,0:T(8,128)(2,1)S(1)} %pad_maximum_fusion.own), channel_id=1, source_target_pairs={{0,1},{1,0},{2,3},{3,2},{4,5},{5,4},{6,7},{7,6},{8,9},{9,8},{10,11... | collective-permute-start | bytes 1572872 | tf_op jit(solution)/shard_map/ppermute | solution.py:65
  41.2 170.1 %all-gather.3.cloned.1.call-start = ((), (), s32[]{:S(2)}) async-start(), calls=%async_computation.2 | async-start | bytes 1474560 | tf_op jit(solution)/shard_map/all_gather | solution.py:536
  93.8 14.6 %collective-permute-start.10 = (bf16[4,16,1024]{2,1,0:T(8,128)(2,1)S(1)}, bf16[4,16,1024]{2,1,0:T(8,128)(2,1)S(1)}, u32[]{:S(2)}, u32[]{:S(2)}) collective-permute-start(bf16[4,16,1024]{2,1,0:T(8,128)(2,1)S(1)} %get-tuple-element.49), channel_id=1, source_target_pairs={{0,16},{8,24},{16,0},{24,8},{1,17},{9,25},{17,1},{25,9},{2,18},{10... | collective-permute-start | bytes 393224 | tf_op jit(solution)/shard_map/ppermute | solution.py:60
  95.1 13.3 %collective-permute-start.11 = (bf16[4,16,1024]{2,1,0:T(8,128)(2,1)S(1)}, bf16[4,16,1024]{2,1,0:T(8,128)(2,1)S(1)}, u32[]{:S(2)}, u32[]{:S(2)}) collective-permute-start(bf16[4,16,1024]{2,1,0:T(8,128)(2,1)S(1)} %get-tuple-element.50), channel_id=1, source_target_pairs={{0,24},{8,0},{16,8},{24,16},{1,25},{9,1},{17,9},{25,17},{2,26},{10... | collective-permute-start | bytes 393224 | tf_op jit(solution)/shard_map/ppermute | solution.py:60
  95.1 13.3 %collective-permute-start.9 = (bf16[4,16,1024]{2,1,0:T(8,128)(2,1)S(1)}, bf16[4,16,1024]{2,1,0:T(8,128)(2,1)S(1)}, u32[]{:S(2)}, u32[]{:S(2)}) collective-permute-start(bf16[4,16,1024]{2,1,0:T(8,128)(2,1)S(1)} %get-tuple-element.48), channel_id=1, source_target_pairs={{0,8},{8,16},{16,24},{24,0},{1,9},{9,17},{17,25},{25,1},{2,10},{10... | collective-permute-start | bytes 393224 | tf_op jit(solution)/shard_map/ppermute | solution.py:60
  97.5 6.7 %collective-permute-start.12 = (f32[64,128]{1,0:T(8,128)S(1)}, f32[64,128]{1,0:T(8,128)S(1)}, u32[]{:S(2)}, u32[]{:S(2)}) collective-permute-start(f32[64,128]{1,0:T(8,128)S(1)} %get-tuple-element.51.refs_3_), channel_id=1, source_target_pairs={{0,8},{8,16},{16,24},{24,0},{1,9},{9,17},{17,25},{25,1},{2,10},{10... | collective-permute-start | bytes 98312 | tf_op jit(solution)/shard_map/ppermute | solution.py:60
  97.5 8.0 %collective-permute-start.13 = (f32[64,128]{1,0:T(8,128)S(1)}, f32[64,128]{1,0:T(8,128)S(1)}, u32[]{:S(2)}, u32[]{:S(2)}) collective-permute-start(f32[64,128]{1,0:T(8,128)S(1)} %get-tuple-element.51.refs_3_), channel_id=1, source_target_pairs={{0,16},{8,24},{16,0},{24,8},{1,17},{9,25},{17,1},{25,9},{2,18},{10... | collective-permute-start | bytes 98312 | tf_op jit(solution)/shard_map/ppermute | solution.py:60
  104.2 4.2 %collective-permute-start.14 = (f32[64,128]{1,0:T(8,128)S(1)}, f32[64,128]{1,0:T(8,128)S(1)}, u32[]{:S(2)}, u32[]{:S(2)}) collective-permute-start(f32[64,128]{1,0:T(8,128)S(1)} %get-tuple-element.51.refs_3_), channel_id=1, source_target_pairs={{0,24},{8,0},{16,8},{24,16},{1,25},{9,1},{17,9},{25,17},{2,26},{10... | collective-permute-start | bytes 98312 | tf_op jit(solution)/shard_map/ppermute | solution.py:60
  109.4 5.7 %collective-permute-start.15 = (bf16[16,1024]{1,0:T(8,128)(2,1)S(1)}, bf16[16,1024]{1,0:T(8,128)(2,1)S(1)}, u32[]{:S(2)}, u32[]{:S(2)}) collective-permute-start(bf16[16,1024]{1,0:T(8,128)(2,1)S(1)} %get-tuple-element.53), channel_id=1, source_target_pairs={{0,2},{1,3},{2,4},{3,5},{4,6},{5,7},{6,0},{7,1},{8,10},{9,11},{10,... | collective-permute-start | bytes 98312 | tf_op jit(solution)/shard_map/ppermute | solution.py:60
  109.6 9.1 %collective-permute-start.18 = (f32[64,128]{1,0:T(8,128)S(1)}, f32[64,128]{1,0:T(8,128)S(1)}, u32[]{:S(2)}, u32[]{:S(2)}) collective-permute-start(f32[64,128]{1,0:T(8,128)S(1)} %get-tuple-element.56.refs_3_), channel_id=1, source_target_pairs={{0,2},{1,3},{2,4},{3,5},{4,6},{5,7},{6,0},{7,1},{8,10},{9,11},{10,... | collective-permute-start | bytes 98312 | tf_op jit(solution)/shard_map/ppermute | solution.py:60
  110.7 8.1 %collective-permute-start.19 = (f32[64,128]{1,0:T(8,128)S(1)}, f32[64,128]{1,0:T(8,128)S(1)}, u32[]{:S(2)}, u32[]{:S(2)}) collective-permute-start(f32[64,128]{1,0:T(8,128)S(1)} %get-tuple-element.56.refs_3_), channel_id=1, source_target_pairs={{0,4},{1,5},{2,6},{3,7},{4,0},{5,1},{6,2},{7,3},{8,12},{9,13},{10,... | collective-permute-start | bytes 98312 | tf_op jit(solution)/shard_map/ppermute | solution.py:60
  113.0 5.8 %collective-permute-start.20 = (f32[64,128]{1,0:T(8,128)S(1)}, f32[64,128]{1,0:T(8,128)S(1)}, u32[]{:S(2)}, u32[]{:S(2)}) collective-permute-start(f32[64,128]{1,0:T(8,128)S(1)} %get-tuple-element.56.refs_3_), channel_id=1, source_target_pairs={{0,6},{1,7},{2,0},{3,1},{4,2},{5,3},{6,4},{7,5},{8,14},{9,15},{10,... | collective-permute-start | bytes 98312 | tf_op jit(solution)/shard_map/ppermute | solution.py:60
  172.8 5.5 %collective-permute-start.21 = (bf16[16,1024]{1,0:T(8,128)(2,1)S(1)}, bf16[16,1024]{1,0:T(8,128)(2,1)S(1)}, u32[]{:S(2)}, u32[]{:S(2)}) collective-permute-start(bf16[16,1024]{1,0:T(8,128)(2,1)S(1)} %get-tuple-element.60.refs_0_), channel_id=1, source_target_pairs={{0,8},{8,16},{16,24},{24,0},{1,9},{9,17},{17,25},{25,1},{2,10},{10... | collective-permute-start | bytes 98312 | tf_op jit(solution)/shard_map/ppermute | solution.py:60
  173.6 5.9 %collective-permute-start.22 = (bf16[16,1024]{1,0:T(8,128)(2,1)S(1)}, bf16[16,1024]{1,0:T(8,128)(2,1)S(1)}, u32[]{:S(2)}, u32[]{:S(2)}) collective-permute-start(bf16[16,1024]{1,0:T(8,128)(2,1)S(1)} %get-tuple-element.60.refs_0_), channel_id=1, source_target_pairs={{0,16},{8,24},{16,0},{24,8},{1,17},{9,25},{17,1},{25,9},{2,18},{10... | collective-permute-start | bytes 98312 | tf_op jit(solution)/shard_map/ppermute | solution.py:60
  178.2 3.9 %collective-permute-start.23 = (bf16[16,1024]{1,0:T(8,128)(2,1)S(1)}, bf16[16,1024]{1,0:T(8,128)(2,1)S(1)}, u32[]{:S(2)}, u32[]{:S(2)}) collective-permute-start(bf16[16,1024]{1,0:T(8,128)(2,1)S(1)} %get-tuple-element.60.refs_0_), channel_id=1, source_target_pairs={{0,24},{8,0},{16,8},{24,16},{1,25},{9,1},{17,9},{25,17},{2,26},{10... | collective-permute-start | bytes 98312 | tf_op jit(solution)/shard_map/ppermute | solution.py:60
  186.7 13.2 %collective-permute-start.24 = (bf16[16,1024]{1,0:T(8,128)(2,1)S(1)}, bf16[16,1024]{1,0:T(8,128)(2,1)S(1)}, u32[]{:S(2)}, u32[]{:S(2)}) collective-permute-start(bf16[16,1024]{1,0:T(8,128)(2,1)S(1)} %get-tuple-element.62), channel_id=1, source_target_pairs={{0,1},{1,2},{2,3},{3,4},{4,5},{5,6},{6,7},{7,0},{8,9},{9,10},{10,1... | collective-permute-start | bytes 98312 | tf_op jit(solution)/shard_map/ppermute | solution.py:60
  186.7 13.2 %collective-permute-start.25 = (bf16[16,1024]{1,0:T(8,128)(2,1)S(1)}, bf16[16,1024]{1,0:T(8,128)(2,1)S(1)}, u32[]{:S(2)}, u32[]{:S(2)}) collective-permute-start(bf16[16,1024]{1,0:T(8,128)(2,1)S(1)} %get-tuple-element.63), channel_id=1, source_target_pairs={{0,2},{1,3},{2,4},{3,5},{4,6},{5,7},{6,0},{7,1},{8,10},{9,11},{10,... | collective-permute-start | bytes 98312 | tf_op jit(solution)/shard_map/ppermute | solution.py:60
  186.7 13.7 %collective-permute-start.26 = (bf16[16,1024]{1,0:T(8,128)(2,1)S(1)}, bf16[16,1024]{1,0:T(8,128)(2,1)S(1)}, u32[]{:S(2)}, u32[]{:S(2)}) collective-permute-start(bf16[16,1024]{1,0:T(8,128)(2,1)S(1)} %get-tuple-element.64), channel_id=1, source_target_pairs={{0,3},{1,4},{2,5},{3,6},{4,7},{5,0},{6,1},{7,2},{8,11},{9,12},{10,... | collective-permute-start | bytes 98312 | tf_op jit(solution)/shard_map/ppermute | solution.py:60
  191.3 9.1 %collective-permute-start.27 = (bf16[16,1024]{1,0:T(8,128)(2,1)S(1)}, bf16[16,1024]{1,0:T(8,128)(2,1)S(1)}, u32[]{:S(2)}, u32[]{:S(2)}) collective-permute-start(bf16[16,1024]{1,0:T(8,128)(2,1)S(1)} %get-tuple-element.65), channel_id=1, source_target_pairs={{0,4},{1,5},{2,6},{3,7},{4,0},{5,1},{6,2},{7,3},{8,12},{9,13},{10,... | collective-permute-start | bytes 98312 | tf_op jit(solution)/shard_map/ppermute | solution.py:60
  197.0 5.4 %collective-permute-start.28 = (bf16[16,1024]{1,0:T(8,128)(2,1)S(1)}, bf16[16,1024]{1,0:T(8,128)(2,1)S(1)}, u32[]{:S(2)}, u32[]{:S(2)}) collective-permute-start(bf16[16,1024]{1,0:T(8,128)(2,1)S(1)} %get-tuple-element.66), channel_id=1, source_target_pairs={{0,5},{1,6},{2,7},{3,0},{4,1},{5,2},{6,3},{7,4},{8,13},{9,14},{10,... | collective-permute-start | bytes 98312 | tf_op jit(solution)/shard_map/ppermute | solution.py:60
  203.5 6.2 %collective-permute-start.31 = (bf16[16,1024]{1,0:T(8,128)(2,1)S(1)}, bf16[16,1024]{1,0:T(8,128)(2,1)S(1)}, u32[]{:S(2)}, u32[]{:S(2)}) collective-permute-start(bf16[16,1024]{1,0:T(8,128)(2,1)S(1)} %shard_map.143.refs_0_), channel_id=1, source_target_pairs={{0,1},{1,2},{2,3},{3,4},{4,5},{5,6},{6,7},{7,0},{8,9},{9,10},{10,1... | collective-permute-start | bytes 98312 | tf_op jit(solution)/shard_map/ppermute | solution.py:60
  203.9 7.3 %collective-permute-start.32 = (bf16[16,1024]{1,0:T(8,128)(2,1)S(1)}, bf16[16,1024]{1,0:T(8,128)(2,1)S(1)}, u32[]{:S(2)}, u32[]{:S(2)}) collective-permute-start(bf16[16,1024]{1,0:T(8,128)(2,1)S(1)} %shard_map.143.refs_0_), channel_id=1, source_target_pairs={{0,2},{1,3},{2,4},{3,5},{4,6},{5,7},{6,0},{7,1},{8,10},{9,11},{10,... | collective-permute-start | bytes 98312 | tf_op jit(solution)/shard_map/ppermute | solution.py:60
  205.5 11.2 %collective-permute-start.33 = (bf16[16,1024]{1,0:T(8,128)(2,1)S(1)}, bf16[16,1024]{1,0:T(8,128)(2,1)S(1)}, u32[]{:S(2)}, u32[]{:S(2)}) collective-permute-start(bf16[16,1024]{1,0:T(8,128)(2,1)S(1)} %shard_map.143.refs_0_), channel_id=1, source_target_pairs={{0,3},{1,4},{2,5},{3,6},{4,7},{5,0},{6,1},{7,2},{8,11},{9,12},{10,... | collective-permute-start | bytes 98312 | tf_op jit(solution)/shard_map/ppermute | solution.py:60
  207.2 9.5 %collective-permute-start.34 = (bf16[16,1024]{1,0:T(8,128)(2,1)S(1)}, bf16[16,1024]{1,0:T(8,128)(2,1)S(1)}, u32[]{:S(2)}, u32[]{:S(2)}) collective-permute-start(bf16[16,1024]{1,0:T(8,128)(2,1)S(1)} %shard_map.143.refs_0_), channel_id=1, source_target_pairs={{0,4},{1,5},{2,6},{3,7},{4,0},{5,1},{6,2},{7,3},{8,12},{9,13},{10,... | collective-permute-start | bytes 98312 | tf_op jit(solution)/shard_map/ppermute | solution.py:60
  208.5 8.2 %collective-permute-start.35 = (bf16[16,1024]{1,0:T(8,128)(2,1)S(1)}, bf16[16,1024]{1,0:T(8,128)(2,1)S(1)}, u32[]{:S(2)}, u32[]{:S(2)}) collective-permute-start(bf16[16,1024]{1,0:T(8,128)(2,1)S(1)} %shard_map.143.refs_0_), channel_id=1, source_target_pairs={{0,5},{1,6},{2,7},{3,0},{4,1},{5,2},{6,3},{7,4},{8,13},{9,14},{10,... | collective-permute-start | bytes 98312 | tf_op jit(solution)/shard_map/ppermute | solution.py:60
  209.7 7.0 %collective-permute-start.36 = (bf16[16,1024]{1,0:T(8,128)(2,1)S(1)}, bf16[16,1024]{1,0:T(8,128)(2,1)S(1)}, u32[]{:S(2)}, u32[]{:S(2)}) collective-permute-start(bf16[16,1024]{1,0:T(8,128)(2,1)S(1)} %shard_map.143.refs_0_), channel_id=1, source_target_pairs={{0,6},{1,7},{2,0},{3,1},{4,2},{5,3},{6,4},{7,5},{8,14},{9,15},{10,... | collective-permute-start | bytes 98312 | tf_op jit(solution)/shard_map/ppermute | solution.py:60
  211.2 5.6 %collective-permute-start.37 = (bf16[16,1024]{1,0:T(8,128)(2,1)S(1)}, bf16[16,1024]{1,0:T(8,128)(2,1)S(1)}, u32[]{:S(2)}, u32[]{:S(2)}) collective-permute-start(bf16[16,1024]{1,0:T(8,128)(2,1)S(1)} %shard_map.143.refs_0_), channel_id=1, source_target_pairs={{0,7},{1,0},{2,1},{3,2},{4,3},{5,4},{6,5},{7,6},{8,15},{9,8},{10,9... | collective-permute-start | bytes 98312 | tf_op jit(solution)/shard_map/ppermute | solution.py:60
  (21 other events, 485.7 us)
Sparse Core Ops, SparseCore 0:
  41.4 129.6 reduce-scatter.1
Sparse Core Ops, SparseCore 1:
  43.5 24.0 all-gather.2

commit v2 on v1

--- a/solution.py
+++ b/solution.py
@@ -53,7 +53,7 @@
     )
 
 
-def shifted(value, axis, step, inner=1, ring=None):
+def shifted(value, axis, step, inner=1):
     size = lax.axis_size(axis)
     outer = size // inner
     pairs = [(i, ((i // inner + step) % outer) * inner + i % inner) for i in range(size)]
@@ -65,25 +65,70 @@
     return lax.ppermute(value, "ctx", [(i, i ^ 1) for i in range(size)])
 
 
-def pick_body(loss_per, place, rows, hidden, queries, keys, values, picked, packed):
+def row_choice(loss_per, tokens, place, rows):
     base = place[3] * loss_per
-    tokens, width = hidden.shape
     row_iota = lax.broadcasted_iota(jnp.int32, (loss_per, tokens), 0)
     col_iota = lax.broadcasted_iota(jnp.int32, (loss_per, tokens), 1)
     sel = jnp.zeros((loss_per, tokens), f32)
     for j in range(loss_per):
         sel = jnp.where((row_iota == j) & (col_iota == rows[base + j]), 1.0, sel)
-    sel = sel.astype(bf16)
-    mine = dot(sel, hidden[...], NN)
+    return sel.astype(bf16)
+
+
+def pick_body(loss_per, place, rows, hidden, picked):
+    tokens, width = hidden.shape
+    mine = dot(row_choice(loss_per, tokens, place, rows), hidden[...], NN)
     half = width // 2
     picked[...] = jnp.concatenate([mine[:, :half], mine[:, half:]], axis=0).astype(bf16)
-    mine = dot(sel, queries[...], NN)
-    key_width = keys.shape[1]
+
+
+def pack_body(loss_per, place, rows, queries, keys, values, packed):
+    tokens, key_width = keys.shape
+    mine = dot(row_choice(loss_per, tokens, place, rows), queries[...], NN)
     packed[0:tokens, 0:key_width] = keys[...]
     packed[0:tokens, key_width : 2 * key_width] = values[...]
     parts = queries.shape[1] // (2 * key_width)
     stacked = [mine[:, b * 2 * key_width : (b + 1) * 2 * key_width] for b in range(parts)]
     packed[tokens : tokens + parts * loss_per, :] = jnp.concatenate(stacked, axis=0).astype(bf16)
+
+
+def target_body(place, targets, weight, out, buf, rows, sems):
+    loss, width = rows.shape
+    blocks, _, block_width = out.shape
+    total_rows = weight.shape[0]
+
+    def local(i):
+        at = targets[i] - place[4]
+        return at, (at >= 0) & (at < total_rows)
+
+    def copy(i, at):
+        start = pl.multiple_of(lax.div(at, 16) * 16, 16)
+        return pltpu.make_async_copy(weight.at[pl.ds(start, 16), :], buf.at[i], sems.at[i])
+
+    @pl.loop(0, loss)
+    def _(i):
+        at, here = local(i)
+
+        @pl.when(here)
+        def _():
+            copy(i, at).start()
+
+    rows[...] = jnp.zeros_like(rows)
+
+    @pl.loop(0, loss)
+    def _(i):
+        at, here = local(i)
+
+        @pl.when(here)
+        def _():
+            copy(i, at).wait()
+            line = lax.broadcasted_iota(jnp.int32, (16, width), 0)
+            block = buf[i].astype(f32)
+            row = jnp.sum(jnp.where(line == lax.rem(at, 16), block, 0.0), axis=0, keepdims=True)
+            rows[pl.ds(i, 1), :] = row
+
+    for b in range(blocks):
+        out[b] = rows[:, b * block_width : (b + 1) * block_width].astype(bf16)
 
 
 def flash_body(
@@ -154,7 +199,7 @@
         row_at = pl.multiple_of(z_src * 16, 16)
         state[pl.ds(row_at, 16), :] = jnp.broadcast_to(inv, (16, LANES))
         for vr in range(nv):
-            v_src = lax.rem(vocab_at - vr + nv, nv)
+            v_src = vr
             a = own[vr, zr].astype(f32)
             b = other[vr, zr].astype(f32)
             low = jnp.where(is_even, a, b)
@@ -200,7 +245,7 @@
         return masked, scale, (top, total, moment, logit)
 
     def scores_of(block):
-        return dot(normed[...], block, NT)
+        return dot(block, normed[...], NT).T
 
     def add_product(p, scale, read):
         for b in range(blocks):
@@ -240,16 +285,37 @@
 
     for z in range(nz):
         keep[z] = acc[CORES * z + core_at]
-        send[z] = acc[CORES * z + 1 - core_at].astype(bf16)
-    lane = lax.broadcasted_iota(jnp.int32, (loss, LANES), 1)
-    table = state[...]
-    for k in range(4):
-        table = jnp.where(lane == k, run[k], table)
-    stats[...] = table
-
-
-def merge_stats(tables):
-    columns = [[t[:, k : k + 1] for k in range(4)] for t in tables]
+        send[:, z * block_width : (z + 1) * block_width] = acc[CORES * z + 1 - core_at].astype(bf16)
+    send[:, nz * block_width :] = split_columns(run)
+    stats[...] = with_stats(state[...], run)
+
+
+def split_columns(columns):
+    rows = columns[0].shape[0]
+    lane = lax.broadcasted_iota(jnp.int32, (rows, LANES), 1)
+    table = jnp.zeros((rows, LANES), f32)
+    for k, column in enumerate(columns):
+        rest = column
+        for j in range(3):
+            term = rest.astype(bf16).astype(f32)
+            table = jnp.where(lane == 3 * k + j, term, table)
+            rest = rest - term
+    return table.astype(bf16)
+
+
+def joined_columns(block, count):
+    block = block.astype(f32)
+    return [
+        block[:, 3 * k : 3 * k + 1] + block[:, 3 * k + 1 : 3 * k + 2] + block[:, 3 * k + 2 : 3 * k + 3]
+        for k in range(count)
+    ]
+
+
+def stats_of(table):
+    return [table[:, k : k + 1] for k in range(4)]
+
+
+def merge_stats(columns):
     top = functools.reduce(jnp.maximum, [c[0] for c in columns])
     gaps = [c[0] - top for c in columns]
     scales = [jnp.exp(g) for g in gaps]
@@ -266,101 +332,100 @@
     return table
 
 
-def core_body(count, place, keep, got, mine, theirs, new_stats, new_keep, *sends_and_scratch):
-    sends, (total,) = sends_and_scratch[:count], sends_and_scratch[count:]
-    scales, merged = merge_stats([mine[...], theirs[...]])
-    new_stats[...] = with_stats(mine[...], merged)
-    nz, loss, _ = keep.shape
+def core_body(count, place, keep, got, mine, target_rows, new_stats, new_keep, *rest):
+    sends, (total, table, message) = rest[:count], rest[count:]
+    nz, loss, block = keep.shape
+    columns = [stats_of(mine[...]), joined_columns(got[:, nz * block :], 4)]
+    scales, merged = merge_stats(columns)
+    table[...] = with_stats(mine[...], merged)
+    message[...] = split_columns(merged)
     per = loss // (count + 1)
     for z in range(nz):
-        total[z] = keep[z] * scales[0] + got[z].astype(f32) * scales[1]
-    new_keep[...] = total[:, pl.ds(pl.multiple_of(place[0] * per, per), per), :]
+        other = got[:, z * block : (z + 1) * block].astype(f32)
+        total[z] = keep[z] * scales[0] + other * scales[1]
+    at = pl.multiple_of(place[0] * per, per)
+    new_stats[...] = table[pl.ds(at, per), :]
+    new_keep[...] = total[:, pl.ds(at, per), :]
     for s in range(count):
         to = lax.rem(place[0] + s + 1, count + 1)
-        sends[s][...] = total[:, pl.ds(pl.multiple_of(to * per, per), per), :].astype(bf16)
-
-
-def plane_body(count, nz, place, keep, *refs):
-    got, refs = refs[:count], refs[count:]
-    tables, refs = refs[: count + 1], refs[count + 1 :]
-    new_stats, new_keep = refs[:2]
-    sends, (scale_ref, total) = refs[2 : 1 + nz], refs[1 + nz :]
-    scales, merged = merge_stats([t[...] for t in tables])
-    new_stats[...] = with_stats(tables[0][...], merged)
-    per = keep.shape[1]
-    at = pl.multiple_of(place[0] * per, per)
-    for k in range(count + 1):
-        scale_ref[k] = jnp.broadcast_to(scales[k], scale_ref.shape[1:])
-    factors = [scale_ref[k, pl.ds(at, per), 0:1] for k in range(count + 1)]
+        rows = pl.ds(pl.multiple_of(to * per, per), per)
+        for z in range(nz):
+            sends[s][:, z * block : (z + 1) * block] = total[z, rows, :].astype(bf16)
+        sends[s][:, nz * block : (nz + 1) * block] = target_rows[rows, :]
+        sends[s][:, (nz + 1) * block :] = message[rows, :]
+
+
+def plane_body(count, place, keep, mine, target_rows, *rest):
+    got, rest = rest[:count], rest[count:]
+    new_stats, new_keep, new_target = rest[:3]
+    sends, (total,) = rest[3:-1], rest[-1:]
+    nz, per, block = keep.shape
+    columns = [stats_of(mine[...])] + [joined_columns(g[:, (nz + 1) * block :], 4) for g in got]
+    scales, merged = merge_stats(columns)
+    new_stats[...] = with_stats(mine[...], merged)
+    message = split_columns(merged)
     for z in range(nz):
-        value = keep[z] * factors[0]
+        value = keep[z] * scales[0]
         for k in range(count):
-            value = value + got[k][z].astype(f32) * factors[k + 1]
+            value = value + got[k][:, z * block : (z + 1) * block].astype(f32) * scales[k + 1]
         total[z] = value
     new_keep[...] = total[place[1]]
+    rows = target_rows[pl.ds(pl.multiple_of(place[0] * per, per), per), :].astype(f32)
+    for k in range(count):
+        rows = rows + got[k][:, nz * block : (nz + 1) * block].astype(f32)
+    new_target[...] = rows.astype(bf16)
     for s in range(nz - 1):
-        sends[s][...] = total[lax.rem(place[1] + s + 1, nz)].astype(bf16)
-
-
-def line_body(nz, width, place, keep, *refs):
-    got, refs = refs[: nz - 1], refs[nz - 1 :]
-    tables, refs = refs[:nz], refs[nz:]
-    target_rows, unit, gain, resid, loss_out, scale_ref, final = refs
-    scales, merged = merge_stats([t[...] for t in tables])
-    top, total, moment, logit = merged
+        sends[s][:, :block] = total[lax.rem(place[1] + s + 1, nz)].astype(bf16)
+        sends[s][:, block:] = message
+
+
+def line_body(count, width, place, keep, mine, target_rows, unit, gain, *rest):
+    got, (message,) = rest[:count], rest[count:]
+    per, block = keep.shape
+    columns = [stats_of(mine[...])] + [joined_columns(g[:, block:], 4) for g in got]
+    scales, (top, total, moment, logit) = merge_stats(columns)
     log_total = top + jnp.log(total)
-    loss_out[...] = jnp.broadcast_to(
-        jnp.mean(log_total - logit, axis=0, keepdims=True), loss_out.shape
-    )
-    per, block_width = keep.shape
-    at = pl.multiple_of(place[0] * per, per)
-    for k in range(nz):
-        scale_ref[k] = jnp.broadcast_to(scales[k] / total, scale_ref.shape[1:])
-    value = keep[...] * scale_ref[0, pl.ds(at, per), 0:1]
-    for k in range(nz - 1):
-        value = value + got[k][...].astype(f32) * scale_ref[k + 1, pl.ds(at, per), 0:1]
-    inner_all = grad_weight * (moment / total + (top - logit)) / width
-    short_all = jnp.exp(logit - log_total) - 1.0
-    lane = lax.broadcasted_iota(jnp.int32, final.shape, 1)
-    final[...] = jnp.where(
-        lane == 0, inner_all, jnp.where(lane == 1, short_all, tables[0][...])
-    )
-    inner = final[pl.ds(at, per), 0:1]
-    short = final[pl.ds(at, per), 1:2]
-    inv = final[pl.ds(at, per), 4:5]
+    value = keep[...] * (scales[0] / total)
+    for k in range(count):
+        value = value + got[k][:, :block].astype(f32) * (scales[k + 1] / total)
+    inner = grad_weight * (moment / total + (top - logit)) / width
+    short = jnp.exp(logit - log_total) - 1.0
+    inv = mine[:, 4:5]
     grad = grad_weight * (value + short * target_rows[...].astype(f32))
-    gain_at = pl.multiple_of(place[3] * block_width, block_width)
-    scaled = grad * gain[:, pl.ds(gain_at, block_width)]
-    resid[...] = (inv * (scaled - unit[...] * inner)).astype(bf16)
-
-
-def project_body(nv, nc, place, *refs):
-    pieces, refs = refs[:nv], refs[nv:]
-    weight, resid, keep = refs[:3]
-    sends, (whole, partial) = refs[3 : 2 + nc], refs[2 + nc :]
-    per = pieces[0].shape[0]
-    for s in range(nv):
-        src = lax.rem(place[0] - s + nv, nv)
-        whole[pl.ds(pl.multiple_of(src * per, per), per), :] = pieces[s][...]
+    gain_at = pl.multiple_of(place[3] * block, block)
+    scaled = grad * gain[:, pl.ds(gain_at, block)]
+    message[:, :block] = (inv * (scaled - unit[...] * inner)).astype(bf16)
+    message[:, block:] = split_columns([log_total - logit])
+
+
+def project_body(place, gathered, weight, resid, loss_out, keep, send, whole, partial):
+    nv, per, _ = gathered.shape
+    block = whole.shape[1]
+    loss_sum = jnp.zeros((1, 1), f32)
+    for v in range(nv):
+        whole[v * per : (v + 1) * per, :] = gathered[v, :, :block]
+        (column,) = joined_columns(gathered[v, :, block:], 1)
+        loss_sum = loss_sum + jnp.sum(column, axis=0, keepdims=True)
+    loss_out[...] = jnp.broadcast_to(loss_sum / (nv * per), loss_out.shape)
     resid[...] = whole[...]
     partial[...] = dot(whole[...], weight[...], NT)
-    rows, cols = keep.shape
-    for s in range(nc):
-        to = lax.rem(place[3] + s, nc)
-        row_at = pl.multiple_of(lax.div(to, CORES) * rows, rows)
-        col_at = pl.multiple_of(lax.rem(to, CORES) * cols, cols)
-        value = partial[pl.ds(row_at, rows), pl.ds(col_at, cols)]
-        if s == 0:
-            keep[...] = value
-        else:
-            sends[s - 1][...] = value.astype(bf16)
-
-
-def sum_body(keep, *refs):
-    value = keep[...]
-    for ref in refs[:-1]:
-        value = value + ref[...].astype(f32)
-    refs[-1][...] = value.astype(bf16)
+    cols = keep.shape[1]
+    keep[...] = partial[:, pl.ds(pl.multiple_of(place[2] * cols, cols), cols)]
+    send[...] = partial[:, pl.ds(pl.multiple_of((1 - place[2]) * cols, cols), cols)].astype(bf16)
+
+
+def half_body(keep, got, out):
+    value = (keep[...] + got[...].astype(f32)).astype(bf16)
+    per = out.shape[1]
+    for z in range(out.shape[0]):
+        out[z] = value[z * per : (z + 1) * per]
+
+
+def sum_body(parts, out):
+    value = parts[0].astype(f32)
+    for z in range(1, parts.shape[0]):
+        value = value + parts[z].astype(f32)
+    out[...] = value.astype(bf16)
 
 
 def forward_body(
@@ -416,20 +481,22 @@
     return jnp.concatenate(parts, axis=0)
 
 
-def backward_body(loss_per, heads, group, nc, place, *refs):
-    pieces, refs = refs[:nc], refs[nc:]
-    packed, p_own, p_rows, out, query_grad, key_grad, value_grad, grad = refs
+def backward_body(
+    loss_per, heads, group, place, half, other, packed, p_own, p_rows, out, query_grad, key_grad, value_grad, grad
+):
+    nc = packed.shape[0]
     tokens = p_own.shape[2]
     loss = loss_per * nc
     key_width = heads * HEAD_SIZE
     score_scale = HEAD_SIZE ** (-0.5)
     ctx_at = place[3]
-    rows, cols = pieces[0].shape
-    for s in range(nc):
-        src = lax.rem(ctx_at - s + nc, nc)
-        row_at = pl.multiple_of(lax.div(src, CORES) * rows, rows)
-        col_at = pl.multiple_of(lax.rem(src, CORES) * cols, cols)
-        grad[pl.ds(row_at, rows), pl.ds(col_at, cols)] = pieces[s][...].astype(f32)
+    nz, rows, cols = half.shape
+    col_at = pl.multiple_of(place[2] * cols, cols)
+    other_at = pl.multiple_of((1 - place[2]) * cols, cols)
+    for s in range(nz):
+        row_at = pl.multiple_of(lax.rem(place[1] - s + nz, nz) * rows, rows)
+        grad[pl.ds(row_at, rows), pl.ds(col_at, cols)] = half[s].astype(f32)
+        grad[pl.ds(row_at, rows), pl.ds(other_at, cols)] = other[s].astype(f32)
     mine_at = pl.multiple_of(ctx_at * loss_per, loss_per)
     for j in range(heads):
         lanes = [slice((j * group + g) * HEAD_SIZE, (j * group + g + 1) * HEAD_SIZE) for g in range(group)]
@@ -509,34 +576,46 @@
         stretch_of_slot[:, None] * stretch_len
         + lax.broadcasted_iota(jnp.int32, (1, stretch_len), 1)
     ).reshape(1, all_tokens)
-    local = targets - first_id
-    is_local = (local >= 0) & (local < voc_rows)
-    target_rows = head_weight.at[jnp.clip(local, 0, voc_rows - 1)].get(mode="promise_in_bounds")
-    target_rows = jnp.where(is_local[:, None], target_rows, jnp.zeros((), bf16))
-
+    if voc_rows % 16:
+        local = targets - first_id
+        is_local = (local >= 0) & (local < voc_rows)
+        target_rows = head_weight.at[jnp.clip(local, 0, voc_rows - 1)].get(mode="promise_in_bounds")
+        target_rows = jnp.where(is_local[:, None], target_rows, jnp.zeros((), bf16))
+        target_rows = target_rows.reshape(loss, nc, block_width).transpose(1, 0, 2)
+    else:
+        target_rows = pl.pallas_call(
+            target_body,
+            out_shape=shape((nc, loss, block_width), bf16),
+            in_specs=[smem(), smem(), pl.BlockSpec(memory_space=pl.ANY)],
+            out_specs=vmem(),
+            scratch_shapes=[
+                pltpu.VMEM((loss, 16, width), bf16),
+                pltpu.VMEM((loss, width), f32),
+                pltpu.SemaphoreType.DMA((loss,)),
+            ],
+            compiler_params=pltpu.CompilerParams(vmem_limit_bytes=40 * 2**20),
+        )(place, targets, head_weight)
+    target_rows = lax.psum_scatter(
+        target_rows.reshape(nc * loss, block_width), "ctx", scatter_dimension=0, tiled=True
+    )
+
+    picked = call(
+        functools.partial(pick_body, loss_per),
+        shape((2 * loss_per, part_width // 2), bf16),
+        [smem(), smem(), vmem()],
+    )(place, loss_rows, hidden)
+    picked, queries = lax.optimization_barrier((picked, queries))
     extra = (query_width // (2 * key_width)) * loss_per
-    picked, packed = call(
-        functools.partial(pick_body, loss_per),
-        (
-            shape((2 * loss_per, part_width // 2), bf16),
-            shape((tokens + extra, 2 * key_width), bf16),
-        ),
-        [smem(), smem()] + [vmem()] * 4,
-    )(place, loss_rows, hidden, queries, key_states, attention_values)
+    packed = call(
+        functools.partial(pack_body, loss_per),
+        shape((tokens + extra, 2 * key_width), bf16),
+        [smem(), smem()] + [vmem()] * 3,
+    )(place, loss_rows, queries, key_states, attention_values)
     by_z = jnp.stack([picked] + [shifted(picked, "ctx", s, CORES) for s in range(1, nz)])
-    by_plane = jnp.stack([by_z] + [shifted(by_z, "vocab", s) for s in range(1, nv)])
+    by_plane = lax.all_gather(by_z, "vocab")
     other = swapped(by_plane)
-
-    target_blocks = (
-        target_rows.reshape(nv, per_vocab, nc, block_width)
-        .transpose(2, 0, 1, 3)
-        .reshape(nc * nv * per_vocab, block_width)
-    )
-    other, packed, target_blocks = lax.optimization_barrier((other, packed, target_blocks))
+    other, packed = lax.optimization_barrier((other, packed))
     packed_all = lax.all_gather(packed, "ctx")
-    target_mine = lax.psum_scatter(
-        target_blocks, ("ctx", "vocab"), scatter_dimension=0, tiled=True
-    )
 
     first = voc_rows % CHUNK
     if voc_rows < SLOTS * CHUNK or first % 16 or not first:
@@ -547,7 +626,7 @@
         functools.partial(flash_body, first),
         out_shape=(
             shape((nz, loss, block_width), f32),
-            shape((nz, loss, block_width), bf16),
+            shape((loss, nz * block_width + LANES), bf16),
             shape((loss, LANES), f32),
             shape((per_vocab, block_width), f32),
         ),
@@ -587,60 +666,88 @@
         exps=heads * group * loss * all_tokens,
     )(place, key_pos, query_pos, packed_all)
 
-    got, got_stats = swapped(send), swapped(stats)
+    got = swapped(send)
     stats, keep, *sends = call(
         functools.partial(core_body, nv - 1),
         (
-            shape((loss, LANES), f32),
+            shape((per_vocab, LANES), f32),
             shape((nz, per_vocab, block_width), f32),
         )
-        + (shape((nz, per_vocab, block_width), bf16),) * (nv - 1),
+        + (shape((per_vocab, (nz + 1) * block_width + LANES), bf16),) * (nv - 1),
         [smem()] + [vmem()] * 4,
-        [pltpu.VMEM((nz, loss, block_width), f32)],
-    )(place, keep, got, stats, got_stats)
+        [
+            pltpu.VMEM((nz, loss, block_width), f32),
+            pltpu.VMEM((loss, LANES), f32),
+            pltpu.VMEM((loss, LANES), bf16),
+        ],
+    )(place, keep, got, stats, target_rows)
     got = [shifted(sends[s - 1], "vocab", s) for s in range(1, nv)]
-    tables = [stats] + [shifted(stats, "vocab", s) for s in range(1, nv)]
-    stats, keep, *sends = call(
-        functools.partial(plane_body, nv - 1, nz),
-        (shape((loss, LANES), f32), shape((per_vocab, block_width), f32))
-        + (shape((per_vocab, block_width), bf16),) * (nz - 1),
-        [smem()] + [vmem()] * (1 + (nv - 1) + nv),
-        [
-            pltpu.VMEM((nv, loss, LANES), f32),
-            pltpu.VMEM((nz, per_vocab, block_width), f32),
-        ],
-    )(place, keep, *got, *tables)
+
+    stats, packed_all = lax.optimization_barrier((stats, packed_all))
+    at_once = max(1, min(group, (4 * 2**20) // (loss * all_tokens * 4)))
+    p_own, p_rows, out = call(
+        functools.partial(forward_body, loss_per, heads, group, at_once),
+        (
+            shape((heads, group * loss, tokens), f32),
+            shape((heads, group * loss_per, all_tokens), f32),
+            shape((heads, group * loss, HEAD_SIZE), f32),
+        ),
+        [smem()] + [vmem()] * 3,
+        [pltpu.VMEM((at_once * loss, all_tokens), f32)],
+        flops=6 * heads * group * loss * all_tokens * HEAD_SIZE,
+        moved=2 * packed_all.size,
+        exps=heads * group * loss * all_tokens,
+    )(place, key_pos, query_pos, packed_all)
+    stats, p_own, p_rows, out = lax.optimization_barrier((stats, p_own, p_rows, out))
+
+    stats, keep, target_rows, *sends = call(
+        functools.partial(plane_body, nv - 1),
+        (
+            shape((per_vocab, LANES), f32),
+            shape((per_vocab, block_width), f32),
+            shape((per_vocab, block_width), bf16),
+        )
+        + (shape((per_vocab, block_width + LANES), bf16),) * (nz - 1),
+        [smem()] + [vmem()] * (3 + nv - 1),
+        [pltpu.VMEM((nz, per_vocab, block_width), f32)],
+    )(place, keep, stats, target_rows, *got)
     got = [shifted(sends[s - 1], "ctx", s, CORES) for s in range(1, nz)]
-    tables = [stats] + [shifted(stats, "ctx", s, CORES) for s in range(1, nz)]
-    resid, mean_loss = call(
-        functools.partial(line_body, nz, width),
-        (shape((per_vocab, block_width), bf16), shape((8, LANES), f32)),
-        [smem()] + [vmem()] * (1 + (nz - 1) + nz + 3),
-        [pltpu.VMEM((nz, loss, LANES), f32), pltpu.VMEM((loss, LANES), f32)],
-    )(place, keep, *got, *tables, target_mine, unit, gain)
-
-    pieces = [resid] + [shifted(resid, "vocab", s) for s in range(1, nv)]
-    rows, cols = loss // nz, query_width // CORES
-    resid_rows, keep, *sends = call(
-        functools.partial(project_body, nv, nc),
-        (shape((loss, block_width), bf16), shape((rows, cols), f32))
-        + (shape((rows, cols), bf16),) * (nc - 1),
-        [smem()] + [vmem()] * (nv + 1),
+    message = call(
+        functools.partial(line_body, nz - 1, width),
+        shape((per_vocab, block_width + LANES), bf16),
+        [smem()] + [vmem()] * (5 + nz - 1),
+    )(place, keep, stats, target_rows, unit, gain, *got)
+
+    gathered = lax.all_gather(message, "vocab")
+    cols = query_width // CORES
+    rows = loss // nz
+    resid_rows, mean_loss, keep, send = call(
+        project_body,
+        (
+            shape((loss, block_width), bf16),
+            shape((8, LANES), f32),
+            shape((loss, cols), f32),
+            shape((loss, cols), bf16),
+        ),
+        [smem()] + [vmem()] * 2,
         [pltpu.VMEM((loss, block_width), bf16), pltpu.VMEM((loss, query_width), f32)],
-    )(place, *pieces, output_weight)
-    got = [shifted(sends[s - 1], "ctx", s) for s in range(1, nc)]
-    piece = call(sum_body, shape((rows, cols), bf16), [vmem()] * nc)(keep, *got)
-    pieces = [piece] + [shifted(piece, "ctx", s) for s in range(1, nc)]
+    )(place, gathered, output_weight)
+    parts = call(half_body, shape((nz, rows, cols), bf16), [vmem()] * 2)(keep, swapped(send))
+    lines = [[CORES * z + c for z in range(nz)] for c in range(CORES)]
+    parts = lax.all_to_all(parts, "ctx", 0, 0, axis_index_groups=lines)
+    piece = call(sum_body, shape((rows, cols), bf16), [vmem()])(parts)
+    half = jnp.stack([piece] + [shifted(piece, "ctx", s, CORES) for s in range(1, nz)])
+    other = swapped(half)
     query_grad, key_grad, value_grad = call(
-        functools.partial(backward_body, loss_per, heads, group, nc),
+        functools.partial(backward_body, loss_per, heads, group),
         (
             shape((loss_per, query_width), bf16),
             shape((tokens, key_width), bf16),
             shape((tokens, key_width), bf16),
         ),
-        [smem()] + [vmem()] * (nc + 4),
+        [smem()] + [vmem()] * 6,
         [pltpu.VMEM((loss, query_width), f32)],
-    )(place, *pieces, packed_all, p_own, p_rows, out)
+    )(place, half, other, packed_all, p_own, p_rows, out)
     return (mean_loss[0, 0], query_grad, key_grad, value_grad, resid_rows.T)
 
 

time: 229 us -> 148 us (0.65)
  waiting for transfers between devices: 77.8 us -> 14.9 us
  starting transfers between devices: 50.1 us -> 25.6 us
  blocking collectives: 0 us -> 23.2 us
  local copies, waits for them, and re-layouts: 19.4 us -> 3.94 us
  other arithmetic: 3.8 us -> 0.22 us
  Pallas kernels: 61.1 us -> 64.3 us
    reduce_scatter x1, waiting for transfers between devices: 52.3 us -> 0.01 us  [per_device(): lax.psum_scatter(target_rows.reshape(nc * loss, block_width), 'ctx', scat...]
    ppermute x35 -> x12, starting transfers between devices: 45.9 us -> 12.6 us  [shifted(): return lax.ppermute(value, axis, pairs)]
    all_gather x0 -> x2, blocking collectives: none -> 14.7 us  [the longest x1 8.27 us: per_device(): by_plane = lax.all_gather(by_z, 'vocab')]
    ppermute x35 -> x12, waiting for transfers between devices: 24 us -> 11.9 us  [shifted(): return lax.ppermute(value, axis, pairs)]
    ppermute x3 -> x4, starting transfers between devices: 3.91 us -> 12.9 us  [swapped(): return lax.ppermute(value, 'ctx', [(i, i ^ 1) for i in range(size)])]
    all_to_all x0 -> x1, blocking collectives: none -> 8.49 us  [per_device(): parts = lax.all_to_all(parts, 'ctx', 0, 0, axis_index_groups=lines)]
    unnamed x27 -> x28, local copies, waits for them, and re-layouts: 11.4 us -> 3.07 us
    gather x1 -> x0, local copies, waits for them, and re-layouts: 6.46 us -> none  [per_device(): head_weight.at[jnp.clip(local, 0, voc_rows - 1)]]
  transfers between devices with their start and end apart: 40 -> 18, of which waited for: 15 -> 13; matrix products, arithmetic and copies ran while one was open for 5% -> 1% of each run, Pallas kernels for 25% -> 37%
where the time goes in v2:
time: 148 us; the launch traced here: 146 us
  Pallas kernels  64.3 us (43%)
  starting transfers between devices  25.6 us (17%)
  blocking collectives  23.2 us (16%)
  waiting for transfers between devices  14.9 us (10%)
  between operations  14.2 us (10%)
  local copies, waits for them, and re-layouts  3.94 us (3%)
    pallas_call x1, Pallas kernels, per_device(): pl.pallas_call(functools.partial(flash_body, first), out_shape=(shape((nz...  46.7 us
    ppermute x4, starting transfers between devices, swapped(): return lax.ppermute(value, 'ctx', [(i, i ^ 1) for i in range(size)])  12.9 us
    ppermute x12, starting transfers between devices, shifted(): return lax.ppermute(value, axis, pairs)  12.6 us
    ppermute x12, waiting for transfers between devices, shifted(): return lax.ppermute(value, axis, pairs)  11.9 us
    all_to_all x1, blocking collectives, per_device(): parts = lax.all_to_all(parts, 'ctx', 0, 0, axis_index_groups=lines)  8.49 us
    all_gather x1, blocking collectives, per_device(): by_plane = lax.all_gather(by_z, 'vocab')  8.27 us
    all_gather x1, blocking collectives, per_device(): gathered = lax.all_gather(message, 'vocab')  6.44 us
    pallas_call x1, Pallas kernels, per_device(): call(functools.partial(forward_body, loss_per, heads, group, at_once), (s...  4.08 us
  transfers between devices with their start and end apart: 18, of which 13 were waited for; matrix products, arithmetic and copies ran while one was open for 1% of the time, Pallas kernels for 37%

profile of v2, /device:TPU:3, one launch (start us, length us, event | category | flops | bytes accessed | tf_op | source)
XLA Modules:
  0.0 146.4 jit_solution(10179602702109028237)
XLA Ops:
  8.0 4.1 %shard_map.140 = bf16[8,64,1024]{2,1,0:T(8,128)(2,1)} custom-call(s32[5]{0:T(128)S(1)} %stack.53.place, s32[64]{0:T(128)S(1)} %copy-done.11, bf16[4752,8192]{1,0:T(8,128)(2,1)} %weight.4), custom_call_target="tpu_custom_call" | custom-call | tf_op jit(solution)/shard_map/pallas_call | solution.py:586
  12.2 0.7 shard_map.137
  12.9 1.4 collective-permute-start
  14.3 2.5 %collective-permute-start.1 = (bf16[16,1024]{1,0:T(8,128)(2,1)S(1)}, bf16[16,1024]{1,0:T(8,128)(2,1)S(1)}, u32[]{:S(2)}, u32[]{:S(2)}) collective-permute-start(bf16[16,1024]{1,0:T(8,128)(2,1)S(1)} %shard_map.137), channel_id=1, source_target_pairs={{0,4},{1,5},{2,6},{3,7},{4,0},{5,1},{6,2},{7,3},{8,12},{9,13},{10,... | collective-permute-start | bytes 98312 | tf_op jit(solution)/shard_map/ppermute | solution.py:60
  18.2 1.9 %collective-permute-done.2 = bf16[16,1024]{1,0:T(8,128)(2,1)S(1)} collective-permute-done((bf16[16,1024]{1,0:T(8,128)(2,1)S(1)}, bf16[16,1024]{1,0:T(8,128)(2,1)S(1)}, u32[]{:S(2)}, u32[]{:S(2)}) %collective-permute-start.2) | collective-permute-done | bytes 32800 | tf_op jit(solution)/shard_map/ppermute | solution.py:60
  20.2 8.3 %all-gather = bf16[16,16,1024]{2,1,0:T(8,128)(2,1)S(1)} all-gather(bf16[4,16,1024]{2,1,0:T(8,128)(2,1)S(1)} %pad_maximum_fusion), channel_id=2, replica_groups=mesh['vocab'=4,'ctx'=8] {'vocab'}, dimensions={0}, use_global_device_ids=true | all-gather | bytes 655360 | tf_op jit(solution)/shard_map/all_gather | solution.py:615
  28.4 4.3 %collective-permute-start.3 = (bf16[4,4,16,1024]{3,2,1,0:T(8,128)(2,1)S(1)}, bf16[4,4,16,1024]{3,2,1,0:T(8,128)(2,1)S(1)}, u32[]{:S(2)}, u32[]{:S(2)}) collective-permute-start(bf16[4,4,16,1024]{3,2,1,0:T(8,128)(2,1)S(1)} %bitcast.23), channel_id=1, source_target_pairs={{0,1},{1,0},{2,3},{3,2},{4,5},{5,4},{6,7},{7,6},{8,9},{9,8},{10,11... | collective-permute-start | bytes 1572872 | tf_op jit(solution)/shard_map/ppermute | solution.py:65
  32.7 1.4 shard_map.138
  34.4 46.7 %shard_map.139 = (f32[4,64,1024]{2,1,0:T(8,128)S(1)}, bf16[64,4224]{1,0:T(8,128)(2,1)S(1)}, f32[64,128]{1,0:T(8,128)S(1)}, f32[16,1024]{1,0:T(8,128)S(1)}) custom-call(s32[5]{0:T(128)S(1)} %stack.53.place, bf16[4,4,16,1024]{3,2,1,0:T(8,128)(2,1)S(1)} %bitcast.24, bf16[4,4,16,1024]{3,2,1,0:T(8,128)(2,1)S(1)} %collective-permute-done.3.other, ...), custom_call_target="tpu_custom_call" | custom-call | flops 9965666304 | bytes 77856768 | tf_op jit(solution)/shard_map/pallas_call | solution.py:625
  81.7 1.4 collective-permute-done.4.got
  83.1 0.9 copy-done.3
  84.0 1.1 shard_map.141
  85.1 1.2 collective-permute-start.5
  86.9 1.5 copy-done.1
  88.4 4.1 %shard_map.142 = (f32[2,512,128]{2,1,0:T(8,128)S(1)}, f32[2,64,1024]{2,1,0:T(8,128)S(1)}, f32[2,512,128]{2,1,0:T(8,128)S(1)}) custom-call(s32[5]{0:T(128)S(1)} %stack.53.place, s32[1,1024]{1,0:T(1,128)S(1)} %add.58.key_pos, s32[64,1]{1,0:T(8,128)S(1)} %copy.20.query_pos, bf16[8,160,512]{2,1,0:T(8,128)(2,1)S(1)} %bitcast.25), custom_call_target="tpu_custom_call" | custom-call | flops 805306368 | bytes 1310720 | tf_op jit(solution)/shard_map/pallas_call | solution.py:688
  92.5 2.6 %collective-permute-done.6.rest_1_ = bf16[16,5248]{1,0:T(8,128)(2,1)S(1)} collective-permute-done((bf16[16,5248]{1,0:T(8,128)(2,1)S(1)}, bf16[16,5248]{1,0:T(8,128)(2,1)S(1)}, u32[]{:S(2)}, u32[]{:S(2)}) %collective-permute-start.6) | collective-permute-done | bytes 167968 | tf_op jit(solution)/shard_map/ppermute | solution.py:60
  95.2 1.0 shard_map.143
  96.2 2.7 %collective-permute-start.10 = (bf16[16,1152]{1,0:T(8,128)(2,1)S(1)}, bf16[16,1152]{1,0:T(8,128)(2,1)S(1)}, u32[]{:S(2)}, u32[]{:S(2)}) collective-permute-start(bf16[16,1152]{1,0:T(8,128)(2,1)S(1)} %get-tuple-element.64), channel_id=1, source_target_pairs={{0,6},{1,7},{2,0},{3,1},{4,2},{5,3},{6,4},{7,5},{8,14},{9,15},{10,... | collective-permute-start | bytes 110600 | tf_op jit(solution)/shard_map/ppermute | solution.py:60
  99.3 0.7 collective-permute-done.10.rest_2_
  100.0 3.5 %collective-permute-done.8.rest_0_ = bf16[16,1152]{1,0:T(8,128)(2,1)S(1)} collective-permute-done((bf16[16,1152]{1,0:T(8,128)(2,1)S(1)}, bf16[16,1152]{1,0:T(8,128)(2,1)S(1)}, u32[]{:S(2)}, u32[]{:S(2)}) %collective-permute-start.8) | collective-permute-done | bytes 36896 | tf_op jit(solution)/shard_map/ppermute | solution.py:60
  103.5 0.9 shard_map.144
  104.5 6.4 %all-gather.2 = bf16[64,1152]{1,0:T(8,128)(2,1)S(1)} all-gather(bf16[16,1152]{1,0:T(8,128)(2,1)S(1)} %shard_map.144), channel_id=4, replica_groups=mesh['vocab'=4,'ctx'=8] {'vocab'}, dimensions={0}, use_global_device_ids=true | all-gather | bytes 184320 | tf_op jit(solution)/shard_map/all_gather | solution.py:721
  110.9 2.0 %shard_map.145 = (bf16[64,1024]{1,0:T(8,128)(2,1)}, f32[8,128]{1,0:T(8,128)S(1)}, f32[64,1024]{1,0:T(8,128)S(1)}, bf16[64,1024]{1,0:T(8,128)(2,1)S(1)}) custom-call(s32[5]{0:T(128)S(1)} %stack.53.place, bf16[4,16,1152]{2,1,0:T(8,128)(2,1)S(1)} %bitcast.27, bf16[2048,1024]{1,0:T(8,128)(2,1)S(1)} %copy-done), custom_call_target="tpu_custom_call" | custom-call | tf_op jit(solution)/shard_map/pallas_call | solution.py:724
  112.9 5.0 %collective-permute-start.11 = (bf16[64,1024]{1,0:T(8,128)(2,1)S(1)}, bf16[64,1024]{1,0:T(8,128)(2,1)S(1)}, u32[]{:S(2)}, u32[]{:S(2)}) collective-permute-start(bf16[64,1024]{1,0:T(8,128)(2,1)S(1)} %get-tuple-element.67), channel_id=1, source_target_pairs={{0,1},{1,0},{2,3},{3,2},{4,5},{5,4},{6,7},{7,6},{8,9},{9,8},{10,11... | collective-permute-start | bytes 393224 | tf_op jit(solution)/shard_map/ppermute | solution.py:65
  117.9 1.0 collective-permute-done.11.got
  118.9 8.5 %all_to_all.5.parts = bf16[4,16,1024]{2,1,0:T(8,128)(2,1)S(1)} all-to-all(bf16[4,16,1024]{2,1,0:T(8,128)(2,1)S(1)} %shard_map.146), channel_id=1, replica_groups={{0,2,4,6},{1,3,5,7},{8,10,12,14},{9,11,13,15},{16,18,20,22},{17,19,21,2..., dimensions={0} | all-to-all | bytes 262144 | tf_op jit(solution)/shard_map/all_to_all | solution.py:737
  127.4 1.0 collective-permute-start.12
  128.5 1.6 %collective-permute-start.13 = (bf16[16,1024]{1,0:T(8,128)(2,1)S(1)}, bf16[16,1024]{1,0:T(8,128)(2,1)S(1)}, u32[]{:S(2)}, u32[]{:S(2)}) collective-permute-start(bf16[16,1024]{1,0:T(8,128)(2,1)S(1)} %shard_map.147), channel_id=1, source_target_pairs={{0,4},{1,5},{2,6},{3,7},{4,0},{5,1},{6,2},{7,3},{8,12},{9,13},{10,... | collective-permute-start | bytes 98312 | tf_op jit(solution)/shard_map/ppermute | solution.py:60
  130.8 1.3 collective-permute-done.12
  132.1 0.7 collective-permute-done.13
  133.1 3.1 %collective-permute-start.15 = (bf16[4,16,1024]{2,1,0:T(8,128)(2,1)S(1)}, bf16[4,16,1024]{2,1,0:T(8,128)(2,1)S(1)}, u32[]{:S(2)}, u32[]{:S(2)}) collective-permute-start(bf16[4,16,1024]{2,1,0:T(8,128)(2,1)S(1)} %pad_maximum_fusion.1.half), channel_id=1, source_target_pairs={{0,1},{1,0},{2,3},{3,2},{4,5},{5,4},{6,7},{7,6},{8,9},{9,8},{10,11... | collective-permute-start | bytes 393224 | tf_op jit(solution)/shard_map/ppermute | solution.py:65
  137.2 2.3 %shard_map.148 = (bf16[8,2048]{1,0:T(8,128)(2,1)}, bf16[128,256]{1,0:T(8,128)(2,1)}, bf16[128,256]{1,0:T(8,128)(2,1)}) custom-call(s32[5]{0:T(128)S(1)} %stack.53.place, bf16[4,16,1024]{2,1,0:T(8,128)(2,1)S(1)} %pad_maximum_fusion.1.half, bf16[4,16,1024]{2,1,0:T(8,128)(2,1)S(1)} %collective-permute-done.15.other, bf16[8,160,512]{2,1,0:T(8,128)(2,1)S(1)} %bitcast.26, ...), custom_call_target="tpu_custom_call" | custom-call | tf_op jit(solution)/shard_map/pallas_call | solution.py:741
  (61 shorter events, 6.1 us)
Async XLA Ops:
  7.2 76.0 %reduce-scatter.2.cloned.1.call-start = ((), (), s32[]{:S(2)}) async-start(), calls=%async_computation.2 | async-start | bytes 1179648 | tf_op jit(solution)/shard_map/reduce_scatter | solution.py:598
  7.3 0.7 copy-start.11
  8.0 4.2 %copy-start.6 = (bf16[128,2048]{1,0:T(8,128)(2,1)S(1)}, bf16[128,2048]{1,0:T(8,128)(2,1)}, u32[]{:S(2)}) copy-start(bf16[128,2048]{1,0:T(8,128)(2,1)} %hidden.1) | copy-start | bytes 1572868
  8.0 4.2 %copy-start.10 = (s32[64]{0:T(128)S(1)}, s32[64]{0:T(128)}, u32[]{:S(2)}) copy-start(s32[64]{0:T(128)} %rows.3) | copy-start | bytes 772
  8.0 24.8 %copy-start.5 = (bf16[128,2048]{1,0:T(8,128)(2,1)S(1)}, bf16[128,2048]{1,0:T(8,128)(2,1)}, u32[]{:S(2)}) copy-start(bf16[128,2048]{1,0:T(8,128)(2,1)} %queries) | copy-start | bytes 1572868
  8.0 24.8 %copy-start.8 = (bf16[128,256]{1,0:T(8,128)(2,1)S(1)}, bf16[128,256]{1,0:T(8,128)(2,1)}, u32[]{:S(2)}) copy-start(bf16[128,256]{1,0:T(8,128)(2,1)} %keys.1) | copy-start | bytes 196612
  8.0 24.8 %copy-start.9 = (bf16[128,256]{1,0:T(8,128)(2,1)S(1)}, bf16[128,256]{1,0:T(8,128)(2,1)}, u32[]{:S(2)}) copy-start(bf16[128,256]{1,0:T(8,128)(2,1)} %values.1) | copy-start | bytes 196612
  8.0 26.3 %copy-start.12 = (s32[64]{0:T(128)S(1)}, s32[64]{0:T(128)}, u32[]{:S(2)}) copy-start(s32[64]{0:T(128)} %targets.1) | copy-start | bytes 772
  8.0 26.4 %copy-start.7 = (f32[8192]{0:T(1024)S(1)}, f32[8192]{0:T(1024)}, u32[]{:S(2)}) copy-start(f32[8192]{0:T(1024)} %param.11) | copy-start | bytes 98308
  12.1 74.8 %all-gather.5.cloned.1.call-start = ((), (), s32[]{:S(2)}) async-start(), calls=%async_computation.3 | async-start | bytes 1474560 | tf_op jit(solution)/shard_map/all_gather | solution.py:618
  12.9 5.0 %collective-permute-start = (bf16[16,1024]{1,0:T(8,128)(2,1)S(1)}, bf16[16,1024]{1,0:T(8,128)(2,1)S(1)}, u32[]{:S(2)}, u32[]{:S(2)}) collective-permute-start(bf16[16,1024]{1,0:T(8,128)(2,1)S(1)} %shard_map.137), channel_id=1, source_target_pairs={{0,2},{1,3},{2,4},{3,5},{4,6},{5,7},{6,0},{7,1},{8,10},{9,11},{10,... | collective-permute-start | bytes 98312 | tf_op jit(solution)/shard_map/ppermute | solution.py:60
  14.3 3.9 %collective-permute-start.1 = (bf16[16,1024]{1,0:T(8,128)(2,1)S(1)}, bf16[16,1024]{1,0:T(8,128)(2,1)S(1)}, u32[]{:S(2)}, u32[]{:S(2)}) collective-permute-start(bf16[16,1024]{1,0:T(8,128)(2,1)S(1)} %shard_map.137), channel_id=1, source_target_pairs={{0,4},{1,5},{2,6},{3,7},{4,0},{5,1},{6,2},{7,3},{8,12},{9,13},{10,... | collective-permute-start | bytes 98312 | tf_op jit(solution)/shard_map/ppermute | solution.py:60
  16.8 3.3 %collective-permute-start.2 = (bf16[16,1024]{1,0:T(8,128)(2,1)S(1)}, bf16[16,1024]{1,0:T(8,128)(2,1)S(1)}, u32[]{:S(2)}, u32[]{:S(2)}) collective-permute-start(bf16[16,1024]{1,0:T(8,128)(2,1)S(1)} %shard_map.137), channel_id=1, source_target_pairs={{0,6},{1,7},{2,0},{3,1},{4,2},{5,3},{6,4},{7,5},{8,14},{9,15},{10,... | collective-permute-start | bytes 98312 | tf_op jit(solution)/shard_map/ppermute | solution.py:60
  28.4 5.8 %collective-permute-start.3 = (bf16[4,4,16,1024]{3,2,1,0:T(8,128)(2,1)S(1)}, bf16[4,4,16,1024]{3,2,1,0:T(8,128)(2,1)S(1)}, u32[]{:S(2)}, u32[]{:S(2)}) collective-permute-start(bf16[4,4,16,1024]{3,2,1,0:T(8,128)(2,1)S(1)} %bitcast.23), channel_id=1, source_target_pairs={{0,1},{1,0},{2,3},{3,2},{4,5},{5,4},{6,7},{7,6},{8,9},{9,8},{10,11... | collective-permute-start | bytes 1572872 | tf_op jit(solution)/shard_map/ppermute | solution.py:65
  34.4 47.1 %copy-start.13 = (s32[16]{0:T(128)S(1)}, s32[16]{0:T(128)}, u32[]{:S(2)}) copy-start(s32[16]{0:T(128)} %param.15) | copy-start | bytes 196
  81.1 2.0 %collective-permute-start.4 = (bf16[64,4224]{1,0:T(8,128)(2,1)S(1)}, bf16[64,4224]{1,0:T(8,128)(2,1)S(1)}, u32[]{:S(2)}, u32[]{:S(2)}) collective-permute-start(bf16[64,4224]{1,0:T(8,128)(2,1)S(1)} %get-tuple-element.44), channel_id=1, source_target_pairs={{0,1},{1,0},{2,3},{3,2},{4,5},{5,4},{6,7},{7,6},{8,9},{9,8},{10,11... | collective-permute-start | bytes 1622024 | tf_op jit(solution)/shard_map/ppermute | solution.py:65
  83.1 0.9 copy-start.3
  84.0 11.1 %copy-start.4 = (bf16[64,1024]{1,0:T(8,128)(2,1)S(1)}, bf16[64,1024]{1,0:T(8,128)(2,1)}, u32[]{:S(2)}) copy-start(bf16[64,1024]{1,0:T(8,128)(2,1)} %reduce-scatter.2.cloned.1.call-done.target_rows) | copy-start | bytes 393220
  85.1 7.4 %collective-permute-start.5 = (bf16[16,5248]{1,0:T(8,128)(2,1)S(1)}, bf16[16,5248]{1,0:T(8,128)(2,1)S(1)}, u32[]{:S(2)}, u32[]{:S(2)}) collective-permute-start(bf16[16,5248]{1,0:T(8,128)(2,1)S(1)} %get-tuple-element.55), channel_id=1, source_target_pairs={{0,8},{8,16},{16,24},{24,0},{1,9},{9,17},{17,25},{25,1},{2,10},{10... | collective-permute-start | bytes 503816 | tf_op jit(solution)/shard_map/ppermute | solution.py:60
  86.4 8.8 %collective-permute-start.6 = (bf16[16,5248]{1,0:T(8,128)(2,1)S(1)}, bf16[16,5248]{1,0:T(8,128)(2,1)S(1)}, u32[]{:S(2)}, u32[]{:S(2)}) collective-permute-start(bf16[16,5248]{1,0:T(8,128)(2,1)S(1)} %get-tuple-element.56), channel_id=1, source_target_pairs={{0,16},{8,24},{16,0},{24,8},{1,17},{9,25},{17,1},{25,9},{2,18},{10... | collective-permute-start | bytes 503816 | tf_op jit(solution)/shard_map/ppermute | solution.py:60
  86.4 8.8 %collective-permute-start.7 = (bf16[16,5248]{1,0:T(8,128)(2,1)S(1)}, bf16[16,5248]{1,0:T(8,128)(2,1)S(1)}, u32[]{:S(2)}, u32[]{:S(2)}) collective-permute-start(bf16[16,5248]{1,0:T(8,128)(2,1)S(1)} %get-tuple-element.57), channel_id=1, source_target_pairs={{0,24},{8,0},{16,8},{24,16},{1,25},{9,1},{17,9},{25,17},{2,26},{10... | collective-permute-start | bytes 503816 | tf_op jit(solution)/shard_map/ppermute | solution.py:60
  86.9 24.0 %copy-start = (bf16[2048,1024]{1,0:T(8,128)(2,1)S(1)}, bf16[2048,1024]{1,0:T(8,128)(2,1)}, u32[]{:S(2)}) copy-start(bf16[2048,1024]{1,0:T(8,128)(2,1)} %weight.5) | copy-start | bytes 12582916
  86.9 1.5 %copy-start.1 = (bf16[1280,512]{1,0:T(8,128)(2,1)S(1)}, bf16[1280,512]{1,0:T(8,128)(2,1)}, u32[]{:S(2)}) copy-start(bf16[1280,512]{1,0:T(8,128)(2,1)} %all-gather.5.cloned.1.call-done) | copy-start | bytes 3932164
  92.5 44.8 %copy-start.2 = (bf16[1280,512]{1,0:T(8,128)(2,1)S(1)}, bf16[1280,512]{1,0:T(8,128)(2,1)}, u32[]{:S(2)}) copy-start(bf16[1280,512]{1,0:T(8,128)(2,1)} %all-gather.5.cloned.1.call-done) | copy-start | bytes 3932164
  96.2 3.8 %collective-permute-start.10 = (bf16[16,1152]{1,0:T(8,128)(2,1)S(1)}, bf16[16,1152]{1,0:T(8,128)(2,1)S(1)}, u32[]{:S(2)}, u32[]{:S(2)}) collective-permute-start(bf16[16,1152]{1,0:T(8,128)(2,1)S(1)} %get-tuple-element.64), channel_id=1, source_target_pairs={{0,6},{1,7},{2,0},{3,1},{4,2},{5,3},{6,4},{7,5},{8,14},{9,15},{10,... | collective-permute-start | bytes 110600 | tf_op jit(solution)/shard_map/ppermute | solution.py:60
  98.9 4.6 %collective-permute-start.8 = (bf16[16,1152]{1,0:T(8,128)(2,1)S(1)}, bf16[16,1152]{1,0:T(8,128)(2,1)S(1)}, u32[]{:S(2)}, u32[]{:S(2)}) collective-permute-start(bf16[16,1152]{1,0:T(8,128)(2,1)S(1)} %get-tuple-element.62), channel_id=1, source_target_pairs={{0,2},{1,3},{2,4},{3,5},{4,6},{5,7},{6,0},{7,1},{8,10},{9,11},{10,... | collective-permute-start | bytes 110600 | tf_op jit(solution)/shard_map/ppermute | solution.py:60
  98.9 4.6 %collective-permute-start.9 = (bf16[16,1152]{1,0:T(8,128)(2,1)S(1)}, bf16[16,1152]{1,0:T(8,128)(2,1)S(1)}, u32[]{:S(2)}, u32[]{:S(2)}) collective-permute-start(bf16[16,1152]{1,0:T(8,128)(2,1)S(1)} %get-tuple-element.63), channel_id=1, source_target_pairs={{0,4},{1,5},{2,6},{3,7},{4,0},{5,1},{6,2},{7,3},{8,12},{9,13},{10,... | collective-permute-start | bytes 110600 | tf_op jit(solution)/shard_map/ppermute | solution.py:60
  112.9 6.0 %collective-permute-start.11 = (bf16[64,1024]{1,0:T(8,128)(2,1)S(1)}, bf16[64,1024]{1,0:T(8,128)(2,1)S(1)}, u32[]{:S(2)}, u32[]{:S(2)}) collective-permute-start(bf16[64,1024]{1,0:T(8,128)(2,1)S(1)} %get-tuple-element.67), channel_id=1, source_target_pairs={{0,1},{1,0},{2,3},{3,2},{4,5},{5,4},{6,7},{7,6},{8,9},{9,8},{10,11... | collective-permute-start | bytes 393224 | tf_op jit(solution)/shard_map/ppermute | solution.py:65
  127.4 4.6 %collective-permute-start.12 = (bf16[16,1024]{1,0:T(8,128)(2,1)S(1)}, bf16[16,1024]{1,0:T(8,128)(2,1)S(1)}, u32[]{:S(2)}, u32[]{:S(2)}) collective-permute-start(bf16[16,1024]{1,0:T(8,128)(2,1)S(1)} %shard_map.147), channel_id=1, source_target_pairs={{0,2},{1,3},{2,4},{3,5},{4,6},{5,7},{6,0},{7,1},{8,10},{9,11},{10,... | collective-permute-start | bytes 98312 | tf_op jit(solution)/shard_map/ppermute | solution.py:60
  128.5 4.3 %collective-permute-start.13 = (bf16[16,1024]{1,0:T(8,128)(2,1)S(1)}, bf16[16,1024]{1,0:T(8,128)(2,1)S(1)}, u32[]{:S(2)}, u32[]{:S(2)}) collective-permute-start(bf16[16,1024]{1,0:T(8,128)(2,1)S(1)} %shard_map.147), channel_id=1, source_target_pairs={{0,4},{1,5},{2,6},{3,7},{4,0},{5,1},{6,2},{7,3},{8,12},{9,13},{10,... | collective-permute-start | bytes 98312 | tf_op jit(solution)/shard_map/ppermute | solution.py:60
  130.1 3.0 %collective-permute-start.14 = (bf16[16,1024]{1,0:T(8,128)(2,1)S(1)}, bf16[16,1024]{1,0:T(8,128)(2,1)S(1)}, u32[]{:S(2)}, u32[]{:S(2)}) collective-permute-start(bf16[16,1024]{1,0:T(8,128)(2,1)S(1)} %shard_map.147), channel_id=1, source_target_pairs={{0,6},{1,7},{2,0},{3,1},{4,2},{5,3},{6,4},{7,5},{8,14},{9,15},{10,... | collective-permute-start | bytes 98312 | tf_op jit(solution)/shard_map/ppermute | solution.py:60
  133.1 4.1 %collective-permute-start.15 = (bf16[4,16,1024]{2,1,0:T(8,128)(2,1)S(1)}, bf16[4,16,1024]{2,1,0:T(8,128)(2,1)S(1)}, u32[]{:S(2)}, u32[]{:S(2)}) collective-permute-start(bf16[4,16,1024]{2,1,0:T(8,128)(2,1)S(1)} %pad_maximum_fusion.1.half), channel_id=1, source_target_pairs={{0,1},{1,0},{2,3},{3,2},{4,5},{5,4},{6,7},{7,6},{8,9},{9,8},{10,11... | collective-permute-start | bytes 393224 | tf_op jit(solution)/shard_map/ppermute | solution.py:65
Sparse Core Ops, SparseCore 0:
  12.2 30.9 reduce-scatter.1
  44.8 24.8 all-gather.4

commit v3 on v2

--- a/solution.py
+++ b/solution.py
@@ -92,43 +92,43 @@
     packed[tokens : tokens + parts * loss_per, :] = jnp.concatenate(stacked, axis=0).astype(bf16)
 
 
-def target_body(place, targets, weight, out, buf, rows, sems):
-    loss, width = rows.shape
-    blocks, _, block_width = out.shape
+def target_body(place, targets, weight, out, buf, spots, sems):
+    blocks, loss, block_width = out.shape
+    width = blocks * block_width
     total_rows = weight.shape[0]
-
-    def local(i):
-        at = targets[i] - place[4]
-        return at, (at >= 0) & (at < total_rows)
-
-    def copy(i, at):
+    offset = targets[...] - place[4]
+    local = (offset >= 0) & (offset < total_rows)
+    offset = offset.astype(f32)
+    index = lax.broadcasted_iota(jnp.int32, (1, loss), 1).astype(f32)
+    none = float(loss)
+    count = jnp.sum(jnp.where(local, 1.0, 0.0)).astype(jnp.int32)
+
+    def copy(k, at):
         start = pl.multiple_of(lax.div(at, 16) * 16, 16)
-        return pltpu.make_async_copy(weight.at[pl.ds(start, 16), :], buf.at[i], sems.at[i])
-
-    @pl.loop(0, loss)
-    def _(i):
-        at, here = local(i)
-
-        @pl.when(here)
-        def _():
-            copy(i, at).start()
-
-    rows[...] = jnp.zeros_like(rows)
-
-    @pl.loop(0, loss)
-    def _(i):
-        at, here = local(i)
-
-        @pl.when(here)
-        def _():
-            copy(i, at).wait()
-            line = lax.broadcasted_iota(jnp.int32, (16, width), 0)
-            block = buf[i].astype(f32)
+        return pltpu.make_async_copy(weight.at[pl.ds(start, 16), :], buf.at[k], sems.at[k])
+
+    def begin(k, left):
+        spot = jnp.min(left)
+        at = jnp.sum(jnp.where(index == spot, offset, 0.0)).astype(jnp.int32)
+        spots[0, k] = spot.astype(jnp.int32)
+        spots[1, k] = at
+        copy(k, at).start()
+        return jnp.where(index == spot, none, left)
+
+    lax.fori_loop(0, count, begin, jnp.where(local, index, none))
+    out[...] = jnp.zeros_like(out)
+    line = lax.broadcasted_iota(jnp.int32, (16, block_width), 0)
+
+    @pl.loop(0, count)
+    def _(k):
+        spot, at = spots[0, k], spots[1, k]
+        copy(k, at).wait()
+        group = pl.ds(pl.multiple_of(lax.div(spot, 16) * 16, 16), 16)
+        for b in range(blocks):
+            block = buf[k, :, b * block_width : (b + 1) * block_width].astype(f32)
             row = jnp.sum(jnp.where(line == lax.rem(at, 16), block, 0.0), axis=0, keepdims=True)
-            rows[pl.ds(i, 1), :] = row
-
-    for b in range(blocks):
-        out[b] = rows[:, b * block_width : (b + 1) * block_width].astype(bf16)
+            before = out[b, group, :].astype(f32)
+            out[b, group, :] = jnp.where(line == lax.rem(spot, 16), row, before).astype(bf16)
 
 
 def flash_body(
@@ -199,7 +199,7 @@
         row_at = pl.multiple_of(z_src * 16, 16)
         state[pl.ds(row_at, 16), :] = jnp.broadcast_to(inv, (16, LANES))
         for vr in range(nv):
-            v_src = vr
+            v_src = lax.rem(vocab_at - vr + nv, nv)
             a = own[vr, zr].astype(f32)
             b = other[vr, zr].astype(f32)
             low = jnp.where(is_even, a, b)
@@ -271,12 +271,13 @@
             scores = scores_of(buf[here])
             add_product(probs[...], scale, lambda at, n: buf[there, :, at : at + n])
 
+            p, scale, run = softmax(scores, first_id + first + c * CHUNK, run)
+            probs[...] = p
+
             @pl.when(c + SLOTS - 1 < chunks)
             def _():
                 body_copy(c + SLOTS - 1).start()
 
-            p, scale, run = softmax(scores, first_id + first + c * CHUNK, run)
-            probs[...] = p
             return scale, run
 
         scale, run = lax.fori_loop(1, chunks, step, (scale, run))
@@ -332,9 +333,11 @@
     return table
 
 
-def core_body(count, place, keep, got, mine, target_rows, new_stats, new_keep, *rest):
-    sends, (total, table, message) = rest[:count], rest[count:]
+def core_body(count, place, keep, got, mine, target_rows, new_stats, new_keep, new_rows, *rest):
+    sends, (total, table, message, rows_here, sem) = rest[:count], rest[count:]
     nz, loss, block = keep.shape
+    rows_copy = pltpu.make_async_copy(target_rows, rows_here, sem)
+    rows_copy.start()
     columns = [stats_of(mine[...]), joined_columns(got[:, nz * block :], 4)]
     scales, merged = merge_stats(columns)
     table[...] = with_stats(mine[...], merged)
@@ -351,8 +354,13 @@
         rows = pl.ds(pl.multiple_of(to * per, per), per)
         for z in range(nz):
             sends[s][:, z * block : (z + 1) * block] = total[z, rows, :].astype(bf16)
-        sends[s][:, nz * block : (nz + 1) * block] = target_rows[rows, :]
         sends[s][:, (nz + 1) * block :] = message[rows, :]
+    rows_copy.wait()
+    for s in range(count):
+        to = lax.rem(place[0] + s + 1, count + 1)
+        rows = pl.ds(pl.multiple_of(to * per, per), per)
+        sends[s][:, nz * block : (nz + 1) * block] = rows_here[rows, :]
+    new_rows[...] = rows_here[pl.ds(at, per), :]
 
 
 def plane_body(count, place, keep, mine, target_rows, *rest):
@@ -370,7 +378,7 @@
             value = value + got[k][:, z * block : (z + 1) * block].astype(f32) * scales[k + 1]
         total[z] = value
     new_keep[...] = total[place[1]]
-    rows = target_rows[pl.ds(pl.multiple_of(place[0] * per, per), per), :].astype(f32)
+    rows = target_rows[...].astype(f32)
     for k in range(count):
         rows = rows + got[k][:, nz * block : (nz + 1) * block].astype(f32)
     new_target[...] = rows.astype(bf16)
@@ -398,13 +406,15 @@
     message[:, block:] = split_columns([log_total - logit])
 
 
-def project_body(place, gathered, weight, resid, loss_out, keep, send, whole, partial):
-    nv, per, _ = gathered.shape
+def project_body(nv, place, *refs):
+    gathered, (weight, resid, loss_out, keep, send, whole, partial) = refs[:nv], refs[nv:]
+    per = gathered[0].shape[0]
     block = whole.shape[1]
     loss_sum = jnp.zeros((1, 1), f32)
     for v in range(nv):
-        whole[v * per : (v + 1) * per, :] = gathered[v, :, :block]
-        (column,) = joined_columns(gathered[v, :, block:], 1)
+        src = lax.rem(place[0] - v + nv, nv)
+        whole[pl.ds(pl.multiple_of(src * per, per), per), :] = gathered[v][:, :block]
+        (column,) = joined_columns(gathered[v][:, block:], 1)
         loss_sum = loss_sum + jnp.sum(column, axis=0, keepdims=True)
     loss_out[...] = jnp.broadcast_to(loss_sum / (nv * per), loss_out.shape)
     resid[...] = whole[...]
@@ -414,18 +424,22 @@
     send[...] = partial[:, pl.ds(pl.multiple_of((1 - place[2]) * cols, cols), cols)].astype(bf16)
 
 
-def half_body(keep, got, out):
-    value = (keep[...] + got[...].astype(f32)).astype(bf16)
-    per = out.shape[1]
-    for z in range(out.shape[0]):
-        out[z] = value[z * per : (z + 1) * per]
-
-
-def sum_body(parts, out):
-    value = parts[0].astype(f32)
-    for z in range(1, parts.shape[0]):
-        value = value + parts[z].astype(f32)
-    out[...] = value.astype(bf16)
+def half_body(place, keep, got, new_keep, *rest):
+    sends, (total,) = rest[:-1], rest[-1:]
+    per = new_keep.shape[0]
+    nz = len(sends) + 1
+    total[...] = keep[...] + got[...].astype(f32)
+    new_keep[...] = total[pl.ds(pl.multiple_of(place[1] * per, per), per), :]
+    for s in range(nz - 1):
+        to = lax.rem(place[1] + s + 1, nz)
+        sends[s][...] = total[pl.ds(pl.multiple_of(to * per, per), per), :].astype(bf16)
+
+
+def sum_body(keep, *refs):
+    value = keep[...]
+    for ref in refs[:-1]:
+        value = value + ref[...].astype(f32)
+    refs[-1][...] = value.astype(bf16)
 
 
 def forward_body(
@@ -576,29 +590,6 @@
         stretch_of_slot[:, None] * stretch_len
         + lax.broadcasted_iota(jnp.int32, (1, stretch_len), 1)
     ).reshape(1, all_tokens)
-    if voc_rows % 16:
-        local = targets - first_id
-        is_local = (local >= 0) & (local < voc_rows)
-        target_rows = head_weight.at[jnp.clip(local, 0, voc_rows - 1)].get(mode="promise_in_bounds")
-        target_rows = jnp.where(is_local[:, None], target_rows, jnp.zeros((), bf16))
-        target_rows = target_rows.reshape(loss, nc, block_width).transpose(1, 0, 2)
-    else:
-        target_rows = pl.pallas_call(
-            target_body,
-            out_shape=shape((nc, loss, block_width), bf16),
-            in_specs=[smem(), smem(), pl.BlockSpec(memory_space=pl.ANY)],
-            out_specs=vmem(),
-            scratch_shapes=[
-                pltpu.VMEM((loss, 16, width), bf16),
-                pltpu.VMEM((loss, width), f32),
-                pltpu.SemaphoreType.DMA((loss,)),
-            ],
-            compiler_params=pltpu.CompilerParams(vmem_limit_bytes=40 * 2**20),
-        )(place, targets, head_weight)
-    target_rows = lax.psum_scatter(
-        target_rows.reshape(nc * loss, block_width), "ctx", scatter_dimension=0, tiled=True
-    )
-
     picked = call(
         functools.partial(pick_body, loss_per),
         shape((2 * loss_per, part_width // 2), bf16),
@@ -612,7 +603,34 @@
         [smem(), smem()] + [vmem()] * 3,
     )(place, loss_rows, queries, key_states, attention_values)
     by_z = jnp.stack([picked] + [shifted(picked, "ctx", s, CORES) for s in range(1, nz)])
-    by_plane = lax.all_gather(by_z, "vocab")
+    planes = [by_z] + [shifted(by_z, "vocab", s) for s in range(1, nv)]
+    by_z, targets_late = lax.optimization_barrier((by_z, targets))
+    if voc_rows % 16:
+        local = targets_late - first_id
+        is_local = (local >= 0) & (local < voc_rows)
+        target_rows = head_weight.at[jnp.clip(local, 0, voc_rows - 1)].get(mode="promise_in_bounds")
+        target_rows = jnp.where(is_local[:, None], target_rows, jnp.zeros((), bf16))
+        target_rows = target_rows.reshape(loss, nc, block_width).transpose(1, 0, 2)
+    else:
+        target_rows = pl.pallas_call(
+            target_body,
+            out_shape=shape((nc, loss, block_width), bf16),
+            in_specs=[smem(), vmem(), pl.BlockSpec(memory_space=pl.ANY)],
+            out_specs=vmem(),
+            scratch_shapes=[
+                pltpu.VMEM((loss, 16, width), bf16),
+                pltpu.SMEM((2, loss), jnp.int32),
+                pltpu.SemaphoreType.DMA((loss,)),
+            ],
+            compiler_params=pltpu.CompilerParams(vmem_limit_bytes=40 * 2**20),
+            cost_estimate=pl.CostEstimate(
+                flops=0, bytes_accessed=2 * 16 * loss * width, transcendentals=0
+            ),
+        )(place, targets_late.reshape(1, loss), head_weight)
+    target_rows = lax.psum_scatter(
+        target_rows.reshape(nc * loss, block_width), "ctx", scatter_dimension=0, tiled=True
+    )
+    by_plane = jnp.stack(planes)
     other = swapped(by_plane)
     other, packed = lax.optimization_barrier((other, packed))
     packed_all = lax.all_gather(packed, "ctx")
@@ -645,8 +663,8 @@
         ],
         compiler_params=pltpu.CompilerParams(vmem_limit_bytes=50 * 2**20),
         cost_estimate=pl.CostEstimate(
-            flops=4 * loss * width * voc_rows,
-            bytes_accessed=2 * width * voc_rows,
+            flops=4 * max(loss, 256) * width * voc_rows,
+            bytes_accessed=4 * width * voc_rows,
             transcendentals=loss * voc_rows,
         ),
     )(place, by_plane, other, gain, targets.reshape(loss, 1), head_weight)
@@ -667,23 +685,26 @@
     )(place, key_pos, query_pos, packed_all)
 
     got = swapped(send)
-    stats, keep, *sends = call(
+    stats, keep, target_rows, *sends = call(
         functools.partial(core_body, nv - 1),
         (
             shape((per_vocab, LANES), f32),
             shape((nz, per_vocab, block_width), f32),
+            shape((per_vocab, block_width), bf16),
         )
         + (shape((per_vocab, (nz + 1) * block_width + LANES), bf16),) * (nv - 1),
-        [smem()] + [vmem()] * 4,
+        [smem()] + [vmem()] * 3 + [pl.BlockSpec(memory_space=pl.ANY)],
         [
             pltpu.VMEM((nz, loss, block_width), f32),
             pltpu.VMEM((loss, LANES), f32),
             pltpu.VMEM((loss, LANES), bf16),
+            pltpu.VMEM((loss, block_width), bf16),
+            pltpu.SemaphoreType.DMA,
         ],
     )(place, keep, got, stats, target_rows)
     got = [shifted(sends[s - 1], "vocab", s) for s in range(1, nv)]
 
-    stats, packed_all = lax.optimization_barrier((stats, packed_all))
+    stats, query_pos = lax.optimization_barrier((stats, query_pos))
     at_once = max(1, min(group, (4 * 2**20) // (loss * all_tokens * 4)))
     p_own, p_rows, out = call(
         functools.partial(forward_body, loss_per, heads, group, at_once),
@@ -718,24 +739,28 @@
         [smem()] + [vmem()] * (5 + nz - 1),
     )(place, keep, stats, target_rows, unit, gain, *got)
 
-    gathered = lax.all_gather(message, "vocab")
+    gathered = [message] + [shifted(message, "vocab", s) for s in range(1, nv)]
     cols = query_width // CORES
     rows = loss // nz
     resid_rows, mean_loss, keep, send = call(
-        project_body,
+        functools.partial(project_body, nv),
         (
             shape((loss, block_width), bf16),
             shape((8, LANES), f32),
             shape((loss, cols), f32),
             shape((loss, cols), bf16),
         ),
+        [smem()] + [vmem()] * (nv + 1),
+        [pltpu.VMEM((loss, block_width), bf16), pltpu.VMEM((loss, query_width), f32)],
+    )(place, *gathered, output_weight)
+    keep, *sends = call(
+        half_body,
+        (shape((rows, cols), f32),) + (shape((rows, cols), bf16),) * (nz - 1),
         [smem()] + [vmem()] * 2,
-        [pltpu.VMEM((loss, block_width), bf16), pltpu.VMEM((loss, query_width), f32)],
-    )(place, gathered, output_weight)
-    parts = call(half_body, shape((nz, rows, cols), bf16), [vmem()] * 2)(keep, swapped(send))
-    lines = [[CORES * z + c for z in range(nz)] for c in range(CORES)]
-    parts = lax.all_to_all(parts, "ctx", 0, 0, axis_index_groups=lines)
-    piece = call(sum_body, shape((rows, cols), bf16), [vmem()])(parts)
+        [pltpu.VMEM((loss, cols), f32)],
+    )(place, keep, swapped(send))
+    got = [shifted(sends[s - 1], "ctx", s, CORES) for s in range(1, nz)]
+    piece = call(sum_body, shape((rows, cols), bf16), [vmem()] * nz)(keep, *got)
     half = jnp.stack([piece] + [shifted(piece, "ctx", s, CORES) for s in range(1, nz)])
     other = swapped(half)
     query_grad, key_grad, value_grad = call(

time: 148 us -> 144 us (0.973)
  blocking collectives: 23.2 us -> 0 us
  starting transfers between devices: 25.6 us -> 35.2 us
  waiting for transfers between devices: 14.9 us -> 21.5 us
  local copies, waits for them, and re-layouts: 3.94 us -> 7.65 us
    all_gather x2 -> x0, blocking collectives: 14.7 us -> none  [the longest x1 8.27 us: per_device(): by_plane = lax.all_gather(by_z, 'vocab')]
    ppermute x12 -> x21, starting transfers between devices: 12.6 us -> 23.5 us  [shifted(): return lax.ppermute(value, axis, pairs)]
    all_to_all x1 -> x0, blocking collectives: 8.49 us -> none  [per_device(): parts = lax.all_to_all(parts, 'ctx', 0, 0, axis_index_groups=lines)]
    ppermute x12 -> x21, waiting for transfers between devices: 11.9 us -> 18.5 us  [shifted(): return lax.ppermute(value, axis, pairs)]
    unnamed x28, local copies, waits for them, and re-layouts: 3.07 us -> 6.79 us
  transfers between devices with their start and end apart: 18 -> 27, of which waited for: 13 -> 19; matrix products, arithmetic and copies ran while one was open for 1% -> 1% of each run, Pallas kernels for 37% -> 37%
where the time goes in v3:
time: 144 us
  Pallas kernels  64.6 us (45%)
  starting transfers between devices  35.2 us (24%)
  waiting for transfers between devices  21.5 us (15%)
  between operations  14.3 us (10%)
  local copies, waits for them, and re-layouts  7.65 us (5%)
    pallas_call x1, Pallas kernels, per_device(): pl.pallas_call(functools.partial(flash_body, first), out_shape=(shape((nz...  46.8 us
    ppermute x21, starting transfers between devices, shifted(): return lax.ppermute(value, axis, pairs)  23.5 us
    ppermute x21, waiting for transfers between devices, shifted(): return lax.ppermute(value, axis, pairs)  18.5 us
    ppermute x4, starting transfers between devices, swapped(): return lax.ppermute(value, 'ctx', [(i, i ^ 1) for i in range(size)])  11.6 us
    unnamed x28, local copies, waits for them, and re-layouts  6.79 us
    pallas_call x1, Pallas kernels, per_device(): call(functools.partial(forward_body, loss_per, heads, group, at_once), (s...  4.08 us
    pallas_call x1, Pallas kernels, per_device(): pl.pallas_call(target_body, out_shape=shape((nc, loss, block_width), bf16...  3.55 us
    ppermute x4, waiting for transfers between devices, swapped(): return lax.ppermute(value, 'ctx', [(i, i ^ 1) for i in range(size)])  2.89 us
  transfers between devices with their start and end apart: 27, of which 19 were waited for; matrix products, arithmetic and copies ran while one was open for 1% of the time, Pallas kernels for 37%

profile of v3, /device:TPU:3, one launch (start us, length us, event | category | flops | bytes accessed | tf_op | source)
XLA Modules:
  0.0 143.5 jit_solution(2255357178061455598)
XLA Ops:
  9.7 1.3 collective-permute-start
  11.1 2.3 %collective-permute-start.1 = (bf16[16,1024]{1,0:T(8,128)(2,1)S(1)}, bf16[16,1024]{1,0:T(8,128)(2,1)S(1)}, u32[]{:S(2)}, u32[]{:S(2)}) collective-permute-start(bf16[16,1024]{1,0:T(8,128)(2,1)S(1)} %shard_map.137), channel_id=1, source_target_pairs={{0,4},{1,5},{2,6},{3,7},{4,0},{5,1},{6,2},{7,3},{8,12},{9,13},{10,... | collective-permute-start | bytes 98312 | tf_op jit(solution)/shard_map/ppermute | solution.py:60
  14.7 2.0 %collective-permute-done.2 = bf16[16,1024]{1,0:T(8,128)(2,1)S(1)} collective-permute-done((bf16[16,1024]{1,0:T(8,128)(2,1)S(1)}, bf16[16,1024]{1,0:T(8,128)(2,1)S(1)}, u32[]{:S(2)}, u32[]{:S(2)}) %collective-permute-start.2) | collective-permute-done | bytes 32800 | tf_op jit(solution)/shard_map/ppermute | solution.py:60
  17.4 3.5 %shard_map.140 = bf16[8,64,1024]{2,1,0:T(8,128)(2,1)} custom-call(s32[5]{0:T(128)S(1)} %stack.68.place, s32[1,64]{1,0:T(1,128)S(1)} %bitcast.33, bf16[4752,8192]{1,0:T(8,128)(2,1)} %weight.3), custom_call_target="tpu_custom_call" | custom-call | bytes 16777216 | tf_op jit(solution)/shard_map/pallas_call | solution.py:615
  21.1 1.5 %collective-permute-start.3 = (bf16[4,16,1024]{2,1,0:T(8,128)(2,1)S(1)}, bf16[4,16,1024]{2,1,0:T(8,128)(2,1)S(1)}, u32[]{:S(2)}, u32[]{:S(2)}) collective-permute-start(bf16[4,16,1024]{2,1,0:T(8,128)(2,1)S(1)} %get-tuple-element.88), channel_id=1, source_target_pairs={{0,8},{8,16},{16,24},{24,0},{1,9},{9,17},{17,25},{25,1},{2,10},{10... | collective-permute-start | bytes 393224 | tf_op jit(solution)/shard_map/ppermute | solution.py:60
  22.7 1.4 collective-permute-start.5
  24.9 2.7 %collective-permute-done.4 = bf16[4,16,1024]{2,1,0:T(8,128)(2,1)S(1)} collective-permute-done((bf16[4,16,1024]{2,1,0:T(8,128)(2,1)S(1)}, bf16[4,16,1024]{2,1,0:T(8,128)(2,1)S(1)}, u32[]{:S(2)}, u32[]{:S(2)}) %collective-permute-start.4) | collective-permute-done | bytes 131104 | tf_op jit(solution)/shard_map/ppermute | solution.py:60
  28.4 3.4 %collective-permute-start.6 = (bf16[4,4,16,1024]{3,2,1,0:T(8,128)(2,1)S(1)}, bf16[4,4,16,1024]{3,2,1,0:T(8,128)(2,1)S(1)}, u32[]{:S(2)}, u32[]{:S(2)}) collective-permute-start(bf16[4,4,16,1024]{3,2,1,0:T(8,128)(2,1)S(1)} %pad_maximum_fusion.own), channel_id=1, source_target_pairs={{0,1},{1,0},{2,3},{3,2},{4,5},{5,4},{6,7},{7,6},{8,9},{9,8},{10,11... | collective-permute-start | bytes 1572872 | tf_op jit(solution)/shard_map/ppermute | solution.py:65
  32.0 1.4 shard_map.138
  33.4 46.8 %shard_map.139 = (f32[4,64,1024]{2,1,0:T(8,128)S(1)}, bf16[64,4224]{1,0:T(8,128)(2,1)S(1)}, f32[64,128]{1,0:T(8,128)S(1)}, f32[16,1024]{1,0:T(8,128)S(1)}) custom-call(s32[5]{0:T(128)S(1)} %stack.68.place, bf16[4,4,16,1024]{3,2,1,0:T(8,128)(2,1)S(1)} %pad_maximum_fusion.own, bf16[4,4,16,1024]{3,2,1,0:T(8,128)(2,1)S(1)} %collective-permute-done.6.other, ...), custom_call_target="tpu_custom_call" | custom-call | flops 39862665216 | bytes 155713536 | tf_op jit(solution)/shard_map/pallas_call | solution.py:643
  80.8 1.4 collective-permute-done.7.got
  83.1 1.3 shard_map.141
  84.4 2.4 %collective-permute-start.8 = (bf16[16,5248]{1,0:T(8,128)(2,1)S(1)}, bf16[16,5248]{1,0:T(8,128)(2,1)S(1)}, u32[]{:S(2)}, u32[]{:S(2)}) collective-permute-start(bf16[16,5248]{1,0:T(8,128)(2,1)S(1)} %get-tuple-element.63), channel_id=1, source_target_pairs={{0,8},{8,16},{16,24},{24,0},{1,9},{9,17},{17,25},{25,1},{2,10},{10... | collective-permute-start | bytes 503816 | tf_op jit(solution)/shard_map/ppermute | solution.py:60
  86.8 1.1 collective-permute-start.9
  88.1 1.3 copy-done.1
  89.4 4.1 %shard_map.142 = (f32[2,512,128]{2,1,0:T(8,128)S(1)}, f32[2,64,1024]{2,1,0:T(8,128)S(1)}, f32[2,512,128]{2,1,0:T(8,128)S(1)}) custom-call(s32[5]{0:T(128)S(1)} %stack.68.place, s32[1,1024]{1,0:T(1,128)S(1)} %add.63.key_pos, s32[64,1]{1,0:T(8,128)S(1)} %copy.18.query_pos, bf16[8,160,512]{2,1,0:T(8,128)(2,1)S(1)} %bitcast.27), custom_call_target="tpu_custom_call" | custom-call | flops 805306368 | bytes 1310720 | tf_op jit(solution)/shard_map/pallas_call | solution.py:709
  96.7 2.3 %collective-permute-start.12 = (bf16[16,1152]{1,0:T(8,128)(2,1)S(1)}, bf16[16,1152]{1,0:T(8,128)(2,1)S(1)}, u32[]{:S(2)}, u32[]{:S(2)}) collective-permute-start(bf16[16,1152]{1,0:T(8,128)(2,1)S(1)} %get-tuple-element.71), channel_id=1, source_target_pairs={{0,4},{1,5},{2,6},{3,7},{4,0},{5,1},{6,2},{7,3},{8,12},{9,13},{10,... | collective-permute-start | bytes 110600 | tf_op jit(solution)/shard_map/ppermute | solution.py:60
  99.5 1.3 collective-permute-done.11.rest_0_
  100.8 1.9 %collective-permute-done.13.rest_2_ = bf16[16,1152]{1,0:T(8,128)(2,1)S(1)} collective-permute-done((bf16[16,1152]{1,0:T(8,128)(2,1)S(1)}, bf16[16,1152]{1,0:T(8,128)(2,1)S(1)}, u32[]{:S(2)}, u32[]{:S(2)}) %collective-permute-start.13) | collective-permute-done | bytes 36896 | tf_op jit(solution)/shard_map/ppermute | solution.py:60
  104.6 1.4 collective-permute-start.16
  106.6 1.7 %collective-permute-done.16.refs_3_ = bf16[16,1152]{1,0:T(8,128)(2,1)S(1)} collective-permute-done((bf16[16,1152]{1,0:T(8,128)(2,1)S(1)}, bf16[16,1152]{1,0:T(8,128)(2,1)S(1)}, u32[]{:S(2)}, u32[]{:S(2)}) %collective-permute-start.16) | collective-permute-done | bytes 36896 | tf_op jit(solution)/shard_map/ppermute | solution.py:60
  108.3 2.2 %copy-done = bf16[2048,1024]{1,0:T(8,128)(2,1)S(1)} copy-done((bf16[2048,1024]{1,0:T(8,128)(2,1)S(1)}, bf16[2048,1024]{1,0:T(8,128)(2,1)}, u32[]{:S(2)}) %copy-start) | copy-done | bytes 4194328
  110.5 2.0 %shard_map.145 = (bf16[64,1024]{1,0:T(8,128)(2,1)}, f32[8,128]{1,0:T(8,128)S(1)}, f32[64,1024]{1,0:T(8,128)S(1)}, bf16[64,1024]{1,0:T(8,128)(2,1)S(1)}) custom-call(s32[5]{0:T(128)S(1)} %stack.68.place, bf16[16,1152]{1,0:T(8,128)(2,1)S(1)} %shard_map.144.refs_0_, bf16[16,1152]{1,0:T(8,128)(2,1)S(1)} %collective-permute-done.14.refs_1_, ...), custom_call_target="tpu_custom_call" | custom-call | tf_op jit(solution)/shard_map/pallas_call | solution.py:745
  112.4 4.6 %collective-permute-start.17 = (bf16[64,1024]{1,0:T(8,128)(2,1)S(1)}, bf16[64,1024]{1,0:T(8,128)(2,1)S(1)}, u32[]{:S(2)}, u32[]{:S(2)}) collective-permute-start(bf16[64,1024]{1,0:T(8,128)(2,1)S(1)} %get-tuple-element.75), channel_id=1, source_target_pairs={{0,1},{1,0},{2,3},{3,2},{4,5},{5,4},{6,7},{7,6},{8,9},{9,8},{10,11... | collective-permute-start | bytes 393224 | tf_op jit(solution)/shard_map/ppermute | solution.py:65
  119.6 1.5 %collective-permute-start.19 = (bf16[16,1024]{1,0:T(8,128)(2,1)S(1)}, bf16[16,1024]{1,0:T(8,128)(2,1)S(1)}, u32[]{:S(2)}, u32[]{:S(2)}) collective-permute-start(bf16[16,1024]{1,0:T(8,128)(2,1)S(1)} %get-tuple-element.78), channel_id=1, source_target_pairs={{0,4},{1,5},{2,6},{3,7},{4,0},{5,1},{6,2},{7,3},{8,12},{9,13},{10,... | collective-permute-start | bytes 98312 | tf_op jit(solution)/shard_map/ppermute | solution.py:60
  121.9 1.3 collective-permute-done.18.refs_0_
  123.3 1.9 %collective-permute-done.19.refs_1_ = bf16[16,1024]{1,0:T(8,128)(2,1)S(1)} collective-permute-done((bf16[16,1024]{1,0:T(8,128)(2,1)S(1)}, bf16[16,1024]{1,0:T(8,128)(2,1)S(1)}, u32[]{:S(2)}, u32[]{:S(2)}) %collective-permute-start.19) | collective-permute-done | bytes 32800 | tf_op jit(solution)/shard_map/ppermute | solution.py:60
  125.7 1.2 collective-permute-start.22
  126.9 1.6 %collective-permute-start.23 = (bf16[16,1024]{1,0:T(8,128)(2,1)S(1)}, bf16[16,1024]{1,0:T(8,128)(2,1)S(1)}, u32[]{:S(2)}, u32[]{:S(2)}) collective-permute-start(bf16[16,1024]{1,0:T(8,128)(2,1)S(1)} %shard_map.147), channel_id=1, source_target_pairs={{0,6},{1,7},{2,0},{3,1},{4,2},{5,3},{6,4},{7,5},{8,14},{9,15},{10,... | collective-permute-start | bytes 98312 | tf_op jit(solution)/shard_map/ppermute | solution.py:60
  128.5 1.3 collective-permute-done.21
  130.2 3.2 %collective-permute-start.24 = (bf16[4,16,1024]{2,1,0:T(8,128)(2,1)S(1)}, bf16[4,16,1024]{2,1,0:T(8,128)(2,1)S(1)}, u32[]{:S(2)}, u32[]{:S(2)}) collective-permute-start(bf16[4,16,1024]{2,1,0:T(8,128)(2,1)S(1)} %pad_maximum_fusion.2.half), channel_id=1, source_target_pairs={{0,1},{1,0},{2,3},{3,2},{4,5},{5,4},{6,7},{7,6},{8,9},{9,8},{10,11... | collective-permute-start | bytes 393224 | tf_op jit(solution)/shard_map/ppermute | solution.py:65
  134.3 2.3 %shard_map.148 = (bf16[8,2048]{1,0:T(8,128)(2,1)}, bf16[128,256]{1,0:T(8,128)(2,1)}, bf16[128,256]{1,0:T(8,128)(2,1)}) custom-call(s32[5]{0:T(128)S(1)} %stack.68.place, bf16[4,16,1024]{2,1,0:T(8,128)(2,1)S(1)} %pad_maximum_fusion.2.half, bf16[4,16,1024]{2,1,0:T(8,128)(2,1)S(1)} %collective-permute-done.24.other, bf16[8,160,512]{2,1,0:T(8,128)(2,1)S(1)} %bitcast.28, ...), custom_call_target="tpu_custom_call" | custom-call | tf_op jit(solution)/shard_map/pallas_call | solution.py:766
  (77 shorter events, 19.6 us)
Async XLA Ops:
  7.2 75.0 %reduce-scatter.2.cloned.1.call-start = ((), (), s32[]{:S(2)}) async-start(), calls=%async_computation.1 | async-start | bytes 1179648 | tf_op jit(solution)/shard_map/reduce_scatter | solution.py:630
  9.7 4.7 %collective-permute-start = (bf16[16,1024]{1,0:T(8,128)(2,1)S(1)}, bf16[16,1024]{1,0:T(8,128)(2,1)S(1)}, u32[]{:S(2)}, u32[]{:S(2)}) collective-permute-start(bf16[16,1024]{1,0:T(8,128)(2,1)S(1)} %shard_map.137), channel_id=1, source_target_pairs={{0,2},{1,3},{2,4},{3,5},{4,6},{5,7},{6,0},{7,1},{8,10},{9,11},{10,... | collective-permute-start | bytes 98312 | tf_op jit(solution)/shard_map/ppermute | solution.py:60
  11.1 3.7 %collective-permute-start.1 = (bf16[16,1024]{1,0:T(8,128)(2,1)S(1)}, bf16[16,1024]{1,0:T(8,128)(2,1)S(1)}, u32[]{:S(2)}, u32[]{:S(2)}) collective-permute-start(bf16[16,1024]{1,0:T(8,128)(2,1)S(1)} %shard_map.137), channel_id=1, source_target_pairs={{0,4},{1,5},{2,6},{3,7},{4,0},{5,1},{6,2},{7,3},{8,12},{9,13},{10,... | collective-permute-start | bytes 98312 | tf_op jit(solution)/shard_map/ppermute | solution.py:60
  13.4 3.4 %collective-permute-start.2 = (bf16[16,1024]{1,0:T(8,128)(2,1)S(1)}, bf16[16,1024]{1,0:T(8,128)(2,1)S(1)}, u32[]{:S(2)}, u32[]{:S(2)}) collective-permute-start(bf16[16,1024]{1,0:T(8,128)(2,1)S(1)} %shard_map.137), channel_id=1, source_target_pairs={{0,6},{1,7},{2,0},{3,1},{4,2},{5,3},{6,4},{7,5},{8,14},{9,15},{10,... | collective-permute-start | bytes 98312 | tf_op jit(solution)/shard_map/ppermute | solution.py:60
  17.4 14.5 %copy-start.7 = (bf16[128,256]{1,0:T(8,128)(2,1)S(1)}, bf16[128,256]{1,0:T(8,128)(2,1)}, u32[]{:S(2)}) copy-start(bf16[128,256]{1,0:T(8,128)(2,1)} %values.1) | copy-start | bytes 196612
  17.4 14.5 %copy-start.10 = (s32[64]{0:T(128)S(1)}, s32[64]{0:T(128)}, u32[]{:S(2)}) copy-start(s32[64]{0:T(128)} %rows.3) | copy-start | bytes 772
  17.4 16.0 %copy-start.8 = (f32[8192]{0:T(1024)S(1)}, f32[8192]{0:T(1024)}, u32[]{:S(2)}) copy-start(f32[8192]{0:T(1024)} %param.11) | copy-start | bytes 98308
  21.0 67.1 %all-gather.3.cloned.1.call-start = ((), (), s32[]{:S(2)}) async-start(), calls=%async_computation.2 | async-start | bytes 1474560 | tf_op jit(solution)/shard_map/all_gather | solution.py:636
  21.1 3.9 %collective-permute-start.3 = (bf16[4,16,1024]{2,1,0:T(8,128)(2,1)S(1)}, bf16[4,16,1024]{2,1,0:T(8,128)(2,1)S(1)}, u32[]{:S(2)}, u32[]{:S(2)}) collective-permute-start(bf16[4,16,1024]{2,1,0:T(8,128)(2,1)S(1)} %get-tuple-element.88), channel_id=1, source_target_pairs={{0,8},{8,16},{16,24},{24,0},{1,9},{9,17},{17,25},{25,1},{2,10},{10... | collective-permute-start | bytes 393224 | tf_op jit(solution)/shard_map/ppermute | solution.py:60
  22.6 5.0 %collective-permute-start.4 = (bf16[4,16,1024]{2,1,0:T(8,128)(2,1)S(1)}, bf16[4,16,1024]{2,1,0:T(8,128)(2,1)S(1)}, u32[]{:S(2)}, u32[]{:S(2)}) collective-permute-start(bf16[4,16,1024]{2,1,0:T(8,128)(2,1)S(1)} %get-tuple-element.88), channel_id=1, source_target_pairs={{0,16},{8,24},{16,0},{24,8},{1,17},{9,25},{17,1},{25,9},{2,18},{10... | collective-permute-start | bytes 393224 | tf_op jit(solution)/shard_map/ppermute | solution.py:60
  22.7 5.6 %collective-permute-start.5 = (bf16[4,16,1024]{2,1,0:T(8,128)(2,1)S(1)}, bf16[4,16,1024]{2,1,0:T(8,128)(2,1)S(1)}, u32[]{:S(2)}, u32[]{:S(2)}) collective-permute-start(bf16[4,16,1024]{2,1,0:T(8,128)(2,1)S(1)} %get-tuple-element.88), channel_id=1, source_target_pairs={{0,24},{8,0},{16,8},{24,16},{1,25},{9,1},{17,9},{25,17},{2,26},{10... | collective-permute-start | bytes 393224 | tf_op jit(solution)/shard_map/ppermute | solution.py:60
  28.4 5.0 %collective-permute-start.6 = (bf16[4,4,16,1024]{3,2,1,0:T(8,128)(2,1)S(1)}, bf16[4,4,16,1024]{3,2,1,0:T(8,128)(2,1)S(1)}, u32[]{:S(2)}, u32[]{:S(2)}) collective-permute-start(bf16[4,4,16,1024]{3,2,1,0:T(8,128)(2,1)S(1)} %pad_maximum_fusion.own), channel_id=1, source_target_pairs={{0,1},{1,0},{2,3},{3,2},{4,5},{5,4},{6,7},{7,6},{8,9},{9,8},{10,11... | collective-permute-start | bytes 1572872 | tf_op jit(solution)/shard_map/ppermute | solution.py:65
  33.4 47.2 %copy-start.13 = (s32[16]{0:T(128)S(1)}, s32[16]{0:T(128)}, u32[]{:S(2)}) copy-start(s32[16]{0:T(128)} %param.15) | copy-start | bytes 196
  80.2 2.0 %collective-permute-start.7 = (bf16[64,4224]{1,0:T(8,128)(2,1)S(1)}, bf16[64,4224]{1,0:T(8,128)(2,1)S(1)}, u32[]{:S(2)}, u32[]{:S(2)}) collective-permute-start(bf16[64,4224]{1,0:T(8,128)(2,1)S(1)} %get-tuple-element.50), channel_id=1, source_target_pairs={{0,1},{1,0},{2,3},{3,2},{4,5},{5,4},{6,7},{7,6},{8,9},{9,8},{10,11... | collective-permute-start | bytes 1622024 | tf_op jit(solution)/shard_map/ppermute | solution.py:65
  84.4 9.2 %collective-permute-start.10 = (bf16[16,5248]{1,0:T(8,128)(2,1)S(1)}, bf16[16,5248]{1,0:T(8,128)(2,1)S(1)}, u32[]{:S(2)}, u32[]{:S(2)}) collective-permute-start(bf16[16,5248]{1,0:T(8,128)(2,1)S(1)} %get-tuple-element.65), channel_id=1, source_target_pairs={{0,24},{8,0},{16,8},{24,16},{1,25},{9,1},{17,9},{25,17},{2,26},{10... | collective-permute-start | bytes 503816 | tf_op jit(solution)/shard_map/ppermute | solution.py:60
  84.4 10.0 %collective-permute-start.8 = (bf16[16,5248]{1,0:T(8,128)(2,1)S(1)}, bf16[16,5248]{1,0:T(8,128)(2,1)S(1)}, u32[]{:S(2)}, u32[]{:S(2)}) collective-permute-start(bf16[16,5248]{1,0:T(8,128)(2,1)S(1)} %get-tuple-element.63), channel_id=1, source_target_pairs={{0,8},{8,16},{16,24},{24,0},{1,9},{9,17},{17,25},{25,1},{2,10},{10... | collective-permute-start | bytes 503816 | tf_op jit(solution)/shard_map/ppermute | solution.py:60
  86.8 8.3 %collective-permute-start.9 = (bf16[16,5248]{1,0:T(8,128)(2,1)S(1)}, bf16[16,5248]{1,0:T(8,128)(2,1)S(1)}, u32[]{:S(2)}, u32[]{:S(2)}) collective-permute-start(bf16[16,5248]{1,0:T(8,128)(2,1)S(1)} %get-tuple-element.64), channel_id=1, source_target_pairs={{0,16},{8,24},{16,0},{24,8},{1,17},{9,25},{17,1},{25,9},{2,18},{10... | collective-permute-start | bytes 503816 | tf_op jit(solution)/shard_map/ppermute | solution.py:60
  89.4 44.9 %copy-start.2 = (bf16[1280,512]{1,0:T(8,128)(2,1)S(1)}, bf16[1280,512]{1,0:T(8,128)(2,1)}, u32[]{:S(2)}) copy-start(bf16[1280,512]{1,0:T(8,128)(2,1)} %all-gather.3.cloned.1.call-done) | copy-start | bytes 3932164
  96.2 4.7 %collective-permute-start.11 = (bf16[16,1152]{1,0:T(8,128)(2,1)S(1)}, bf16[16,1152]{1,0:T(8,128)(2,1)S(1)}, u32[]{:S(2)}, u32[]{:S(2)}) collective-permute-start(bf16[16,1152]{1,0:T(8,128)(2,1)S(1)} %get-tuple-element.70), channel_id=1, source_target_pairs={{0,2},{1,3},{2,4},{3,5},{4,6},{5,7},{6,0},{7,1},{8,10},{9,11},{10,... | collective-permute-start | bytes 110600 | tf_op jit(solution)/shard_map/ppermute | solution.py:60
  96.7 4.1 %collective-permute-start.12 = (bf16[16,1152]{1,0:T(8,128)(2,1)S(1)}, bf16[16,1152]{1,0:T(8,128)(2,1)S(1)}, u32[]{:S(2)}, u32[]{:S(2)}) collective-permute-start(bf16[16,1152]{1,0:T(8,128)(2,1)S(1)} %get-tuple-element.71), channel_id=1, source_target_pairs={{0,4},{1,5},{2,6},{3,7},{4,0},{5,1},{6,2},{7,3},{8,12},{9,13},{10,... | collective-permute-start | bytes 110600 | tf_op jit(solution)/shard_map/ppermute | solution.py:60
  99.0 3.7 %collective-permute-start.13 = (bf16[16,1152]{1,0:T(8,128)(2,1)S(1)}, bf16[16,1152]{1,0:T(8,128)(2,1)S(1)}, u32[]{:S(2)}, u32[]{:S(2)}) collective-permute-start(bf16[16,1152]{1,0:T(8,128)(2,1)S(1)} %get-tuple-element.72), channel_id=1, source_target_pairs={{0,6},{1,7},{2,0},{3,1},{4,2},{5,3},{6,4},{7,5},{8,14},{9,15},{10,... | collective-permute-start | bytes 110600 | tf_op jit(solution)/shard_map/ppermute | solution.py:60
  103.6 2.9 %collective-permute-start.14 = (bf16[16,1152]{1,0:T(8,128)(2,1)S(1)}, bf16[16,1152]{1,0:T(8,128)(2,1)S(1)}, u32[]{:S(2)}, u32[]{:S(2)}) collective-permute-start(bf16[16,1152]{1,0:T(8,128)(2,1)S(1)} %shard_map.144.refs_0_), channel_id=1, source_target_pairs={{0,8},{8,16},{16,24},{24,0},{1,9},{9,17},{17,25},{25,1},{2,10},{10... | collective-permute-start | bytes 110600 | tf_op jit(solution)/shard_map/ppermute | solution.py:60
  103.7 2.9 %collective-permute-start.15 = (bf16[16,1152]{1,0:T(8,128)(2,1)S(1)}, bf16[16,1152]{1,0:T(8,128)(2,1)S(1)}, u32[]{:S(2)}, u32[]{:S(2)}) collective-permute-start(bf16[16,1152]{1,0:T(8,128)(2,1)S(1)} %shard_map.144.refs_0_), channel_id=1, source_target_pairs={{0,16},{8,24},{16,0},{24,8},{1,17},{9,25},{17,1},{25,9},{2,18},{10... | collective-permute-start | bytes 110600 | tf_op jit(solution)/shard_map/ppermute | solution.py:60
  104.6 3.7 %collective-permute-start.16 = (bf16[16,1152]{1,0:T(8,128)(2,1)S(1)}, bf16[16,1152]{1,0:T(8,128)(2,1)S(1)}, u32[]{:S(2)}, u32[]{:S(2)}) collective-permute-start(bf16[16,1152]{1,0:T(8,128)(2,1)S(1)} %shard_map.144.refs_0_), channel_id=1, source_target_pairs={{0,24},{8,0},{16,8},{24,16},{1,25},{9,1},{17,9},{25,17},{2,26},{10... | collective-permute-start | bytes 110600 | tf_op jit(solution)/shard_map/ppermute | solution.py:60
  112.4 5.6 %collective-permute-start.17 = (bf16[64,1024]{1,0:T(8,128)(2,1)S(1)}, bf16[64,1024]{1,0:T(8,128)(2,1)S(1)}, u32[]{:S(2)}, u32[]{:S(2)}) collective-permute-start(bf16[64,1024]{1,0:T(8,128)(2,1)S(1)} %get-tuple-element.75), channel_id=1, source_target_pairs={{0,1},{1,0},{2,3},{3,2},{4,5},{5,4},{6,7},{7,6},{8,9},{9,8},{10,11... | collective-permute-start | bytes 393224 | tf_op jit(solution)/shard_map/ppermute | solution.py:65
  118.6 4.6 %collective-permute-start.18 = (bf16[16,1024]{1,0:T(8,128)(2,1)S(1)}, bf16[16,1024]{1,0:T(8,128)(2,1)S(1)}, u32[]{:S(2)}, u32[]{:S(2)}) collective-permute-start(bf16[16,1024]{1,0:T(8,128)(2,1)S(1)} %get-tuple-element.77), channel_id=1, source_target_pairs={{0,2},{1,3},{2,4},{3,5},{4,6},{5,7},{6,0},{7,1},{8,10},{9,11},{10,... | collective-permute-start | bytes 98312 | tf_op jit(solution)/shard_map/ppermute | solution.py:60
  119.6 5.5 %collective-permute-start.19 = (bf16[16,1024]{1,0:T(8,128)(2,1)S(1)}, bf16[16,1024]{1,0:T(8,128)(2,1)S(1)}, u32[]{:S(2)}, u32[]{:S(2)}) collective-permute-start(bf16[16,1024]{1,0:T(8,128)(2,1)S(1)} %get-tuple-element.78), channel_id=1, source_target_pairs={{0,4},{1,5},{2,6},{3,7},{4,0},{5,1},{6,2},{7,3},{8,12},{9,13},{10,... | collective-permute-start | bytes 98312 | tf_op jit(solution)/shard_map/ppermute | solution.py:60
  121.1 4.0 %collective-permute-start.20 = (bf16[16,1024]{1,0:T(8,128)(2,1)S(1)}, bf16[16,1024]{1,0:T(8,128)(2,1)S(1)}, u32[]{:S(2)}, u32[]{:S(2)}) collective-permute-start(bf16[16,1024]{1,0:T(8,128)(2,1)S(1)} %get-tuple-element.79), channel_id=1, source_target_pairs={{0,6},{1,7},{2,0},{3,1},{4,2},{5,3},{6,4},{7,5},{8,14},{9,15},{10,... | collective-permute-start | bytes 98312 | tf_op jit(solution)/shard_map/ppermute | solution.py:60
  125.2 4.6 %collective-permute-start.21 = (bf16[16,1024]{1,0:T(8,128)(2,1)S(1)}, bf16[16,1024]{1,0:T(8,128)(2,1)S(1)}, u32[]{:S(2)}, u32[]{:S(2)}) collective-permute-start(bf16[16,1024]{1,0:T(8,128)(2,1)S(1)} %shard_map.147), channel_id=1, source_target_pairs={{0,2},{1,3},{2,4},{3,5},{4,6},{5,7},{6,0},{7,1},{8,10},{9,11},{10,... | collective-permute-start | bytes 98312 | tf_op jit(solution)/shard_map/ppermute | solution.py:60
  125.7 4.1 %collective-permute-start.22 = (bf16[16,1024]{1,0:T(8,128)(2,1)S(1)}, bf16[16,1024]{1,0:T(8,128)(2,1)S(1)}, u32[]{:S(2)}, u32[]{:S(2)}) collective-permute-start(bf16[16,1024]{1,0:T(8,128)(2,1)S(1)} %shard_map.147), channel_id=1, source_target_pairs={{0,4},{1,5},{2,6},{3,7},{4,0},{5,1},{6,2},{7,3},{8,12},{9,13},{10,... | collective-permute-start | bytes 98312 | tf_op jit(solution)/shard_map/ppermute | solution.py:60
  126.9 3.2 %collective-permute-start.23 = (bf16[16,1024]{1,0:T(8,128)(2,1)S(1)}, bf16[16,1024]{1,0:T(8,128)(2,1)S(1)}, u32[]{:S(2)}, u32[]{:S(2)}) collective-permute-start(bf16[16,1024]{1,0:T(8,128)(2,1)S(1)} %shard_map.147), channel_id=1, source_target_pairs={{0,6},{1,7},{2,0},{3,1},{4,2},{5,3},{6,4},{7,5},{8,14},{9,15},{10,... | collective-permute-start | bytes 98312 | tf_op jit(solution)/shard_map/ppermute | solution.py:60
  130.2 4.1 %collective-permute-start.24 = (bf16[4,16,1024]{2,1,0:T(8,128)(2,1)S(1)}, bf16[4,16,1024]{2,1,0:T(8,128)(2,1)S(1)}, u32[]{:S(2)}, u32[]{:S(2)}) collective-permute-start(bf16[4,16,1024]{2,1,0:T(8,128)(2,1)S(1)} %pad_maximum_fusion.2.half), channel_id=1, source_target_pairs={{0,1},{1,0},{2,3},{3,2},{4,5},{5,4},{6,7},{7,6},{8,9},{9,8},{10,11... | collective-permute-start | bytes 393224 | tf_op jit(solution)/shard_map/ppermute | solution.py:65
  (9 other events, 50.2 us)
Sparse Core Ops, SparseCore 0:
  21.2 31.1 reduce-scatter.1
  54.0 25.1 all-gather.2

commit v4 on v3

--- a/solution.py
+++ b/solution.py
@@ -33,6 +33,10 @@
     return pl.BlockSpec(memory_space=pltpu.SMEM)
 
 
+def hbm():
+    return pl.BlockSpec(memory_space=pltpu.HBM)
+
+
 def vmem():
     return pl.BlockSpec(memory_space=pltpu.VMEM)
 
@@ -41,7 +45,7 @@
     return jax.ShapeDtypeStruct(dims, dtype)
 
 
-def call(body, outs, ins, scratch=(), limit=48, flops=0, moved=0, exps=0):
+def call(body, outs, ins, scratch=(), limit=16, flops=0, moved=0, exps=0):
     return pl.pallas_call(
         body,
         out_shape=outs,
@@ -60,6 +64,11 @@
     return lax.ppermute(value, axis, pairs)
 
 
+def crossed(value, bit):
+    size = lax.axis_size("ctx")
+    return lax.ppermute(value, "ctx", [(i, i ^ (bit * CORES)) for i in range(size)])
+
+
 def swapped(value):
     size = lax.axis_size("ctx")
     return lax.ppermute(value, "ctx", [(i, i ^ 1) for i in range(size)])
@@ -75,9 +84,13 @@
     return sel.astype(bf16)
 
 
-def pick_body(loss_per, place, rows, hidden, picked):
+def pick_body(loss_per, place, rows, hidden, picked, here, sem):
     tokens, width = hidden.shape
-    mine = dot(row_choice(loss_per, tokens, place, rows), hidden[...], NN)
+    copy = pltpu.make_async_copy(hidden, here, sem)
+    copy.start()
+    choice = row_choice(loss_per, tokens, place, rows)
+    copy.wait()
+    mine = dot(choice, here[...], NN)
     half = width // 2
     picked[...] = jnp.concatenate([mine[:, :half], mine[:, half:]], axis=0).astype(bf16)
 
@@ -178,7 +191,7 @@
 
     is_even = core_at == 0
     for zr in range(nz):
-        z_src = lax.rem(z_at - zr + nz, nz)
+        z_src = lax.bitwise_xor(z_at, zr)
         square_own = jnp.zeros((8, 1), f32)
         square_other = jnp.zeros((8, 1), f32)
         for vr in range(nv):
@@ -407,7 +420,15 @@
 
 
 def project_body(nv, place, *refs):
-    gathered, (weight, resid, loss_out, keep, send, whole, partial) = refs[:nv], refs[nv:]
+    gathered, refs = refs[:nv], refs[nv:]
+    weight, resid, loss_out, keep, send, whole, partial, here, sems = refs
+    parts, part, _ = here.shape
+    copies = [
+        pltpu.make_async_copy(weight.at[pl.ds(k * part, part), :], here.at[k], sems.at[k])
+        for k in range(parts)
+    ]
+    for copy in copies:
+        copy.start()
     per = gathered[0].shape[0]
     block = whole.shape[1]
     loss_sum = jnp.zeros((1, 1), f32)
@@ -416,73 +437,63 @@
         whole[pl.ds(pl.multiple_of(src * per, per), per), :] = gathered[v][:, :block]
         (column,) = joined_columns(gathered[v][:, block:], 1)
         loss_sum = loss_sum + jnp.sum(column, axis=0, keepdims=True)
-    loss_out[...] = jnp.broadcast_to(loss_sum / (nv * per), loss_out.shape)
+    loss_out[...] = loss_sum / (nv * per)
     resid[...] = whole[...]
-    partial[...] = dot(whole[...], weight[...], NT)
+    for k in range(parts):
+        copies[k].wait()
+        partial[:, k * part : (k + 1) * part] = dot(whole[...], here[k], NT)
     cols = keep.shape[1]
     keep[...] = partial[:, pl.ds(pl.multiple_of(place[2] * cols, cols), cols)]
     send[...] = partial[:, pl.ds(pl.multiple_of((1 - place[2]) * cols, cols), cols)].astype(bf16)
 
 
-def half_body(place, keep, got, new_keep, *rest):
-    sends, (total,) = rest[:-1], rest[-1:]
-    per = new_keep.shape[0]
-    nz = len(sends) + 1
-    total[...] = keep[...] + got[...].astype(f32)
-    new_keep[...] = total[pl.ds(pl.multiple_of(place[1] * per, per), per), :]
-    for s in range(nz - 1):
-        to = lax.rem(place[1] + s + 1, nz)
-        sends[s][...] = total[pl.ds(pl.multiple_of(to * per, per), per), :].astype(bf16)
-
-
 def sum_body(keep, *refs):
-    value = keep[...]
+    value = keep[...].astype(f32)
     for ref in refs[:-1]:
         value = value + ref[...].astype(f32)
     refs[-1][...] = value.astype(bf16)
 
 
 def forward_body(
-    loss_per, heads, group, heads_at_once, place, key_pos, query_pos, packed, p_own, p_rows, out, scratch
+    loss_per, heads, group, heads_at_once, j, place, key_pos, query_pos, packed, p_own, p_rows, out, scratch
 ):
     nc = packed.shape[0]
-    tokens = p_own.shape[2]
+    tokens = p_own.shape[1]
     loss = loss_per * nc
     key_width = heads * HEAD_SIZE
     score_scale = HEAD_SIZE ** (-0.5)
     ctx_at = place[3]
     own_at = pl.multiple_of(ctx_at * tokens, tokens)
     row_at = pl.multiple_of(ctx_at * loss_per, loss_per)
-    for j in range(heads):
-        key = jnp.concatenate(
-            [packed[c, 0:tokens, j * HEAD_SIZE : (j + 1) * HEAD_SIZE] for c in range(nc)], axis=0
-        )
-        at = key_width + j * HEAD_SIZE
-        value = jnp.concatenate(
-            [packed[c, 0:tokens, at : at + HEAD_SIZE] for c in range(nc)], axis=0
-        )
-        for g0 in range(0, group, heads_at_once):
-            stacked = []
-            for g in range(g0, g0 + heads_at_once):
-                stacked.append(query_of(packed, j * group + g, tokens, loss_per, key_width))
-            query = jnp.concatenate(stacked, axis=0).astype(bf16)
-            where_at = jnp.concatenate([query_pos[...]] * heads_at_once, axis=0)
-            visible = key_pos[...] <= where_at
-            scores = jnp.where(visible, dot(query, key, NT) * score_scale, masked_fill)
-            top = jnp.max(scores, axis=1, keepdims=True)
-            raw = jnp.where(visible, jnp.exp(scores - top), 0.0)
-            prob = raw / jnp.sum(raw, axis=1, keepdims=True)
-            scratch[...] = prob
-            coarse = prob.astype(bf16)
-            fine = (prob - coarse.astype(f32)).astype(bf16)
-            first = g0 * loss
-            n = heads_at_once * loss
-            out[j, first : first + n, :] = dot(coarse, value, NN) + dot(fine, value, NN)
-            p_own[j, first : first + n, :] = scratch[:, pl.ds(own_at, tokens)]
-            for k in range(heads_at_once):
-                p_rows[j, (g0 + k) * loss_per : (g0 + k + 1) * loss_per, :] = scratch[
-                    pl.ds(pl.multiple_of(k * loss + row_at, loss_per), loss_per), :
-                ]
+    key = jnp.concatenate(
+        [packed[c, 0:tokens, j * HEAD_SIZE : (j + 1) * HEAD_SIZE] for c in range(nc)], axis=0
+    )
+    at = key_width + j * HEAD_SIZE
+    value = jnp.concatenate(
+        [packed[c, 0:tokens, at : at + HEAD_SIZE] for c in range(nc)], axis=0
+    )
+    for g0 in range(0, group, heads_at_once):
+        stacked = []
+        for g in range(g0, g0 + heads_at_once):
+            stacked.append(query_of(packed, j * group + g, tokens, loss_per, key_width))
+        query = jnp.concatenate(stacked, axis=0).astype(bf16)
+        where_at = jnp.concatenate([query_pos[...]] * heads_at_once, axis=0)
+        visible = key_pos[...] <= where_at
+        scores = jnp.where(visible, dot(query, key, NT) * score_scale, masked_fill)
+        top = jnp.max(scores, axis=1, keepdims=True)
+        raw = jnp.where(visible, jnp.exp(scores - top), 0.0)
+        prob = raw / jnp.sum(raw, axis=1, keepdims=True)
+        scratch[...] = prob
+        coarse = prob.astype(bf16)
+        fine = (prob - coarse.astype(f32)).astype(bf16)
+        first = g0 * loss
+        n = heads_at_once * loss
+        out[first : first + n, :] = dot(coarse, value, NN) + dot(fine, value, NN)
+        p_own[first : first + n, :] = scratch[:, pl.ds(own_at, tokens)]
+        for k in range(heads_at_once):
+            p_rows[(g0 + k) * loss_per : (g0 + k + 1) * loss_per, :] = scratch[
+                pl.ds(pl.multiple_of(k * loss + row_at, loss_per), loss_per), :
+            ]
 
 
 def query_of(packed, head, tokens, loss_per, key_width):
@@ -495,34 +506,31 @@
     return jnp.concatenate(parts, axis=0)
 
 
-def backward_body(
-    loss_per, heads, group, place, half, other, packed, p_own, p_rows, out, query_grad, key_grad, value_grad, grad
-):
+def backward_body(loss_per, heads, group, place, half, other, packed, *refs):
+    attention = [refs[3 * j : 3 * j + 3] for j in range(heads)]
+    query_grad, key_grad, value_grad, grad = refs[3 * heads :]
     nc = packed.shape[0]
-    tokens = p_own.shape[2]
+    tokens = key_grad.shape[0]
     loss = loss_per * nc
     key_width = heads * HEAD_SIZE
     score_scale = HEAD_SIZE ** (-0.5)
     ctx_at = place[3]
-    nz, rows, cols = half.shape
-    col_at = pl.multiple_of(place[2] * cols, cols)
-    other_at = pl.multiple_of((1 - place[2]) * cols, cols)
-    for s in range(nz):
-        row_at = pl.multiple_of(lax.rem(place[1] - s + nz, nz) * rows, rows)
-        grad[pl.ds(row_at, rows), pl.ds(col_at, cols)] = half[s].astype(f32)
-        grad[pl.ds(row_at, rows), pl.ds(other_at, cols)] = other[s].astype(f32)
+    cols = half.shape[1]
+    grad[:, pl.ds(pl.multiple_of(place[2] * cols, cols), cols)] = half[...].astype(f32)
+    grad[:, pl.ds(pl.multiple_of((1 - place[2]) * cols, cols), cols)] = other[...].astype(f32)
     mine_at = pl.multiple_of(ctx_at * loss_per, loss_per)
     for j in range(heads):
+        p_own, p_rows, out = attention[j]
         lanes = [slice((j * group + g) * HEAD_SIZE, (j * group + g + 1) * HEAD_SIZE) for g in range(group)]
         d_out = jnp.concatenate([grad[:, s] for s in lanes], axis=0)
         d_half = d_out.astype(bf16)
-        delta = jnp.sum(d_out * out[j], axis=1, keepdims=True)
+        delta = jnp.sum(d_out * out[...], axis=1, keepdims=True)
         query = jnp.concatenate(
             [query_of(packed, j * group + g, tokens, loss_per, key_width) for g in range(group)], axis=0
         ).astype(bf16)
         at = key_width + j * HEAD_SIZE
         own_value = packed[ctx_at, 0:tokens, at : at + HEAD_SIZE]
-        prob = p_own[j]
+        prob = p_own[...]
         score_grad = (prob * (dot(d_half, own_value, NT) - delta)).astype(bf16)
         k_lanes = slice(j * HEAD_SIZE, (j + 1) * HEAD_SIZE)
         key_grad[:, k_lanes] = (dot(score_grad, query, TN) * score_scale).astype(bf16)
@@ -532,14 +540,14 @@
         d_mine = jnp.concatenate([grad[pl.ds(mine_at, loss_per), s] for s in lanes], axis=0)
         out_mine = jnp.concatenate(
             [
-                out[j, pl.ds(pl.multiple_of(g * loss + mine_at, loss_per), loss_per), :]
+                out[pl.ds(pl.multiple_of(g * loss + mine_at, loss_per), loss_per), :]
                 for g in range(group)
             ],
             axis=0,
         )
         delta = jnp.sum(d_mine * out_mine, axis=1, keepdims=True)
         d_prob = dot(d_mine.astype(bf16), value, NT)
-        score_grad = (p_rows[j] * (d_prob - delta)).astype(bf16)
+        score_grad = (p_rows[...] * (d_prob - delta)).astype(bf16)
         result = dot(score_grad, key, NN) * score_scale
         for g in range(group):
             query_grad[:, lanes[g]] = result[g * loss_per : (g + 1) * loss_per].astype(bf16)
@@ -593,18 +601,23 @@
     picked = call(
         functools.partial(pick_body, loss_per),
         shape((2 * loss_per, part_width // 2), bf16),
-        [smem(), smem(), vmem()],
+        [smem(), smem(), hbm()],
+        [pltpu.VMEM((tokens, part_width), bf16), pltpu.SemaphoreType.DMA],
     )(place, loss_rows, hidden)
-    picked, queries = lax.optimization_barrier((picked, queries))
+    picked, queries, targets_late = lax.optimization_barrier((picked, queries, targets))
     extra = (query_width // (2 * key_width)) * loss_per
     packed = call(
         functools.partial(pack_body, loss_per),
         shape((tokens + extra, 2 * key_width), bf16),
         [smem(), smem()] + [vmem()] * 3,
+        moved=2 * queries.size,
     )(place, loss_rows, queries, key_states, attention_values)
-    by_z = jnp.stack([picked] + [shifted(picked, "ctx", s, CORES) for s in range(1, nz)])
+    by_z = picked[None]
+    bit = 1
+    while bit < nz:
+        by_z = jnp.concatenate([by_z, crossed(by_z, bit)], axis=0)
+        bit *= 2
     planes = [by_z] + [shifted(by_z, "vocab", s) for s in range(1, nv)]
-    by_z, targets_late = lax.optimization_barrier((by_z, targets))
     if voc_rows % 16:
         local = targets_late - first_id
         is_local = (local >= 0) & (local < voc_rows)
@@ -627,12 +640,12 @@
                 flops=0, bytes_accessed=2 * 16 * loss * width, transcendentals=0
             ),
         )(place, targets_late.reshape(1, loss), head_weight)
+    by_plane = jnp.stack(planes)
+    other = swapped(by_plane)
+    other, packed, target_rows = lax.optimization_barrier((other, packed, target_rows))
     target_rows = lax.psum_scatter(
         target_rows.reshape(nc * loss, block_width), "ctx", scatter_dimension=0, tiled=True
     )
-    by_plane = jnp.stack(planes)
-    other = swapped(by_plane)
-    other, packed = lax.optimization_barrier((other, packed))
     packed_all = lax.all_gather(packed, "ctx")
 
     first = voc_rows % CHUNK
@@ -669,21 +682,6 @@
         ),
     )(place, by_plane, other, gain, targets.reshape(loss, 1), head_weight)
 
-    at_once = max(1, min(group, (4 * 2**20) // (loss * all_tokens * 4)))
-    p_own, p_rows, out = call(
-        functools.partial(forward_body, loss_per, heads, group, at_once),
-        (
-            shape((heads, group * loss, tokens), f32),
-            shape((heads, group * loss_per, all_tokens), f32),
-            shape((heads, group * loss, HEAD_SIZE), f32),
-        ),
-        [smem()] + [vmem()] * 3,
-        [pltpu.VMEM((at_once * loss, all_tokens), f32)],
-        flops=6 * heads * group * loss * all_tokens * HEAD_SIZE,
-        moved=2 * packed_all.size,
-        exps=heads * group * loss * all_tokens,
-    )(place, key_pos, query_pos, packed_all)
-
     got = swapped(send)
     stats, keep, target_rows, *sends = call(
         functools.partial(core_body, nv - 1),
@@ -693,7 +691,7 @@
             shape((per_vocab, block_width), bf16),
         )
         + (shape((per_vocab, (nz + 1) * block_width + LANES), bf16),) * (nv - 1),
-        [smem()] + [vmem()] * 3 + [pl.BlockSpec(memory_space=pl.ANY)],
+        [smem()] + [vmem()] * 3 + [hbm()],
         [
             pltpu.VMEM((nz, loss, block_width), f32),
             pltpu.VMEM((loss, LANES), f32),
@@ -704,22 +702,23 @@
     )(place, keep, got, stats, target_rows)
     got = [shifted(sends[s - 1], "vocab", s) for s in range(1, nv)]
 
-    stats, query_pos = lax.optimization_barrier((stats, query_pos))
     at_once = max(1, min(group, (4 * 2**20) // (loss * all_tokens * 4)))
-    p_own, p_rows, out = call(
-        functools.partial(forward_body, loss_per, heads, group, at_once),
-        (
-            shape((heads, group * loss, tokens), f32),
-            shape((heads, group * loss_per, all_tokens), f32),
-            shape((heads, group * loss, HEAD_SIZE), f32),
-        ),
-        [smem()] + [vmem()] * 3,
-        [pltpu.VMEM((at_once * loss, all_tokens), f32)],
-        flops=6 * heads * group * loss * all_tokens * HEAD_SIZE,
-        moved=2 * packed_all.size,
-        exps=heads * group * loss * all_tokens,
-    )(place, key_pos, query_pos, packed_all)
-    stats, p_own, p_rows, out = lax.optimization_barrier((stats, p_own, p_rows, out))
+
+    def forward(j, query_pos):
+        return call(
+            functools.partial(forward_body, loss_per, heads, group, at_once, j),
+            (
+                shape((group * loss, tokens), f32),
+                shape((group * loss_per, all_tokens), f32),
+                shape((group * loss, HEAD_SIZE), f32),
+            ),
+            [smem()] + [vmem()] * 3,
+            [pltpu.VMEM((at_once * loss, all_tokens), f32)],
+            limit=40,
+            flops=24 * group * loss * all_tokens * HEAD_SIZE,
+            moved=2 * packed_all.size,
+            exps=group * loss * all_tokens,
+        )(place, key_pos, query_pos, packed_all)
 
     stats, keep, target_rows, *sends = call(
         functools.partial(plane_body, nv - 1),
@@ -733,6 +732,9 @@
         [pltpu.VMEM((nz, per_vocab, block_width), f32)],
     )(place, keep, stats, target_rows, *got)
     got = [shifted(sends[s - 1], "ctx", s, CORES) for s in range(1, nz)]
+    stats, query_pos = lax.optimization_barrier((stats, query_pos))
+    attention = [forward(j, query_pos) for j in range(heads // 2)]
+    stats, attention = lax.optimization_barrier((stats, attention))
     message = call(
         functools.partial(line_body, nz - 1, width),
         shape((per_vocab, block_width + LANES), bf16),
@@ -741,27 +743,32 @@
 
     gathered = [message] + [shifted(message, "vocab", s) for s in range(1, nv)]
     cols = query_width // CORES
-    rows = loss // nz
     resid_rows, mean_loss, keep, send = call(
         functools.partial(project_body, nv),
         (
             shape((loss, block_width), bf16),
-            shape((8, LANES), f32),
+            shape((1, 1), f32),
             shape((loss, cols), f32),
             shape((loss, cols), bf16),
         ),
-        [smem()] + [vmem()] * (nv + 1),
-        [pltpu.VMEM((loss, block_width), bf16), pltpu.VMEM((loss, query_width), f32)],
+        [smem()] + [vmem()] * nv + [hbm()],
+        [
+            pltpu.VMEM((loss, block_width), bf16),
+            pltpu.VMEM((loss, query_width), f32),
+            pltpu.VMEM((4, query_width // 4, block_width), bf16),
+            pltpu.SemaphoreType.DMA((4,)),
+        ],
     )(place, *gathered, output_weight)
-    keep, *sends = call(
-        half_body,
-        (shape((rows, cols), f32),) + (shape((rows, cols), bf16),) * (nz - 1),
-        [smem()] + [vmem()] * 2,
-        [pltpu.VMEM((loss, cols), f32)],
-    )(place, keep, swapped(send))
-    got = [shifted(sends[s - 1], "ctx", s, CORES) for s in range(1, nz)]
-    piece = call(sum_body, shape((rows, cols), bf16), [vmem()] * nz)(keep, *got)
-    half = jnp.stack([piece] + [shifted(piece, "ctx", s, CORES) for s in range(1, nz)])
+    half = call(sum_body, shape((loss, cols), bf16), [vmem()] * 2)(keep, swapped(send))
+    bit = 1
+    while bit < nz:
+        got = crossed(half, bit)
+        if 2 * bit == nz:
+            half, query_pos = lax.optimization_barrier((half, query_pos))
+            attention += [forward(j, query_pos) for j in range(heads // 2, heads)]
+            half, attention = lax.optimization_barrier((half, attention))
+        half = call(sum_body, shape((loss, cols), bf16), [vmem()] * 2)(half, got)
+        bit *= 2
     other = swapped(half)
     query_grad, key_grad, value_grad = call(
         functools.partial(backward_body, loss_per, heads, group),
@@ -770,10 +777,10 @@
             shape((tokens, key_width), bf16),
             shape((tokens, key_width), bf16),
         ),
-        [smem()] + [vmem()] * 6,
+        [smem()] + [vmem()] * (3 + 3 * heads),
         [pltpu.VMEM((loss, query_width), f32)],
-    )(place, half, other, packed_all, p_own, p_rows, out)
-    return (mean_loss[0, 0], query_grad, key_grad, value_grad, resid_rows.T)
+    )(place, half, other, packed_all, *jax.tree.leaves(attention))
+    return (mean_loss.reshape(()), query_grad, key_grad, value_grad, resid_rows.T)
 
 
 def solution(mesh):

time: 144 us -> 146 us (1.014)
  waiting for transfers between devices: 21.5 us -> 30.8 us
  starting transfers between devices: 35.2 us -> 27.5 us
  Pallas kernels: 64.6 us -> 67.1 us
  local copies, waits for them, and re-layouts: 7.65 us -> 5.22 us
    ppermute x0 -> x4, waiting for transfers between devices: none -> 11.4 us  [crossed(): lax.ppermute(value, 'ctx', [(i, i ^ bit * CORES) for i in range(size)])]
    ppermute x21 -> x12, starting transfers between devices: 23.5 us -> 12.3 us  [shifted(): return lax.ppermute(value, axis, pairs)]
    ppermute x0 -> x4, starting transfers between devices: none -> 6.26 us  [crossed(): lax.ppermute(value, 'ctx', [(i, i ^ bit * CORES) for i in range(size)])]
    ppermute x21 -> x12, waiting for transfers between devices: 18.5 us -> 15.2 us  [shifted(): return lax.ppermute(value, axis, pairs)]
    ppermute x4, starting transfers between devices: 11.6 us -> 8.89 us  [swapped(): return lax.ppermute(value, 'ctx', [(i, i ^ 1) for i in range(size)])]
    unnamed x28, local copies, waits for them, and re-layouts: 6.79 us -> 4.76 us
    pallas_call x3 -> x5, Pallas kernels: 4.68 us -> 5.7 us  [the longest x2 5.6 us: forward(): call(functools.partial(forward_body, loss_per, heads, group, at_once, j),...]
  transfers between devices with their start and end apart: 27 -> 22, of which waited for: 19 -> 14; matrix products, arithmetic and copies ran while one was open for 1% -> 0% of each run, Pallas kernels for 37% -> 41%
where the time goes in v4:
time: 146 us; the launch traced here: 145 us
  Pallas kernels  67.1 us (46%)
  waiting for transfers between devices  30.8 us (21%)
  starting transfers between devices  27.5 us (19%)
  between operations  14.3 us (10%)
  local copies, waits for them, and re-layouts  5.22 us (4%)
    pallas_call x1, Pallas kernels, per_device(): pl.pallas_call(functools.partial(flash_body, first), out_shape=(shape((nz...  46.7 us
    ppermute x12, waiting for transfers between devices, shifted(): return lax.ppermute(value, axis, pairs)  15.2 us
    ppermute x12, starting transfers between devices, shifted(): return lax.ppermute(value, axis, pairs)  12.3 us
    ppermute x4, waiting for transfers between devices, crossed(): lax.ppermute(value, 'ctx', [(i, i ^ bit * CORES) for i in range(size)])  11.4 us
    ppermute x4, starting transfers between devices, swapped(): return lax.ppermute(value, 'ctx', [(i, i ^ 1) for i in range(size)])  8.89 us
    ppermute x4, starting transfers between devices, crossed(): lax.ppermute(value, 'ctx', [(i, i ^ bit * CORES) for i in range(size)])  6.26 us
    pallas_call x2, Pallas kernels, forward(): call(functools.partial(forward_body, loss_per, heads, group, at_once, j),...  5.6 us
    unnamed x28, local copies, waits for them, and re-layouts  4.76 us
  transfers between devices with their start and end apart: 22, of which 14 were waited for; matrix products, arithmetic and copies ran while one was open for 0% of the time, Pallas kernels for 41%

profile of v4, /device:TPU:3, one launch (start us, length us, event | category | flops | bytes accessed | tf_op | source)
XLA Modules:
  0.0 145.2 jit_solution(2615805828263686437)
XLA Ops:
  9.8 1.4 collective-permute-start
  11.2 1.5 %collective-permute-done = bf16[1,16,1024]{2,1,0:T(8,128)(2,1)S(1)} collective-permute-done((bf16[1,16,1024]{2,1,0:T(8,128)(2,1)S(1)}, bf16[1,16,1024]{2,1,0:T(8,128)(2,1)S(1)}, u32[]{:S(2)}, u32[]{:S(2)}) %collective-permute-start) | collective-permute-done | bytes 32800 | tf_op jit(solution)/shard_map/ppermute | solution.py:69
  12.7 2.4 %collective-permute-start.1 = (bf16[2,16,1024]{2,1,0:T(8,128)(2,1)S(1)}, bf16[2,16,1024]{2,1,0:T(8,128)(2,1)S(1)}, u32[]{:S(2)}, u32[]{:S(2)}) collective-permute-start(bf16[2,16,1024]{2,1,0:T(8,128)(2,1)S(1)} %pad_maximum_fusion.2), channel_id=1, source_target_pairs={{0,4},{1,5},{2,6},{3,7},{4,0},{5,1},{6,2},{7,3},{8,12},{9,13},{10,... | collective-permute-start | bytes 196616 | tf_op jit(solution)/shard_map/ppermute | solution.py:69
  15.0 1.7 %collective-permute-done.1 = bf16[2,16,1024]{2,1,0:T(8,128)(2,1)S(1)} collective-permute-done((bf16[2,16,1024]{2,1,0:T(8,128)(2,1)S(1)}, bf16[2,16,1024]{2,1,0:T(8,128)(2,1)S(1)}, u32[]{:S(2)}, u32[]{:S(2)}) %collective-permute-start.1) | collective-permute-done | bytes 65568 | tf_op jit(solution)/shard_map/ppermute | solution.py:69
  16.8 1.3 collective-permute-start.2
  18.2 1.3 collective-permute-start.4
  19.5 1.1 collective-permute-done.2
  20.6 2.9 %collective-permute-done.3 = bf16[4,16,1024]{2,1,0:T(8,128)(2,1)S(1)} collective-permute-done((bf16[4,16,1024]{2,1,0:T(8,128)(2,1)S(1)}, bf16[4,16,1024]{2,1,0:T(8,128)(2,1)S(1)}, u32[]{:S(2)}, u32[]{:S(2)}) %collective-permute-start.3) | collective-permute-done | bytes 131104 | tf_op jit(solution)/shard_map/ppermute | solution.py:64
  23.6 4.2 %collective-permute-start.5 = (bf16[4,4,16,1024]{3,2,1,0:T(8,128)(2,1)S(1)}, bf16[4,4,16,1024]{3,2,1,0:T(8,128)(2,1)S(1)}, u32[]{:S(2)}, u32[]{:S(2)}) collective-permute-start(bf16[4,4,16,1024]{3,2,1,0:T(8,128)(2,1)S(1)} %pad_maximum_fusion.own), channel_id=1, source_target_pairs={{0,1},{1,0},{2,3},{3,2},{4,5},{5,4},{6,7},{7,6},{8,9},{9,8},{10,11... | collective-permute-start | bytes 1572872 | tf_op jit(solution)/shard_map/ppermute | solution.py:74
  28.5 4.1 %shard_map.139 = bf16[8,64,1024]{2,1,0:T(8,128)(2,1)} custom-call(s32[5]{0:T(128)S(1)} %stack.38.place, s32[1,64]{1,0:T(1,128)S(1)} %bitcast.28, bf16[4752,8192]{1,0:T(8,128)(2,1)} %weight.3), custom_call_target="tpu_custom_call" | custom-call | bytes 16777216 | tf_op jit(solution)/shard_map/pallas_call | solution.py:628
  32.6 1.4 shard_map.138
  34.8 46.7 %shard_map.140 = (f32[4,64,1024]{2,1,0:T(8,128)S(1)}, bf16[64,4224]{1,0:T(8,128)(2,1)S(1)}, f32[64,128]{1,0:T(8,128)S(1)}, f32[16,1024]{1,0:T(8,128)S(1)}) custom-call(s32[5]{0:T(128)S(1)} %stack.38.place, bf16[4,4,16,1024]{3,2,1,0:T(8,128)(2,1)S(1)} %pad_maximum_fusion.own, bf16[4,4,16,1024]{3,2,1,0:T(8,128)(2,1)S(1)} %collective-permute-done.5.other, ...), custom_call_target="tpu_custom_call" | custom-call | flops 39862665216 | bytes 155713536 | tf_op jit(solution)/shard_map/pallas_call | solution.py:656
  81.9 1.7 %collective-permute-done.6.got = bf16[64,4224]{1,0:T(8,128)(2,1)S(1)} collective-permute-done((bf16[64,4224]{1,0:T(8,128)(2,1)S(1)}, bf16[64,4224]{1,0:T(8,128)(2,1)S(1)}, u32[]{:S(2)}, u32[]{:S(2)}) %collective-permute-start.6) | collective-permute-done | bytes 540704 | tf_op jit(solution)/shard_map/ppermute | solution.py:74
  84.4 1.3 shard_map.141
  86.2 1.2 collective-permute-start.8
  87.4 1.1 collective-permute-start.9
  88.5 3.0 %collective-permute-done.7.rest_0_ = bf16[16,5248]{1,0:T(8,128)(2,1)S(1)} collective-permute-done((bf16[16,5248]{1,0:T(8,128)(2,1)S(1)}, bf16[16,5248]{1,0:T(8,128)(2,1)S(1)}, u32[]{:S(2)}, u32[]{:S(2)}) %collective-permute-start.7) | collective-permute-done | bytes 167968 | tf_op jit(solution)/shard_map/ppermute | solution.py:64
  91.5 4.6 %collective-permute-done.9.rest_2_ = bf16[16,5248]{1,0:T(8,128)(2,1)S(1)} collective-permute-done((bf16[16,5248]{1,0:T(8,128)(2,1)S(1)}, bf16[16,5248]{1,0:T(8,128)(2,1)S(1)}, u32[]{:S(2)}, u32[]{:S(2)}) %collective-permute-start.9) | collective-permute-done | bytes 167968 | tf_op jit(solution)/shard_map/ppermute | solution.py:64
  97.2 1.4 collective-permute-start.10
  98.6 3.4 %collective-permute-start.11 = (bf16[16,1152]{1,0:T(8,128)(2,1)S(1)}, bf16[16,1152]{1,0:T(8,128)(2,1)S(1)}, u32[]{:S(2)}, u32[]{:S(2)}) collective-permute-start(bf16[16,1152]{1,0:T(8,128)(2,1)S(1)} %get-tuple-element.81), channel_id=1, source_target_pairs={{0,4},{1,5},{2,6},{3,7},{4,0},{5,1},{6,2},{7,3},{8,12},{9,13},{10,... | collective-permute-start | bytes 110600 | tf_op jit(solution)/shard_map/ppermute | solution.py:64
  102.1 1.5 %copy-done.1 = bf16[1280,512]{1,0:T(8,128)(2,1)S(1)} copy-done((bf16[1280,512]{1,0:T(8,128)(2,1)S(1)}, bf16[1280,512]{1,0:T(8,128)(2,1)}, u32[]{:S(2)}) %copy-start.1) | copy-done | bytes 1310744
  103.6 2.8 %shard_map.143 = (f32[512,128]{1,0:T(8,128)S(1)}, f32[64,1024]{1,0:T(8,128)S(1)}, f32[512,128]{1,0:T(8,128)S(1)}) custom-call(s32[5]{0:T(128)S(1)} %stack.38.place, s32[1,1024]{1,0:T(1,128)S(1)} %add.63.key_pos, s32[64,1]{1,0:T(8,128)S(1)} %copy.19.query_pos, bf16[8,160,512]{2,1,0:T(8,128)(2,1)S(1)} %bitcast.20), custom_call_target="tpu_custom_call" | custom-call | flops 1610612736 | bytes 1310720 | tf_op jit(solution)/shard_map/pallas_call | solution.py:708
  107.8 1.2 collective-permute-start.14
  110.6 2.2 %collective-permute-done.15.refs_3_ = bf16[16,1152]{1,0:T(8,128)(2,1)S(1)} collective-permute-done((bf16[16,1152]{1,0:T(8,128)(2,1)S(1)}, bf16[16,1152]{1,0:T(8,128)(2,1)S(1)}, u32[]{:S(2)}, u32[]{:S(2)}) %collective-permute-start.15) | collective-permute-done | bytes 36896 | tf_op jit(solution)/shard_map/ppermute | solution.py:64
  112.8 2.9 %shard_map.145 = (bf16[64,1024]{1,0:T(8,128)(2,1)}, f32[1,1]{1,0:T(1,128)}, f32[64,1024]{1,0:T(8,128)S(1)}, bf16[64,1024]{1,0:T(8,128)(2,1)S(1)}) custom-call(s32[5]{0:T(128)S(1)} %stack.38.place, bf16[16,1152]{1,0:T(8,128)(2,1)S(1)} %shard_map.144.refs_0_, bf16[16,1152]{1,0:T(8,128)(2,1)S(1)} %collective-permute-done.13.refs_1_, ...), custom_call_target="tpu_custom_call" | custom-call | tf_op jit(solution)/shard_map/pallas_call | solution.py:746
  115.7 3.2 %collective-permute-start.16 = (bf16[64,1024]{1,0:T(8,128)(2,1)S(1)}, bf16[64,1024]{1,0:T(8,128)(2,1)S(1)}, u32[]{:S(2)}, u32[]{:S(2)}) collective-permute-start(bf16[64,1024]{1,0:T(8,128)(2,1)S(1)} %get-tuple-element.85), channel_id=1, source_target_pairs={{0,1},{1,0},{2,3},{3,2},{4,5},{5,4},{6,7},{7,6},{8,9},{9,8},{10,11... | collective-permute-start | bytes 393224 | tf_op jit(solution)/shard_map/ppermute | solution.py:74
  119.9 1.8 %collective-permute-start.17 = (bf16[64,1024]{1,0:T(8,128)(2,1)S(1)}, bf16[64,1024]{1,0:T(8,128)(2,1)S(1)}, u32[]{:S(2)}, u32[]{:S(2)}) collective-permute-start(bf16[64,1024]{1,0:T(8,128)(2,1)S(1)} %shard_map.146.keep), channel_id=1, source_target_pairs={{0,2},{1,3},{2,0},{3,1},{4,6},{5,7},{6,4},{7,5},{8,10},{9,11},{10,... | collective-permute-start | bytes 393224 | tf_op jit(solution)/shard_map/ppermute | solution.py:69
  121.7 3.6 %collective-permute-done.17.refs_0_ = bf16[64,1024]{1,0:T(8,128)(2,1)S(1)} collective-permute-done((bf16[64,1024]{1,0:T(8,128)(2,1)S(1)}, bf16[64,1024]{1,0:T(8,128)(2,1)S(1)}, u32[]{:S(2)}, u32[]{:S(2)}) %collective-permute-start.17) | collective-permute-done | bytes 131104 | tf_op jit(solution)/shard_map/ppermute | solution.py:69
  126.1 2.8 %shard_map.148 = (f32[512,128]{1,0:T(8,128)S(1)}, f32[64,1024]{1,0:T(8,128)S(1)}, f32[512,128]{1,0:T(8,128)S(1)}) custom-call(s32[5]{0:T(128)S(1)} %stack.38.place, s32[1,1024]{1,0:T(1,128)S(1)} %add.63.key_pos, s32[64,1]{1,0:T(8,128)S(1)} %copy.20.query_pos, bf16[8,160,512]{2,1,0:T(8,128)(2,1)S(1)} %bitcast.21), custom_call_target="tpu_custom_call" | custom-call | flops 1610612736 | bytes 1310720 | tf_op jit(solution)/shard_map/pallas_call | solution.py:708
  128.9 4.6 %collective-permute-done.18.refs_0_ = bf16[64,1024]{1,0:T(8,128)(2,1)S(1)} collective-permute-done((bf16[64,1024]{1,0:T(8,128)(2,1)S(1)}, bf16[64,1024]{1,0:T(8,128)(2,1)S(1)}, u32[]{:S(2)}, u32[]{:S(2)}) %collective-permute-start.18) | collective-permute-done | bytes 131104 | tf_op jit(solution)/shard_map/ppermute | solution.py:69
  133.6 1.5 %collective-permute-start.19 = (bf16[64,1024]{1,0:T(8,128)(2,1)S(1)}, bf16[64,1024]{1,0:T(8,128)(2,1)S(1)}, u32[]{:S(2)}, u32[]{:S(2)}) collective-permute-start(bf16[64,1024]{1,0:T(8,128)(2,1)S(1)} %shard_map.149.half), channel_id=1, source_target_pairs={{0,1},{1,0},{2,3},{3,2},{4,5},{5,4},{6,7},{7,6},{8,9},{9,8},{10,11... | collective-permute-start | bytes 393224 | tf_op jit(solution)/shard_map/ppermute | solution.py:74
  136.1 2.3 %shard_map.150 = (bf16[8,2048]{1,0:T(8,128)(2,1)}, bf16[128,256]{1,0:T(8,128)(2,1)}, bf16[128,256]{1,0:T(8,128)(2,1)}) custom-call(s32[5]{0:T(128)S(1)} %stack.38.place, bf16[64,1024]{1,0:T(8,128)(2,1)S(1)} %shard_map.149.half, bf16[64,1024]{1,0:T(8,128)(2,1)S(1)} %collective-permute-done.19.other, bf16[8,160,512]{2,1,0:T(8,128)(2,1)S(1)} %bitcast.22, ...), custom_call_target="tpu_custom_call" | custom-call | tf_op jit(solution)/shard_map/pallas_call | solution.py:773
  (69 shorter events, 13.0 us)
Async XLA Ops:
  7.2 76.4 %reduce-scatter.2.cloned.1.call-start = ((), (), s32[]{:S(2)}) async-start(), calls=%async_computation.1 | async-start | bytes 1179648 | tf_op jit(solution)/shard_map/reduce_scatter | solution.py:646
  9.8 2.8 %collective-permute-start = (bf16[1,16,1024]{2,1,0:T(8,128)(2,1)S(1)}, bf16[1,16,1024]{2,1,0:T(8,128)(2,1)S(1)}, u32[]{:S(2)}, u32[]{:S(2)}) collective-permute-start(bf16[1,16,1024]{2,1,0:T(8,128)(2,1)S(1)} %bitcast.23), channel_id=1, source_target_pairs={{0,2},{1,3},{2,0},{3,1},{4,6},{5,7},{6,4},{7,5},{8,10},{9,11},{10,... | collective-permute-start | bytes 98312 | tf_op jit(solution)/shard_map/ppermute | solution.py:69
  12.7 4.1 %collective-permute-start.1 = (bf16[2,16,1024]{2,1,0:T(8,128)(2,1)S(1)}, bf16[2,16,1024]{2,1,0:T(8,128)(2,1)S(1)}, u32[]{:S(2)}, u32[]{:S(2)}) collective-permute-start(bf16[2,16,1024]{2,1,0:T(8,128)(2,1)S(1)} %pad_maximum_fusion.2), channel_id=1, source_target_pairs={{0,4},{1,5},{2,6},{3,7},{4,0},{5,1},{6,2},{7,3},{8,12},{9,13},{10,... | collective-permute-start | bytes 196616 | tf_op jit(solution)/shard_map/ppermute | solution.py:69
  16.8 3.9 %collective-permute-start.2 = (bf16[4,16,1024]{2,1,0:T(8,128)(2,1)S(1)}, bf16[4,16,1024]{2,1,0:T(8,128)(2,1)S(1)}, u32[]{:S(2)}, u32[]{:S(2)}) collective-permute-start(bf16[4,16,1024]{2,1,0:T(8,128)(2,1)S(1)} %get-tuple-element.106), channel_id=1, source_target_pairs={{0,8},{8,16},{16,24},{24,0},{1,9},{9,17},{17,25},{25,1},{2,10},{10... | collective-permute-start | bytes 393224 | tf_op jit(solution)/shard_map/ppermute | solution.py:64
  18.0 5.5 %collective-permute-start.3 = (bf16[4,16,1024]{2,1,0:T(8,128)(2,1)S(1)}, bf16[4,16,1024]{2,1,0:T(8,128)(2,1)S(1)}, u32[]{:S(2)}, u32[]{:S(2)}) collective-permute-start(bf16[4,16,1024]{2,1,0:T(8,128)(2,1)S(1)} %get-tuple-element.106), channel_id=1, source_target_pairs={{0,16},{8,24},{16,0},{24,8},{1,17},{9,25},{17,1},{25,9},{2,18},{10... | collective-permute-start | bytes 393224 | tf_op jit(solution)/shard_map/ppermute | solution.py:64
  18.2 5.3 %collective-permute-start.4 = (bf16[4,16,1024]{2,1,0:T(8,128)(2,1)S(1)}, bf16[4,16,1024]{2,1,0:T(8,128)(2,1)S(1)}, u32[]{:S(2)}, u32[]{:S(2)}) collective-permute-start(bf16[4,16,1024]{2,1,0:T(8,128)(2,1)S(1)} %get-tuple-element.106), channel_id=1, source_target_pairs={{0,24},{8,0},{16,8},{24,16},{1,25},{9,1},{17,9},{25,17},{2,26},{10... | collective-permute-start | bytes 393224 | tf_op jit(solution)/shard_map/ppermute | solution.py:64
  23.6 10.4 %collective-permute-start.5 = (bf16[4,4,16,1024]{3,2,1,0:T(8,128)(2,1)S(1)}, bf16[4,4,16,1024]{3,2,1,0:T(8,128)(2,1)S(1)}, u32[]{:S(2)}, u32[]{:S(2)}) collective-permute-start(bf16[4,4,16,1024]{3,2,1,0:T(8,128)(2,1)S(1)} %pad_maximum_fusion.own), channel_id=1, source_target_pairs={{0,1},{1,0},{2,3},{3,2},{4,5},{5,4},{6,7},{7,6},{8,9},{9,8},{10,11... | collective-permute-start | bytes 1572872 | tf_op jit(solution)/shard_map/ppermute | solution.py:74
  28.4 4.1 %copy-start.3 = (bf16[128,2048]{1,0:T(8,128)(2,1)S(1)}, bf16[128,2048]{1,0:T(8,128)(2,1)}, u32[]{:S(2)}) copy-start(bf16[128,2048]{1,0:T(8,128)(2,1)} %queries) | copy-start | bytes 1572868
  28.4 4.1 %copy-start.6 = (bf16[128,256]{1,0:T(8,128)(2,1)S(1)}, bf16[128,256]{1,0:T(8,128)(2,1)}, u32[]{:S(2)}) copy-start(bf16[128,256]{1,0:T(8,128)(2,1)} %keys.1) | copy-start | bytes 196612
  28.5 4.1 %copy-start.7 = (bf16[128,256]{1,0:T(8,128)(2,1)S(1)}, bf16[128,256]{1,0:T(8,128)(2,1)}, u32[]{:S(2)}) copy-start(bf16[128,256]{1,0:T(8,128)(2,1)} %values.1) | copy-start | bytes 196612
  28.5 4.1 %copy-start.10 = (s32[64]{0:T(128)S(1)}, s32[64]{0:T(128)}, u32[]{:S(2)}) copy-start(s32[64]{0:T(128)} %rows.3) | copy-start | bytes 772
  28.5 5.6 %copy-start.12 = (s32[64]{0:T(128)S(1)}, s32[64]{0:T(128)}, u32[]{:S(2)}) copy-start(s32[64]{0:T(128)} %param.13) | copy-start | bytes 772
  28.5 5.7 %copy-start.13 = (s32[16]{0:T(128)S(1)}, s32[16]{0:T(128)}, u32[]{:S(2)}) copy-start(s32[16]{0:T(128)} %param.15) | copy-start | bytes 196
  28.5 6.3 %copy-start.8 = (f32[8192]{0:T(1024)S(1)}, f32[8192]{0:T(1024)}, u32[]{:S(2)}) copy-start(f32[8192]{0:T(1024)} %param.11) | copy-start | bytes 98308
  34.0 68.1 %all-gather.3.cloned.1.call-start = ((), (), s32[]{:S(2)}) async-start(), calls=%async_computation.2 | async-start | bytes 1474560 | tf_op jit(solution)/shard_map/all_gather | solution.py:649
  81.5 2.0 %collective-permute-start.6 = (bf16[64,4224]{1,0:T(8,128)(2,1)S(1)}, bf16[64,4224]{1,0:T(8,128)(2,1)S(1)}, u32[]{:S(2)}, u32[]{:S(2)}) collective-permute-start(bf16[64,4224]{1,0:T(8,128)(2,1)S(1)} %get-tuple-element.60), channel_id=1, source_target_pairs={{0,1},{1,0},{2,3},{3,2},{4,5},{5,4},{6,7},{7,6},{8,9},{9,8},{10,11... | collective-permute-start | bytes 1622024 | tf_op jit(solution)/shard_map/ppermute | solution.py:74
  85.7 5.8 %collective-permute-start.7 = (bf16[16,5248]{1,0:T(8,128)(2,1)S(1)}, bf16[16,5248]{1,0:T(8,128)(2,1)S(1)}, u32[]{:S(2)}, u32[]{:S(2)}) collective-permute-start(bf16[16,5248]{1,0:T(8,128)(2,1)S(1)} %get-tuple-element.66), channel_id=1, source_target_pairs={{0,8},{8,16},{16,24},{24,0},{1,9},{9,17},{17,25},{25,1},{2,10},{10... | collective-permute-start | bytes 503816 | tf_op jit(solution)/shard_map/ppermute | solution.py:64
  86.2 5.3 %collective-permute-start.8 = (bf16[16,5248]{1,0:T(8,128)(2,1)S(1)}, bf16[16,5248]{1,0:T(8,128)(2,1)S(1)}, u32[]{:S(2)}, u32[]{:S(2)}) collective-permute-start(bf16[16,5248]{1,0:T(8,128)(2,1)S(1)} %get-tuple-element.67), channel_id=1, source_target_pairs={{0,16},{8,24},{16,0},{24,8},{1,17},{9,25},{17,1},{25,9},{2,18},{10... | collective-permute-start | bytes 503816 | tf_op jit(solution)/shard_map/ppermute | solution.py:64
  87.4 8.6 %collective-permute-start.9 = (bf16[16,5248]{1,0:T(8,128)(2,1)S(1)}, bf16[16,5248]{1,0:T(8,128)(2,1)S(1)}, u32[]{:S(2)}, u32[]{:S(2)}) collective-permute-start(bf16[16,5248]{1,0:T(8,128)(2,1)S(1)} %get-tuple-element.68), channel_id=1, source_target_pairs={{0,24},{8,0},{16,8},{24,16},{1,25},{9,1},{17,9},{25,17},{2,26},{10... | collective-permute-start | bytes 503816 | tf_op jit(solution)/shard_map/ppermute | solution.py:64
  97.2 9.2 %collective-permute-start.10 = (bf16[16,1152]{1,0:T(8,128)(2,1)S(1)}, bf16[16,1152]{1,0:T(8,128)(2,1)S(1)}, u32[]{:S(2)}, u32[]{:S(2)}) collective-permute-start(bf16[16,1152]{1,0:T(8,128)(2,1)S(1)} %get-tuple-element.80), channel_id=1, source_target_pairs={{0,2},{1,3},{2,4},{3,5},{4,6},{5,7},{6,0},{7,1},{8,10},{9,11},{10,... | collective-permute-start | bytes 110600 | tf_op jit(solution)/shard_map/ppermute | solution.py:64
  98.6 7.8 %collective-permute-start.11 = (bf16[16,1152]{1,0:T(8,128)(2,1)S(1)}, bf16[16,1152]{1,0:T(8,128)(2,1)S(1)}, u32[]{:S(2)}, u32[]{:S(2)}) collective-permute-start(bf16[16,1152]{1,0:T(8,128)(2,1)S(1)} %get-tuple-element.81), channel_id=1, source_target_pairs={{0,4},{1,5},{2,6},{3,7},{4,0},{5,1},{6,2},{7,3},{8,12},{9,13},{10,... | collective-permute-start | bytes 110600 | tf_op jit(solution)/shard_map/ppermute | solution.py:64
  102.1 4.4 %collective-permute-start.12 = (bf16[16,1152]{1,0:T(8,128)(2,1)S(1)}, bf16[16,1152]{1,0:T(8,128)(2,1)S(1)}, u32[]{:S(2)}, u32[]{:S(2)}) collective-permute-start(bf16[16,1152]{1,0:T(8,128)(2,1)S(1)} %get-tuple-element.82), channel_id=1, source_target_pairs={{0,6},{1,7},{2,0},{3,1},{4,2},{5,3},{6,4},{7,5},{8,14},{9,15},{10,... | collective-permute-start | bytes 110600 | tf_op jit(solution)/shard_map/ppermute | solution.py:64
  102.1 10.6 %copy-start = (bf16[2048,1024]{1,0:T(8,128)(2,1)S(1)}, bf16[2048,1024]{1,0:T(8,128)(2,1)}, u32[]{:S(2)}) copy-start(bf16[2048,1024]{1,0:T(8,128)(2,1)} %refs_4_.1) | copy-start | bytes 12582916
  102.1 1.5 %copy-start.1 = (bf16[1280,512]{1,0:T(8,128)(2,1)S(1)}, bf16[1280,512]{1,0:T(8,128)(2,1)}, u32[]{:S(2)}) copy-start(bf16[1280,512]{1,0:T(8,128)(2,1)} %all-gather.3.cloned.1.call-done) | copy-start | bytes 3932164
  106.4 19.7 %copy-start.2 = (bf16[1280,512]{1,0:T(8,128)(2,1)S(1)}, bf16[1280,512]{1,0:T(8,128)(2,1)}, u32[]{:S(2)}) copy-start(bf16[1280,512]{1,0:T(8,128)(2,1)} %all-gather.3.cloned.1.call-done) | copy-start | bytes 3932164
  107.4 2.9 %collective-permute-start.13 = (bf16[16,1152]{1,0:T(8,128)(2,1)S(1)}, bf16[16,1152]{1,0:T(8,128)(2,1)S(1)}, u32[]{:S(2)}, u32[]{:S(2)}) collective-permute-start(bf16[16,1152]{1,0:T(8,128)(2,1)S(1)} %shard_map.144.refs_0_), channel_id=1, source_target_pairs={{0,8},{8,16},{16,24},{24,0},{1,9},{9,17},{17,25},{25,1},{2,10},{10... | collective-permute-start | bytes 110600 | tf_op jit(solution)/shard_map/ppermute | solution.py:64
  107.8 2.8 %collective-permute-start.14 = (bf16[16,1152]{1,0:T(8,128)(2,1)S(1)}, bf16[16,1152]{1,0:T(8,128)(2,1)S(1)}, u32[]{:S(2)}, u32[]{:S(2)}) collective-permute-start(bf16[16,1152]{1,0:T(8,128)(2,1)S(1)} %shard_map.144.refs_0_), channel_id=1, source_target_pairs={{0,16},{8,24},{16,0},{24,8},{1,17},{9,25},{17,1},{25,9},{2,18},{10... | collective-permute-start | bytes 110600 | tf_op jit(solution)/shard_map/ppermute | solution.py:64
  109.0 3.8 %collective-permute-start.15 = (bf16[16,1152]{1,0:T(8,128)(2,1)S(1)}, bf16[16,1152]{1,0:T(8,128)(2,1)S(1)}, u32[]{:S(2)}, u32[]{:S(2)}) collective-permute-start(bf16[16,1152]{1,0:T(8,128)(2,1)S(1)} %shard_map.144.refs_0_), channel_id=1, source_target_pairs={{0,24},{8,0},{16,8},{24,16},{1,25},{9,1},{17,9},{25,17},{2,26},{10... | collective-permute-start | bytes 110600 | tf_op jit(solution)/shard_map/ppermute | solution.py:64
  115.7 4.2 %collective-permute-start.16 = (bf16[64,1024]{1,0:T(8,128)(2,1)S(1)}, bf16[64,1024]{1,0:T(8,128)(2,1)S(1)}, u32[]{:S(2)}, u32[]{:S(2)}) collective-permute-start(bf16[64,1024]{1,0:T(8,128)(2,1)S(1)} %get-tuple-element.85), channel_id=1, source_target_pairs={{0,1},{1,0},{2,3},{3,2},{4,5},{5,4},{6,7},{7,6},{8,9},{9,8},{10,11... | collective-permute-start | bytes 393224 | tf_op jit(solution)/shard_map/ppermute | solution.py:74
  119.9 5.4 %collective-permute-start.17 = (bf16[64,1024]{1,0:T(8,128)(2,1)S(1)}, bf16[64,1024]{1,0:T(8,128)(2,1)S(1)}, u32[]{:S(2)}, u32[]{:S(2)}) collective-permute-start(bf16[64,1024]{1,0:T(8,128)(2,1)S(1)} %shard_map.146.keep), channel_id=1, source_target_pairs={{0,2},{1,3},{2,0},{3,1},{4,6},{5,7},{6,4},{7,5},{8,10},{9,11},{10,... | collective-permute-start | bytes 393224 | tf_op jit(solution)/shard_map/ppermute | solution.py:69
  125.3 8.3 %collective-permute-start.18 = (bf16[64,1024]{1,0:T(8,128)(2,1)S(1)}, bf16[64,1024]{1,0:T(8,128)(2,1)S(1)}, u32[]{:S(2)}, u32[]{:S(2)}) collective-permute-start(bf16[64,1024]{1,0:T(8,128)(2,1)S(1)} %shard_map.147.keep), channel_id=1, source_target_pairs={{0,4},{1,5},{2,6},{3,7},{4,0},{5,1},{6,2},{7,3},{8,12},{9,13},{10,... | collective-permute-start | bytes 393224 | tf_op jit(solution)/shard_map/ppermute | solution.py:69
  133.6 2.5 %collective-permute-start.19 = (bf16[64,1024]{1,0:T(8,128)(2,1)S(1)}, bf16[64,1024]{1,0:T(8,128)(2,1)S(1)}, u32[]{:S(2)}, u32[]{:S(2)}) collective-permute-start(bf16[64,1024]{1,0:T(8,128)(2,1)S(1)} %shard_map.149.half), channel_id=1, source_target_pairs={{0,1},{1,0},{2,3},{3,2},{4,5},{5,4},{6,7},{7,6},{8,9},{9,8},{10,11... | collective-permute-start | bytes 393224 | tf_op jit(solution)/shard_map/ppermute | solution.py:74
  (4 other events, 3.3 us)
Sparse Core Ops, SparseCore 0:
  34.1 30.3 reduce-scatter.1
  66.2 25.2 all-gather.2

commit v5 on v4

--- a/solution.py
+++ b/solution.py
@@ -10,7 +10,7 @@
 HEAD_SIZE = 128
 CORES = 2
 CHUNK = 512
-SLOTS = 3
+SLOTS = 4
 LANES = 128
 
 norm_eps = 1e-06
@@ -160,6 +160,7 @@
     raw,
     acc,
     probs,
+    fresh,
     state,
     head_buf,
     buf,
@@ -191,7 +192,7 @@
 
     is_even = core_at == 0
     for zr in range(nz):
-        z_src = lax.bitwise_xor(z_at, zr)
+        z_src = lax.rem(z_at - zr + nz, nz)
         square_own = jnp.zeros((8, 1), f32)
         square_other = jnp.zeros((8, 1), f32)
         for vr in range(nv):
@@ -268,34 +269,45 @@
             else:
                 acc[b] = acc[b] * scale + part
 
+    def part(ref, slot):
+        return lambda at, n: ref[slot, :, at : at + n]
+
     head_copy().wait()
     p, _, run = softmax(scores_of(head_buf[...]), first_id, None)
-    add_product(p, None, lambda at, n: head_buf[:, at : at + n])
-    if chunks:
+    if not chunks:
+        add_product(p, None, lambda at, n: head_buf[:, at : at + n])
+    else:
+        def start_of(c):
+            return first_id + first + c * CHUNK
+
         body_copy(0).wait()
-        p, scale, run = softmax(scores_of(buf[0]), first_id + first, run)
+        fresh[...] = scores_of(buf[0])
+        add_product(p, None, lambda at, n: head_buf[:, at : at + n])
+        body_copy(1).wait()
+        scores = scores_of(buf[1])
+        p, scale, run = softmax(fresh[...], start_of(0), run)
         probs[...] = p
+        fresh[...] = scores
 
         def step(c, carry):
             scale, run = carry
             body_copy(c).wait()
-            here = lax.rem(c, SLOTS)
-            there = lax.rem(c - 1, SLOTS)
-            scores = scores_of(buf[here])
-            add_product(probs[...], scale, lambda at, n: buf[there, :, at : at + n])
-
-            p, scale, run = softmax(scores, first_id + first + c * CHUNK, run)
+            scores = scores_of(buf[lax.rem(c, SLOTS)])
+            p, next_scale, run = softmax(fresh[...], start_of(c - 1), run)
+            add_product(probs[...], scale, part(buf, lax.rem(c - 2, SLOTS)))
             probs[...] = p
-
-            @pl.when(c + SLOTS - 1 < chunks)
+            fresh[...] = scores
+
+            @pl.when(c + 2 < chunks)
             def _():
-                body_copy(c + SLOTS - 1).start()
-
-            return scale, run
-
-        scale, run = lax.fori_loop(1, chunks, step, (scale, run))
-        last = (chunks - 1) % SLOTS
-        add_product(probs[...], scale, lambda at, n: buf[last, :, at : at + n])
+                body_copy(c + 2).start()
+
+            return next_scale, run
+
+        scale, run = lax.fori_loop(2, chunks, step, (scale, run))
+        p, next_scale, run = softmax(fresh[...], start_of(chunks - 1), run)
+        add_product(probs[...], scale, part(buf, (chunks - 2) % SLOTS))
+        add_product(p, next_scale, part(buf, (chunks - 1) % SLOTS))
 
     for z in range(nz):
         keep[z] = acc[CORES * z + core_at]
@@ -612,11 +624,7 @@
         [smem(), smem()] + [vmem()] * 3,
         moved=2 * queries.size,
     )(place, loss_rows, queries, key_states, attention_values)
-    by_z = picked[None]
-    bit = 1
-    while bit < nz:
-        by_z = jnp.concatenate([by_z, crossed(by_z, bit)], axis=0)
-        bit *= 2
+    by_z = jnp.stack([picked] + [shifted(picked, "ctx", s, CORES) for s in range(1, nz)])
     planes = [by_z] + [shifted(by_z, "vocab", s) for s in range(1, nv)]
     if voc_rows % 16:
         local = targets_late - first_id
@@ -640,12 +648,13 @@
                 flops=0, bytes_accessed=2 * 16 * loss * width, transcendentals=0
             ),
         )(place, targets_late.reshape(1, loss), head_weight)
+    planes, target_rows = lax.optimization_barrier((planes, target_rows))
     by_plane = jnp.stack(planes)
     other = swapped(by_plane)
-    other, packed, target_rows = lax.optimization_barrier((other, packed, target_rows))
     target_rows = lax.psum_scatter(
         target_rows.reshape(nc * loss, block_width), "ctx", scatter_dimension=0, tiled=True
     )
+    other, packed = lax.optimization_barrier((other, packed))
     packed_all = lax.all_gather(packed, "ctx")
 
     first = voc_rows % CHUNK
@@ -668,13 +677,14 @@
             pltpu.VMEM((loss, width), bf16),
             pltpu.VMEM((nc, loss, block_width), f32),
             pltpu.VMEM((loss, CHUNK), bf16),
+            pltpu.VMEM((loss, CHUNK), f32),
             pltpu.VMEM((loss, LANES), f32),
             pltpu.VMEM((first, width), bf16),
             pltpu.VMEM((SLOTS if chunks else 1, CHUNK if chunks else 16, width), bf16),
             pltpu.SemaphoreType.DMA,
             pltpu.SemaphoreType.DMA((SLOTS,)),
         ],
-        compiler_params=pltpu.CompilerParams(vmem_limit_bytes=50 * 2**20),
+        compiler_params=pltpu.CompilerParams(vmem_limit_bytes=47 * 2**20),
         cost_estimate=pl.CostEstimate(
             flops=4 * max(loss, 256) * width * voc_rows,
             bytes_accessed=4 * width * voc_rows,
@@ -682,6 +692,7 @@
         ),
     )(place, by_plane, other, gain, targets.reshape(loss, 1), head_weight)
 
+    send, target_rows = lax.optimization_barrier((send, target_rows))
     got = swapped(send)
     stats, keep, target_rows, *sends = call(
         functools.partial(core_body, nv - 1),
@@ -720,6 +731,7 @@
             exps=group * loss * all_tokens,
         )(place, key_pos, query_pos, packed_all)
 
+    stats, packed_all = lax.optimization_barrier((stats, packed_all))
     stats, keep, target_rows, *sends = call(
         functools.partial(plane_body, nv - 1),
         (
@@ -732,9 +744,6 @@
         [pltpu.VMEM((nz, per_vocab, block_width), f32)],
     )(place, keep, stats, target_rows, *got)
     got = [shifted(sends[s - 1], "ctx", s, CORES) for s in range(1, nz)]
-    stats, query_pos = lax.optimization_barrier((stats, query_pos))
-    attention = [forward(j, query_pos) for j in range(heads // 2)]
-    stats, attention = lax.optimization_barrier((stats, attention))
     message = call(
         functools.partial(line_body, nz - 1, width),
         shape((per_vocab, block_width + LANES), bf16),
@@ -760,15 +769,17 @@
         ],
     )(place, *gathered, output_weight)
     half = call(sum_body, shape((loss, cols), bf16), [vmem()] * 2)(keep, swapped(send))
-    bit = 1
-    while bit < nz:
-        got = crossed(half, bit)
-        if 2 * bit == nz:
-            half, query_pos = lax.optimization_barrier((half, query_pos))
-            attention += [forward(j, query_pos) for j in range(heads // 2, heads)]
-            half, attention = lax.optimization_barrier((half, attention))
+    windows = nz.bit_length() - 1
+    attention = [None] * heads
+    for k in range(windows):
+        got = crossed(half, 2**k)
+        here = range(k, heads, windows)
+        half, query_pos = lax.optimization_barrier((half, query_pos))
+        made = [forward(j, query_pos) for j in here]
+        half, made = lax.optimization_barrier((half, made))
+        for j, result in zip(here, made):
+            attention[j] = result
         half = call(sum_body, shape((loss, cols), bf16), [vmem()] * 2)(half, got)
-        bit *= 2
     other = swapped(half)
     query_grad, key_grad, value_grad = call(
         functools.partial(backward_body, loss_per, heads, group),

time: 146 us -> 143 us (0.979)
  waiting for transfers between devices: 30.8 us -> 25.8 us
  Pallas kernels: 67.1 us -> 68.7 us
    ppermute x4 -> x2, waiting for transfers between devices: 11.4 us -> 6.51 us  [crossed(): lax.ppermute(value, 'ctx', [(i, i ^ bit * CORES) for i in range(size)])]
    ppermute x4 -> x2, starting transfers between devices: 6.26 us -> 1.48 us  [crossed(): lax.ppermute(value, 'ctx', [(i, i ^ bit * CORES) for i in range(size)])]
    ppermute x12 -> x15, starting transfers between devices: 12.3 us -> 16.4 us  [shifted(): return lax.ppermute(value, axis, pairs)]
    pallas_call x1, Pallas kernels: 46.7 us -> 50.1 us  [per_device(): pl.pallas_call(functools.partial(flash_body, first), out_shape=(shape((nz...]
    pallas_call x1, Pallas kernels: 4.05 us -> 2.29 us  [per_device(): pl.pallas_call(target_body, out_shape=shape((nc, loss, block_width), bf16...]
    unnamed x28 -> x26, local copies, waits for them, and re-layouts: 4.76 us -> 5.48 us
    ppermute x12 -> x15, waiting for transfers between devices: 15.2 us -> 15.7 us  [shifted(): return lax.ppermute(value, axis, pairs)]
  transfers between devices with their start and end apart: 22 -> 23, of which waited for: 14 -> 15; matrix products, arithmetic and copies ran while one was open for 0% -> 0% of each run, Pallas kernels for 41% -> 42%
where the time goes in v5:
time: 143 us
  Pallas kernels  68.7 us (48%)
  starting transfers between devices  28.2 us (20%)
  waiting for transfers between devices  25.8 us (18%)
  between operations  14.3 us (10%)
  local copies, waits for them, and re-layouts  5.93 us (4%)
    pallas_call x1, Pallas kernels, per_device(): pl.pallas_call(functools.partial(flash_body, first), out_shape=(shape((nz...  50.1 us
    ppermute x15, starting transfers between devices, shifted(): return lax.ppermute(value, axis, pairs)  16.4 us
    ppermute x15, waiting for transfers between devices, shifted(): return lax.ppermute(value, axis, pairs)  15.7 us
    ppermute x4, starting transfers between devices, swapped(): return lax.ppermute(value, 'ctx', [(i, i ^ 1) for i in range(size)])  10.3 us
    ppermute x2, waiting for transfers between devices, crossed(): lax.ppermute(value, 'ctx', [(i, i ^ bit * CORES) for i in range(size)])  6.51 us
    pallas_call x2, Pallas kernels, forward(): call(functools.partial(forward_body, loss_per, heads, group, at_once, j),...  5.6 us
    unnamed x26, local copies, waits for them, and re-layouts  5.48 us
    ppermute x4, waiting for transfers between devices, swapped(): return lax.ppermute(value, 'ctx', [(i, i ^ 1) for i in range(size)])  3.55 us
  transfers between devices with their start and end apart: 23, of which 15 were waited for; matrix products, arithmetic and copies ran while one was open for 0% of the time, Pallas kernels for 42%

profile of v5, /device:TPU:3, one launch (start us, length us, event | category | flops | bytes accessed | tf_op | source)
XLA Modules:
  0.0 143.2 jit_solution(3979425807393656244)
XLA Ops:
  7.3 1.0 copy-done.3
  9.8 1.3 collective-permute-start
  11.2 2.3 %collective-permute-start.1 = (bf16[16,1024]{1,0:T(8,128)(2,1)S(1)}, bf16[16,1024]{1,0:T(8,128)(2,1)S(1)}, u32[]{:S(2)}, u32[]{:S(2)}) collective-permute-start(bf16[16,1024]{1,0:T(8,128)(2,1)S(1)} %shard_map.137), channel_id=1, source_target_pairs={{0,4},{1,5},{2,6},{3,7},{4,0},{5,1},{6,2},{7,3},{8,12},{9,13},{10,... | collective-permute-start | bytes 98312 | tf_op jit(solution)/shard_map/ppermute | solution.py:64
  13.5 1.1 collective-permute-start.2
  14.8 2.0 %collective-permute-done.2 = bf16[16,1024]{1,0:T(8,128)(2,1)S(1)} collective-permute-done((bf16[16,1024]{1,0:T(8,128)(2,1)S(1)}, bf16[16,1024]{1,0:T(8,128)(2,1)S(1)}, u32[]{:S(2)}, u32[]{:S(2)}) %collective-permute-start.2) | collective-permute-done | bytes 32800 | tf_op jit(solution)/shard_map/ppermute | solution.py:64
  16.9 1.3 collective-permute-start.3
  18.3 1.3 collective-permute-start.5
  20.3 2.3 %shard_map.138 = bf16[8,64,1024]{2,1,0:T(8,128)(2,1)} custom-call(s32[5]{0:T(128)S(1)} %stack.53.place, s32[1,64]{1,0:T(1,128)S(1)} %bitcast.28, bf16[4752,8192]{1,0:T(8,128)(2,1)} %weight.3), custom_call_target="tpu_custom_call" | custom-call | bytes 16777216 | tf_op jit(solution)/shard_map/pallas_call | solution.py:636
  23.7 4.3 %collective-permute-start.6 = (bf16[4,4,16,1024]{3,2,1,0:T(8,128)(2,1)S(1)}, bf16[4,4,16,1024]{3,2,1,0:T(8,128)(2,1)S(1)}, u32[]{:S(2)}, u32[]{:S(2)}) collective-permute-start(bf16[4,4,16,1024]{3,2,1,0:T(8,128)(2,1)S(1)} %pad_maximum_fusion.own), channel_id=1, source_target_pairs={{0,1},{1,0},{2,3},{3,2},{4,5},{5,4},{6,7},{7,6},{8,9},{9,8},{10,11... | collective-permute-start | bytes 1572872 | tf_op jit(solution)/shard_map/ppermute | solution.py:74
  28.1 1.4 shard_map.139
  29.6 50.1 %shard_map.140 = (f32[4,64,1024]{2,1,0:T(8,128)S(1)}, bf16[64,4224]{1,0:T(8,128)(2,1)S(1)}, f32[64,128]{1,0:T(8,128)S(1)}, f32[16,1024]{1,0:T(8,128)S(1)}) custom-call(s32[5]{0:T(128)S(1)} %stack.53.place, bf16[4,4,16,1024]{3,2,1,0:T(8,128)(2,1)S(1)} %pad_maximum_fusion.own, bf16[4,4,16,1024]{3,2,1,0:T(8,128)(2,1)S(1)} %collective-permute-done.6.other, ...), custom_call_target="tpu_custom_call" | custom-call | flops 39862665216 | bytes 155713536 | tf_op jit(solution)/shard_map/pallas_call | solution.py:665
  80.1 1.6 %collective-permute-done.7.got = bf16[64,4224]{1,0:T(8,128)(2,1)S(1)} collective-permute-done((bf16[64,4224]{1,0:T(8,128)(2,1)S(1)}, bf16[64,4224]{1,0:T(8,128)(2,1)S(1)}, u32[]{:S(2)}, u32[]{:S(2)}) %collective-permute-start.7) | collective-permute-done | bytes 540704 | tf_op jit(solution)/shard_map/ppermute | solution.py:74
  82.6 1.3 shard_map.141
  84.1 2.2 %collective-permute-start.8 = (bf16[16,5248]{1,0:T(8,128)(2,1)S(1)}, bf16[16,5248]{1,0:T(8,128)(2,1)S(1)}, u32[]{:S(2)}, u32[]{:S(2)}) collective-permute-start(bf16[16,5248]{1,0:T(8,128)(2,1)S(1)} %get-tuple-element.79), channel_id=1, source_target_pairs={{0,8},{8,16},{16,24},{24,0},{1,9},{9,17},{17,25},{25,1},{2,10},{10... | collective-permute-start | bytes 503816 | tf_op jit(solution)/shard_map/ppermute | solution.py:64
  86.6 3.7 %collective-permute-done.10.rest_2_ = bf16[16,5248]{1,0:T(8,128)(2,1)S(1)} collective-permute-done((bf16[16,5248]{1,0:T(8,128)(2,1)S(1)}, bf16[16,5248]{1,0:T(8,128)(2,1)S(1)}, u32[]{:S(2)}, u32[]{:S(2)}) %collective-permute-start.10) | collective-permute-done | bytes 167968 | tf_op jit(solution)/shard_map/ppermute | solution.py:64
  90.3 2.7 %collective-permute-done.8.rest_0_ = bf16[16,5248]{1,0:T(8,128)(2,1)S(1)} collective-permute-done((bf16[16,5248]{1,0:T(8,128)(2,1)S(1)}, bf16[16,5248]{1,0:T(8,128)(2,1)S(1)}, u32[]{:S(2)}, u32[]{:S(2)}) %collective-permute-start.8) | collective-permute-done | bytes 167968 | tf_op jit(solution)/shard_map/ppermute | solution.py:64
  93.1 1.5 %collective-permute-done.9.rest_1_ = bf16[16,5248]{1,0:T(8,128)(2,1)S(1)} collective-permute-done((bf16[16,5248]{1,0:T(8,128)(2,1)S(1)}, bf16[16,5248]{1,0:T(8,128)(2,1)S(1)}, u32[]{:S(2)}, u32[]{:S(2)}) %collective-permute-start.9) | collective-permute-done | bytes 167968 | tf_op jit(solution)/shard_map/ppermute | solution.py:64
  94.6 1.0 shard_map.142
  95.7 1.9 %collective-permute-start.12 = (bf16[16,1152]{1,0:T(8,128)(2,1)S(1)}, bf16[16,1152]{1,0:T(8,128)(2,1)S(1)}, u32[]{:S(2)}, u32[]{:S(2)}) collective-permute-start(bf16[16,1152]{1,0:T(8,128)(2,1)S(1)} %get-tuple-element.87), channel_id=1, source_target_pairs={{0,4},{1,5},{2,6},{3,7},{4,0},{5,1},{6,2},{7,3},{8,12},{9,13},{10,... | collective-permute-start | bytes 110600 | tf_op jit(solution)/shard_map/ppermute | solution.py:64
  97.6 1.3 collective-permute-start.13
  99.0 1.4 collective-permute-done.11.rest_0_
  102.1 1.5 %collective-permute-start.15 = (bf16[16,1152]{1,0:T(8,128)(2,1)S(1)}, bf16[16,1152]{1,0:T(8,128)(2,1)S(1)}, u32[]{:S(2)}, u32[]{:S(2)}) collective-permute-start(bf16[16,1152]{1,0:T(8,128)(2,1)S(1)} %shard_map.143.refs_0_), channel_id=1, source_target_pairs={{0,16},{8,24},{16,0},{24,8},{1,17},{9,25},{17,1},{25,9},{2,18},{10... | collective-permute-start | bytes 110600 | tf_op jit(solution)/shard_map/ppermute | solution.py:64
  103.7 1.2 collective-permute-start.16
  105.1 2.3 %collective-permute-done.16.refs_3_ = bf16[16,1152]{1,0:T(8,128)(2,1)S(1)} collective-permute-done((bf16[16,1152]{1,0:T(8,128)(2,1)S(1)}, bf16[16,1152]{1,0:T(8,128)(2,1)S(1)}, u32[]{:S(2)}, u32[]{:S(2)}) %collective-permute-start.16) | collective-permute-done | bytes 36896 | tf_op jit(solution)/shard_map/ppermute | solution.py:64
  107.4 2.2 %copy-done = bf16[2048,1024]{1,0:T(8,128)(2,1)S(1)} copy-done((bf16[2048,1024]{1,0:T(8,128)(2,1)S(1)}, bf16[2048,1024]{1,0:T(8,128)(2,1)}, u32[]{:S(2)}) %copy-start) | copy-done | bytes 4194328
  109.6 2.9 %shard_map.144 = (bf16[64,1024]{1,0:T(8,128)(2,1)}, f32[1,1]{1,0:T(1,128)}, f32[64,1024]{1,0:T(8,128)S(1)}, bf16[64,1024]{1,0:T(8,128)(2,1)S(1)}) custom-call(s32[5]{0:T(128)S(1)} %stack.53.place, bf16[16,1152]{1,0:T(8,128)(2,1)S(1)} %shard_map.143.refs_0_, bf16[16,1152]{1,0:T(8,128)(2,1)S(1)} %collective-permute-done.14.refs_1_, ...), custom_call_target="tpu_custom_call" | custom-call | tf_op jit(solution)/shard_map/pallas_call | solution.py:755
  112.5 4.9 %collective-permute-start.17 = (bf16[64,1024]{1,0:T(8,128)(2,1)S(1)}, bf16[64,1024]{1,0:T(8,128)(2,1)S(1)}, u32[]{:S(2)}, u32[]{:S(2)}) collective-permute-start(bf16[64,1024]{1,0:T(8,128)(2,1)S(1)} %get-tuple-element.91), channel_id=1, source_target_pairs={{0,1},{1,0},{2,3},{3,2},{4,5},{5,4},{6,7},{7,6},{8,9},{9,8},{10,11... | collective-permute-start | bytes 393224 | tf_op jit(solution)/shard_map/ppermute | solution.py:74
  119.0 2.8 %shard_map.146 = (f32[512,128]{1,0:T(8,128)S(1)}, f32[64,1024]{1,0:T(8,128)S(1)}, f32[512,128]{1,0:T(8,128)S(1)}) custom-call(s32[5]{0:T(128)S(1)} %stack.53.place, s32[1,1024]{1,0:T(1,128)S(1)} %add.63.key_pos, s32[64,1]{1,0:T(8,128)S(1)} %copy.19.query_pos, bf16[8,160,512]{2,1,0:T(8,128)(2,1)S(1)} %bitcast.22), custom_call_target="tpu_custom_call" | custom-call | flops 1610612736 | bytes 1310720 | tf_op jit(solution)/shard_map/pallas_call | solution.py:719
  121.8 1.3 collective-permute-done.18.refs_0_
  124.3 2.8 %shard_map.148 = (f32[512,128]{1,0:T(8,128)S(1)}, f32[64,1024]{1,0:T(8,128)S(1)}, f32[512,128]{1,0:T(8,128)S(1)}) custom-call(s32[5]{0:T(128)S(1)} %stack.53.place, s32[1,1024]{1,0:T(1,128)S(1)} %add.63.key_pos, s32[64,1]{1,0:T(8,128)S(1)} %copy.20.query_pos, bf16[8,160,512]{2,1,0:T(8,128)(2,1)S(1)} %bitcast.23), custom_call_target="tpu_custom_call" | custom-call | flops 1610612736 | bytes 1310720 | tf_op jit(solution)/shard_map/pallas_call | solution.py:719
  127.1 5.2 %collective-permute-done.19.refs_0_ = bf16[64,1024]{1,0:T(8,128)(2,1)S(1)} collective-permute-done((bf16[64,1024]{1,0:T(8,128)(2,1)S(1)}, bf16[64,1024]{1,0:T(8,128)(2,1)S(1)}, u32[]{:S(2)}, u32[]{:S(2)}) %collective-permute-start.19) | collective-permute-done | bytes 131104 | tf_op jit(solution)/shard_map/ppermute | solution.py:69
  134.0 2.3 %shard_map.150 = (bf16[8,2048]{1,0:T(8,128)(2,1)}, bf16[128,256]{1,0:T(8,128)(2,1)}, bf16[128,256]{1,0:T(8,128)(2,1)}) custom-call(s32[5]{0:T(128)S(1)} %stack.53.place, bf16[64,1024]{1,0:T(8,128)(2,1)S(1)} %shard_map.149.half, bf16[64,1024]{1,0:T(8,128)(2,1)S(1)} %collective-permute-done.20.other, bf16[8,160,512]{2,1,0:T(8,128)(2,1)S(1)} %bitcast.24, ...), custom_call_target="tpu_custom_call" | custom-call | tf_op jit(solution)/shard_map/pallas_call | solution.py:784
  (68 shorter events, 12.5 us)
Async XLA Ops:
  7.2 72.5 %reduce-scatter.2.cloned.1.call-start = ((), (), s32[]{:S(2)}) async-start(), calls=%async_computation.1 | async-start | bytes 1179648 | tf_op jit(solution)/shard_map/reduce_scatter | solution.py:654
  9.8 4.7 %collective-permute-start = (bf16[16,1024]{1,0:T(8,128)(2,1)S(1)}, bf16[16,1024]{1,0:T(8,128)(2,1)S(1)}, u32[]{:S(2)}, u32[]{:S(2)}) collective-permute-start(bf16[16,1024]{1,0:T(8,128)(2,1)S(1)} %shard_map.137), channel_id=1, source_target_pairs={{0,2},{1,3},{2,4},{3,5},{4,6},{5,7},{6,0},{7,1},{8,10},{9,11},{10,... | collective-permute-start | bytes 98312 | tf_op jit(solution)/shard_map/ppermute | solution.py:64
  11.2 3.7 %collective-permute-start.1 = (bf16[16,1024]{1,0:T(8,128)(2,1)S(1)}, bf16[16,1024]{1,0:T(8,128)(2,1)S(1)}, u32[]{:S(2)}, u32[]{:S(2)}) collective-permute-start(bf16[16,1024]{1,0:T(8,128)(2,1)S(1)} %shard_map.137), channel_id=1, source_target_pairs={{0,4},{1,5},{2,6},{3,7},{4,0},{5,1},{6,2},{7,3},{8,12},{9,13},{10,... | collective-permute-start | bytes 98312 | tf_op jit(solution)/shard_map/ppermute | solution.py:64
  13.5 3.4 %collective-permute-start.2 = (bf16[16,1024]{1,0:T(8,128)(2,1)S(1)}, bf16[16,1024]{1,0:T(8,128)(2,1)S(1)}, u32[]{:S(2)}, u32[]{:S(2)}) collective-permute-start(bf16[16,1024]{1,0:T(8,128)(2,1)S(1)} %shard_map.137), channel_id=1, source_target_pairs={{0,6},{1,7},{2,0},{3,1},{4,2},{5,3},{6,4},{7,5},{8,14},{9,15},{10,... | collective-permute-start | bytes 98312 | tf_op jit(solution)/shard_map/ppermute | solution.py:64
  16.9 5.7 %collective-permute-start.3 = (bf16[4,16,1024]{2,1,0:T(8,128)(2,1)S(1)}, bf16[4,16,1024]{2,1,0:T(8,128)(2,1)S(1)}, u32[]{:S(2)}, u32[]{:S(2)}) collective-permute-start(bf16[4,16,1024]{2,1,0:T(8,128)(2,1)S(1)} %pad_maximum_fusion.1), channel_id=1, source_target_pairs={{0,8},{8,16},{16,24},{24,0},{1,9},{9,17},{17,25},{25,1},{2,10},{10... | collective-permute-start | bytes 393224 | tf_op jit(solution)/shard_map/ppermute | solution.py:64
  18.1 5.3 %collective-permute-start.4 = (bf16[4,16,1024]{2,1,0:T(8,128)(2,1)S(1)}, bf16[4,16,1024]{2,1,0:T(8,128)(2,1)S(1)}, u32[]{:S(2)}, u32[]{:S(2)}) collective-permute-start(bf16[4,16,1024]{2,1,0:T(8,128)(2,1)S(1)} %pad_maximum_fusion.1), channel_id=1, source_target_pairs={{0,16},{8,24},{16,0},{24,8},{1,17},{9,25},{17,1},{25,9},{2,18},{10... | collective-permute-start | bytes 393224 | tf_op jit(solution)/shard_map/ppermute | solution.py:64
  18.3 5.2 %collective-permute-start.5 = (bf16[4,16,1024]{2,1,0:T(8,128)(2,1)S(1)}, bf16[4,16,1024]{2,1,0:T(8,128)(2,1)S(1)}, u32[]{:S(2)}, u32[]{:S(2)}) collective-permute-start(bf16[4,16,1024]{2,1,0:T(8,128)(2,1)S(1)} %pad_maximum_fusion.1), channel_id=1, source_target_pairs={{0,24},{8,0},{16,8},{24,16},{1,25},{9,1},{17,9},{25,17},{2,26},{10... | collective-permute-start | bytes 393224 | tf_op jit(solution)/shard_map/ppermute | solution.py:64
  20.3 7.7 %copy-start.11 = (s32[64]{0:T(128)S(1)}, s32[64]{0:T(128)}, u32[]{:S(2)}) copy-start(s32[64]{0:T(128)} %param.13) | copy-start | bytes 772
  20.3 7.8 %copy-start.2 = (bf16[128,2048]{1,0:T(8,128)(2,1)S(1)}, bf16[128,2048]{1,0:T(8,128)(2,1)}, u32[]{:S(2)}) copy-start(bf16[128,2048]{1,0:T(8,128)(2,1)} %queries) | copy-start | bytes 1572868
  20.3 7.8 %copy-start.5 = (bf16[128,256]{1,0:T(8,128)(2,1)S(1)}, bf16[128,256]{1,0:T(8,128)(2,1)}, u32[]{:S(2)}) copy-start(bf16[128,256]{1,0:T(8,128)(2,1)} %keys.1) | copy-start | bytes 196612
  20.3 7.8 %copy-start.6 = (bf16[128,256]{1,0:T(8,128)(2,1)S(1)}, bf16[128,256]{1,0:T(8,128)(2,1)}, u32[]{:S(2)}) copy-start(bf16[128,256]{1,0:T(8,128)(2,1)} %values.1) | copy-start | bytes 196612
  20.3 7.8 %copy-start.9 = (s32[64]{0:T(128)S(1)}, s32[64]{0:T(128)}, u32[]{:S(2)}) copy-start(s32[64]{0:T(128)} %rows.3) | copy-start | bytes 772
  20.3 9.3 %copy-start.7 = (f32[8192]{0:T(1024)S(1)}, f32[8192]{0:T(1024)}, u32[]{:S(2)}) copy-start(f32[8192]{0:T(1024)} %param.11) | copy-start | bytes 98308
  23.6 63.0 %all-gather.3.cloned.1.call-start = ((), (), s32[]{:S(2)}) async-start(), calls=%async_computation.2 | async-start | bytes 1474560 | tf_op jit(solution)/shard_map/all_gather | solution.py:658
  23.7 5.8 %collective-permute-start.6 = (bf16[4,4,16,1024]{3,2,1,0:T(8,128)(2,1)S(1)}, bf16[4,4,16,1024]{3,2,1,0:T(8,128)(2,1)S(1)}, u32[]{:S(2)}, u32[]{:S(2)}) collective-permute-start(bf16[4,4,16,1024]{3,2,1,0:T(8,128)(2,1)S(1)} %pad_maximum_fusion.own), channel_id=1, source_target_pairs={{0,1},{1,0},{2,3},{3,2},{4,5},{5,4},{6,7},{7,6},{8,9},{9,8},{10,11... | collective-permute-start | bytes 1572872 | tf_op jit(solution)/shard_map/ppermute | solution.py:74
  29.6 50.5 %copy-start.12 = (s32[16]{0:T(128)S(1)}, s32[16]{0:T(128)}, u32[]{:S(2)}) copy-start(s32[16]{0:T(128)} %param.15) | copy-start | bytes 196
  79.7 2.0 %collective-permute-start.7 = (bf16[64,4224]{1,0:T(8,128)(2,1)S(1)}, bf16[64,4224]{1,0:T(8,128)(2,1)S(1)}, u32[]{:S(2)}, u32[]{:S(2)}) collective-permute-start(bf16[64,4224]{1,0:T(8,128)(2,1)S(1)} %get-tuple-element.71), channel_id=1, source_target_pairs={{0,1},{1,0},{2,3},{3,2},{4,5},{5,4},{6,7},{7,6},{8,9},{9,8},{10,11... | collective-permute-start | bytes 1622024 | tf_op jit(solution)/shard_map/ppermute | solution.py:74
  83.9 6.5 %collective-permute-start.10 = (bf16[16,5248]{1,0:T(8,128)(2,1)S(1)}, bf16[16,5248]{1,0:T(8,128)(2,1)S(1)}, u32[]{:S(2)}, u32[]{:S(2)}) collective-permute-start(bf16[16,5248]{1,0:T(8,128)(2,1)S(1)} %get-tuple-element.81), channel_id=1, source_target_pairs={{0,24},{8,0},{16,8},{24,16},{1,25},{9,1},{17,9},{25,17},{2,26},{10... | collective-permute-start | bytes 503816 | tf_op jit(solution)/shard_map/ppermute | solution.py:64
  84.1 9.0 %collective-permute-start.8 = (bf16[16,5248]{1,0:T(8,128)(2,1)S(1)}, bf16[16,5248]{1,0:T(8,128)(2,1)S(1)}, u32[]{:S(2)}, u32[]{:S(2)}) collective-permute-start(bf16[16,5248]{1,0:T(8,128)(2,1)S(1)} %get-tuple-element.79), channel_id=1, source_target_pairs={{0,8},{8,16},{16,24},{24,0},{1,9},{9,17},{17,25},{25,1},{2,10},{10... | collective-permute-start | bytes 503816 | tf_op jit(solution)/shard_map/ppermute | solution.py:64
  86.3 8.3 %collective-permute-start.9 = (bf16[16,5248]{1,0:T(8,128)(2,1)S(1)}, bf16[16,5248]{1,0:T(8,128)(2,1)S(1)}, u32[]{:S(2)}, u32[]{:S(2)}) collective-permute-start(bf16[16,5248]{1,0:T(8,128)(2,1)S(1)} %get-tuple-element.80), channel_id=1, source_target_pairs={{0,16},{8,24},{16,0},{24,8},{1,17},{9,25},{17,1},{25,9},{2,18},{10... | collective-permute-start | bytes 503816 | tf_op jit(solution)/shard_map/ppermute | solution.py:64
  95.7 4.7 %collective-permute-start.11 = (bf16[16,1152]{1,0:T(8,128)(2,1)S(1)}, bf16[16,1152]{1,0:T(8,128)(2,1)S(1)}, u32[]{:S(2)}, u32[]{:S(2)}) collective-permute-start(bf16[16,1152]{1,0:T(8,128)(2,1)S(1)} %get-tuple-element.86), channel_id=1, source_target_pairs={{0,2},{1,3},{2,4},{3,5},{4,6},{5,7},{6,0},{7,1},{8,10},{9,11},{10,... | collective-permute-start | bytes 110600 | tf_op jit(solution)/shard_map/ppermute | solution.py:64
  95.7 4.6 %collective-permute-start.12 = (bf16[16,1152]{1,0:T(8,128)(2,1)S(1)}, bf16[16,1152]{1,0:T(8,128)(2,1)S(1)}, u32[]{:S(2)}, u32[]{:S(2)}) collective-permute-start(bf16[16,1152]{1,0:T(8,128)(2,1)S(1)} %get-tuple-element.87), channel_id=1, source_target_pairs={{0,4},{1,5},{2,6},{3,7},{4,0},{5,1},{6,2},{7,3},{8,12},{9,13},{10,... | collective-permute-start | bytes 110600 | tf_op jit(solution)/shard_map/ppermute | solution.py:64
  97.6 3.4 %collective-permute-start.13 = (bf16[16,1152]{1,0:T(8,128)(2,1)S(1)}, bf16[16,1152]{1,0:T(8,128)(2,1)S(1)}, u32[]{:S(2)}, u32[]{:S(2)}) collective-permute-start(bf16[16,1152]{1,0:T(8,128)(2,1)S(1)} %get-tuple-element.88), channel_id=1, source_target_pairs={{0,6},{1,7},{2,0},{3,1},{4,2},{5,3},{6,4},{7,5},{8,14},{9,15},{10,... | collective-permute-start | bytes 110600 | tf_op jit(solution)/shard_map/ppermute | solution.py:64
  102.0 3.1 %collective-permute-start.14 = (bf16[16,1152]{1,0:T(8,128)(2,1)S(1)}, bf16[16,1152]{1,0:T(8,128)(2,1)S(1)}, u32[]{:S(2)}, u32[]{:S(2)}) collective-permute-start(bf16[16,1152]{1,0:T(8,128)(2,1)S(1)} %shard_map.143.refs_0_), channel_id=1, source_target_pairs={{0,8},{8,16},{16,24},{24,0},{1,9},{9,17},{17,25},{25,1},{2,10},{10... | collective-permute-start | bytes 110600 | tf_op jit(solution)/shard_map/ppermute | solution.py:64
  102.1 2.9 %collective-permute-start.15 = (bf16[16,1152]{1,0:T(8,128)(2,1)S(1)}, bf16[16,1152]{1,0:T(8,128)(2,1)S(1)}, u32[]{:S(2)}, u32[]{:S(2)}) collective-permute-start(bf16[16,1152]{1,0:T(8,128)(2,1)S(1)} %shard_map.143.refs_0_), channel_id=1, source_target_pairs={{0,16},{8,24},{16,0},{24,8},{1,17},{9,25},{17,1},{25,9},{2,18},{10... | collective-permute-start | bytes 110600 | tf_op jit(solution)/shard_map/ppermute | solution.py:64
  103.7 3.7 %collective-permute-start.16 = (bf16[16,1152]{1,0:T(8,128)(2,1)S(1)}, bf16[16,1152]{1,0:T(8,128)(2,1)S(1)}, u32[]{:S(2)}, u32[]{:S(2)}) collective-permute-start(bf16[16,1152]{1,0:T(8,128)(2,1)S(1)} %shard_map.143.refs_0_), channel_id=1, source_target_pairs={{0,24},{8,0},{16,8},{24,16},{1,25},{9,1},{17,9},{25,17},{2,26},{10... | collective-permute-start | bytes 110600 | tf_op jit(solution)/shard_map/ppermute | solution.py:64
  107.4 2.2 %copy-start = (bf16[2048,1024]{1,0:T(8,128)(2,1)S(1)}, bf16[2048,1024]{1,0:T(8,128)(2,1)}, u32[]{:S(2)}) copy-start(bf16[2048,1024]{1,0:T(8,128)(2,1)} %refs_4_.1) | copy-start | bytes 12582916
  109.6 9.5 %copy-start.1 = (bf16[1280,512]{1,0:T(8,128)(2,1)S(1)}, bf16[1280,512]{1,0:T(8,128)(2,1)}, u32[]{:S(2)}) copy-start(bf16[1280,512]{1,0:T(8,128)(2,1)} %all-gather.3.cloned.1.call-done) | copy-start | bytes 3932164
  112.5 5.8 %collective-permute-start.17 = (bf16[64,1024]{1,0:T(8,128)(2,1)S(1)}, bf16[64,1024]{1,0:T(8,128)(2,1)S(1)}, u32[]{:S(2)}, u32[]{:S(2)}) collective-permute-start(bf16[64,1024]{1,0:T(8,128)(2,1)S(1)} %get-tuple-element.91), channel_id=1, source_target_pairs={{0,1},{1,0},{2,3},{3,2},{4,5},{5,4},{6,7},{7,6},{8,9},{9,8},{10,11... | collective-permute-start | bytes 393224 | tf_op jit(solution)/shard_map/ppermute | solution.py:74
  118.4 4.8 %collective-permute-start.18 = (bf16[64,1024]{1,0:T(8,128)(2,1)S(1)}, bf16[64,1024]{1,0:T(8,128)(2,1)S(1)}, u32[]{:S(2)}, u32[]{:S(2)}) collective-permute-start(bf16[64,1024]{1,0:T(8,128)(2,1)S(1)} %shard_map.145.keep), channel_id=1, source_target_pairs={{0,2},{1,3},{2,0},{3,1},{4,6},{5,7},{6,4},{7,5},{8,10},{9,11},{10,... | collective-permute-start | bytes 393224 | tf_op jit(solution)/shard_map/ppermute | solution.py:69
  123.2 9.0 %collective-permute-start.19 = (bf16[64,1024]{1,0:T(8,128)(2,1)S(1)}, bf16[64,1024]{1,0:T(8,128)(2,1)S(1)}, u32[]{:S(2)}, u32[]{:S(2)}) collective-permute-start(bf16[64,1024]{1,0:T(8,128)(2,1)S(1)} %shard_map.147.keep), channel_id=1, source_target_pairs={{0,4},{1,5},{2,6},{3,7},{4,0},{5,1},{6,2},{7,3},{8,12},{9,13},{10,... | collective-permute-start | bytes 393224 | tf_op jit(solution)/shard_map/ppermute | solution.py:69
  132.3 1.7 %collective-permute-start.20 = (bf16[64,1024]{1,0:T(8,128)(2,1)S(1)}, bf16[64,1024]{1,0:T(8,128)(2,1)S(1)}, u32[]{:S(2)}, u32[]{:S(2)}) collective-permute-start(bf16[64,1024]{1,0:T(8,128)(2,1)S(1)} %shard_map.149.half), channel_id=1, source_target_pairs={{0,1},{1,0},{2,3},{3,2},{4,5},{5,4},{6,7},{7,6},{8,9},{9,8},{10,11... | collective-permute-start | bytes 393224 | tf_op jit(solution)/shard_map/ppermute | solution.py:74
  (4 other events, 3.3 us)
Sparse Core Ops, SparseCore 0:
  23.7 32.4 reduce-scatter.1
  57.8 25.0 all-gather.2

commit v6 on v5

--- a/solution.py
+++ b/solution.py
@@ -10,7 +10,7 @@
 HEAD_SIZE = 128
 CORES = 2
 CHUNK = 512
-SLOTS = 4
+SLOTS = 3
 LANES = 128
 
 norm_eps = 1e-06
@@ -160,7 +160,6 @@
     raw,
     acc,
     probs,
-    fresh,
     state,
     head_buf,
     buf,
@@ -187,8 +186,19 @@
         )
 
     head_copy().start()
-    for c in range(min(SLOTS, chunks)):
-        body_copy(c).start()
+    def half_copy(k):
+        piece = CHUNK // 2
+        return pltpu.make_async_copy(
+            weight.at[pl.ds(first + k * piece, piece), :],
+            buf.at[0, pl.ds(k * piece, piece), :],
+            (sems.at[0], sems.at[SLOTS])[k],
+        )
+
+    if chunks:
+        half_copy(0).start()
+        half_copy(1).start()
+        for c in range(1, min(SLOTS, chunks)):
+            body_copy(c).start()
 
     is_even = core_at == 0
     for zr in range(nz):
@@ -280,34 +290,40 @@
         def start_of(c):
             return first_id + first + c * CHUNK
 
-        body_copy(0).wait()
-        fresh[...] = scores_of(buf[0])
+        piece = CHUNK // 2
+        low, high = buf.at[0, pl.ds(0, piece), :], buf.at[0, pl.ds(piece, piece), :]
+        half_copy(0).wait()
+        scores = scores_of(low[...])
         add_product(p, None, lambda at, n: head_buf[:, at : at + n])
+        p, scale, run = softmax(scores, start_of(0), run)
+        half_copy(1).wait()
+        scores = scores_of(high[...])
+        add_product(p, scale, lambda at, n: low[:, at : at + n])
+        p, scale, run = softmax(scores, start_of(0) + piece, run)
         body_copy(1).wait()
         scores = scores_of(buf[1])
-        p, scale, run = softmax(fresh[...], start_of(0), run)
+        add_product(p, scale, lambda at, n: high[:, at : at + n])
+        p, scale, run = softmax(scores, start_of(1), run)
         probs[...] = p
-        fresh[...] = scores
+        if chunks > SLOTS:
+            body_copy(SLOTS).start()
 
         def step(c, carry):
             scale, run = carry
             body_copy(c).wait()
             scores = scores_of(buf[lax.rem(c, SLOTS)])
-            p, next_scale, run = softmax(fresh[...], start_of(c - 1), run)
-            add_product(probs[...], scale, part(buf, lax.rem(c - 2, SLOTS)))
+            add_product(probs[...], scale, part(buf, lax.rem(c - 1, SLOTS)))
+            p, scale, run = softmax(scores, start_of(c), run)
             probs[...] = p
-            fresh[...] = scores
 
             @pl.when(c + 2 < chunks)
             def _():
                 body_copy(c + 2).start()
 
-            return next_scale, run
+            return scale, run
 
         scale, run = lax.fori_loop(2, chunks, step, (scale, run))
-        p, next_scale, run = softmax(fresh[...], start_of(chunks - 1), run)
-        add_product(probs[...], scale, part(buf, (chunks - 2) % SLOTS))
-        add_product(p, next_scale, part(buf, (chunks - 1) % SLOTS))
+        add_product(probs[...], scale, part(buf, (chunks - 1) % SLOTS))
 
     for z in range(nz):
         keep[z] = acc[CORES * z + core_at]
@@ -615,6 +631,7 @@
         shape((2 * loss_per, part_width // 2), bf16),
         [smem(), smem(), hbm()],
         [pltpu.VMEM((tokens, part_width), bf16), pltpu.SemaphoreType.DMA],
+        limit=56,
     )(place, loss_rows, hidden)
     picked, queries, targets_late = lax.optimization_barrier((picked, queries, targets))
     extra = (query_width // (2 * key_width)) * loss_per
@@ -677,12 +694,11 @@
             pltpu.VMEM((loss, width), bf16),
             pltpu.VMEM((nc, loss, block_width), f32),
             pltpu.VMEM((loss, CHUNK), bf16),
-            pltpu.VMEM((loss, CHUNK), f32),
             pltpu.VMEM((loss, LANES), f32),
             pltpu.VMEM((first, width), bf16),
             pltpu.VMEM((SLOTS if chunks else 1, CHUNK if chunks else 16, width), bf16),
             pltpu.SemaphoreType.DMA,
-            pltpu.SemaphoreType.DMA((SLOTS,)),
+            pltpu.SemaphoreType.DMA((SLOTS + 1,)),
         ],
         compiler_params=pltpu.CompilerParams(vmem_limit_bytes=47 * 2**20),
         cost_estimate=pl.CostEstimate(
@@ -767,6 +783,7 @@
             pltpu.VMEM((4, query_width // 4, block_width), bf16),
             pltpu.SemaphoreType.DMA((4,)),
         ],
+        limit=52,
     )(place, *gathered, output_weight)
     half = call(sum_body, shape((loss, cols), bf16), [vmem()] * 2)(keep, swapped(send))
     windows = nz.bit_length() - 1

time: 143 us -> 144 us (level)
  waiting for transfers between devices: 25.8 us -> 22.9 us
  Pallas kernels: 68.7 us -> 71.4 us
    ppermute x2, waiting for transfers between devices: 6.51 us -> 3.65 us  [crossed(): lax.ppermute(value, 'ctx', [(i, i ^ bit * CORES) for i in range(size)])]
    ppermute x2, starting transfers between devices: 1.48 us -> 3.42 us  [crossed(): lax.ppermute(value, 'ctx', [(i, i ^ bit * CORES) for i in range(size)])]
    pallas_call x1, Pallas kernels: 2.29 us -> 4.05 us  [per_device(): pl.pallas_call(target_body, out_shape=shape((nc, loss, block_width), bf16...]
    pallas_call x1, Pallas kernels: 0.79 us -> 2.52 us  [per_device(): call(functools.partial(pick_body, loss_per), shape((2 * loss_per, part_wi...]
    pallas_call x1, Pallas kernels: 50.1 us -> 48.3 us  [per_device(): pl.pallas_call(functools.partial(flash_body, first), out_shape=(shape((nz...]
    unnamed x26 -> x28, local copies, waits for them, and re-layouts: 5.48 us -> 4.11 us
  transfers between devices with their start and end apart: 23 -> 23, of which waited for: 15 -> 17; matrix products, arithmetic and copies ran while one was open for 0% -> 0% of each run, Pallas kernels for 42% -> 42%
where the time goes in v6:
time: 144 us; the launch traced here: 143 us
  Pallas kernels  71.4 us (50%)
  starting transfers between devices  28.7 us (20%)
  waiting for transfers between devices  22.9 us (16%)
  between operations  14.3 us (10%)
  local copies, waits for them, and re-layouts  5.15 us (4%)
    pallas_call x1, Pallas kernels, per_device(): pl.pallas_call(functools.partial(flash_body, first), out_shape=(shape((nz...  48.3 us
    ppermute x15, starting transfers between devices, shifted(): return lax.ppermute(value, axis, pairs)  16 us
    ppermute x15, waiting for transfers between devices, shifted(): return lax.ppermute(value, axis, pairs)  15.6 us
    ppermute x4, starting transfers between devices, swapped(): return lax.ppermute(value, 'ctx', [(i, i ^ 1) for i in range(size)])  9.18 us
    pallas_call x2, Pallas kernels, forward(): call(functools.partial(forward_body, loss_per, heads, group, at_once, j),...  5.63 us
    unnamed x28, local copies, waits for them, and re-layouts  4.11 us
    pallas_call x1, Pallas kernels, per_device(): pl.pallas_call(target_body, out_shape=shape((nc, loss, block_width), bf16...  4.05 us
    pallas_call x1, Pallas kernels, per_device(): call(functools.partial(project_body, nv), (shape((loss, block_width), bf1...  3.81 us
  transfers between devices with their start and end apart: 23, of which 17 were waited for; matrix products, arithmetic and copies ran while one was open for 0% of the time, Pallas kernels for 42%

profile of v6, /device:TPU:3, one launch (start us, length us, event | category | flops | bytes accessed | tf_op | source)
XLA Modules:
  0.0 143.4 jit_solution(7550610773889889723)
XLA Ops:
  7.9 2.5 %shard_map.137 = bf16[16,1024]{1,0:T(8,128)(2,1)} custom-call(s32[5]{0:T(128)} %stack.53.place, s32[64]{0:T(128)} %rows.3, bf16[128,2048]{1,0:T(8,128)(2,1)} %hidden.1), custom_call_target="tpu_custom_call" | custom-call | tf_op jit(solution)/shard_map/pallas_call | solution.py:629
  10.4 1.3 collective-permute-start
  11.8 2.3 %collective-permute-start.1 = (bf16[16,1024]{1,0:T(8,128)(2,1)}, bf16[16,1024]{1,0:T(8,128)(2,1)S(1)}, u32[]{:S(2)}, u32[]{:S(2)}) collective-permute-start(bf16[16,1024]{1,0:T(8,128)(2,1)} %shard_map.137), channel_id=1, source_target_pairs={{0,4},{1,5},{2,6},{3,7},{4,0},{5,1},{6,2},{7,3},{8,12},{9,13},{10,... | collective-permute-start | bytes 98312 | tf_op jit(solution)/shard_map/ppermute | solution.py:64
  14.1 1.1 collective-permute-start.2
  15.7 2.0 %collective-permute-done.2 = bf16[16,1024]{1,0:T(8,128)(2,1)S(1)} collective-permute-done((bf16[16,1024]{1,0:T(8,128)(2,1)}, bf16[16,1024]{1,0:T(8,128)(2,1)S(1)}, u32[]{:S(2)}, u32[]{:S(2)}) %collective-permute-start.2) | collective-permute-done | bytes 32800 | tf_op jit(solution)/shard_map/ppermute | solution.py:64
  18.4 1.3 collective-permute-start.3
  19.9 1.3 collective-permute-start.5
  22.6 4.1 %shard_map.138 = bf16[8,64,1024]{2,1,0:T(8,128)(2,1)} custom-call(s32[5]{0:T(128)S(1)} %copy-done.5, s32[1,64]{1,0:T(1,128)S(1)} %bitcast.27, bf16[4752,8192]{1,0:T(8,128)(2,1)} %weight.3), custom_call_target="tpu_custom_call" | custom-call | bytes 16777216 | tf_op jit(solution)/shard_map/pallas_call | solution.py:653
  26.8 2.4 %collective-permute-start.6 = (bf16[4,4,16,1024]{3,2,1,0:T(8,128)(2,1)S(1)}, bf16[4,4,16,1024]{3,2,1,0:T(8,128)(2,1)S(1)}, u32[]{:S(2)}, u32[]{:S(2)}) collective-permute-start(bf16[4,4,16,1024]{3,2,1,0:T(8,128)(2,1)S(1)} %pad_maximum_fusion.own), channel_id=1, source_target_pairs={{0,1},{1,0},{2,3},{3,2},{4,5},{5,4},{6,7},{7,6},{8,9},{9,8},{10,11... | collective-permute-start | bytes 1572872 | tf_op jit(solution)/shard_map/ppermute | solution.py:74
  29.4 1.4 shard_map.139
  32.7 48.3 %shard_map.140 = (f32[4,64,1024]{2,1,0:T(8,128)S(1)}, bf16[64,4224]{1,0:T(8,128)(2,1)S(1)}, f32[64,128]{1,0:T(8,128)S(1)}, f32[16,1024]{1,0:T(8,128)S(1)}) custom-call(s32[5]{0:T(128)S(1)} %copy-done.6, bf16[4,4,16,1024]{3,2,1,0:T(8,128)(2,1)S(1)} %pad_maximum_fusion.own, bf16[4,4,16,1024]{3,2,1,0:T(8,128)(2,1)S(1)} %copy-done.12, f32[1,8192]{1,0:T(1,128)S(1)} %bitcast.25, ...), custom_call_target="tpu_custom_call" | custom-call | flops 39862665216 | bytes 155713536 | tf_op jit(solution)/shard_map/pallas_call | solution.py:682
  81.4 1.7 %collective-permute-done.7.got = bf16[64,4224]{1,0:T(8,128)(2,1)S(1)} collective-permute-done((bf16[64,4224]{1,0:T(8,128)(2,1)S(1)}, bf16[64,4224]{1,0:T(8,128)(2,1)S(1)}, u32[]{:S(2)}, u32[]{:S(2)}) %collective-permute-start.7) | collective-permute-done | bytes 540704 | tf_op jit(solution)/shard_map/ppermute | solution.py:74
  84.0 1.3 shard_map.141
  85.3 1.4 collective-permute-start.10
  86.6 1.1 collective-permute-start.8
  88.3 3.5 %collective-permute-done.10.rest_2_ = bf16[16,5248]{1,0:T(8,128)(2,1)S(1)} collective-permute-done((bf16[16,5248]{1,0:T(8,128)(2,1)S(1)}, bf16[16,5248]{1,0:T(8,128)(2,1)S(1)}, u32[]{:S(2)}, u32[]{:S(2)}) %collective-permute-start.10) | collective-permute-done | bytes 167968 | tf_op jit(solution)/shard_map/ppermute | solution.py:64
  91.8 2.9 %collective-permute-done.8.rest_0_ = bf16[16,5248]{1,0:T(8,128)(2,1)S(1)} collective-permute-done((bf16[16,5248]{1,0:T(8,128)(2,1)S(1)}, bf16[16,5248]{1,0:T(8,128)(2,1)S(1)}, u32[]{:S(2)}, u32[]{:S(2)}) %collective-permute-start.8) | collective-permute-done | bytes 167968 | tf_op jit(solution)/shard_map/ppermute | solution.py:64
  94.8 1.2 collective-permute-done.9.rest_1_
  97.3 2.9 %collective-permute-start.12 = (bf16[16,1152]{1,0:T(8,128)(2,1)S(1)}, bf16[16,1152]{1,0:T(8,128)(2,1)S(1)}, u32[]{:S(2)}, u32[]{:S(2)}) collective-permute-start(bf16[16,1152]{1,0:T(8,128)(2,1)S(1)} %get-tuple-element.87), channel_id=1, source_target_pairs={{0,4},{1,5},{2,6},{3,7},{4,0},{5,1},{6,2},{7,3},{8,12},{9,13},{10,... | collective-permute-start | bytes 110600 | tf_op jit(solution)/shard_map/ppermute | solution.py:64
  100.6 1.2 collective-permute-done.11.rest_0_
  101.8 1.3 collective-permute-done.12.rest_1_
  105.3 1.3 collective-permute-start.16
  107.5 1.5 %collective-permute-done.16.refs_3_ = bf16[16,1152]{1,0:T(8,128)(2,1)S(1)} collective-permute-done((bf16[16,1152]{1,0:T(8,128)(2,1)S(1)}, bf16[16,1152]{1,0:T(8,128)(2,1)S(1)}, u32[]{:S(2)}, u32[]{:S(2)}) %collective-permute-start.16) | collective-permute-done | bytes 36896 | tf_op jit(solution)/shard_map/ppermute | solution.py:64
  109.0 3.8 %shard_map.144 = (bf16[64,1024]{1,0:T(8,128)(2,1)}, f32[1,1]{1,0:T(1,128)}, f32[64,1024]{1,0:T(8,128)S(1)}, bf16[64,1024]{1,0:T(8,128)(2,1)S(1)}) custom-call(s32[5]{0:T(128)S(1)} %copy-done.6, bf16[16,1152]{1,0:T(8,128)(2,1)S(1)} %shard_map.143.refs_0_, bf16[16,1152]{1,0:T(8,128)(2,1)S(1)} %collective-permute-done.14.refs_1_, ...), custom_call_target="tpu_custom_call" | custom-call | tf_op jit(solution)/shard_map/pallas_call | solution.py:771
  112.8 4.6 %collective-permute-start.17 = (bf16[64,1024]{1,0:T(8,128)(2,1)S(1)}, bf16[64,1024]{1,0:T(8,128)(2,1)S(1)}, u32[]{:S(2)}, u32[]{:S(2)}) collective-permute-start(bf16[64,1024]{1,0:T(8,128)(2,1)S(1)} %get-tuple-element.91), channel_id=1, source_target_pairs={{0,1},{1,0},{2,3},{3,2},{4,5},{5,4},{6,7},{7,6},{8,9},{9,8},{10,11... | collective-permute-start | bytes 393224 | tf_op jit(solution)/shard_map/ppermute | solution.py:74
  118.5 1.6 %collective-permute-start.18 = (bf16[64,1024]{1,0:T(8,128)(2,1)S(1)}, bf16[64,1024]{1,0:T(8,128)(2,1)S(1)}, u32[]{:S(2)}, u32[]{:S(2)}) collective-permute-start(bf16[64,1024]{1,0:T(8,128)(2,1)S(1)} %shard_map.145.keep), channel_id=1, source_target_pairs={{0,2},{1,3},{2,0},{3,1},{4,6},{5,7},{6,4},{7,5},{8,10},{9,11},{10,... | collective-permute-start | bytes 393224 | tf_op jit(solution)/shard_map/ppermute | solution.py:69
  120.2 2.8 %shard_map.146 = (f32[512,128]{1,0:T(8,128)S(1)}, f32[64,1024]{1,0:T(8,128)S(1)}, f32[512,128]{1,0:T(8,128)S(1)}) custom-call(s32[5]{0:T(128)S(1)} %copy-done.6, s32[1,1024]{1,0:T(1,128)S(1)} %add.63.key_pos, s32[64,1]{1,0:T(8,128)S(1)} %copy.19.query_pos, bf16[8,160,512]{2,1,0:T(8,128)(2,1)S(1)} %bitcast.22), custom_call_target="tpu_custom_call" | custom-call | flops 1610612736 | bytes 1310720 | tf_op jit(solution)/shard_map/pallas_call | solution.py:735
  123.4 1.8 %collective-permute-start.19 = (bf16[64,1024]{1,0:T(8,128)(2,1)S(1)}, bf16[64,1024]{1,0:T(8,128)(2,1)S(1)}, u32[]{:S(2)}, u32[]{:S(2)}) collective-permute-start(bf16[64,1024]{1,0:T(8,128)(2,1)S(1)} %shard_map.147.keep), channel_id=1, source_target_pairs={{0,4},{1,5},{2,6},{3,7},{4,0},{5,1},{6,2},{7,3},{8,12},{9,13},{10,... | collective-permute-start | bytes 393224 | tf_op jit(solution)/shard_map/ppermute | solution.py:69
  125.4 2.8 %shard_map.148 = (f32[512,128]{1,0:T(8,128)S(1)}, f32[64,1024]{1,0:T(8,128)S(1)}, f32[512,128]{1,0:T(8,128)S(1)}) custom-call(s32[5]{0:T(128)S(1)} %copy-done.6, s32[1,1024]{1,0:T(1,128)S(1)} %add.63.key_pos, s32[64,1]{1,0:T(8,128)S(1)} %copy.20.query_pos, bf16[8,160,512]{2,1,0:T(8,128)(2,1)S(1)} %bitcast.23), custom_call_target="tpu_custom_call" | custom-call | flops 1610612736 | bytes 1310720 | tf_op jit(solution)/shard_map/pallas_call | solution.py:735
  128.2 3.3 %collective-permute-done.19.refs_0_ = bf16[64,1024]{1,0:T(8,128)(2,1)S(1)} collective-permute-done((bf16[64,1024]{1,0:T(8,128)(2,1)S(1)}, bf16[64,1024]{1,0:T(8,128)(2,1)S(1)}, u32[]{:S(2)}, u32[]{:S(2)}) %collective-permute-start.19) | collective-permute-done | bytes 131104 | tf_op jit(solution)/shard_map/ppermute | solution.py:69
  131.5 1.7 %collective-permute-start.20 = (bf16[64,1024]{1,0:T(8,128)(2,1)S(1)}, bf16[64,1024]{1,0:T(8,128)(2,1)S(1)}, u32[]{:S(2)}, u32[]{:S(2)}) collective-permute-start(bf16[64,1024]{1,0:T(8,128)(2,1)S(1)} %shard_map.149.half), channel_id=1, source_target_pairs={{0,1},{1,0},{2,3},{3,2},{4,5},{5,4},{6,7},{7,6},{8,9},{9,8},{10,11... | collective-permute-start | bytes 393224 | tf_op jit(solution)/shard_map/ppermute | solution.py:74
  134.2 2.3 %shard_map.150 = (bf16[8,2048]{1,0:T(8,128)(2,1)}, bf16[128,256]{1,0:T(8,128)(2,1)}, bf16[128,256]{1,0:T(8,128)(2,1)}) custom-call(s32[5]{0:T(128)S(1)} %copy-done.6, bf16[64,1024]{1,0:T(8,128)(2,1)S(1)} %shard_map.149.half, bf16[64,1024]{1,0:T(8,128)(2,1)S(1)} %collective-permute-done.20.other, bf16[8,160,512]{2,1,0:T(8,128)(2,1)S(1)} %bitcast.24, ...), custom_call_target="tpu_custom_call" | custom-call | tf_op jit(solution)/shard_map/pallas_call | solution.py:801
  (70 shorter events, 14.9 us)
Async XLA Ops:
  7.2 73.9 %reduce-scatter.2.cloned.1.call-start = ((), (), s32[]{:S(2)}) async-start(), calls=%async_computation.1 | async-start | bytes 1179648 | tf_op jit(solution)/shard_map/reduce_scatter | solution.py:671
  10.4 4.9 %collective-permute-start = (bf16[16,1024]{1,0:T(8,128)(2,1)}, bf16[16,1024]{1,0:T(8,128)(2,1)S(1)}, u32[]{:S(2)}, u32[]{:S(2)}) collective-permute-start(bf16[16,1024]{1,0:T(8,128)(2,1)} %shard_map.137), channel_id=1, source_target_pairs={{0,2},{1,3},{2,4},{3,5},{4,6},{5,7},{6,0},{7,1},{8,10},{9,11},{10,... | collective-permute-start | bytes 98312 | tf_op jit(solution)/shard_map/ppermute | solution.py:64
  11.8 3.9 %collective-permute-start.1 = (bf16[16,1024]{1,0:T(8,128)(2,1)}, bf16[16,1024]{1,0:T(8,128)(2,1)S(1)}, u32[]{:S(2)}, u32[]{:S(2)}) collective-permute-start(bf16[16,1024]{1,0:T(8,128)(2,1)} %shard_map.137), channel_id=1, source_target_pairs={{0,4},{1,5},{2,6},{3,7},{4,0},{5,1},{6,2},{7,3},{8,12},{9,13},{10,... | collective-permute-start | bytes 98312 | tf_op jit(solution)/shard_map/ppermute | solution.py:64
  14.1 3.6 %collective-permute-start.2 = (bf16[16,1024]{1,0:T(8,128)(2,1)}, bf16[16,1024]{1,0:T(8,128)(2,1)S(1)}, u32[]{:S(2)}, u32[]{:S(2)}) collective-permute-start(bf16[16,1024]{1,0:T(8,128)(2,1)} %shard_map.137), channel_id=1, source_target_pairs={{0,6},{1,7},{2,0},{3,1},{4,2},{5,3},{6,4},{7,5},{8,14},{9,15},{10,... | collective-permute-start | bytes 98312 | tf_op jit(solution)/shard_map/ppermute | solution.py:64
  18.4 8.2 %collective-permute-start.3 = (bf16[4,16,1024]{2,1,0:T(8,128)(2,1)S(1)}, bf16[4,16,1024]{2,1,0:T(8,128)(2,1)S(1)}, u32[]{:S(2)}, u32[]{:S(2)}) collective-permute-start(bf16[4,16,1024]{2,1,0:T(8,128)(2,1)S(1)} %pad_maximum_fusion.1), channel_id=1, source_target_pairs={{0,8},{8,16},{16,24},{24,0},{1,9},{9,17},{17,25},{25,1},{2,10},{10... | collective-permute-start | bytes 393224 | tf_op jit(solution)/shard_map/ppermute | solution.py:64
  19.7 7.0 %collective-permute-start.4 = (bf16[4,16,1024]{2,1,0:T(8,128)(2,1)S(1)}, bf16[4,16,1024]{2,1,0:T(8,128)(2,1)S(1)}, u32[]{:S(2)}, u32[]{:S(2)}) collective-permute-start(bf16[4,16,1024]{2,1,0:T(8,128)(2,1)S(1)} %pad_maximum_fusion.1), channel_id=1, source_target_pairs={{0,16},{8,24},{16,0},{24,8},{1,17},{9,25},{17,1},{25,9},{2,18},{10... | collective-permute-start | bytes 393224 | tf_op jit(solution)/shard_map/ppermute | solution.py:64
  19.9 6.7 %collective-permute-start.5 = (bf16[4,16,1024]{2,1,0:T(8,128)(2,1)S(1)}, bf16[4,16,1024]{2,1,0:T(8,128)(2,1)S(1)}, u32[]{:S(2)}, u32[]{:S(2)}) collective-permute-start(bf16[4,16,1024]{2,1,0:T(8,128)(2,1)S(1)} %pad_maximum_fusion.1), channel_id=1, source_target_pairs={{0,24},{8,0},{16,8},{24,16},{1,25},{9,1},{17,9},{25,17},{2,26},{10... | collective-permute-start | bytes 393224 | tf_op jit(solution)/shard_map/ppermute | solution.py:64
  22.5 6.7 %copy-start.10 = (s32[64]{0:T(128)S(1)}, s32[64]{0:T(128)}, u32[]{:S(2)}) copy-start(s32[64]{0:T(128)} %param.13) | copy-start | bytes 772
  22.5 6.8 %copy-start.1 = (bf16[128,2048]{1,0:T(8,128)(2,1)S(1)}, bf16[128,2048]{1,0:T(8,128)(2,1)}, u32[]{:S(2)}) copy-start(bf16[128,2048]{1,0:T(8,128)(2,1)} %queries) | copy-start | bytes 1572868
  22.5 6.8 %copy-start.3 = (bf16[128,256]{1,0:T(8,128)(2,1)S(1)}, bf16[128,256]{1,0:T(8,128)(2,1)}, u32[]{:S(2)}) copy-start(bf16[128,256]{1,0:T(8,128)(2,1)} %keys.1) | copy-start | bytes 196612
  22.5 6.8 %copy-start.4 = (bf16[128,256]{1,0:T(8,128)(2,1)S(1)}, bf16[128,256]{1,0:T(8,128)(2,1)}, u32[]{:S(2)}) copy-start(bf16[128,256]{1,0:T(8,128)(2,1)} %values.1) | copy-start | bytes 196612
  22.6 6.8 %copy-start.6 = (s32[5]{0:T(128)S(1)}, s32[5]{0:T(128)}, u32[]{:S(2)}) copy-start(s32[5]{0:T(128)} %stack.53.place) | copy-start | bytes 64
  22.6 6.8 %copy-start.8 = (s32[64]{0:T(128)S(1)}, s32[64]{0:T(128)}, u32[]{:S(2)}) copy-start(s32[64]{0:T(128)} %rows.3) | copy-start | bytes 772
  22.6 9.1 %copy-start.7 = (f32[8192]{0:T(1024)S(1)}, f32[8192]{0:T(1024)}, u32[]{:S(2)}) copy-start(f32[8192]{0:T(1024)} %param.11) | copy-start | bytes 98308
  26.7 61.6 %all-gather.3.cloned.1.call-start = ((), (), s32[]{:S(2)}) async-start(), calls=%async_computation.2 | async-start | bytes 1474560 | tf_op jit(solution)/shard_map/all_gather | solution.py:675
  26.8 4.0 %collective-permute-start.6 = (bf16[4,4,16,1024]{3,2,1,0:T(8,128)(2,1)S(1)}, bf16[4,4,16,1024]{3,2,1,0:T(8,128)(2,1)S(1)}, u32[]{:S(2)}, u32[]{:S(2)}) collective-permute-start(bf16[4,4,16,1024]{3,2,1,0:T(8,128)(2,1)S(1)} %pad_maximum_fusion.own), channel_id=1, source_target_pairs={{0,1},{1,0},{2,3},{3,2},{4,5},{5,4},{6,7},{7,6},{8,9},{9,8},{10,11... | collective-permute-start | bytes 1572872 | tf_op jit(solution)/shard_map/ppermute | solution.py:74
  32.7 48.7 %copy-start.13 = (s32[16]{0:T(128)S(1)}, s32[16]{0:T(128)}, u32[]{:S(2)}) copy-start(s32[16]{0:T(128)} %param.15) | copy-start | bytes 196
  81.0 2.0 %collective-permute-start.7 = (bf16[64,4224]{1,0:T(8,128)(2,1)S(1)}, bf16[64,4224]{1,0:T(8,128)(2,1)S(1)}, u32[]{:S(2)}, u32[]{:S(2)}) collective-permute-start(bf16[64,4224]{1,0:T(8,128)(2,1)S(1)} %get-tuple-element.71), channel_id=1, source_target_pairs={{0,1},{1,0},{2,3},{3,2},{4,5},{5,4},{6,7},{7,6},{8,9},{9,8},{10,11... | collective-permute-start | bytes 1622024 | tf_op jit(solution)/shard_map/ppermute | solution.py:74
  85.3 6.6 %collective-permute-start.10 = (bf16[16,5248]{1,0:T(8,128)(2,1)S(1)}, bf16[16,5248]{1,0:T(8,128)(2,1)S(1)}, u32[]{:S(2)}, u32[]{:S(2)}) collective-permute-start(bf16[16,5248]{1,0:T(8,128)(2,1)S(1)} %get-tuple-element.81), channel_id=1, source_target_pairs={{0,24},{8,0},{16,8},{24,16},{1,25},{9,1},{17,9},{25,17},{2,26},{10... | collective-permute-start | bytes 503816 | tf_op jit(solution)/shard_map/ppermute | solution.py:64
  86.6 8.2 %collective-permute-start.8 = (bf16[16,5248]{1,0:T(8,128)(2,1)S(1)}, bf16[16,5248]{1,0:T(8,128)(2,1)S(1)}, u32[]{:S(2)}, u32[]{:S(2)}) collective-permute-start(bf16[16,5248]{1,0:T(8,128)(2,1)S(1)} %get-tuple-element.79), channel_id=1, source_target_pairs={{0,8},{8,16},{16,24},{24,0},{1,9},{9,17},{17,25},{25,1},{2,10},{10... | collective-permute-start | bytes 503816 | tf_op jit(solution)/shard_map/ppermute | solution.py:64
  87.7 8.3 %collective-permute-start.9 = (bf16[16,5248]{1,0:T(8,128)(2,1)S(1)}, bf16[16,5248]{1,0:T(8,128)(2,1)S(1)}, u32[]{:S(2)}, u32[]{:S(2)}) collective-permute-start(bf16[16,5248]{1,0:T(8,128)(2,1)S(1)} %get-tuple-element.80), channel_id=1, source_target_pairs={{0,16},{8,24},{16,0},{24,8},{1,17},{9,25},{17,1},{25,9},{2,18},{10... | collective-permute-start | bytes 503816 | tf_op jit(solution)/shard_map/ppermute | solution.py:64
  88.3 31.9 %copy-start = (bf16[1280,512]{1,0:T(8,128)(2,1)S(1)}, bf16[1280,512]{1,0:T(8,128)(2,1)}, u32[]{:S(2)}) copy-start(bf16[1280,512]{1,0:T(8,128)(2,1)} %all-gather.3.cloned.1.call-done) | copy-start | bytes 3932164
  97.1 4.8 %collective-permute-start.11 = (bf16[16,1152]{1,0:T(8,128)(2,1)S(1)}, bf16[16,1152]{1,0:T(8,128)(2,1)S(1)}, u32[]{:S(2)}, u32[]{:S(2)}) collective-permute-start(bf16[16,1152]{1,0:T(8,128)(2,1)S(1)} %get-tuple-element.86), channel_id=1, source_target_pairs={{0,2},{1,3},{2,4},{3,5},{4,6},{5,7},{6,0},{7,1},{8,10},{9,11},{10,... | collective-permute-start | bytes 110600 | tf_op jit(solution)/shard_map/ppermute | solution.py:64
  97.3 5.9 %collective-permute-start.12 = (bf16[16,1152]{1,0:T(8,128)(2,1)S(1)}, bf16[16,1152]{1,0:T(8,128)(2,1)S(1)}, u32[]{:S(2)}, u32[]{:S(2)}) collective-permute-start(bf16[16,1152]{1,0:T(8,128)(2,1)S(1)} %get-tuple-element.87), channel_id=1, source_target_pairs={{0,4},{1,5},{2,6},{3,7},{4,0},{5,1},{6,2},{7,3},{8,12},{9,13},{10,... | collective-permute-start | bytes 110600 | tf_op jit(solution)/shard_map/ppermute | solution.py:64
  100.2 3.5 %collective-permute-start.13 = (bf16[16,1152]{1,0:T(8,128)(2,1)S(1)}, bf16[16,1152]{1,0:T(8,128)(2,1)S(1)}, u32[]{:S(2)}, u32[]{:S(2)}) collective-permute-start(bf16[16,1152]{1,0:T(8,128)(2,1)S(1)} %get-tuple-element.88), channel_id=1, source_target_pairs={{0,6},{1,7},{2,0},{3,1},{4,2},{5,3},{6,4},{7,5},{8,14},{9,15},{10,... | collective-permute-start | bytes 110600 | tf_op jit(solution)/shard_map/ppermute | solution.py:64
  104.6 2.9 %collective-permute-start.14 = (bf16[16,1152]{1,0:T(8,128)(2,1)S(1)}, bf16[16,1152]{1,0:T(8,128)(2,1)S(1)}, u32[]{:S(2)}, u32[]{:S(2)}) collective-permute-start(bf16[16,1152]{1,0:T(8,128)(2,1)S(1)} %shard_map.143.refs_0_), channel_id=1, source_target_pairs={{0,8},{8,16},{16,24},{24,0},{1,9},{9,17},{17,25},{25,1},{2,10},{10... | collective-permute-start | bytes 110600 | tf_op jit(solution)/shard_map/ppermute | solution.py:64
  104.7 2.9 %collective-permute-start.15 = (bf16[16,1152]{1,0:T(8,128)(2,1)S(1)}, bf16[16,1152]{1,0:T(8,128)(2,1)S(1)}, u32[]{:S(2)}, u32[]{:S(2)}) collective-permute-start(bf16[16,1152]{1,0:T(8,128)(2,1)S(1)} %shard_map.143.refs_0_), channel_id=1, source_target_pairs={{0,16},{8,24},{16,0},{24,8},{1,17},{9,25},{17,1},{25,9},{2,18},{10... | collective-permute-start | bytes 110600 | tf_op jit(solution)/shard_map/ppermute | solution.py:64
  105.3 3.7 %collective-permute-start.16 = (bf16[16,1152]{1,0:T(8,128)(2,1)S(1)}, bf16[16,1152]{1,0:T(8,128)(2,1)S(1)}, u32[]{:S(2)}, u32[]{:S(2)}) collective-permute-start(bf16[16,1152]{1,0:T(8,128)(2,1)S(1)} %shard_map.143.refs_0_), channel_id=1, source_target_pairs={{0,24},{8,0},{16,8},{24,16},{1,25},{9,1},{17,9},{25,17},{2,26},{10... | collective-permute-start | bytes 110600 | tf_op jit(solution)/shard_map/ppermute | solution.py:64
  112.8 5.6 %collective-permute-start.17 = (bf16[64,1024]{1,0:T(8,128)(2,1)S(1)}, bf16[64,1024]{1,0:T(8,128)(2,1)S(1)}, u32[]{:S(2)}, u32[]{:S(2)}) collective-permute-start(bf16[64,1024]{1,0:T(8,128)(2,1)S(1)} %get-tuple-element.91), channel_id=1, source_target_pairs={{0,1},{1,0},{2,3},{3,2},{4,5},{5,4},{6,7},{7,6},{8,9},{9,8},{10,11... | collective-permute-start | bytes 393224 | tf_op jit(solution)/shard_map/ppermute | solution.py:74
  118.5 4.9 %collective-permute-start.18 = (bf16[64,1024]{1,0:T(8,128)(2,1)S(1)}, bf16[64,1024]{1,0:T(8,128)(2,1)S(1)}, u32[]{:S(2)}, u32[]{:S(2)}) collective-permute-start(bf16[64,1024]{1,0:T(8,128)(2,1)S(1)} %shard_map.145.keep), channel_id=1, source_target_pairs={{0,2},{1,3},{2,0},{3,1},{4,6},{5,7},{6,4},{7,5},{8,10},{9,11},{10,... | collective-permute-start | bytes 393224 | tf_op jit(solution)/shard_map/ppermute | solution.py:69
  123.4 8.0 %collective-permute-start.19 = (bf16[64,1024]{1,0:T(8,128)(2,1)S(1)}, bf16[64,1024]{1,0:T(8,128)(2,1)S(1)}, u32[]{:S(2)}, u32[]{:S(2)}) collective-permute-start(bf16[64,1024]{1,0:T(8,128)(2,1)S(1)} %shard_map.147.keep), channel_id=1, source_target_pairs={{0,4},{1,5},{2,6},{3,7},{4,0},{5,1},{6,2},{7,3},{8,12},{9,13},{10,... | collective-permute-start | bytes 393224 | tf_op jit(solution)/shard_map/ppermute | solution.py:69
  131.5 2.7 %collective-permute-start.20 = (bf16[64,1024]{1,0:T(8,128)(2,1)S(1)}, bf16[64,1024]{1,0:T(8,128)(2,1)S(1)}, u32[]{:S(2)}, u32[]{:S(2)}) collective-permute-start(bf16[64,1024]{1,0:T(8,128)(2,1)S(1)} %shard_map.149.half), channel_id=1, source_target_pairs={{0,1},{1,0},{2,3},{3,2},{4,5},{5,4},{6,7},{7,6},{8,9},{9,8},{10,11... | collective-permute-start | bytes 393224 | tf_op jit(solution)/shard_map/ppermute | solution.py:74
  (5 other events, 4.1 us)
Sparse Core Ops, SparseCore 0:
  26.8 30.8 reduce-scatter.1
  59.3 25.1 all-gather.2

commit v7 on v5

--- a/solution.py
+++ b/solution.py
@@ -9,8 +9,8 @@
 
 HEAD_SIZE = 128
 CORES = 2
-CHUNK = 512
-SLOTS = 4
+CHUNK = 768
+SLOTS = 3
 LANES = 128
 
 norm_eps = 1e-06
@@ -160,7 +160,6 @@
     raw,
     acc,
     probs,
-    fresh,
     state,
     head_buf,
     buf,
@@ -281,33 +280,27 @@
             return first_id + first + c * CHUNK
 
         body_copy(0).wait()
-        fresh[...] = scores_of(buf[0])
+        scores = scores_of(buf[0])
         add_product(p, None, lambda at, n: head_buf[:, at : at + n])
-        body_copy(1).wait()
-        scores = scores_of(buf[1])
-        p, scale, run = softmax(fresh[...], start_of(0), run)
+        p, scale, run = softmax(scores, start_of(0), run)
         probs[...] = p
-        fresh[...] = scores
 
         def step(c, carry):
             scale, run = carry
             body_copy(c).wait()
             scores = scores_of(buf[lax.rem(c, SLOTS)])
-            p, next_scale, run = softmax(fresh[...], start_of(c - 1), run)
-            add_product(probs[...], scale, part(buf, lax.rem(c - 2, SLOTS)))
+            add_product(probs[...], scale, part(buf, lax.rem(c - 1, SLOTS)))
+            p, scale, run = softmax(scores, start_of(c), run)
             probs[...] = p
-            fresh[...] = scores
 
             @pl.when(c + 2 < chunks)
             def _():
                 body_copy(c + 2).start()
 
-            return next_scale, run
-
-        scale, run = lax.fori_loop(2, chunks, step, (scale, run))
-        p, next_scale, run = softmax(fresh[...], start_of(chunks - 1), run)
-        add_product(probs[...], scale, part(buf, (chunks - 2) % SLOTS))
-        add_product(p, next_scale, part(buf, (chunks - 1) % SLOTS))
+            return scale, run
+
+        scale, run = lax.fori_loop(1, chunks, step, (scale, run))
+        add_product(probs[...], scale, part(buf, (chunks - 1) % SLOTS))
 
     for z in range(nz):
         keep[z] = acc[CORES * z + core_at]
@@ -677,14 +670,13 @@
             pltpu.VMEM((loss, width), bf16),
             pltpu.VMEM((nc, loss, block_width), f32),
             pltpu.VMEM((loss, CHUNK), bf16),
-            pltpu.VMEM((loss, CHUNK), f32),
             pltpu.VMEM((loss, LANES), f32),
             pltpu.VMEM((first, width), bf16),
             pltpu.VMEM((SLOTS if chunks else 1, CHUNK if chunks else 16, width), bf16),
             pltpu.SemaphoreType.DMA,
             pltpu.SemaphoreType.DMA((SLOTS,)),
         ],
-        compiler_params=pltpu.CompilerParams(vmem_limit_bytes=47 * 2**20),
+        compiler_params=pltpu.CompilerParams(vmem_limit_bytes=48 * 2**20),
         cost_estimate=pl.CostEstimate(
             flops=4 * max(loss, 256) * width * voc_rows,
             bytes_accessed=4 * width * voc_rows,
@@ -767,6 +759,7 @@
             pltpu.VMEM((4, query_width // 4, block_width), bf16),
             pltpu.SemaphoreType.DMA((4,)),
         ],
+        limit=52,
     )(place, *gathered, output_weight)
     half = call(sum_body, shape((loss, cols), bf16), [vmem()] * 2)(keep, swapped(send))
     windows = nz.bit_length() - 1

time: 143 us -> 143 us (level)
    pallas_call x1, Pallas kernels: 50.1 us -> 48.2 us  [per_device(): pl.pallas_call(functools.partial(flash_body, first), out_shape=(shape((nz...]
    unnamed x26 -> x28, local copies, waits for them, and re-layouts: 5.48 us -> 5.12 us
  transfers between devices with their start and end apart: 23 -> 23, of which waited for: 15 -> 16; matrix products, arithmetic and copies ran while one was open for 0% -> 0% of each run, Pallas kernels for 42% -> 42%
where the time goes in v7:
time: 143 us
  Pallas kernels  69 us (48%)
  starting transfers between devices  27.8 us (19%)
  waiting for transfers between devices  25.8 us (18%)
  between operations  14.3 us (10%)
  local copies, waits for them, and re-layouts  5.57 us (4%)
    pallas_call x1, Pallas kernels, per_device(): pl.pallas_call(functools.partial(flash_body, first), out_shape=(shape((nz...  48.2 us
    ppermute x15, starting transfers between devices, shifted(): return lax.ppermute(value, axis, pairs)  16.6 us
    ppermute x15, waiting for transfers between devices, shifted(): return lax.ppermute(value, axis, pairs)  15.1 us
    ppermute x4, starting transfers between devices, swapped(): return lax.ppermute(value, 'ctx', [(i, i ^ 1) for i in range(size)])  10.1 us
    ppermute x2, waiting for transfers between devices, crossed(): lax.ppermute(value, 'ctx', [(i, i ^ bit * CORES) for i in range(size)])  7.11 us
    pallas_call x2, Pallas kernels, forward(): call(functools.partial(forward_body, loss_per, heads, group, at_once, j),...  5.6 us
    unnamed x28, local copies, waits for them, and re-layouts  5.12 us
    pallas_call x1, Pallas kernels, per_device(): call(functools.partial(project_body, nv), (shape((loss, block_width), bf1...  3.81 us
  transfers between devices with their start and end apart: 23, of which 16 were waited for; matrix products, arithmetic and copies ran while one was open for 0% of the time, Pallas kernels for 42%

profile of v7, /device:TPU:3, one launch (start us, length us, event | category | flops | bytes accessed | tf_op | source)
XLA Modules:
  0.0 142.7 jit_solution(18282670815659787491)
XLA Ops:
  7.3 1.0 copy-done.2
  9.8 1.3 collective-permute-start
  11.2 2.3 %collective-permute-start.1 = (bf16[16,1024]{1,0:T(8,128)(2,1)S(1)}, bf16[16,1024]{1,0:T(8,128)(2,1)S(1)}, u32[]{:S(2)}, u32[]{:S(2)}) collective-permute-start(bf16[16,1024]{1,0:T(8,128)(2,1)S(1)} %shard_map.137), channel_id=1, source_target_pairs={{0,4},{1,5},{2,6},{3,7},{4,0},{5,1},{6,2},{7,3},{8,12},{9,13},{10,... | collective-permute-start | bytes 98312 | tf_op jit(solution)/shard_map/ppermute | solution.py:64
  13.5 1.1 collective-permute-start.2
  14.8 2.0 %collective-permute-done.2 = bf16[16,1024]{1,0:T(8,128)(2,1)S(1)} collective-permute-done((bf16[16,1024]{1,0:T(8,128)(2,1)S(1)}, bf16[16,1024]{1,0:T(8,128)(2,1)S(1)}, u32[]{:S(2)}, u32[]{:S(2)}) %collective-permute-start.2) | collective-permute-done | bytes 32800 | tf_op jit(solution)/shard_map/ppermute | solution.py:64
  16.9 1.3 collective-permute-start.3
  18.3 1.3 collective-permute-start.5
  20.3 3.5 %shard_map.138 = bf16[8,64,1024]{2,1,0:T(8,128)(2,1)} custom-call(s32[5]{0:T(128)S(1)} %stack.53.place, s32[1,64]{1,0:T(1,128)S(1)} %bitcast.28, bf16[4752,8192]{1,0:T(8,128)(2,1)} %weight.3), custom_call_target="tpu_custom_call" | custom-call | bytes 16777216 | tf_op jit(solution)/shard_map/pallas_call | solution.py:629
  24.0 3.2 %collective-permute-start.6 = (bf16[4,4,16,1024]{3,2,1,0:T(8,128)(2,1)S(1)}, bf16[4,4,16,1024]{3,2,1,0:T(8,128)(2,1)S(1)}, u32[]{:S(2)}, u32[]{:S(2)}) collective-permute-start(bf16[4,4,16,1024]{3,2,1,0:T(8,128)(2,1)S(1)} %pad_maximum_fusion.own), channel_id=1, source_target_pairs={{0,1},{1,0},{2,3},{3,2},{4,5},{5,4},{6,7},{7,6},{8,9},{9,8},{10,11... | collective-permute-start | bytes 1572872 | tf_op jit(solution)/shard_map/ppermute | solution.py:74
  27.4 1.4 shard_map.139
  29.6 1.0 copy-done.12
  30.7 48.2 %shard_map.140 = (f32[4,64,1024]{2,1,0:T(8,128)S(1)}, bf16[64,4224]{1,0:T(8,128)(2,1)S(1)}, f32[64,128]{1,0:T(8,128)S(1)}, f32[16,1024]{1,0:T(8,128)S(1)}) custom-call(s32[5]{0:T(128)S(1)} %stack.53.place, bf16[4,4,16,1024]{3,2,1,0:T(8,128)(2,1)S(1)} %pad_maximum_fusion.own, bf16[4,4,16,1024]{3,2,1,0:T(8,128)(2,1)S(1)} %copy-done.12, ...), custom_call_target="tpu_custom_call" | custom-call | flops 39862665216 | bytes 155713536 | tf_op jit(solution)/shard_map/pallas_call | solution.py:658
  79.3 1.6 %collective-permute-done.7.got = bf16[64,4224]{1,0:T(8,128)(2,1)S(1)} collective-permute-done((bf16[64,4224]{1,0:T(8,128)(2,1)S(1)}, bf16[64,4224]{1,0:T(8,128)(2,1)S(1)}, u32[]{:S(2)}, u32[]{:S(2)}) %collective-permute-start.7) | collective-permute-done | bytes 540704 | tf_op jit(solution)/shard_map/ppermute | solution.py:74
  81.8 1.3 shard_map.141
  83.1 1.2 collective-permute-start.10
  84.3 1.2 collective-permute-start.8
  86.6 3.0 %collective-permute-done.10.rest_2_ = bf16[16,5248]{1,0:T(8,128)(2,1)S(1)} collective-permute-done((bf16[16,5248]{1,0:T(8,128)(2,1)S(1)}, bf16[16,5248]{1,0:T(8,128)(2,1)S(1)}, u32[]{:S(2)}, u32[]{:S(2)}) %collective-permute-start.10) | collective-permute-done | bytes 167968 | tf_op jit(solution)/shard_map/ppermute | solution.py:64
  89.6 3.4 %collective-permute-done.8.rest_0_ = bf16[16,5248]{1,0:T(8,128)(2,1)S(1)} collective-permute-done((bf16[16,5248]{1,0:T(8,128)(2,1)S(1)}, bf16[16,5248]{1,0:T(8,128)(2,1)S(1)}, u32[]{:S(2)}, u32[]{:S(2)}) %collective-permute-start.8) | collective-permute-done | bytes 167968 | tf_op jit(solution)/shard_map/ppermute | solution.py:64
  93.9 1.0 shard_map.142
  95.0 3.1 %collective-permute-start.12 = (bf16[16,1152]{1,0:T(8,128)(2,1)S(1)}, bf16[16,1152]{1,0:T(8,128)(2,1)S(1)}, u32[]{:S(2)}, u32[]{:S(2)}) collective-permute-start(bf16[16,1152]{1,0:T(8,128)(2,1)S(1)} %get-tuple-element.87), channel_id=1, source_target_pairs={{0,4},{1,5},{2,6},{3,7},{4,0},{5,1},{6,2},{7,3},{8,12},{9,13},{10,... | collective-permute-start | bytes 110600 | tf_op jit(solution)/shard_map/ppermute | solution.py:64
  98.2 1.4 %collective-permute-done.11.rest_0_ = bf16[16,1152]{1,0:T(8,128)(2,1)S(1)} collective-permute-done((bf16[16,1152]{1,0:T(8,128)(2,1)S(1)}, bf16[16,1152]{1,0:T(8,128)(2,1)S(1)}, u32[]{:S(2)}, u32[]{:S(2)}) %collective-permute-start.11) | collective-permute-done | bytes 36896 | tf_op jit(solution)/shard_map/ppermute | solution.py:64
  99.7 1.5 %collective-permute-done.12.rest_1_ = bf16[16,1152]{1,0:T(8,128)(2,1)S(1)} collective-permute-done((bf16[16,1152]{1,0:T(8,128)(2,1)S(1)}, bf16[16,1152]{1,0:T(8,128)(2,1)S(1)}, u32[]{:S(2)}, u32[]{:S(2)}) %collective-permute-start.12) | collective-permute-done | bytes 36896 | tf_op jit(solution)/shard_map/ppermute | solution.py:64
  102.5 1.1 collective-permute-start.14
  103.6 1.4 collective-permute-start.16
  105.3 1.0 collective-permute-done.15.refs_2_
  107.3 3.8 %shard_map.144 = (bf16[64,1024]{1,0:T(8,128)(2,1)}, f32[1,1]{1,0:T(1,128)}, f32[64,1024]{1,0:T(8,128)S(1)}, bf16[64,1024]{1,0:T(8,128)(2,1)S(1)}) custom-call(s32[5]{0:T(128)S(1)} %stack.53.place, bf16[16,1152]{1,0:T(8,128)(2,1)S(1)} %shard_map.143.refs_0_, bf16[16,1152]{1,0:T(8,128)(2,1)S(1)} %collective-permute-done.14.refs_1_, ...), custom_call_target="tpu_custom_call" | custom-call | tf_op jit(solution)/shard_map/pallas_call | solution.py:747
  111.1 5.9 %collective-permute-start.17 = (bf16[64,1024]{1,0:T(8,128)(2,1)S(1)}, bf16[64,1024]{1,0:T(8,128)(2,1)S(1)}, u32[]{:S(2)}, u32[]{:S(2)}) collective-permute-start(bf16[64,1024]{1,0:T(8,128)(2,1)S(1)} %get-tuple-element.91), channel_id=1, source_target_pairs={{0,1},{1,0},{2,3},{3,2},{4,5},{5,4},{6,7},{7,6},{8,9},{9,8},{10,11... | collective-permute-start | bytes 393224 | tf_op jit(solution)/shard_map/ppermute | solution.py:74
  118.2 2.8 %shard_map.146 = (f32[512,128]{1,0:T(8,128)S(1)}, f32[64,1024]{1,0:T(8,128)S(1)}, f32[512,128]{1,0:T(8,128)S(1)}) custom-call(s32[5]{0:T(128)S(1)} %stack.53.place, s32[1,1024]{1,0:T(1,128)S(1)} %add.63.key_pos, s32[64,1]{1,0:T(8,128)S(1)} %copy.19.query_pos, bf16[8,160,512]{2,1,0:T(8,128)(2,1)S(1)} %bitcast.22), custom_call_target="tpu_custom_call" | custom-call | flops 1610612736 | bytes 1310720 | tf_op jit(solution)/shard_map/pallas_call | solution.py:711
  121.0 1.8 %collective-permute-done.18.refs_0_ = bf16[64,1024]{1,0:T(8,128)(2,1)S(1)} collective-permute-done((bf16[64,1024]{1,0:T(8,128)(2,1)S(1)}, bf16[64,1024]{1,0:T(8,128)(2,1)S(1)}, u32[]{:S(2)}, u32[]{:S(2)}) %collective-permute-start.18) | collective-permute-done | bytes 131104 | tf_op jit(solution)/shard_map/ppermute | solution.py:69
  123.9 2.8 %shard_map.148 = (f32[512,128]{1,0:T(8,128)S(1)}, f32[64,1024]{1,0:T(8,128)S(1)}, f32[512,128]{1,0:T(8,128)S(1)}) custom-call(s32[5]{0:T(128)S(1)} %stack.53.place, s32[1,1024]{1,0:T(1,128)S(1)} %add.63.key_pos, s32[64,1]{1,0:T(8,128)S(1)} %copy.20.query_pos, bf16[8,160,512]{2,1,0:T(8,128)(2,1)S(1)} %bitcast.23), custom_call_target="tpu_custom_call" | custom-call | flops 1610612736 | bytes 1310720 | tf_op jit(solution)/shard_map/pallas_call | solution.py:711
  126.7 5.3 %collective-permute-done.19.refs_0_ = bf16[64,1024]{1,0:T(8,128)(2,1)S(1)} collective-permute-done((bf16[64,1024]{1,0:T(8,128)(2,1)S(1)}, bf16[64,1024]{1,0:T(8,128)(2,1)S(1)}, u32[]{:S(2)}, u32[]{:S(2)}) %collective-permute-start.19) | collective-permute-done | bytes 131104 | tf_op jit(solution)/shard_map/ppermute | solution.py:69
  133.6 2.3 %shard_map.150 = (bf16[8,2048]{1,0:T(8,128)(2,1)}, bf16[128,256]{1,0:T(8,128)(2,1)}, bf16[128,256]{1,0:T(8,128)(2,1)}) custom-call(s32[5]{0:T(128)S(1)} %stack.53.place, bf16[64,1024]{1,0:T(8,128)(2,1)S(1)} %shard_map.149.half, bf16[64,1024]{1,0:T(8,128)(2,1)S(1)} %collective-permute-done.20.other, bf16[8,160,512]{2,1,0:T(8,128)(2,1)S(1)} %bitcast.24, ...), custom_call_target="tpu_custom_call" | custom-call | tf_op jit(solution)/shard_map/pallas_call | solution.py:777
  (70 shorter events, 13.7 us)
Async XLA Ops:
  7.2 71.7 %reduce-scatter.2.cloned.1.call-start = ((), (), s32[]{:S(2)}) async-start(), calls=%async_computation.1 | async-start | bytes 1179648 | tf_op jit(solution)/shard_map/reduce_scatter | solution.py:647
  7.3 1.0 copy-start.2
  9.8 4.7 %collective-permute-start = (bf16[16,1024]{1,0:T(8,128)(2,1)S(1)}, bf16[16,1024]{1,0:T(8,128)(2,1)S(1)}, u32[]{:S(2)}, u32[]{:S(2)}) collective-permute-start(bf16[16,1024]{1,0:T(8,128)(2,1)S(1)} %shard_map.137), channel_id=1, source_target_pairs={{0,2},{1,3},{2,4},{3,5},{4,6},{5,7},{6,0},{7,1},{8,10},{9,11},{10,... | collective-permute-start | bytes 98312 | tf_op jit(solution)/shard_map/ppermute | solution.py:64
  11.2 3.7 %collective-permute-start.1 = (bf16[16,1024]{1,0:T(8,128)(2,1)S(1)}, bf16[16,1024]{1,0:T(8,128)(2,1)S(1)}, u32[]{:S(2)}, u32[]{:S(2)}) collective-permute-start(bf16[16,1024]{1,0:T(8,128)(2,1)S(1)} %shard_map.137), channel_id=1, source_target_pairs={{0,4},{1,5},{2,6},{3,7},{4,0},{5,1},{6,2},{7,3},{8,12},{9,13},{10,... | collective-permute-start | bytes 98312 | tf_op jit(solution)/shard_map/ppermute | solution.py:64
  13.5 3.4 %collective-permute-start.2 = (bf16[16,1024]{1,0:T(8,128)(2,1)S(1)}, bf16[16,1024]{1,0:T(8,128)(2,1)S(1)}, u32[]{:S(2)}, u32[]{:S(2)}) collective-permute-start(bf16[16,1024]{1,0:T(8,128)(2,1)S(1)} %shard_map.137), channel_id=1, source_target_pairs={{0,6},{1,7},{2,0},{3,1},{4,2},{5,3},{6,4},{7,5},{8,14},{9,15},{10,... | collective-permute-start | bytes 98312 | tf_op jit(solution)/shard_map/ppermute | solution.py:64
  16.9 7.0 %collective-permute-start.3 = (bf16[4,16,1024]{2,1,0:T(8,128)(2,1)S(1)}, bf16[4,16,1024]{2,1,0:T(8,128)(2,1)S(1)}, u32[]{:S(2)}, u32[]{:S(2)}) collective-permute-start(bf16[4,16,1024]{2,1,0:T(8,128)(2,1)S(1)} %pad_maximum_fusion.1), channel_id=1, source_target_pairs={{0,8},{8,16},{16,24},{24,0},{1,9},{9,17},{17,25},{25,1},{2,10},{10... | collective-permute-start | bytes 393224 | tf_op jit(solution)/shard_map/ppermute | solution.py:64
  18.1 5.7 %collective-permute-start.4 = (bf16[4,16,1024]{2,1,0:T(8,128)(2,1)S(1)}, bf16[4,16,1024]{2,1,0:T(8,128)(2,1)S(1)}, u32[]{:S(2)}, u32[]{:S(2)}) collective-permute-start(bf16[4,16,1024]{2,1,0:T(8,128)(2,1)S(1)} %pad_maximum_fusion.1), channel_id=1, source_target_pairs={{0,16},{8,24},{16,0},{24,8},{1,17},{9,25},{17,1},{25,9},{2,18},{10... | collective-permute-start | bytes 393224 | tf_op jit(solution)/shard_map/ppermute | solution.py:64
  18.3 5.5 %collective-permute-start.5 = (bf16[4,16,1024]{2,1,0:T(8,128)(2,1)S(1)}, bf16[4,16,1024]{2,1,0:T(8,128)(2,1)S(1)}, u32[]{:S(2)}, u32[]{:S(2)}) collective-permute-start(bf16[4,16,1024]{2,1,0:T(8,128)(2,1)S(1)} %pad_maximum_fusion.1), channel_id=1, source_target_pairs={{0,24},{8,0},{16,8},{24,16},{1,25},{9,1},{17,9},{25,17},{2,26},{10... | collective-permute-start | bytes 393224 | tf_op jit(solution)/shard_map/ppermute | solution.py:64
  20.3 7.0 %copy-start.10 = (s32[64]{0:T(128)S(1)}, s32[64]{0:T(128)}, u32[]{:S(2)}) copy-start(s32[64]{0:T(128)} %param.13) | copy-start | bytes 772
  20.3 7.1 %copy-start.1 = (bf16[128,2048]{1,0:T(8,128)(2,1)S(1)}, bf16[128,2048]{1,0:T(8,128)(2,1)}, u32[]{:S(2)}) copy-start(bf16[128,2048]{1,0:T(8,128)(2,1)} %queries) | copy-start | bytes 1572868
  20.3 7.1 %copy-start.4 = (bf16[128,256]{1,0:T(8,128)(2,1)S(1)}, bf16[128,256]{1,0:T(8,128)(2,1)}, u32[]{:S(2)}) copy-start(bf16[128,256]{1,0:T(8,128)(2,1)} %keys.1) | copy-start | bytes 196612
  20.3 7.1 %copy-start.5 = (bf16[128,256]{1,0:T(8,128)(2,1)S(1)}, bf16[128,256]{1,0:T(8,128)(2,1)}, u32[]{:S(2)}) copy-start(bf16[128,256]{1,0:T(8,128)(2,1)} %values.1) | copy-start | bytes 196612
  20.3 7.1 %copy-start.8 = (s32[64]{0:T(128)S(1)}, s32[64]{0:T(128)}, u32[]{:S(2)}) copy-start(s32[64]{0:T(128)} %rows.3) | copy-start | bytes 772
  20.3 9.3 %copy-start.6 = (f32[8192]{0:T(1024)S(1)}, f32[8192]{0:T(1024)}, u32[]{:S(2)}) copy-start(f32[8192]{0:T(1024)} %param.11) | copy-start | bytes 98308
  23.9 62.7 %all-gather.3.cloned.1.call-start = ((), (), s32[]{:S(2)}) async-start(), calls=%async_computation.2 | async-start | bytes 1474560 | tf_op jit(solution)/shard_map/all_gather | solution.py:651
  24.0 4.7 %collective-permute-start.6 = (bf16[4,4,16,1024]{3,2,1,0:T(8,128)(2,1)S(1)}, bf16[4,4,16,1024]{3,2,1,0:T(8,128)(2,1)S(1)}, u32[]{:S(2)}, u32[]{:S(2)}) collective-permute-start(bf16[4,4,16,1024]{3,2,1,0:T(8,128)(2,1)S(1)} %pad_maximum_fusion.own), channel_id=1, source_target_pairs={{0,1},{1,0},{2,3},{3,2},{4,5},{5,4},{6,7},{7,6},{8,9},{9,8},{10,11... | collective-permute-start | bytes 1572872 | tf_op jit(solution)/shard_map/ppermute | solution.py:74
  30.7 48.7 %copy-start.13 = (s32[16]{0:T(128)S(1)}, s32[16]{0:T(128)}, u32[]{:S(2)}) copy-start(s32[16]{0:T(128)} %param.15) | copy-start | bytes 196
  78.9 2.0 %collective-permute-start.7 = (bf16[64,4224]{1,0:T(8,128)(2,1)S(1)}, bf16[64,4224]{1,0:T(8,128)(2,1)S(1)}, u32[]{:S(2)}, u32[]{:S(2)}) collective-permute-start(bf16[64,4224]{1,0:T(8,128)(2,1)S(1)} %get-tuple-element.71), channel_id=1, source_target_pairs={{0,1},{1,0},{2,3},{3,2},{4,5},{5,4},{6,7},{7,6},{8,9},{9,8},{10,11... | collective-permute-start | bytes 1622024 | tf_op jit(solution)/shard_map/ppermute | solution.py:74
  83.1 6.5 %collective-permute-start.10 = (bf16[16,5248]{1,0:T(8,128)(2,1)S(1)}, bf16[16,5248]{1,0:T(8,128)(2,1)S(1)}, u32[]{:S(2)}, u32[]{:S(2)}) collective-permute-start(bf16[16,5248]{1,0:T(8,128)(2,1)S(1)} %get-tuple-element.81), channel_id=1, source_target_pairs={{0,24},{8,0},{16,8},{24,16},{1,25},{9,1},{17,9},{25,17},{2,26},{10... | collective-permute-start | bytes 503816 | tf_op jit(solution)/shard_map/ppermute | solution.py:64
  84.3 8.7 %collective-permute-start.8 = (bf16[16,5248]{1,0:T(8,128)(2,1)S(1)}, bf16[16,5248]{1,0:T(8,128)(2,1)S(1)}, u32[]{:S(2)}, u32[]{:S(2)}) collective-permute-start(bf16[16,5248]{1,0:T(8,128)(2,1)S(1)} %get-tuple-element.79), channel_id=1, source_target_pairs={{0,8},{8,16},{16,24},{24,0},{1,9},{9,17},{17,25},{25,1},{2,10},{10... | collective-permute-start | bytes 503816 | tf_op jit(solution)/shard_map/ppermute | solution.py:64
  85.5 8.3 %collective-permute-start.9 = (bf16[16,5248]{1,0:T(8,128)(2,1)S(1)}, bf16[16,5248]{1,0:T(8,128)(2,1)S(1)}, u32[]{:S(2)}, u32[]{:S(2)}) collective-permute-start(bf16[16,5248]{1,0:T(8,128)(2,1)S(1)} %get-tuple-element.80), channel_id=1, source_target_pairs={{0,16},{8,24},{16,0},{24,8},{1,17},{9,25},{17,1},{25,9},{2,18},{10... | collective-permute-start | bytes 503816 | tf_op jit(solution)/shard_map/ppermute | solution.py:64
  86.6 31.6 %copy-start = (bf16[1280,512]{1,0:T(8,128)(2,1)S(1)}, bf16[1280,512]{1,0:T(8,128)(2,1)}, u32[]{:S(2)}) copy-start(bf16[1280,512]{1,0:T(8,128)(2,1)} %all-gather.3.cloned.1.call-done) | copy-start | bytes 3932164
  94.9 4.8 %collective-permute-start.11 = (bf16[16,1152]{1,0:T(8,128)(2,1)S(1)}, bf16[16,1152]{1,0:T(8,128)(2,1)S(1)}, u32[]{:S(2)}, u32[]{:S(2)}) collective-permute-start(bf16[16,1152]{1,0:T(8,128)(2,1)S(1)} %get-tuple-element.86), channel_id=1, source_target_pairs={{0,2},{1,3},{2,4},{3,5},{4,6},{5,7},{6,0},{7,1},{8,10},{9,11},{10,... | collective-permute-start | bytes 110600 | tf_op jit(solution)/shard_map/ppermute | solution.py:64
  95.0 6.2 %collective-permute-start.12 = (bf16[16,1152]{1,0:T(8,128)(2,1)S(1)}, bf16[16,1152]{1,0:T(8,128)(2,1)S(1)}, u32[]{:S(2)}, u32[]{:S(2)}) collective-permute-start(bf16[16,1152]{1,0:T(8,128)(2,1)S(1)} %get-tuple-element.87), channel_id=1, source_target_pairs={{0,4},{1,5},{2,6},{3,7},{4,0},{5,1},{6,2},{7,3},{8,12},{9,13},{10,... | collective-permute-start | bytes 110600 | tf_op jit(solution)/shard_map/ppermute | solution.py:64
  98.1 3.5 %collective-permute-start.13 = (bf16[16,1152]{1,0:T(8,128)(2,1)S(1)}, bf16[16,1152]{1,0:T(8,128)(2,1)S(1)}, u32[]{:S(2)}, u32[]{:S(2)}) collective-permute-start(bf16[16,1152]{1,0:T(8,128)(2,1)S(1)} %get-tuple-element.88), channel_id=1, source_target_pairs={{0,6},{1,7},{2,0},{3,1},{4,2},{5,3},{6,4},{7,5},{8,14},{9,15},{10,... | collective-permute-start | bytes 110600 | tf_op jit(solution)/shard_map/ppermute | solution.py:64
  102.5 2.9 %collective-permute-start.14 = (bf16[16,1152]{1,0:T(8,128)(2,1)S(1)}, bf16[16,1152]{1,0:T(8,128)(2,1)S(1)}, u32[]{:S(2)}, u32[]{:S(2)}) collective-permute-start(bf16[16,1152]{1,0:T(8,128)(2,1)S(1)} %shard_map.143.refs_0_), channel_id=1, source_target_pairs={{0,8},{8,16},{16,24},{24,0},{1,9},{9,17},{17,25},{25,1},{2,10},{10... | collective-permute-start | bytes 110600 | tf_op jit(solution)/shard_map/ppermute | solution.py:64
  103.6 2.8 %collective-permute-start.15 = (bf16[16,1152]{1,0:T(8,128)(2,1)S(1)}, bf16[16,1152]{1,0:T(8,128)(2,1)S(1)}, u32[]{:S(2)}, u32[]{:S(2)}) collective-permute-start(bf16[16,1152]{1,0:T(8,128)(2,1)S(1)} %shard_map.143.refs_0_), channel_id=1, source_target_pairs={{0,16},{8,24},{16,0},{24,8},{1,17},{9,25},{17,1},{25,9},{2,18},{10... | collective-permute-start | bytes 110600 | tf_op jit(solution)/shard_map/ppermute | solution.py:64
  103.6 3.7 %collective-permute-start.16 = (bf16[16,1152]{1,0:T(8,128)(2,1)S(1)}, bf16[16,1152]{1,0:T(8,128)(2,1)S(1)}, u32[]{:S(2)}, u32[]{:S(2)}) collective-permute-start(bf16[16,1152]{1,0:T(8,128)(2,1)S(1)} %shard_map.143.refs_0_), channel_id=1, source_target_pairs={{0,24},{8,0},{16,8},{24,16},{1,25},{9,1},{17,9},{25,17},{2,26},{10... | collective-permute-start | bytes 110600 | tf_op jit(solution)/shard_map/ppermute | solution.py:64
  111.1 6.9 %collective-permute-start.17 = (bf16[64,1024]{1,0:T(8,128)(2,1)S(1)}, bf16[64,1024]{1,0:T(8,128)(2,1)S(1)}, u32[]{:S(2)}, u32[]{:S(2)}) collective-permute-start(bf16[64,1024]{1,0:T(8,128)(2,1)S(1)} %get-tuple-element.91), channel_id=1, source_target_pairs={{0,1},{1,0},{2,3},{3,2},{4,5},{5,4},{6,7},{7,6},{8,9},{9,8},{10,11... | collective-permute-start | bytes 393224 | tf_op jit(solution)/shard_map/ppermute | solution.py:74
  118.0 4.8 %collective-permute-start.18 = (bf16[64,1024]{1,0:T(8,128)(2,1)S(1)}, bf16[64,1024]{1,0:T(8,128)(2,1)S(1)}, u32[]{:S(2)}, u32[]{:S(2)}) collective-permute-start(bf16[64,1024]{1,0:T(8,128)(2,1)S(1)} %shard_map.145.keep), channel_id=1, source_target_pairs={{0,2},{1,3},{2,0},{3,1},{4,6},{5,7},{6,4},{7,5},{8,10},{9,11},{10,... | collective-permute-start | bytes 393224 | tf_op jit(solution)/shard_map/ppermute | solution.py:69
  122.8 9.1 %collective-permute-start.19 = (bf16[64,1024]{1,0:T(8,128)(2,1)S(1)}, bf16[64,1024]{1,0:T(8,128)(2,1)S(1)}, u32[]{:S(2)}, u32[]{:S(2)}) collective-permute-start(bf16[64,1024]{1,0:T(8,128)(2,1)S(1)} %shard_map.147.keep), channel_id=1, source_target_pairs={{0,4},{1,5},{2,6},{3,7},{4,0},{5,1},{6,2},{7,3},{8,12},{9,13},{10,... | collective-permute-start | bytes 393224 | tf_op jit(solution)/shard_map/ppermute | solution.py:69
  132.0 1.5 %collective-permute-start.20 = (bf16[64,1024]{1,0:T(8,128)(2,1)S(1)}, bf16[64,1024]{1,0:T(8,128)(2,1)S(1)}, u32[]{:S(2)}, u32[]{:S(2)}) collective-permute-start(bf16[64,1024]{1,0:T(8,128)(2,1)S(1)} %shard_map.149.half), channel_id=1, source_target_pairs={{0,1},{1,0},{2,3},{3,2},{4,5},{5,4},{6,7},{7,6},{8,9},{9,8},{10,11... | collective-permute-start | bytes 393224 | tf_op jit(solution)/shard_map/ppermute | solution.py:74
  (5 other events, 4.1 us)
Sparse Core Ops, SparseCore 0:
  24.0 32.1 reduce-scatter.1
  57.9 25.2 all-gather.2

commit v8 on v7

--- a/solution.py
+++ b/solution.py
@@ -9,7 +9,7 @@
 
 HEAD_SIZE = 128
 CORES = 2
-CHUNK = 768
+CHUNK = 512
 SLOTS = 3
 LANES = 128
 
@@ -676,7 +676,7 @@
             pltpu.SemaphoreType.DMA,
             pltpu.SemaphoreType.DMA((SLOTS,)),
         ],
-        compiler_params=pltpu.CompilerParams(vmem_limit_bytes=48 * 2**20),
+        compiler_params=pltpu.CompilerParams(vmem_limit_bytes=50 * 2**20),
         cost_estimate=pl.CostEstimate(
             flops=4 * max(loss, 256) * width * voc_rows,
             bytes_accessed=4 * width * voc_rows,
@@ -759,7 +759,6 @@
             pltpu.VMEM((4, query_width // 4, block_width), bf16),
             pltpu.SemaphoreType.DMA((4,)),
         ],
-        limit=52,
     )(place, *gathered, output_weight)
     half = call(sum_body, shape((loss, cols), bf16), [vmem()] * 2)(keep, swapped(send))
     windows = nz.bit_length() - 1

time: 143 us -> 140 us (0.979)
  Pallas kernels: 69 us -> 65.4 us
    ppermute x2, waiting for transfers between devices: 7.11 us -> 5.39 us  [crossed(): lax.ppermute(value, 'ctx', [(i, i ^ bit * CORES) for i in range(size)])]
    pallas_call x1, Pallas kernels: 48.2 us -> 46.7 us  [per_device(): pl.pallas_call(functools.partial(flash_body, first), out_shape=(shape((nz...]
    unnamed x28 -> x26, local copies, waits for them, and re-layouts: 5.12 us -> 5.48 us
  transfers between devices with their start and end apart: 23 -> 23, of which waited for: 16 -> 17; matrix products, arithmetic and copies ran while one was open for 0% -> 0% of each run, Pallas kernels for 42% -> 41%
where the time goes in v8:
time: 140 us
  Pallas kernels  65.4 us (47%)
  starting transfers between devices  29 us (21%)
  waiting for transfers between devices  24.8 us (18%)
  between operations  14.3 us (10%)
  local copies, waits for them, and re-layouts  5.93 us (4%)
    pallas_call x1, Pallas kernels, per_device(): pl.pallas_call(functools.partial(flash_body, first), out_shape=(shape((nz...  46.7 us
    ppermute x15, starting transfers between devices, shifted(): return lax.ppermute(value, axis, pairs)  17.1 us
    ppermute x15, waiting for transfers between devices, shifted(): return lax.ppermute(value, axis, pairs)  15.9 us
    ppermute x4, starting transfers between devices, swapped(): return lax.ppermute(value, 'ctx', [(i, i ^ 1) for i in range(size)])  9.69 us
    pallas_call x2, Pallas kernels, forward(): call(functools.partial(forward_body, loss_per, heads, group, at_once, j),...  5.6 us
    unnamed x26, local copies, waits for them, and re-layouts  5.48 us
    ppermute x2, waiting for transfers between devices, crossed(): lax.ppermute(value, 'ctx', [(i, i ^ bit * CORES) for i in range(size)])  5.39 us
    ppermute x4, waiting for transfers between devices, swapped(): return lax.ppermute(value, 'ctx', [(i, i ^ 1) for i in range(size)])  3.53 us
  transfers between devices with their start and end apart: 23, of which 17 were waited for; matrix products, arithmetic and copies ran while one was open for 0% of the time, Pallas kernels for 41%

profile of v8, /device:TPU:3, one launch (start us, length us, event | category | flops | bytes accessed | tf_op | source)
XLA Modules:
  0.0 139.7 jit_solution(5941082647250921124)
XLA Ops:
  7.3 1.0 copy-done.3
  9.8 1.3 collective-permute-start
  11.2 2.3 %collective-permute-start.1 = (bf16[16,1024]{1,0:T(8,128)(2,1)S(1)}, bf16[16,1024]{1,0:T(8,128)(2,1)S(1)}, u32[]{:S(2)}, u32[]{:S(2)}) collective-permute-start(bf16[16,1024]{1,0:T(8,128)(2,1)S(1)} %shard_map.137), channel_id=1, source_target_pairs={{0,4},{1,5},{2,6},{3,7},{4,0},{5,1},{6,2},{7,3},{8,12},{9,13},{10,... | collective-permute-start | bytes 98312 | tf_op jit(solution)/shard_map/ppermute | solution.py:64
  13.5 1.1 collective-permute-start.2
  14.8 2.0 %collective-permute-done.2 = bf16[16,1024]{1,0:T(8,128)(2,1)S(1)} collective-permute-done((bf16[16,1024]{1,0:T(8,128)(2,1)S(1)}, bf16[16,1024]{1,0:T(8,128)(2,1)S(1)}, u32[]{:S(2)}, u32[]{:S(2)}) %collective-permute-start.2) | collective-permute-done | bytes 32800 | tf_op jit(solution)/shard_map/ppermute | solution.py:64
  16.9 1.3 collective-permute-start.3
  18.3 1.3 collective-permute-start.5
  20.3 2.3 %shard_map.138 = bf16[8,64,1024]{2,1,0:T(8,128)(2,1)} custom-call(s32[5]{0:T(128)S(1)} %stack.53.place, s32[1,64]{1,0:T(1,128)S(1)} %bitcast.28, bf16[4752,8192]{1,0:T(8,128)(2,1)} %weight.3), custom_call_target="tpu_custom_call" | custom-call | bytes 16777216 | tf_op jit(solution)/shard_map/pallas_call | solution.py:629
  23.7 3.3 %collective-permute-start.6 = (bf16[4,4,16,1024]{3,2,1,0:T(8,128)(2,1)S(1)}, bf16[4,4,16,1024]{3,2,1,0:T(8,128)(2,1)S(1)}, u32[]{:S(2)}, u32[]{:S(2)}) collective-permute-start(bf16[4,4,16,1024]{3,2,1,0:T(8,128)(2,1)S(1)} %pad_maximum_fusion.own), channel_id=1, source_target_pairs={{0,1},{1,0},{2,3},{3,2},{4,5},{5,4},{6,7},{7,6},{8,9},{9,8},{10,11... | collective-permute-start | bytes 1572872 | tf_op jit(solution)/shard_map/ppermute | solution.py:74
  27.2 1.4 %shard_map.139 = bf16[160,512]{1,0:T(8,128)(2,1)} custom-call(s32[5]{0:T(128)S(1)} %stack.53.place, s32[64]{0:T(128)S(1)} %copy-done.9, bf16[128,2048]{1,0:T(8,128)(2,1)S(1)} %copy-done.2, bf16[128,256]{1,0:T(8,128)(2,1)S(1)} %copy-done.5, bf16[128,256]{1,0:T(8,128)(2,1)S(1)} %copy-done.6), custom_call_target="tpu_custom_call" | custom-call | bytes 524288 | tf_op jit(solution)/shard_map/pallas_call | solution.py:614
  28.6 46.7 %shard_map.140 = (f32[4,64,1024]{2,1,0:T(8,128)S(1)}, bf16[64,4224]{1,0:T(8,128)(2,1)S(1)}, f32[64,128]{1,0:T(8,128)S(1)}, f32[16,1024]{1,0:T(8,128)S(1)}) custom-call(s32[5]{0:T(128)S(1)} %stack.53.place, bf16[4,4,16,1024]{3,2,1,0:T(8,128)(2,1)S(1)} %pad_maximum_fusion.own, bf16[4,4,16,1024]{3,2,1,0:T(8,128)(2,1)S(1)} %collective-permute-done.6.other, ...), custom_call_target="tpu_custom_call" | custom-call | flops 39862665216 | bytes 155713536 | tf_op jit(solution)/shard_map/pallas_call | solution.py:658
  75.9 1.6 %collective-permute-done.7.got = bf16[64,4224]{1,0:T(8,128)(2,1)S(1)} collective-permute-done((bf16[64,4224]{1,0:T(8,128)(2,1)S(1)}, bf16[64,4224]{1,0:T(8,128)(2,1)S(1)}, u32[]{:S(2)}, u32[]{:S(2)}) %collective-permute-start.7) | collective-permute-done | bytes 540704 | tf_op jit(solution)/shard_map/ppermute | solution.py:74
  78.3 1.3 shard_map.141
  79.6 1.4 collective-permute-start.10
  82.0 1.1 collective-permute-start.9
  83.3 2.8 %collective-permute-done.10.rest_2_ = bf16[16,5248]{1,0:T(8,128)(2,1)S(1)} collective-permute-done((bf16[16,5248]{1,0:T(8,128)(2,1)S(1)}, bf16[16,5248]{1,0:T(8,128)(2,1)S(1)}, u32[]{:S(2)}, u32[]{:S(2)}) %collective-permute-start.10) | collective-permute-done | bytes 167968 | tf_op jit(solution)/shard_map/ppermute | solution.py:64
  86.1 3.6 %collective-permute-done.8.rest_0_ = bf16[16,5248]{1,0:T(8,128)(2,1)S(1)} collective-permute-done((bf16[16,5248]{1,0:T(8,128)(2,1)S(1)}, bf16[16,5248]{1,0:T(8,128)(2,1)S(1)}, u32[]{:S(2)}, u32[]{:S(2)}) %collective-permute-start.8) | collective-permute-done | bytes 167968 | tf_op jit(solution)/shard_map/ppermute | solution.py:64
  91.6 3.2 %collective-permute-start.12 = (bf16[16,1152]{1,0:T(8,128)(2,1)S(1)}, bf16[16,1152]{1,0:T(8,128)(2,1)S(1)}, u32[]{:S(2)}, u32[]{:S(2)}) collective-permute-start(bf16[16,1152]{1,0:T(8,128)(2,1)S(1)} %get-tuple-element.87), channel_id=1, source_target_pairs={{0,4},{1,5},{2,6},{3,7},{4,0},{5,1},{6,2},{7,3},{8,12},{9,13},{10,... | collective-permute-start | bytes 110600 | tf_op jit(solution)/shard_map/ppermute | solution.py:64
  94.9 1.2 collective-permute-done.11.rest_0_
  96.1 2.1 %collective-permute-done.12.rest_1_ = bf16[16,1152]{1,0:T(8,128)(2,1)S(1)} collective-permute-done((bf16[16,1152]{1,0:T(8,128)(2,1)S(1)}, bf16[16,1152]{1,0:T(8,128)(2,1)S(1)}, u32[]{:S(2)}, u32[]{:S(2)}) %collective-permute-start.12) | collective-permute-done | bytes 36896 | tf_op jit(solution)/shard_map/ppermute | solution.py:64
  99.2 1.1 collective-permute-start.15
  100.3 1.4 collective-permute-start.16
  102.1 2.0 %collective-permute-done.16.refs_3_ = bf16[16,1152]{1,0:T(8,128)(2,1)S(1)} collective-permute-done((bf16[16,1152]{1,0:T(8,128)(2,1)S(1)}, bf16[16,1152]{1,0:T(8,128)(2,1)S(1)}, u32[]{:S(2)}, u32[]{:S(2)}) %collective-permute-start.16) | collective-permute-done | bytes 36896 | tf_op jit(solution)/shard_map/ppermute | solution.py:64
  104.0 2.2 %copy-done = bf16[2048,1024]{1,0:T(8,128)(2,1)S(1)} copy-done((bf16[2048,1024]{1,0:T(8,128)(2,1)S(1)}, bf16[2048,1024]{1,0:T(8,128)(2,1)}, u32[]{:S(2)}) %copy-start) | copy-done | bytes 4194328
  106.2 2.9 %shard_map.144 = (bf16[64,1024]{1,0:T(8,128)(2,1)}, f32[1,1]{1,0:T(1,128)}, f32[64,1024]{1,0:T(8,128)S(1)}, bf16[64,1024]{1,0:T(8,128)(2,1)S(1)}) custom-call(s32[5]{0:T(128)S(1)} %stack.53.place, bf16[16,1152]{1,0:T(8,128)(2,1)S(1)} %shard_map.143.refs_0_, bf16[16,1152]{1,0:T(8,128)(2,1)S(1)} %collective-permute-done.14.refs_1_, ...), custom_call_target="tpu_custom_call" | custom-call | tf_op jit(solution)/shard_map/pallas_call | solution.py:747
  109.2 4.7 %collective-permute-start.17 = (bf16[64,1024]{1,0:T(8,128)(2,1)S(1)}, bf16[64,1024]{1,0:T(8,128)(2,1)S(1)}, u32[]{:S(2)}, u32[]{:S(2)}) collective-permute-start(bf16[64,1024]{1,0:T(8,128)(2,1)S(1)} %get-tuple-element.91), channel_id=1, source_target_pairs={{0,1},{1,0},{2,3},{3,2},{4,5},{5,4},{6,7},{7,6},{8,9},{9,8},{10,11... | collective-permute-start | bytes 393224 | tf_op jit(solution)/shard_map/ppermute | solution.py:74
  115.9 2.8 %shard_map.146 = (f32[512,128]{1,0:T(8,128)S(1)}, f32[64,1024]{1,0:T(8,128)S(1)}, f32[512,128]{1,0:T(8,128)S(1)}) custom-call(s32[5]{0:T(128)S(1)} %stack.53.place, s32[1,1024]{1,0:T(1,128)S(1)} %add.63.key_pos, s32[64,1]{1,0:T(8,128)S(1)} %copy.19.query_pos, bf16[8,160,512]{2,1,0:T(8,128)(2,1)S(1)} %bitcast.22), custom_call_target="tpu_custom_call" | custom-call | flops 1610612736 | bytes 1310720 | tf_op jit(solution)/shard_map/pallas_call | solution.py:711
  119.7 1.2 collective-permute-start.19
  121.1 2.8 %shard_map.148 = (f32[512,128]{1,0:T(8,128)S(1)}, f32[64,1024]{1,0:T(8,128)S(1)}, f32[512,128]{1,0:T(8,128)S(1)}) custom-call(s32[5]{0:T(128)S(1)} %stack.53.place, s32[1,1024]{1,0:T(1,128)S(1)} %add.63.key_pos, s32[64,1]{1,0:T(8,128)S(1)} %copy.20.query_pos, bf16[8,160,512]{2,1,0:T(8,128)(2,1)S(1)} %bitcast.23), custom_call_target="tpu_custom_call" | custom-call | flops 1610612736 | bytes 1310720 | tf_op jit(solution)/shard_map/pallas_call | solution.py:711
  123.9 4.4 %collective-permute-done.19.refs_0_ = bf16[64,1024]{1,0:T(8,128)(2,1)S(1)} collective-permute-done((bf16[64,1024]{1,0:T(8,128)(2,1)S(1)}, bf16[64,1024]{1,0:T(8,128)(2,1)S(1)}, u32[]{:S(2)}, u32[]{:S(2)}) %collective-permute-start.19) | collective-permute-done | bytes 131104 | tf_op jit(solution)/shard_map/ppermute | solution.py:69
  128.3 1.2 collective-permute-start.20
  130.5 2.3 %shard_map.150 = (bf16[8,2048]{1,0:T(8,128)(2,1)}, bf16[128,256]{1,0:T(8,128)(2,1)}, bf16[128,256]{1,0:T(8,128)(2,1)}) custom-call(s32[5]{0:T(128)S(1)} %stack.53.place, bf16[64,1024]{1,0:T(8,128)(2,1)S(1)} %shard_map.149.half, bf16[64,1024]{1,0:T(8,128)(2,1)S(1)} %collective-permute-done.20.other, bf16[8,160,512]{2,1,0:T(8,128)(2,1)S(1)} %bitcast.24, ...), custom_call_target="tpu_custom_call" | custom-call | tf_op jit(solution)/shard_map/pallas_call | solution.py:776
  (68 shorter events, 14.0 us)
Async XLA Ops:
  7.2 68.3 %reduce-scatter.2.cloned.1.call-start = ((), (), s32[]{:S(2)}) async-start(), calls=%async_computation.1 | async-start | bytes 1179648 | tf_op jit(solution)/shard_map/reduce_scatter | solution.py:647
  9.8 4.7 %collective-permute-start = (bf16[16,1024]{1,0:T(8,128)(2,1)S(1)}, bf16[16,1024]{1,0:T(8,128)(2,1)S(1)}, u32[]{:S(2)}, u32[]{:S(2)}) collective-permute-start(bf16[16,1024]{1,0:T(8,128)(2,1)S(1)} %shard_map.137), channel_id=1, source_target_pairs={{0,2},{1,3},{2,4},{3,5},{4,6},{5,7},{6,0},{7,1},{8,10},{9,11},{10,... | collective-permute-start | bytes 98312 | tf_op jit(solution)/shard_map/ppermute | solution.py:64
  11.2 3.7 %collective-permute-start.1 = (bf16[16,1024]{1,0:T(8,128)(2,1)S(1)}, bf16[16,1024]{1,0:T(8,128)(2,1)S(1)}, u32[]{:S(2)}, u32[]{:S(2)}) collective-permute-start(bf16[16,1024]{1,0:T(8,128)(2,1)S(1)} %shard_map.137), channel_id=1, source_target_pairs={{0,4},{1,5},{2,6},{3,7},{4,0},{5,1},{6,2},{7,3},{8,12},{9,13},{10,... | collective-permute-start | bytes 98312 | tf_op jit(solution)/shard_map/ppermute | solution.py:64
  13.5 3.4 %collective-permute-start.2 = (bf16[16,1024]{1,0:T(8,128)(2,1)S(1)}, bf16[16,1024]{1,0:T(8,128)(2,1)S(1)}, u32[]{:S(2)}, u32[]{:S(2)}) collective-permute-start(bf16[16,1024]{1,0:T(8,128)(2,1)S(1)} %shard_map.137), channel_id=1, source_target_pairs={{0,6},{1,7},{2,0},{3,1},{4,2},{5,3},{6,4},{7,5},{8,14},{9,15},{10,... | collective-permute-start | bytes 98312 | tf_op jit(solution)/shard_map/ppermute | solution.py:64
  16.9 5.7 %collective-permute-start.3 = (bf16[4,16,1024]{2,1,0:T(8,128)(2,1)S(1)}, bf16[4,16,1024]{2,1,0:T(8,128)(2,1)S(1)}, u32[]{:S(2)}, u32[]{:S(2)}) collective-permute-start(bf16[4,16,1024]{2,1,0:T(8,128)(2,1)S(1)} %pad_maximum_fusion.1), channel_id=1, source_target_pairs={{0,8},{8,16},{16,24},{24,0},{1,9},{9,17},{17,25},{25,1},{2,10},{10... | collective-permute-start | bytes 393224 | tf_op jit(solution)/shard_map/ppermute | solution.py:64
  18.1 5.3 %collective-permute-start.4 = (bf16[4,16,1024]{2,1,0:T(8,128)(2,1)S(1)}, bf16[4,16,1024]{2,1,0:T(8,128)(2,1)S(1)}, u32[]{:S(2)}, u32[]{:S(2)}) collective-permute-start(bf16[4,16,1024]{2,1,0:T(8,128)(2,1)S(1)} %pad_maximum_fusion.1), channel_id=1, source_target_pairs={{0,16},{8,24},{16,0},{24,8},{1,17},{9,25},{17,1},{25,9},{2,18},{10... | collective-permute-start | bytes 393224 | tf_op jit(solution)/shard_map/ppermute | solution.py:64
  18.3 5.2 %collective-permute-start.5 = (bf16[4,16,1024]{2,1,0:T(8,128)(2,1)S(1)}, bf16[4,16,1024]{2,1,0:T(8,128)(2,1)S(1)}, u32[]{:S(2)}, u32[]{:S(2)}) collective-permute-start(bf16[4,16,1024]{2,1,0:T(8,128)(2,1)S(1)} %pad_maximum_fusion.1), channel_id=1, source_target_pairs={{0,24},{8,0},{16,8},{24,16},{1,25},{9,1},{17,9},{25,17},{2,26},{10... | collective-permute-start | bytes 393224 | tf_op jit(solution)/shard_map/ppermute | solution.py:64
  20.3 6.8 %copy-start.11 = (s32[64]{0:T(128)S(1)}, s32[64]{0:T(128)}, u32[]{:S(2)}) copy-start(s32[64]{0:T(128)} %param.13) | copy-start | bytes 772
  20.3 6.9 %copy-start.2 = (bf16[128,2048]{1,0:T(8,128)(2,1)S(1)}, bf16[128,2048]{1,0:T(8,128)(2,1)}, u32[]{:S(2)}) copy-start(bf16[128,2048]{1,0:T(8,128)(2,1)} %queries) | copy-start | bytes 1572868
  20.3 6.9 %copy-start.5 = (bf16[128,256]{1,0:T(8,128)(2,1)S(1)}, bf16[128,256]{1,0:T(8,128)(2,1)}, u32[]{:S(2)}) copy-start(bf16[128,256]{1,0:T(8,128)(2,1)} %keys.1) | copy-start | bytes 196612
  20.3 6.9 %copy-start.6 = (bf16[128,256]{1,0:T(8,128)(2,1)S(1)}, bf16[128,256]{1,0:T(8,128)(2,1)}, u32[]{:S(2)}) copy-start(bf16[128,256]{1,0:T(8,128)(2,1)} %values.1) | copy-start | bytes 196612
  20.3 6.9 %copy-start.9 = (s32[64]{0:T(128)S(1)}, s32[64]{0:T(128)}, u32[]{:S(2)}) copy-start(s32[64]{0:T(128)} %rows.3) | copy-start | bytes 772
  20.3 8.3 %copy-start.7 = (f32[8192]{0:T(1024)S(1)}, f32[8192]{0:T(1024)}, u32[]{:S(2)}) copy-start(f32[8192]{0:T(1024)} %param.11) | copy-start | bytes 98308
  23.6 59.7 %all-gather.3.cloned.1.call-start = ((), (), s32[]{:S(2)}) async-start(), calls=%async_computation.2 | async-start | bytes 1474560 | tf_op jit(solution)/shard_map/all_gather | solution.py:651
  23.7 4.9 %collective-permute-start.6 = (bf16[4,4,16,1024]{3,2,1,0:T(8,128)(2,1)S(1)}, bf16[4,4,16,1024]{3,2,1,0:T(8,128)(2,1)S(1)}, u32[]{:S(2)}, u32[]{:S(2)}) collective-permute-start(bf16[4,4,16,1024]{3,2,1,0:T(8,128)(2,1)S(1)} %pad_maximum_fusion.own), channel_id=1, source_target_pairs={{0,1},{1,0},{2,3},{3,2},{4,5},{5,4},{6,7},{7,6},{8,9},{9,8},{10,11... | collective-permute-start | bytes 1572872 | tf_op jit(solution)/shard_map/ppermute | solution.py:74
  28.6 47.2 %copy-start.12 = (s32[16]{0:T(128)S(1)}, s32[16]{0:T(128)}, u32[]{:S(2)}) copy-start(s32[16]{0:T(128)} %param.15) | copy-start | bytes 196
  75.4 2.0 %collective-permute-start.7 = (bf16[64,4224]{1,0:T(8,128)(2,1)S(1)}, bf16[64,4224]{1,0:T(8,128)(2,1)S(1)}, u32[]{:S(2)}, u32[]{:S(2)}) collective-permute-start(bf16[64,4224]{1,0:T(8,128)(2,1)S(1)} %get-tuple-element.71), channel_id=1, source_target_pairs={{0,1},{1,0},{2,3},{3,2},{4,5},{5,4},{6,7},{7,6},{8,9},{9,8},{10,11... | collective-permute-start | bytes 1622024 | tf_op jit(solution)/shard_map/ppermute | solution.py:74
  79.6 6.4 %collective-permute-start.10 = (bf16[16,5248]{1,0:T(8,128)(2,1)S(1)}, bf16[16,5248]{1,0:T(8,128)(2,1)S(1)}, u32[]{:S(2)}, u32[]{:S(2)}) collective-permute-start(bf16[16,5248]{1,0:T(8,128)(2,1)S(1)} %get-tuple-element.81), channel_id=1, source_target_pairs={{0,24},{8,0},{16,8},{24,16},{1,25},{9,1},{17,9},{25,17},{2,26},{10... | collective-permute-start | bytes 503816 | tf_op jit(solution)/shard_map/ppermute | solution.py:64
  81.0 8.6 %collective-permute-start.8 = (bf16[16,5248]{1,0:T(8,128)(2,1)S(1)}, bf16[16,5248]{1,0:T(8,128)(2,1)S(1)}, u32[]{:S(2)}, u32[]{:S(2)}) collective-permute-start(bf16[16,5248]{1,0:T(8,128)(2,1)S(1)} %get-tuple-element.79), channel_id=1, source_target_pairs={{0,8},{8,16},{16,24},{24,0},{1,9},{9,17},{17,25},{25,1},{2,10},{10... | collective-permute-start | bytes 503816 | tf_op jit(solution)/shard_map/ppermute | solution.py:64
  82.0 8.3 %collective-permute-start.9 = (bf16[16,5248]{1,0:T(8,128)(2,1)S(1)}, bf16[16,5248]{1,0:T(8,128)(2,1)S(1)}, u32[]{:S(2)}, u32[]{:S(2)}) collective-permute-start(bf16[16,5248]{1,0:T(8,128)(2,1)S(1)} %get-tuple-element.80), channel_id=1, source_target_pairs={{0,16},{8,24},{16,0},{24,8},{1,17},{9,25},{17,1},{25,9},{2,18},{10... | collective-permute-start | bytes 503816 | tf_op jit(solution)/shard_map/ppermute | solution.py:64
  91.4 4.7 %collective-permute-start.11 = (bf16[16,1152]{1,0:T(8,128)(2,1)S(1)}, bf16[16,1152]{1,0:T(8,128)(2,1)S(1)}, u32[]{:S(2)}, u32[]{:S(2)}) collective-permute-start(bf16[16,1152]{1,0:T(8,128)(2,1)S(1)} %get-tuple-element.86), channel_id=1, source_target_pairs={{0,2},{1,3},{2,4},{3,5},{4,6},{5,7},{6,0},{7,1},{8,10},{9,11},{10,... | collective-permute-start | bytes 110600 | tf_op jit(solution)/shard_map/ppermute | solution.py:64
  91.6 6.6 %collective-permute-start.12 = (bf16[16,1152]{1,0:T(8,128)(2,1)S(1)}, bf16[16,1152]{1,0:T(8,128)(2,1)S(1)}, u32[]{:S(2)}, u32[]{:S(2)}) collective-permute-start(bf16[16,1152]{1,0:T(8,128)(2,1)S(1)} %get-tuple-element.87), channel_id=1, source_target_pairs={{0,4},{1,5},{2,6},{3,7},{4,0},{5,1},{6,2},{7,3},{8,12},{9,13},{10,... | collective-permute-start | bytes 110600 | tf_op jit(solution)/shard_map/ppermute | solution.py:64
  94.9 3.3 %collective-permute-start.13 = (bf16[16,1152]{1,0:T(8,128)(2,1)S(1)}, bf16[16,1152]{1,0:T(8,128)(2,1)S(1)}, u32[]{:S(2)}, u32[]{:S(2)}) collective-permute-start(bf16[16,1152]{1,0:T(8,128)(2,1)S(1)} %get-tuple-element.88), channel_id=1, source_target_pairs={{0,6},{1,7},{2,0},{3,1},{4,2},{5,3},{6,4},{7,5},{8,14},{9,15},{10,... | collective-permute-start | bytes 110600 | tf_op jit(solution)/shard_map/ppermute | solution.py:64
  99.1 2.9 %collective-permute-start.14 = (bf16[16,1152]{1,0:T(8,128)(2,1)S(1)}, bf16[16,1152]{1,0:T(8,128)(2,1)S(1)}, u32[]{:S(2)}, u32[]{:S(2)}) collective-permute-start(bf16[16,1152]{1,0:T(8,128)(2,1)S(1)} %shard_map.143.refs_0_), channel_id=1, source_target_pairs={{0,8},{8,16},{16,24},{24,0},{1,9},{9,17},{17,25},{25,1},{2,10},{10... | collective-permute-start | bytes 110600 | tf_op jit(solution)/shard_map/ppermute | solution.py:64
  99.2 2.9 %collective-permute-start.15 = (bf16[16,1152]{1,0:T(8,128)(2,1)S(1)}, bf16[16,1152]{1,0:T(8,128)(2,1)S(1)}, u32[]{:S(2)}, u32[]{:S(2)}) collective-permute-start(bf16[16,1152]{1,0:T(8,128)(2,1)S(1)} %shard_map.143.refs_0_), channel_id=1, source_target_pairs={{0,16},{8,24},{16,0},{24,8},{1,17},{9,25},{17,1},{25,9},{2,18},{10... | collective-permute-start | bytes 110600 | tf_op jit(solution)/shard_map/ppermute | solution.py:64
  100.3 3.7 %collective-permute-start.16 = (bf16[16,1152]{1,0:T(8,128)(2,1)S(1)}, bf16[16,1152]{1,0:T(8,128)(2,1)S(1)}, u32[]{:S(2)}, u32[]{:S(2)}) collective-permute-start(bf16[16,1152]{1,0:T(8,128)(2,1)S(1)} %shard_map.143.refs_0_), channel_id=1, source_target_pairs={{0,24},{8,0},{16,8},{24,16},{1,25},{9,1},{17,9},{25,17},{2,26},{10... | collective-permute-start | bytes 110600 | tf_op jit(solution)/shard_map/ppermute | solution.py:64
  104.0 2.2 %copy-start = (bf16[2048,1024]{1,0:T(8,128)(2,1)S(1)}, bf16[2048,1024]{1,0:T(8,128)(2,1)}, u32[]{:S(2)}) copy-start(bf16[2048,1024]{1,0:T(8,128)(2,1)} %refs_4_.1) | copy-start | bytes 12582916
  106.2 9.7 %copy-start.1 = (bf16[1280,512]{1,0:T(8,128)(2,1)S(1)}, bf16[1280,512]{1,0:T(8,128)(2,1)}, u32[]{:S(2)}) copy-start(bf16[1280,512]{1,0:T(8,128)(2,1)} %all-gather.3.cloned.1.call-done) | copy-start | bytes 3932164
  109.2 5.7 %collective-permute-start.17 = (bf16[64,1024]{1,0:T(8,128)(2,1)S(1)}, bf16[64,1024]{1,0:T(8,128)(2,1)S(1)}, u32[]{:S(2)}, u32[]{:S(2)}) collective-permute-start(bf16[64,1024]{1,0:T(8,128)(2,1)S(1)} %get-tuple-element.91), channel_id=1, source_target_pairs={{0,1},{1,0},{2,3},{3,2},{4,5},{5,4},{6,7},{7,6},{8,9},{9,8},{10,11... | collective-permute-start | bytes 393224 | tf_op jit(solution)/shard_map/ppermute | solution.py:74
  114.9 4.8 %collective-permute-start.18 = (bf16[64,1024]{1,0:T(8,128)(2,1)S(1)}, bf16[64,1024]{1,0:T(8,128)(2,1)S(1)}, u32[]{:S(2)}, u32[]{:S(2)}) collective-permute-start(bf16[64,1024]{1,0:T(8,128)(2,1)S(1)} %shard_map.145.keep), channel_id=1, source_target_pairs={{0,2},{1,3},{2,0},{3,1},{4,6},{5,7},{6,4},{7,5},{8,10},{9,11},{10,... | collective-permute-start | bytes 393224 | tf_op jit(solution)/shard_map/ppermute | solution.py:69
  119.7 8.6 %collective-permute-start.19 = (bf16[64,1024]{1,0:T(8,128)(2,1)S(1)}, bf16[64,1024]{1,0:T(8,128)(2,1)S(1)}, u32[]{:S(2)}, u32[]{:S(2)}) collective-permute-start(bf16[64,1024]{1,0:T(8,128)(2,1)S(1)} %shard_map.147.keep), channel_id=1, source_target_pairs={{0,4},{1,5},{2,6},{3,7},{4,0},{5,1},{6,2},{7,3},{8,12},{9,13},{10,... | collective-permute-start | bytes 393224 | tf_op jit(solution)/shard_map/ppermute | solution.py:69
  128.3 2.2 %collective-permute-start.20 = (bf16[64,1024]{1,0:T(8,128)(2,1)S(1)}, bf16[64,1024]{1,0:T(8,128)(2,1)S(1)}, u32[]{:S(2)}, u32[]{:S(2)}) collective-permute-start(bf16[64,1024]{1,0:T(8,128)(2,1)S(1)} %shard_map.149.half), channel_id=1, source_target_pairs={{0,1},{1,0},{2,3},{3,2},{4,5},{5,4},{6,7},{7,6},{8,9},{9,8},{10,11... | collective-permute-start | bytes 393224 | tf_op jit(solution)/shard_map/ppermute | solution.py:74
  (4 other events, 3.3 us)
Sparse Core Ops, SparseCore 0:
  23.7 32.5 reduce-scatter.1
  58.0 25.2 all-gather.2

commit v9 on v8

--- a/solution.py
+++ b/solution.py
@@ -352,10 +352,8 @@
 
 
 def core_body(count, place, keep, got, mine, target_rows, new_stats, new_keep, new_rows, *rest):
-    sends, (total, table, message, rows_here, sem) = rest[:count], rest[count:]
+    sends, (total, table, message) = rest[:count], rest[count:]
     nz, loss, block = keep.shape
-    rows_copy = pltpu.make_async_copy(target_rows, rows_here, sem)
-    rows_copy.start()
     columns = [stats_of(mine[...]), joined_columns(got[:, nz * block :], 4)]
     scales, merged = merge_stats(columns)
     table[...] = with_stats(mine[...], merged)
@@ -373,12 +371,11 @@
         for z in range(nz):
             sends[s][:, z * block : (z + 1) * block] = total[z, rows, :].astype(bf16)
         sends[s][:, (nz + 1) * block :] = message[rows, :]
-    rows_copy.wait()
     for s in range(count):
         to = lax.rem(place[0] + s + 1, count + 1)
         rows = pl.ds(pl.multiple_of(to * per, per), per)
-        sends[s][:, nz * block : (nz + 1) * block] = rows_here[rows, :]
-    new_rows[...] = rows_here[pl.ds(at, per), :]
+        sends[s][:, nz * block : (nz + 1) * block] = target_rows[rows, :]
+    new_rows[...] = target_rows[pl.ds(at, per), :]
 
 
 def plane_body(count, place, keep, mine, target_rows, *rest):
@@ -426,14 +423,7 @@
 
 def project_body(nv, place, *refs):
     gathered, refs = refs[:nv], refs[nv:]
-    weight, resid, loss_out, keep, send, whole, partial, here, sems = refs
-    parts, part, _ = here.shape
-    copies = [
-        pltpu.make_async_copy(weight.at[pl.ds(k * part, part), :], here.at[k], sems.at[k])
-        for k in range(parts)
-    ]
-    for copy in copies:
-        copy.start()
+    weight, resid, loss_out, keep, send, whole, partial = refs
     per = gathered[0].shape[0]
     block = whole.shape[1]
     loss_sum = jnp.zeros((1, 1), f32)
@@ -444,12 +434,26 @@
         loss_sum = loss_sum + jnp.sum(column, axis=0, keepdims=True)
     loss_out[...] = loss_sum / (nv * per)
     resid[...] = whole[...]
-    for k in range(parts):
-        copies[k].wait()
-        partial[:, k * part : (k + 1) * part] = dot(whole[...], here[k], NT)
+    partial[...] = dot(whole[...], weight[...], NT)
     cols = keep.shape[1]
     keep[...] = partial[:, pl.ds(pl.multiple_of(place[2] * cols, cols), cols)]
     send[...] = partial[:, pl.ds(pl.multiple_of((1 - place[2]) * cols, cols), cols)].astype(bf16)
+
+
+def stage_body(source, staged, sem):
+    copy = pltpu.make_async_copy(source, staged, sem)
+    copy.start()
+    copy.wait()
+
+
+def staged(value):
+    return call(
+        stage_body,
+        shape(value.shape, value.dtype),
+        [hbm()],
+        [pltpu.SemaphoreType.DMA],
+        moved=2 * value.size * value.dtype.itemsize,
+    )(value)
 
 
 def sum_body(keep, *refs):
@@ -676,7 +680,7 @@
             pltpu.SemaphoreType.DMA,
             pltpu.SemaphoreType.DMA((SLOTS,)),
         ],
-        compiler_params=pltpu.CompilerParams(vmem_limit_bytes=50 * 2**20),
+        compiler_params=pltpu.CompilerParams(vmem_limit_bytes=45 * 2**20),
         cost_estimate=pl.CostEstimate(
             flops=4 * max(loss, 256) * width * voc_rows,
             bytes_accessed=4 * width * voc_rows,
@@ -686,6 +690,7 @@
 
     send, target_rows = lax.optimization_barrier((send, target_rows))
     got = swapped(send)
+    target_rows = staged(target_rows)
     stats, keep, target_rows, *sends = call(
         functools.partial(core_body, nv - 1),
         (
@@ -694,13 +699,11 @@
             shape((per_vocab, block_width), bf16),
         )
         + (shape((per_vocab, (nz + 1) * block_width + LANES), bf16),) * (nv - 1),
-        [smem()] + [vmem()] * 3 + [hbm()],
+        [smem()] + [vmem()] * 4,
         [
             pltpu.VMEM((nz, loss, block_width), f32),
             pltpu.VMEM((loss, LANES), f32),
             pltpu.VMEM((loss, LANES), bf16),
-            pltpu.VMEM((loss, block_width), bf16),
-            pltpu.SemaphoreType.DMA,
         ],
     )(place, keep, got, stats, target_rows)
     got = [shifted(sends[s - 1], "vocab", s) for s in range(1, nv)]
@@ -723,7 +726,9 @@
             exps=group * loss * all_tokens,
         )(place, key_pos, query_pos, packed_all)
 
-    stats, packed_all = lax.optimization_barrier((stats, packed_all))
+    stats, output_weight = lax.optimization_barrier((stats, output_weight))
+    weight_here = staged(output_weight)
+    stats, packed_all, weight_here = lax.optimization_barrier((stats, packed_all, weight_here))
     stats, keep, target_rows, *sends = call(
         functools.partial(plane_body, nv - 1),
         (
@@ -752,14 +757,9 @@
             shape((loss, cols), f32),
             shape((loss, cols), bf16),
         ),
-        [smem()] + [vmem()] * nv + [hbm()],
-        [
-            pltpu.VMEM((loss, block_width), bf16),
-            pltpu.VMEM((loss, query_width), f32),
-            pltpu.VMEM((4, query_width // 4, block_width), bf16),
-            pltpu.SemaphoreType.DMA((4,)),
-        ],
-    )(place, *gathered, output_weight)
+        [smem()] + [vmem()] * (nv + 1),
+        [pltpu.VMEM((loss, block_width), bf16), pltpu.VMEM((loss, query_width), f32)],
+    )(place, *gathered, weight_here)
     half = call(sum_body, shape((loss, cols), bf16), [vmem()] * 2)(keep, swapped(send))
     windows = nz.bit_length() - 1
     attention = [None] * heads

time: 140 us -> 139 us (level)
  waiting for transfers between devices: 24.8 us -> 17.7 us
  local copies, waits for them, and re-layouts: 5.93 us -> 10.1 us
    ppermute x15, waiting for transfers between devices: 15.9 us -> 10.7 us  [shifted(): return lax.ppermute(value, axis, pairs)]
    unnamed x26 -> x30, local copies, waits for them, and re-layouts: 5.48 us -> 9.64 us
  transfers between devices with their start and end apart: 23 -> 23, of which waited for: 17 -> 13; matrix products, arithmetic and copies ran while one was open for 0% -> 0% of each run, Pallas kernels for 41% -> 42%
where the time goes in v9:
time: 139 us; the launch traced here: 138 us
  Pallas kernels  66.4 us (48%)
  starting transfers between devices  29.8 us (21%)
  waiting for transfers between devices  17.7 us (13%)
  between operations  14.3 us (10%)
  local copies, waits for them, and re-layouts  10.1 us (7%)
    pallas_call x1, Pallas kernels, per_device(): pl.pallas_call(functools.partial(flash_body, first), out_shape=(shape((nz...  46.7 us
    ppermute x15, starting transfers between devices, shifted(): return lax.ppermute(value, axis, pairs)  17.4 us
    ppermute x15, waiting for transfers between devices, shifted(): return lax.ppermute(value, axis, pairs)  10.7 us
    unnamed x30, local copies, waits for them, and re-layouts  9.64 us
    ppermute x4, starting transfers between devices, swapped(): return lax.ppermute(value, 'ctx', [(i, i ^ 1) for i in range(size)])  8.91 us
    pallas_call x2, Pallas kernels, forward(): call(functools.partial(forward_body, loss_per, heads, group, at_once, j),...  5.6 us
    ppermute x2, waiting for transfers between devices, crossed(): lax.ppermute(value, 'ctx', [(i, i ^ bit * CORES) for i in range(size)])  4.48 us
    pallas_call x1, Pallas kernels, per_device(): pl.pallas_call(target_body, out_shape=shape((nc, loss, block_width), bf16...  3.56 us
  transfers between devices with their start and end apart: 23, of which 13 were waited for; matrix products, arithmetic and copies ran while one was open for 0% of the time, Pallas kernels for 42%

profile of v9, /device:TPU:3, one launch (start us, length us, event | category | flops | bytes accessed | tf_op | source)
XLA Modules:
  0.0 138.5 jit_solution(2110820738663491254)
XLA Ops:
  7.3 1.0 copy-done.5
  9.8 1.3 collective-permute-start
  11.2 2.3 %collective-permute-start.1 = (bf16[16,1024]{1,0:T(8,128)(2,1)S(1)}, bf16[16,1024]{1,0:T(8,128)(2,1)S(1)}, u32[]{:S(2)}, u32[]{:S(2)}) collective-permute-start(bf16[16,1024]{1,0:T(8,128)(2,1)S(1)} %shard_map.137), channel_id=1, source_target_pairs={{0,4},{1,5},{2,6},{3,7},{4,0},{5,1},{6,2},{7,3},{8,12},{9,13},{10,... | collective-permute-start | bytes 98312 | tf_op jit(solution)/shard_map/ppermute | solution.py:64
  13.5 1.1 collective-permute-start.2
  14.8 2.0 %collective-permute-done.2 = bf16[16,1024]{1,0:T(8,128)(2,1)S(1)} collective-permute-done((bf16[16,1024]{1,0:T(8,128)(2,1)S(1)}, bf16[16,1024]{1,0:T(8,128)(2,1)S(1)}, u32[]{:S(2)}, u32[]{:S(2)}) %collective-permute-start.2) | collective-permute-done | bytes 32800 | tf_op jit(solution)/shard_map/ppermute | solution.py:64
  16.9 1.3 collective-permute-start.3
  18.3 1.3 collective-permute-start.5
  20.3 3.6 %shard_map.138 = bf16[8,64,1024]{2,1,0:T(8,128)(2,1)} custom-call(s32[5]{0:T(128)S(1)} %stack.53.place, s32[1,64]{1,0:T(1,128)S(1)} %bitcast.28, bf16[4752,8192]{1,0:T(8,128)(2,1)} %weight.3), custom_call_target="tpu_custom_call" | custom-call | bytes 16777216 | tf_op jit(solution)/shard_map/pallas_call | solution.py:633
  24.1 3.0 %collective-permute-start.6 = (bf16[4,4,16,1024]{3,2,1,0:T(8,128)(2,1)S(1)}, bf16[4,4,16,1024]{3,2,1,0:T(8,128)(2,1)S(1)}, u32[]{:S(2)}, u32[]{:S(2)}) collective-permute-start(bf16[4,4,16,1024]{3,2,1,0:T(8,128)(2,1)S(1)} %pad_maximum_fusion.own), channel_id=1, source_target_pairs={{0,1},{1,0},{2,3},{3,2},{4,5},{5,4},{6,7},{7,6},{8,9},{9,8},{10,11... | collective-permute-start | bytes 1572872 | tf_op jit(solution)/shard_map/ppermute | solution.py:74
  27.2 1.4 shard_map.139
  28.6 46.7 %shard_map.140 = (f32[4,64,1024]{2,1,0:T(8,128)S(1)}, bf16[64,4224]{1,0:T(8,128)(2,1)S(1)}, f32[64,128]{1,0:T(8,128)S(1)}, f32[16,1024]{1,0:T(8,128)S(1)}) custom-call(s32[5]{0:T(128)S(1)} %stack.53.place, bf16[4,4,16,1024]{3,2,1,0:T(8,128)(2,1)S(1)} %pad_maximum_fusion.own, bf16[4,4,16,1024]{3,2,1,0:T(8,128)(2,1)S(1)} %collective-permute-done.6.other, ...), custom_call_target="tpu_custom_call" | custom-call | flops 39862665216 | bytes 155713536 | tf_op jit(solution)/shard_map/pallas_call | solution.py:662
  77.4 1.1 shard_map.142
  78.5 2.2 %collective-permute-start.10 = (bf16[16,5248]{1,0:T(8,128)(2,1)S(1)}, bf16[16,5248]{1,0:T(8,128)(2,1)S(1)}, u32[]{:S(2)}, u32[]{:S(2)}) collective-permute-start(bf16[16,5248]{1,0:T(8,128)(2,1)S(1)} %get-tuple-element.86), channel_id=1, source_target_pairs={{0,24},{8,0},{16,8},{24,16},{1,25},{9,1},{17,9},{25,17},{2,26},{10... | collective-permute-start | bytes 503816 | tf_op jit(solution)/shard_map/ppermute | solution.py:64
  80.9 1.1 collective-permute-start.9
  82.2 2.2 %copy-done.2 = bf16[2048,1024]{1,0:T(8,128)(2,1)S(1)} copy-done((bf16[2048,1024]{1,0:T(8,128)(2,1)S(1)}, bf16[2048,1024]{1,0:T(8,128)(2,1)}, u32[]{:S(2)}) %copy-start.2) | copy-done | bytes 4194328
  84.7 2.0 %copy-done = bf16[2048,1024]{1,0:T(8,128)(2,1)} copy-done((bf16[2048,1024]{1,0:T(8,128)(2,1)}, bf16[2048,1024]{1,0:T(8,128)(2,1)S(1)}, u32[]{:S(2)}) %copy-start) | copy-done | bytes 4194328
  86.6 1.9 %collective-permute-done.8.rest_0_ = bf16[16,5248]{1,0:T(8,128)(2,1)S(1)} collective-permute-done((bf16[16,5248]{1,0:T(8,128)(2,1)S(1)}, bf16[16,5248]{1,0:T(8,128)(2,1)S(1)}, u32[]{:S(2)}, u32[]{:S(2)}) %collective-permute-start.8) | collective-permute-done | bytes 167968 | tf_op jit(solution)/shard_map/ppermute | solution.py:64
  90.4 2.8 %collective-permute-start.12 = (bf16[16,1152]{1,0:T(8,128)(2,1)S(1)}, bf16[16,1152]{1,0:T(8,128)(2,1)S(1)}, u32[]{:S(2)}, u32[]{:S(2)}) collective-permute-start(bf16[16,1152]{1,0:T(8,128)(2,1)S(1)} %get-tuple-element.92), channel_id=1, source_target_pairs={{0,4},{1,5},{2,6},{3,7},{4,0},{5,1},{6,2},{7,3},{8,12},{9,13},{10,... | collective-permute-start | bytes 110600 | tf_op jit(solution)/shard_map/ppermute | solution.py:64
  93.7 1.3 collective-permute-done.11.rest_0_
  95.0 1.6 %collective-permute-done.13.rest_2_ = bf16[16,1152]{1,0:T(8,128)(2,1)S(1)} collective-permute-done((bf16[16,1152]{1,0:T(8,128)(2,1)S(1)}, bf16[16,1152]{1,0:T(8,128)(2,1)S(1)}, u32[]{:S(2)}, u32[]{:S(2)}) %collective-permute-start.13) | collective-permute-done | bytes 36896 | tf_op jit(solution)/shard_map/ppermute | solution.py:64
  97.9 1.7 %collective-permute-start.15 = (bf16[16,1152]{1,0:T(8,128)(2,1)S(1)}, bf16[16,1152]{1,0:T(8,128)(2,1)S(1)}, u32[]{:S(2)}, u32[]{:S(2)}) collective-permute-start(bf16[16,1152]{1,0:T(8,128)(2,1)S(1)} %shard_map.145.refs_0_), channel_id=1, source_target_pairs={{0,16},{8,24},{16,0},{24,8},{1,17},{9,25},{17,1},{25,9},{2,18},{10... | collective-permute-start | bytes 110600 | tf_op jit(solution)/shard_map/ppermute | solution.py:64
  100.9 2.6 %collective-permute-done.16.refs_3_ = bf16[16,1152]{1,0:T(8,128)(2,1)S(1)} collective-permute-done((bf16[16,1152]{1,0:T(8,128)(2,1)S(1)}, bf16[16,1152]{1,0:T(8,128)(2,1)S(1)}, u32[]{:S(2)}, u32[]{:S(2)}) %collective-permute-start.16) | collective-permute-done | bytes 36896 | tf_op jit(solution)/shard_map/ppermute | solution.py:64
  103.5 2.2 %copy-done.1 = bf16[2048,1024]{1,0:T(8,128)(2,1)S(1)} copy-done((bf16[2048,1024]{1,0:T(8,128)(2,1)S(1)}, bf16[2048,1024]{1,0:T(8,128)(2,1)}, u32[]{:S(2)}) %copy-start.1) | copy-done | bytes 4194328
  105.7 2.4 %shard_map.146 = (bf16[64,1024]{1,0:T(8,128)(2,1)}, f32[1,1]{1,0:T(1,128)}, f32[64,1024]{1,0:T(8,128)S(1)}, bf16[64,1024]{1,0:T(8,128)(2,1)S(1)}) custom-call(s32[5]{0:T(128)S(1)} %stack.53.place, bf16[16,1152]{1,0:T(8,128)(2,1)S(1)} %shard_map.145.refs_0_, bf16[16,1152]{1,0:T(8,128)(2,1)S(1)} %collective-permute-done.14.refs_1_, ...), custom_call_target="tpu_custom_call" | custom-call | tf_op jit(solution)/shard_map/pallas_call | solution.py:752
  108.1 4.0 %collective-permute-start.17 = (bf16[64,1024]{1,0:T(8,128)(2,1)S(1)}, bf16[64,1024]{1,0:T(8,128)(2,1)S(1)}, u32[]{:S(2)}, u32[]{:S(2)}) collective-permute-start(bf16[64,1024]{1,0:T(8,128)(2,1)S(1)} %get-tuple-element.97), channel_id=1, source_target_pairs={{0,1},{1,0},{2,3},{3,2},{4,5},{5,4},{6,7},{7,6},{8,9},{9,8},{10,11... | collective-permute-start | bytes 393224 | tf_op jit(solution)/shard_map/ppermute | solution.py:74
  113.1 1.8 %collective-permute-start.18 = (bf16[64,1024]{1,0:T(8,128)(2,1)S(1)}, bf16[64,1024]{1,0:T(8,128)(2,1)S(1)}, u32[]{:S(2)}, u32[]{:S(2)}) collective-permute-start(bf16[64,1024]{1,0:T(8,128)(2,1)S(1)} %shard_map.147.keep), channel_id=1, source_target_pairs={{0,2},{1,3},{2,0},{3,1},{4,6},{5,7},{6,4},{7,5},{8,10},{9,11},{10,... | collective-permute-start | bytes 393224 | tf_op jit(solution)/shard_map/ppermute | solution.py:69
  115.0 2.8 %shard_map.148 = (f32[512,128]{1,0:T(8,128)S(1)}, f32[64,1024]{1,0:T(8,128)S(1)}, f32[512,128]{1,0:T(8,128)S(1)}) custom-call(s32[5]{0:T(128)S(1)} %stack.53.place, s32[1,1024]{1,0:T(1,128)S(1)} %add.63.key_pos, s32[64,1]{1,0:T(8,128)S(1)} %copy.19.query_pos, bf16[8,160,512]{2,1,0:T(8,128)(2,1)S(1)} %bitcast.22), custom_call_target="tpu_custom_call" | custom-call | flops 1610612736 | bytes 1310720 | tf_op jit(solution)/shard_map/pallas_call | solution.py:714
  118.5 1.6 %collective-permute-start.19 = (bf16[64,1024]{1,0:T(8,128)(2,1)S(1)}, bf16[64,1024]{1,0:T(8,128)(2,1)S(1)}, u32[]{:S(2)}, u32[]{:S(2)}) collective-permute-start(bf16[64,1024]{1,0:T(8,128)(2,1)S(1)} %shard_map.149.keep), channel_id=1, source_target_pairs={{0,4},{1,5},{2,6},{3,7},{4,0},{5,1},{6,2},{7,3},{8,12},{9,13},{10,... | collective-permute-start | bytes 393224 | tf_op jit(solution)/shard_map/ppermute | solution.py:69
  120.2 2.8 %shard_map.150 = (f32[512,128]{1,0:T(8,128)S(1)}, f32[64,1024]{1,0:T(8,128)S(1)}, f32[512,128]{1,0:T(8,128)S(1)}) custom-call(s32[5]{0:T(128)S(1)} %stack.53.place, s32[1,1024]{1,0:T(1,128)S(1)} %add.63.key_pos, s32[64,1]{1,0:T(8,128)S(1)} %copy.20.query_pos, bf16[8,160,512]{2,1,0:T(8,128)(2,1)S(1)} %bitcast.23), custom_call_target="tpu_custom_call" | custom-call | flops 1610612736 | bytes 1310720 | tf_op jit(solution)/shard_map/pallas_call | solution.py:714
  123.0 3.8 %collective-permute-done.19.refs_0_ = bf16[64,1024]{1,0:T(8,128)(2,1)S(1)} collective-permute-done((bf16[64,1024]{1,0:T(8,128)(2,1)S(1)}, bf16[64,1024]{1,0:T(8,128)(2,1)S(1)}, u32[]{:S(2)}, u32[]{:S(2)}) %collective-permute-start.19) | collective-permute-done | bytes 131104 | tf_op jit(solution)/shard_map/ppermute | solution.py:69
  126.8 1.5 %collective-permute-start.20 = (bf16[64,1024]{1,0:T(8,128)(2,1)S(1)}, bf16[64,1024]{1,0:T(8,128)(2,1)S(1)}, u32[]{:S(2)}, u32[]{:S(2)}) collective-permute-start(bf16[64,1024]{1,0:T(8,128)(2,1)S(1)} %shard_map.151.half), channel_id=1, source_target_pairs={{0,1},{1,0},{2,3},{3,2},{4,5},{5,4},{6,7},{7,6},{8,9},{9,8},{10,11... | collective-permute-start | bytes 393224 | tf_op jit(solution)/shard_map/ppermute | solution.py:74
  129.3 2.3 %shard_map.152 = (bf16[8,2048]{1,0:T(8,128)(2,1)}, bf16[128,256]{1,0:T(8,128)(2,1)}, bf16[128,256]{1,0:T(8,128)(2,1)}) custom-call(s32[5]{0:T(128)S(1)} %stack.53.place, bf16[64,1024]{1,0:T(8,128)(2,1)S(1)} %shard_map.151.half, bf16[64,1024]{1,0:T(8,128)(2,1)S(1)} %collective-permute-done.20.other, bf16[8,160,512]{2,1,0:T(8,128)(2,1)S(1)} %bitcast.24, ...), custom_call_target="tpu_custom_call" | custom-call | tf_op jit(solution)/shard_map/pallas_call | solution.py:776
  (74 shorter events, 13.6 us)
Async XLA Ops:
  7.2 68.3 %reduce-scatter.2.cloned.1.call-start = ((), (), s32[]{:S(2)}) async-start(), calls=%async_computation.1 | async-start | bytes 1179648 | tf_op jit(solution)/shard_map/reduce_scatter | solution.py:651
  9.8 4.7 %collective-permute-start = (bf16[16,1024]{1,0:T(8,128)(2,1)S(1)}, bf16[16,1024]{1,0:T(8,128)(2,1)S(1)}, u32[]{:S(2)}, u32[]{:S(2)}) collective-permute-start(bf16[16,1024]{1,0:T(8,128)(2,1)S(1)} %shard_map.137), channel_id=1, source_target_pairs={{0,2},{1,3},{2,4},{3,5},{4,6},{5,7},{6,0},{7,1},{8,10},{9,11},{10,... | collective-permute-start | bytes 98312 | tf_op jit(solution)/shard_map/ppermute | solution.py:64
  11.2 3.7 %collective-permute-start.1 = (bf16[16,1024]{1,0:T(8,128)(2,1)S(1)}, bf16[16,1024]{1,0:T(8,128)(2,1)S(1)}, u32[]{:S(2)}, u32[]{:S(2)}) collective-permute-start(bf16[16,1024]{1,0:T(8,128)(2,1)S(1)} %shard_map.137), channel_id=1, source_target_pairs={{0,4},{1,5},{2,6},{3,7},{4,0},{5,1},{6,2},{7,3},{8,12},{9,13},{10,... | collective-permute-start | bytes 98312 | tf_op jit(solution)/shard_map/ppermute | solution.py:64
  13.5 3.4 %collective-permute-start.2 = (bf16[16,1024]{1,0:T(8,128)(2,1)S(1)}, bf16[16,1024]{1,0:T(8,128)(2,1)S(1)}, u32[]{:S(2)}, u32[]{:S(2)}) collective-permute-start(bf16[16,1024]{1,0:T(8,128)(2,1)S(1)} %shard_map.137), channel_id=1, source_target_pairs={{0,6},{1,7},{2,0},{3,1},{4,2},{5,3},{6,4},{7,5},{8,14},{9,15},{10,... | collective-permute-start | bytes 98312 | tf_op jit(solution)/shard_map/ppermute | solution.py:64
  16.9 7.0 %collective-permute-start.3 = (bf16[4,16,1024]{2,1,0:T(8,128)(2,1)S(1)}, bf16[4,16,1024]{2,1,0:T(8,128)(2,1)S(1)}, u32[]{:S(2)}, u32[]{:S(2)}) collective-permute-start(bf16[4,16,1024]{2,1,0:T(8,128)(2,1)S(1)} %pad_maximum_fusion.1), channel_id=1, source_target_pairs={{0,8},{8,16},{16,24},{24,0},{1,9},{9,17},{17,25},{25,1},{2,10},{10... | collective-permute-start | bytes 393224 | tf_op jit(solution)/shard_map/ppermute | solution.py:64
  18.1 5.8 %collective-permute-start.4 = (bf16[4,16,1024]{2,1,0:T(8,128)(2,1)S(1)}, bf16[4,16,1024]{2,1,0:T(8,128)(2,1)S(1)}, u32[]{:S(2)}, u32[]{:S(2)}) collective-permute-start(bf16[4,16,1024]{2,1,0:T(8,128)(2,1)S(1)} %pad_maximum_fusion.1), channel_id=1, source_target_pairs={{0,16},{8,24},{16,0},{24,8},{1,17},{9,25},{17,1},{25,9},{2,18},{10... | collective-permute-start | bytes 393224 | tf_op jit(solution)/shard_map/ppermute | solution.py:64
  18.3 5.5 %collective-permute-start.5 = (bf16[4,16,1024]{2,1,0:T(8,128)(2,1)S(1)}, bf16[4,16,1024]{2,1,0:T(8,128)(2,1)S(1)}, u32[]{:S(2)}, u32[]{:S(2)}) collective-permute-start(bf16[4,16,1024]{2,1,0:T(8,128)(2,1)S(1)} %pad_maximum_fusion.1), channel_id=1, source_target_pairs={{0,24},{8,0},{16,8},{24,16},{1,25},{9,1},{17,9},{25,17},{2,26},{10... | collective-permute-start | bytes 393224 | tf_op jit(solution)/shard_map/ppermute | solution.py:64
  20.3 6.8 %copy-start.13 = (s32[64]{0:T(128)S(1)}, s32[64]{0:T(128)}, u32[]{:S(2)}) copy-start(s32[64]{0:T(128)} %param.13) | copy-start | bytes 772
  20.3 6.9 %copy-start.4 = (bf16[128,2048]{1,0:T(8,128)(2,1)S(1)}, bf16[128,2048]{1,0:T(8,128)(2,1)}, u32[]{:S(2)}) copy-start(bf16[128,2048]{1,0:T(8,128)(2,1)} %queries) | copy-start | bytes 1572868
  20.3 6.9 %copy-start.7 = (bf16[128,256]{1,0:T(8,128)(2,1)S(1)}, bf16[128,256]{1,0:T(8,128)(2,1)}, u32[]{:S(2)}) copy-start(bf16[128,256]{1,0:T(8,128)(2,1)} %keys.1) | copy-start | bytes 196612
  20.3 6.9 %copy-start.8 = (bf16[128,256]{1,0:T(8,128)(2,1)S(1)}, bf16[128,256]{1,0:T(8,128)(2,1)}, u32[]{:S(2)}) copy-start(bf16[128,256]{1,0:T(8,128)(2,1)} %values.1) | copy-start | bytes 196612
  20.3 6.9 %copy-start.11 = (s32[64]{0:T(128)S(1)}, s32[64]{0:T(128)}, u32[]{:S(2)}) copy-start(s32[64]{0:T(128)} %rows.3) | copy-start | bytes 772
  20.3 8.3 %copy-start.9 = (f32[8192]{0:T(1024)S(1)}, f32[8192]{0:T(1024)}, u32[]{:S(2)}) copy-start(f32[8192]{0:T(1024)} %param.11) | copy-start | bytes 98308
  23.9 62.7 %all-gather.3.cloned.1.call-start = ((), (), s32[]{:S(2)}) async-start(), calls=%async_computation.2 | async-start | bytes 1474560 | tf_op jit(solution)/shard_map/all_gather | solution.py:655
  24.1 4.5 %collective-permute-start.6 = (bf16[4,4,16,1024]{3,2,1,0:T(8,128)(2,1)S(1)}, bf16[4,4,16,1024]{3,2,1,0:T(8,128)(2,1)S(1)}, u32[]{:S(2)}, u32[]{:S(2)}) collective-permute-start(bf16[4,4,16,1024]{3,2,1,0:T(8,128)(2,1)S(1)} %pad_maximum_fusion.own), channel_id=1, source_target_pairs={{0,1},{1,0},{2,3},{3,2},{4,5},{5,4},{6,7},{7,6},{8,9},{9,8},{10,11... | collective-permute-start | bytes 1572872 | tf_op jit(solution)/shard_map/ppermute | solution.py:74
  28.6 47.2 %copy-start.14 = (s32[16]{0:T(128)S(1)}, s32[16]{0:T(128)}, u32[]{:S(2)}) copy-start(s32[16]{0:T(128)} %param.15) | copy-start | bytes 196
  75.4 2.0 %collective-permute-start.7 = (bf16[64,4224]{1,0:T(8,128)(2,1)S(1)}, bf16[64,4224]{1,0:T(8,128)(2,1)S(1)}, u32[]{:S(2)}, u32[]{:S(2)}) collective-permute-start(bf16[64,4224]{1,0:T(8,128)(2,1)S(1)} %get-tuple-element.74), channel_id=1, source_target_pairs={{0,1},{1,0},{2,3},{3,2},{4,5},{5,4},{6,7},{7,6},{8,9},{9,8},{10,11... | collective-permute-start | bytes 1622024 | tf_op jit(solution)/shard_map/ppermute | solution.py:74
  78.5 8.1 %collective-permute-start.10 = (bf16[16,5248]{1,0:T(8,128)(2,1)S(1)}, bf16[16,5248]{1,0:T(8,128)(2,1)S(1)}, u32[]{:S(2)}, u32[]{:S(2)}) collective-permute-start(bf16[16,5248]{1,0:T(8,128)(2,1)S(1)} %get-tuple-element.86), channel_id=1, source_target_pairs={{0,24},{8,0},{16,8},{24,16},{1,25},{9,1},{17,9},{25,17},{2,26},{10... | collective-permute-start | bytes 503816 | tf_op jit(solution)/shard_map/ppermute | solution.py:64
  80.7 7.8 %collective-permute-start.8 = (bf16[16,5248]{1,0:T(8,128)(2,1)S(1)}, bf16[16,5248]{1,0:T(8,128)(2,1)S(1)}, u32[]{:S(2)}, u32[]{:S(2)}) collective-permute-start(bf16[16,5248]{1,0:T(8,128)(2,1)S(1)} %get-tuple-element.84), channel_id=1, source_target_pairs={{0,8},{8,16},{16,24},{24,0},{1,9},{9,17},{17,25},{25,1},{2,10},{10... | collective-permute-start | bytes 503816 | tf_op jit(solution)/shard_map/ppermute | solution.py:64
  80.9 8.3 %collective-permute-start.9 = (bf16[16,5248]{1,0:T(8,128)(2,1)S(1)}, bf16[16,5248]{1,0:T(8,128)(2,1)S(1)}, u32[]{:S(2)}, u32[]{:S(2)}) collective-permute-start(bf16[16,5248]{1,0:T(8,128)(2,1)S(1)} %get-tuple-element.85), channel_id=1, source_target_pairs={{0,16},{8,24},{16,0},{24,8},{1,17},{9,25},{17,1},{25,9},{2,18},{10... | collective-permute-start | bytes 503816 | tf_op jit(solution)/shard_map/ppermute | solution.py:64
  82.2 2.2 %copy-start.2 = (bf16[2048,1024]{1,0:T(8,128)(2,1)S(1)}, bf16[2048,1024]{1,0:T(8,128)(2,1)}, u32[]{:S(2)}) copy-start(bf16[2048,1024]{1,0:T(8,128)(2,1)} %source) | copy-start | bytes 12582916
  90.3 4.7 %collective-permute-start.11 = (bf16[16,1152]{1,0:T(8,128)(2,1)S(1)}, bf16[16,1152]{1,0:T(8,128)(2,1)S(1)}, u32[]{:S(2)}, u32[]{:S(2)}) collective-permute-start(bf16[16,1152]{1,0:T(8,128)(2,1)S(1)} %get-tuple-element.91), channel_id=1, source_target_pairs={{0,2},{1,3},{2,4},{3,5},{4,6},{5,7},{6,0},{7,1},{8,10},{9,11},{10,... | collective-permute-start | bytes 110600 | tf_op jit(solution)/shard_map/ppermute | solution.py:64
  90.4 4.6 %collective-permute-start.12 = (bf16[16,1152]{1,0:T(8,128)(2,1)S(1)}, bf16[16,1152]{1,0:T(8,128)(2,1)S(1)}, u32[]{:S(2)}, u32[]{:S(2)}) collective-permute-start(bf16[16,1152]{1,0:T(8,128)(2,1)S(1)} %get-tuple-element.92), channel_id=1, source_target_pairs={{0,4},{1,5},{2,6},{3,7},{4,0},{5,1},{6,2},{7,3},{8,12},{9,13},{10,... | collective-permute-start | bytes 110600 | tf_op jit(solution)/shard_map/ppermute | solution.py:64
  93.3 3.3 %collective-permute-start.13 = (bf16[16,1152]{1,0:T(8,128)(2,1)S(1)}, bf16[16,1152]{1,0:T(8,128)(2,1)S(1)}, u32[]{:S(2)}, u32[]{:S(2)}) collective-permute-start(bf16[16,1152]{1,0:T(8,128)(2,1)S(1)} %get-tuple-element.93), channel_id=1, source_target_pairs={{0,6},{1,7},{2,0},{3,1},{4,2},{5,3},{6,4},{7,5},{8,14},{9,15},{10,... | collective-permute-start | bytes 110600 | tf_op jit(solution)/shard_map/ppermute | solution.py:64
  97.5 3.2 %collective-permute-start.14 = (bf16[16,1152]{1,0:T(8,128)(2,1)S(1)}, bf16[16,1152]{1,0:T(8,128)(2,1)S(1)}, u32[]{:S(2)}, u32[]{:S(2)}) collective-permute-start(bf16[16,1152]{1,0:T(8,128)(2,1)S(1)} %shard_map.145.refs_0_), channel_id=1, source_target_pairs={{0,8},{8,16},{16,24},{24,0},{1,9},{9,17},{17,25},{25,1},{2,10},{10... | collective-permute-start | bytes 110600 | tf_op jit(solution)/shard_map/ppermute | solution.py:64
  97.9 3.0 %collective-permute-start.15 = (bf16[16,1152]{1,0:T(8,128)(2,1)S(1)}, bf16[16,1152]{1,0:T(8,128)(2,1)S(1)}, u32[]{:S(2)}, u32[]{:S(2)}) collective-permute-start(bf16[16,1152]{1,0:T(8,128)(2,1)S(1)} %shard_map.145.refs_0_), channel_id=1, source_target_pairs={{0,16},{8,24},{16,0},{24,8},{1,17},{9,25},{17,1},{25,9},{2,18},{10... | collective-permute-start | bytes 110600 | tf_op jit(solution)/shard_map/ppermute | solution.py:64
  99.6 3.9 %collective-permute-start.16 = (bf16[16,1152]{1,0:T(8,128)(2,1)S(1)}, bf16[16,1152]{1,0:T(8,128)(2,1)S(1)}, u32[]{:S(2)}, u32[]{:S(2)}) collective-permute-start(bf16[16,1152]{1,0:T(8,128)(2,1)S(1)} %shard_map.145.refs_0_), channel_id=1, source_target_pairs={{0,24},{8,0},{16,8},{24,16},{1,25},{9,1},{17,9},{25,17},{2,26},{10... | collective-permute-start | bytes 110600 | tf_op jit(solution)/shard_map/ppermute | solution.py:64
  105.7 9.3 %copy-start.3 = (bf16[1280,512]{1,0:T(8,128)(2,1)S(1)}, bf16[1280,512]{1,0:T(8,128)(2,1)}, u32[]{:S(2)}) copy-start(bf16[1280,512]{1,0:T(8,128)(2,1)} %all-gather.3.cloned.1.call-done) | copy-start | bytes 3932164
  108.1 5.0 %collective-permute-start.17 = (bf16[64,1024]{1,0:T(8,128)(2,1)S(1)}, bf16[64,1024]{1,0:T(8,128)(2,1)S(1)}, u32[]{:S(2)}, u32[]{:S(2)}) collective-permute-start(bf16[64,1024]{1,0:T(8,128)(2,1)S(1)} %get-tuple-element.97), channel_id=1, source_target_pairs={{0,1},{1,0},{2,3},{3,2},{4,5},{5,4},{6,7},{7,6},{8,9},{9,8},{10,11... | collective-permute-start | bytes 393224 | tf_op jit(solution)/shard_map/ppermute | solution.py:74
  113.1 5.4 %collective-permute-start.18 = (bf16[64,1024]{1,0:T(8,128)(2,1)S(1)}, bf16[64,1024]{1,0:T(8,128)(2,1)S(1)}, u32[]{:S(2)}, u32[]{:S(2)}) collective-permute-start(bf16[64,1024]{1,0:T(8,128)(2,1)S(1)} %shard_map.147.keep), channel_id=1, source_target_pairs={{0,2},{1,3},{2,0},{3,1},{4,6},{5,7},{6,4},{7,5},{8,10},{9,11},{10,... | collective-permute-start | bytes 393224 | tf_op jit(solution)/shard_map/ppermute | solution.py:69
  118.5 8.3 %collective-permute-start.19 = (bf16[64,1024]{1,0:T(8,128)(2,1)S(1)}, bf16[64,1024]{1,0:T(8,128)(2,1)S(1)}, u32[]{:S(2)}, u32[]{:S(2)}) collective-permute-start(bf16[64,1024]{1,0:T(8,128)(2,1)S(1)} %shard_map.149.keep), channel_id=1, source_target_pairs={{0,4},{1,5},{2,6},{3,7},{4,0},{5,1},{6,2},{7,3},{8,12},{9,13},{10,... | collective-permute-start | bytes 393224 | tf_op jit(solution)/shard_map/ppermute | solution.py:69
  126.8 2.5 %collective-permute-start.20 = (bf16[64,1024]{1,0:T(8,128)(2,1)S(1)}, bf16[64,1024]{1,0:T(8,128)(2,1)S(1)}, u32[]{:S(2)}, u32[]{:S(2)}) collective-permute-start(bf16[64,1024]{1,0:T(8,128)(2,1)S(1)} %shard_map.151.half), channel_id=1, source_target_pairs={{0,1},{1,0},{2,3},{3,2},{4,5},{5,4},{6,7},{7,6},{8,9},{9,8},{10,11... | collective-permute-start | bytes 393224 | tf_op jit(solution)/shard_map/ppermute | solution.py:74
  (6 other events, 7.4 us)
Sparse Core Ops, SparseCore 0:
  24.0 32.0 reduce-scatter.1
  57.8 25.1 all-gather.2

commit v10 on v9

--- a/solution.py
+++ b/solution.py
@@ -726,9 +726,7 @@
             exps=group * loss * all_tokens,
         )(place, key_pos, query_pos, packed_all)
 
-    stats, output_weight = lax.optimization_barrier((stats, output_weight))
-    weight_here = staged(output_weight)
-    stats, packed_all, weight_here = lax.optimization_barrier((stats, packed_all, weight_here))
+    stats, packed_all = lax.optimization_barrier((stats, packed_all))
     stats, keep, target_rows, *sends = call(
         functools.partial(plane_body, nv - 1),
         (
@@ -747,6 +745,8 @@
         [smem()] + [vmem()] * (5 + nz - 1),
     )(place, keep, stats, target_rows, unit, gain, *got)
 
+    message, output_weight = lax.optimization_barrier((message, output_weight))
+    weight_here = staged(output_weight)
     gathered = [message] + [shifted(message, "vocab", s) for s in range(1, nv)]
     cols = query_width // CORES
     resid_rows, mean_loss, keep, send = call(

time: 139 us -> 137 us (0.986)
  local copies, waits for them, and re-layouts: 10.1 us -> 5.93 us
  waiting for transfers between devices: 17.7 us -> 21.5 us
  starting transfers between devices: 29.8 us -> 27.6 us
    unnamed x30 -> x26, local copies, waits for them, and re-layouts: 9.64 us -> 5.48 us
    ppermute x2, starting transfers between devices: 3.39 us -> 1.62 us  [crossed(): lax.ppermute(value, 'ctx', [(i, i ^ bit * CORES) for i in range(size)])]
    ppermute x2, waiting for transfers between devices: 4.48 us -> 6.14 us  [crossed(): lax.ppermute(value, 'ctx', [(i, i ^ bit * CORES) for i in range(size)])]
  transfers between devices with their start and end apart: 23 -> 23, of which waited for: 13 -> 14; matrix products, arithmetic and copies ran while one was open for 0% -> 0% of each run, Pallas kernels for 42% -> 43%
where the time goes in v10:
time: 137 us; the launch traced here: 136 us
  Pallas kernels  66.4 us (48%)
  starting transfers between devices  27.6 us (20%)
  waiting for transfers between devices  21.5 us (16%)
  between operations  14.3 us (10%)
  local copies, waits for them, and re-layouts  5.93 us (4%)
    pallas_call x1, Pallas kernels, per_device(): pl.pallas_call(functools.partial(flash_body, first), out_shape=(shape((nz...  46.7 us
    ppermute x15, starting transfers between devices, shifted(): return lax.ppermute(value, axis, pairs)  16.9 us
    ppermute x15, waiting for transfers between devices, shifted(): return lax.ppermute(value, axis, pairs)  11.8 us
    ppermute x4, starting transfers between devices, swapped(): return lax.ppermute(value, 'ctx', [(i, i ^ 1) for i in range(size)])  9 us
    ppermute x2, waiting for transfers between devices, crossed(): lax.ppermute(value, 'ctx', [(i, i ^ bit * CORES) for i in range(size)])  6.14 us
    pallas_call x2, Pallas kernels, forward(): call(functools.partial(forward_body, loss_per, heads, group, at_once, j),...  5.6 us
    unnamed x26, local copies, waits for them, and re-layouts  5.48 us
    pallas_call x1, Pallas kernels, per_device(): pl.pallas_call(target_body, out_shape=shape((nc, loss, block_width), bf16...  3.54 us
  transfers between devices with their start and end apart: 23, of which 14 were waited for; matrix products, arithmetic and copies ran while one was open for 0% of the time, Pallas kernels for 43%

profile of v10, /device:TPU:3, one launch (start us, length us, event | category | flops | bytes accessed | tf_op | source)
XLA Modules:
  0.0 136.0 jit_solution(5181479095694800950)
XLA Ops:
  7.3 1.0 copy-done.3
  9.8 1.3 collective-permute-start
  11.2 2.3 %collective-permute-start.1 = (bf16[16,1024]{1,0:T(8,128)(2,1)S(1)}, bf16[16,1024]{1,0:T(8,128)(2,1)S(1)}, u32[]{:S(2)}, u32[]{:S(2)}) collective-permute-start(bf16[16,1024]{1,0:T(8,128)(2,1)S(1)} %shard_map.137), channel_id=1, source_target_pairs={{0,4},{1,5},{2,6},{3,7},{4,0},{5,1},{6,2},{7,3},{8,12},{9,13},{10,... | collective-permute-start | bytes 98312 | tf_op jit(solution)/shard_map/ppermute | solution.py:64
  13.5 1.1 collective-permute-start.2
  14.8 2.0 %collective-permute-done.2 = bf16[16,1024]{1,0:T(8,128)(2,1)S(1)} collective-permute-done((bf16[16,1024]{1,0:T(8,128)(2,1)S(1)}, bf16[16,1024]{1,0:T(8,128)(2,1)S(1)}, u32[]{:S(2)}, u32[]{:S(2)}) %collective-permute-start.2) | collective-permute-done | bytes 32800 | tf_op jit(solution)/shard_map/ppermute | solution.py:64
  16.9 1.3 collective-permute-start.3
  18.3 1.3 collective-permute-start.5
  20.3 3.5 %shard_map.138 = bf16[8,64,1024]{2,1,0:T(8,128)(2,1)} custom-call(s32[5]{0:T(128)S(1)} %stack.53.place, s32[1,64]{1,0:T(1,128)S(1)} %bitcast.28, bf16[4752,8192]{1,0:T(8,128)(2,1)} %weight.3), custom_call_target="tpu_custom_call" | custom-call | bytes 16777216 | tf_op jit(solution)/shard_map/pallas_call | solution.py:633
  24.0 3.0 %collective-permute-start.6 = (bf16[4,4,16,1024]{3,2,1,0:T(8,128)(2,1)S(1)}, bf16[4,4,16,1024]{3,2,1,0:T(8,128)(2,1)S(1)}, u32[]{:S(2)}, u32[]{:S(2)}) collective-permute-start(bf16[4,4,16,1024]{3,2,1,0:T(8,128)(2,1)S(1)} %pad_maximum_fusion.own), channel_id=1, source_target_pairs={{0,1},{1,0},{2,3},{3,2},{4,5},{5,4},{6,7},{7,6},{8,9},{9,8},{10,11... | collective-permute-start | bytes 1572872 | tf_op jit(solution)/shard_map/ppermute | solution.py:74
  27.2 1.4 %shard_map.139 = bf16[160,512]{1,0:T(8,128)(2,1)} custom-call(s32[5]{0:T(128)S(1)} %stack.53.place, s32[64]{0:T(128)S(1)} %copy-done.9, bf16[128,2048]{1,0:T(8,128)(2,1)S(1)} %copy-done.2, bf16[128,256]{1,0:T(8,128)(2,1)S(1)} %copy-done.5, bf16[128,256]{1,0:T(8,128)(2,1)S(1)} %copy-done.6), custom_call_target="tpu_custom_call" | custom-call | bytes 524288 | tf_op jit(solution)/shard_map/pallas_call | solution.py:618
  28.6 46.7 %shard_map.140 = (f32[4,64,1024]{2,1,0:T(8,128)S(1)}, bf16[64,4224]{1,0:T(8,128)(2,1)S(1)}, f32[64,128]{1,0:T(8,128)S(1)}, f32[16,1024]{1,0:T(8,128)S(1)}) custom-call(s32[5]{0:T(128)S(1)} %stack.53.place, bf16[4,4,16,1024]{3,2,1,0:T(8,128)(2,1)S(1)} %pad_maximum_fusion.own, bf16[4,4,16,1024]{3,2,1,0:T(8,128)(2,1)S(1)} %collective-permute-done.6.other, ...), custom_call_target="tpu_custom_call" | custom-call | flops 39862665216 | bytes 155713536 | tf_op jit(solution)/shard_map/pallas_call | solution.py:662
  77.4 1.1 shard_map.142
  78.5 1.4 %collective-permute-start.10 = (bf16[16,5248]{1,0:T(8,128)(2,1)S(1)}, bf16[16,5248]{1,0:T(8,128)(2,1)S(1)}, u32[]{:S(2)}, u32[]{:S(2)}) collective-permute-start(bf16[16,5248]{1,0:T(8,128)(2,1)S(1)} %get-tuple-element.83), channel_id=1, source_target_pairs={{0,24},{8,0},{16,8},{24,16},{1,25},{9,1},{17,9},{25,17},{2,26},{10... | collective-permute-start | bytes 503816 | tf_op jit(solution)/shard_map/ppermute | solution.py:64
  79.9 1.0 collective-permute-start.8
  80.9 1.1 collective-permute-start.9
  82.2 1.1 all-gather.3.cloned.1.call-done
  83.2 1.8 %collective-permute-done.10.rest_2_ = bf16[16,5248]{1,0:T(8,128)(2,1)S(1)} collective-permute-done((bf16[16,5248]{1,0:T(8,128)(2,1)S(1)}, bf16[16,5248]{1,0:T(8,128)(2,1)S(1)}, u32[]{:S(2)}, u32[]{:S(2)}) %collective-permute-start.10) | collective-permute-done | bytes 167968 | tf_op jit(solution)/shard_map/ppermute | solution.py:64
  85.0 3.6 %collective-permute-done.8.rest_0_ = bf16[16,5248]{1,0:T(8,128)(2,1)S(1)} collective-permute-done((bf16[16,5248]{1,0:T(8,128)(2,1)S(1)}, bf16[16,5248]{1,0:T(8,128)(2,1)S(1)}, u32[]{:S(2)}, u32[]{:S(2)}) %collective-permute-start.8) | collective-permute-done | bytes 167968 | tf_op jit(solution)/shard_map/ppermute | solution.py:64
  89.3 1.0 shard_map.143
  90.5 4.1 %collective-permute-start.12 = (bf16[16,1152]{1,0:T(8,128)(2,1)S(1)}, bf16[16,1152]{1,0:T(8,128)(2,1)S(1)}, u32[]{:S(2)}, u32[]{:S(2)}) collective-permute-start(bf16[16,1152]{1,0:T(8,128)(2,1)S(1)} %get-tuple-element.89), channel_id=1, source_target_pairs={{0,4},{1,5},{2,6},{3,7},{4,0},{5,1},{6,2},{7,3},{8,12},{9,13},{10,... | collective-permute-start | bytes 110600 | tf_op jit(solution)/shard_map/ppermute | solution.py:64
  94.6 1.1 collective-permute-done.11.rest_0_
  95.6 2.2 %collective-permute-done.12.rest_1_ = bf16[16,1152]{1,0:T(8,128)(2,1)S(1)} collective-permute-done((bf16[16,1152]{1,0:T(8,128)(2,1)S(1)}, bf16[16,1152]{1,0:T(8,128)(2,1)S(1)}, u32[]{:S(2)}, u32[]{:S(2)}) %collective-permute-start.12) | collective-permute-done | bytes 36896 | tf_op jit(solution)/shard_map/ppermute | solution.py:64
  99.5 1.0 collective-permute-start.16
  100.7 2.2 %copy-done = bf16[2048,1024]{1,0:T(8,128)(2,1)S(1)} copy-done((bf16[2048,1024]{1,0:T(8,128)(2,1)S(1)}, bf16[2048,1024]{1,0:T(8,128)(2,1)}, u32[]{:S(2)}) %copy-start) | copy-done | bytes 4194328
  103.2 2.4 %shard_map.146 = (bf16[64,1024]{1,0:T(8,128)(2,1)}, f32[1,1]{1,0:T(1,128)}, f32[64,1024]{1,0:T(8,128)S(1)}, bf16[64,1024]{1,0:T(8,128)(2,1)S(1)}) custom-call(s32[5]{0:T(128)S(1)} %stack.53.place, bf16[16,1152]{1,0:T(8,128)(2,1)S(1)} %shard_map.144.refs_0_, bf16[16,1152]{1,0:T(8,128)(2,1)S(1)} %collective-permute-done.14.refs_1_, ...), custom_call_target="tpu_custom_call" | custom-call | tf_op jit(solution)/shard_map/pallas_call | solution.py:752
  105.6 4.6 %collective-permute-start.17 = (bf16[64,1024]{1,0:T(8,128)(2,1)S(1)}, bf16[64,1024]{1,0:T(8,128)(2,1)S(1)}, u32[]{:S(2)}, u32[]{:S(2)}) collective-permute-start(bf16[64,1024]{1,0:T(8,128)(2,1)S(1)} %get-tuple-element.95), channel_id=1, source_target_pairs={{0,1},{1,0},{2,3},{3,2},{4,5},{5,4},{6,7},{7,6},{8,9},{9,8},{10,11... | collective-permute-start | bytes 393224 | tf_op jit(solution)/shard_map/ppermute | solution.py:74
  112.0 2.8 %shard_map.148 = (f32[512,128]{1,0:T(8,128)S(1)}, f32[64,1024]{1,0:T(8,128)S(1)}, f32[512,128]{1,0:T(8,128)S(1)}) custom-call(s32[5]{0:T(128)S(1)} %stack.53.place, s32[1,1024]{1,0:T(1,128)S(1)} %add.63.key_pos, s32[64,1]{1,0:T(8,128)S(1)} %copy.19.query_pos, bf16[8,160,512]{2,1,0:T(8,128)(2,1)S(1)} %bitcast.22), custom_call_target="tpu_custom_call" | custom-call | flops 1610612736 | bytes 1310720 | tf_op jit(solution)/shard_map/pallas_call | solution.py:714
  114.8 1.2 collective-permute-done.18.refs_0_
  117.1 2.8 %shard_map.150 = (f32[512,128]{1,0:T(8,128)S(1)}, f32[64,1024]{1,0:T(8,128)S(1)}, f32[512,128]{1,0:T(8,128)S(1)}) custom-call(s32[5]{0:T(128)S(1)} %stack.53.place, s32[1,1024]{1,0:T(1,128)S(1)} %add.63.key_pos, s32[64,1]{1,0:T(8,128)S(1)} %copy.20.query_pos, bf16[8,160,512]{2,1,0:T(8,128)(2,1)S(1)} %bitcast.23), custom_call_target="tpu_custom_call" | custom-call | flops 1610612736 | bytes 1310720 | tf_op jit(solution)/shard_map/pallas_call | solution.py:714
  119.9 5.0 %collective-permute-done.19.refs_0_ = bf16[64,1024]{1,0:T(8,128)(2,1)S(1)} collective-permute-done((bf16[64,1024]{1,0:T(8,128)(2,1)S(1)}, bf16[64,1024]{1,0:T(8,128)(2,1)S(1)}, u32[]{:S(2)}, u32[]{:S(2)}) %collective-permute-start.19) | collective-permute-done | bytes 131104 | tf_op jit(solution)/shard_map/ppermute | solution.py:69
  125.8 1.0 collective-permute-done.20.other
  126.8 2.3 %shard_map.152 = (bf16[8,2048]{1,0:T(8,128)(2,1)}, bf16[128,256]{1,0:T(8,128)(2,1)}, bf16[128,256]{1,0:T(8,128)(2,1)}) custom-call(s32[5]{0:T(128)S(1)} %stack.53.place, bf16[64,1024]{1,0:T(8,128)(2,1)S(1)} %shard_map.151.half, bf16[64,1024]{1,0:T(8,128)(2,1)S(1)} %collective-permute-done.20.other, bf16[8,160,512]{2,1,0:T(8,128)(2,1)S(1)} %bitcast.24, ...), custom_call_target="tpu_custom_call" | custom-call | tf_op jit(solution)/shard_map/pallas_call | solution.py:776
  (70 shorter events, 12.1 us)
Async XLA Ops:
  7.2 68.3 %reduce-scatter.2.cloned.1.call-start = ((), (), s32[]{:S(2)}) async-start(), calls=%async_computation.1 | async-start | bytes 1179648 | tf_op jit(solution)/shard_map/reduce_scatter | solution.py:651
  9.8 4.7 %collective-permute-start = (bf16[16,1024]{1,0:T(8,128)(2,1)S(1)}, bf16[16,1024]{1,0:T(8,128)(2,1)S(1)}, u32[]{:S(2)}, u32[]{:S(2)}) collective-permute-start(bf16[16,1024]{1,0:T(8,128)(2,1)S(1)} %shard_map.137), channel_id=1, source_target_pairs={{0,2},{1,3},{2,4},{3,5},{4,6},{5,7},{6,0},{7,1},{8,10},{9,11},{10,... | collective-permute-start | bytes 98312 | tf_op jit(solution)/shard_map/ppermute | solution.py:64
  11.2 3.7 %collective-permute-start.1 = (bf16[16,1024]{1,0:T(8,128)(2,1)S(1)}, bf16[16,1024]{1,0:T(8,128)(2,1)S(1)}, u32[]{:S(2)}, u32[]{:S(2)}) collective-permute-start(bf16[16,1024]{1,0:T(8,128)(2,1)S(1)} %shard_map.137), channel_id=1, source_target_pairs={{0,4},{1,5},{2,6},{3,7},{4,0},{5,1},{6,2},{7,3},{8,12},{9,13},{10,... | collective-permute-start | bytes 98312 | tf_op jit(solution)/shard_map/ppermute | solution.py:64
  13.5 3.4 %collective-permute-start.2 = (bf16[16,1024]{1,0:T(8,128)(2,1)S(1)}, bf16[16,1024]{1,0:T(8,128)(2,1)S(1)}, u32[]{:S(2)}, u32[]{:S(2)}) collective-permute-start(bf16[16,1024]{1,0:T(8,128)(2,1)S(1)} %shard_map.137), channel_id=1, source_target_pairs={{0,6},{1,7},{2,0},{3,1},{4,2},{5,3},{6,4},{7,5},{8,14},{9,15},{10,... | collective-permute-start | bytes 98312 | tf_op jit(solution)/shard_map/ppermute | solution.py:64
  16.9 7.0 %collective-permute-start.3 = (bf16[4,16,1024]{2,1,0:T(8,128)(2,1)S(1)}, bf16[4,16,1024]{2,1,0:T(8,128)(2,1)S(1)}, u32[]{:S(2)}, u32[]{:S(2)}) collective-permute-start(bf16[4,16,1024]{2,1,0:T(8,128)(2,1)S(1)} %pad_maximum_fusion.1), channel_id=1, source_target_pairs={{0,8},{8,16},{16,24},{24,0},{1,9},{9,17},{17,25},{25,1},{2,10},{10... | collective-permute-start | bytes 393224 | tf_op jit(solution)/shard_map/ppermute | solution.py:64
  18.1 5.7 %collective-permute-start.4 = (bf16[4,16,1024]{2,1,0:T(8,128)(2,1)S(1)}, bf16[4,16,1024]{2,1,0:T(8,128)(2,1)S(1)}, u32[]{:S(2)}, u32[]{:S(2)}) collective-permute-start(bf16[4,16,1024]{2,1,0:T(8,128)(2,1)S(1)} %pad_maximum_fusion.1), channel_id=1, source_target_pairs={{0,16},{8,24},{16,0},{24,8},{1,17},{9,25},{17,1},{25,9},{2,18},{10... | collective-permute-start | bytes 393224 | tf_op jit(solution)/shard_map/ppermute | solution.py:64
  18.3 5.5 %collective-permute-start.5 = (bf16[4,16,1024]{2,1,0:T(8,128)(2,1)S(1)}, bf16[4,16,1024]{2,1,0:T(8,128)(2,1)S(1)}, u32[]{:S(2)}, u32[]{:S(2)}) collective-permute-start(bf16[4,16,1024]{2,1,0:T(8,128)(2,1)S(1)} %pad_maximum_fusion.1), channel_id=1, source_target_pairs={{0,24},{8,0},{16,8},{24,16},{1,25},{9,1},{17,9},{25,17},{2,26},{10... | collective-permute-start | bytes 393224 | tf_op jit(solution)/shard_map/ppermute | solution.py:64
  20.3 6.8 %copy-start.11 = (s32[64]{0:T(128)S(1)}, s32[64]{0:T(128)}, u32[]{:S(2)}) copy-start(s32[64]{0:T(128)} %param.13) | copy-start | bytes 772
  20.3 6.9 %copy-start.2 = (bf16[128,2048]{1,0:T(8,128)(2,1)S(1)}, bf16[128,2048]{1,0:T(8,128)(2,1)}, u32[]{:S(2)}) copy-start(bf16[128,2048]{1,0:T(8,128)(2,1)} %queries) | copy-start | bytes 1572868
  20.3 6.9 %copy-start.5 = (bf16[128,256]{1,0:T(8,128)(2,1)S(1)}, bf16[128,256]{1,0:T(8,128)(2,1)}, u32[]{:S(2)}) copy-start(bf16[128,256]{1,0:T(8,128)(2,1)} %keys.1) | copy-start | bytes 196612
  20.3 6.9 %copy-start.6 = (bf16[128,256]{1,0:T(8,128)(2,1)S(1)}, bf16[128,256]{1,0:T(8,128)(2,1)}, u32[]{:S(2)}) copy-start(bf16[128,256]{1,0:T(8,128)(2,1)} %values.1) | copy-start | bytes 196612
  20.3 6.9 %copy-start.9 = (s32[64]{0:T(128)S(1)}, s32[64]{0:T(128)}, u32[]{:S(2)}) copy-start(s32[64]{0:T(128)} %rows.3) | copy-start | bytes 772
  20.3 8.3 %copy-start.7 = (f32[8192]{0:T(1024)S(1)}, f32[8192]{0:T(1024)}, u32[]{:S(2)}) copy-start(f32[8192]{0:T(1024)} %param.11) | copy-start | bytes 98308
  23.9 59.3 %all-gather.3.cloned.1.call-start = ((), (), s32[]{:S(2)}) async-start(), calls=%async_computation.2 | async-start | bytes 1474560 | tf_op jit(solution)/shard_map/all_gather | solution.py:655
  24.0 4.6 %collective-permute-start.6 = (bf16[4,4,16,1024]{3,2,1,0:T(8,128)(2,1)S(1)}, bf16[4,4,16,1024]{3,2,1,0:T(8,128)(2,1)S(1)}, u32[]{:S(2)}, u32[]{:S(2)}) collective-permute-start(bf16[4,4,16,1024]{3,2,1,0:T(8,128)(2,1)S(1)} %pad_maximum_fusion.own), channel_id=1, source_target_pairs={{0,1},{1,0},{2,3},{3,2},{4,5},{5,4},{6,7},{7,6},{8,9},{9,8},{10,11... | collective-permute-start | bytes 1572872 | tf_op jit(solution)/shard_map/ppermute | solution.py:74
  28.6 47.2 %copy-start.12 = (s32[16]{0:T(128)S(1)}, s32[16]{0:T(128)}, u32[]{:S(2)}) copy-start(s32[16]{0:T(128)} %param.15) | copy-start | bytes 196
  75.4 2.0 %collective-permute-start.7 = (bf16[64,4224]{1,0:T(8,128)(2,1)S(1)}, bf16[64,4224]{1,0:T(8,128)(2,1)S(1)}, u32[]{:S(2)}, u32[]{:S(2)}) collective-permute-start(bf16[64,4224]{1,0:T(8,128)(2,1)S(1)} %get-tuple-element.73), channel_id=1, source_target_pairs={{0,1},{1,0},{2,3},{3,2},{4,5},{5,4},{6,7},{7,6},{8,9},{9,8},{10,11... | collective-permute-start | bytes 1622024 | tf_op jit(solution)/shard_map/ppermute | solution.py:74
  78.5 6.5 %collective-permute-start.10 = (bf16[16,5248]{1,0:T(8,128)(2,1)S(1)}, bf16[16,5248]{1,0:T(8,128)(2,1)S(1)}, u32[]{:S(2)}, u32[]{:S(2)}) collective-permute-start(bf16[16,5248]{1,0:T(8,128)(2,1)S(1)} %get-tuple-element.83), channel_id=1, source_target_pairs={{0,24},{8,0},{16,8},{24,16},{1,25},{9,1},{17,9},{25,17},{2,26},{10... | collective-permute-start | bytes 503816 | tf_op jit(solution)/shard_map/ppermute | solution.py:64
  79.9 8.6 %collective-permute-start.8 = (bf16[16,5248]{1,0:T(8,128)(2,1)S(1)}, bf16[16,5248]{1,0:T(8,128)(2,1)S(1)}, u32[]{:S(2)}, u32[]{:S(2)}) collective-permute-start(bf16[16,5248]{1,0:T(8,128)(2,1)S(1)} %get-tuple-element.81), channel_id=1, source_target_pairs={{0,8},{8,16},{16,24},{24,0},{1,9},{9,17},{17,25},{25,1},{2,10},{10... | collective-permute-start | bytes 503816 | tf_op jit(solution)/shard_map/ppermute | solution.py:64
  80.9 8.3 %collective-permute-start.9 = (bf16[16,5248]{1,0:T(8,128)(2,1)S(1)}, bf16[16,5248]{1,0:T(8,128)(2,1)S(1)}, u32[]{:S(2)}, u32[]{:S(2)}) collective-permute-start(bf16[16,5248]{1,0:T(8,128)(2,1)S(1)} %get-tuple-element.82), channel_id=1, source_target_pairs={{0,16},{8,24},{16,0},{24,8},{1,17},{9,25},{17,1},{25,9},{2,18},{10... | collective-permute-start | bytes 503816 | tf_op jit(solution)/shard_map/ppermute | solution.py:64
  90.3 5.3 %collective-permute-start.11 = (bf16[16,1152]{1,0:T(8,128)(2,1)S(1)}, bf16[16,1152]{1,0:T(8,128)(2,1)S(1)}, u32[]{:S(2)}, u32[]{:S(2)}) collective-permute-start(bf16[16,1152]{1,0:T(8,128)(2,1)S(1)} %get-tuple-element.88), channel_id=1, source_target_pairs={{0,2},{1,3},{2,4},{3,5},{4,6},{5,7},{6,0},{7,1},{8,10},{9,11},{10,... | collective-permute-start | bytes 110600 | tf_op jit(solution)/shard_map/ppermute | solution.py:64
  90.5 7.3 %collective-permute-start.12 = (bf16[16,1152]{1,0:T(8,128)(2,1)S(1)}, bf16[16,1152]{1,0:T(8,128)(2,1)S(1)}, u32[]{:S(2)}, u32[]{:S(2)}) collective-permute-start(bf16[16,1152]{1,0:T(8,128)(2,1)S(1)} %get-tuple-element.89), channel_id=1, source_target_pairs={{0,4},{1,5},{2,6},{3,7},{4,0},{5,1},{6,2},{7,3},{8,12},{9,13},{10,... | collective-permute-start | bytes 110600 | tf_op jit(solution)/shard_map/ppermute | solution.py:64
  94.5 3.4 %collective-permute-start.13 = (bf16[16,1152]{1,0:T(8,128)(2,1)S(1)}, bf16[16,1152]{1,0:T(8,128)(2,1)S(1)}, u32[]{:S(2)}, u32[]{:S(2)}) collective-permute-start(bf16[16,1152]{1,0:T(8,128)(2,1)S(1)} %get-tuple-element.90), channel_id=1, source_target_pairs={{0,6},{1,7},{2,0},{3,1},{4,2},{5,3},{6,4},{7,5},{8,14},{9,15},{10,... | collective-permute-start | bytes 110600 | tf_op jit(solution)/shard_map/ppermute | solution.py:64
  98.9 4.3 %collective-permute-start.14 = (bf16[16,1152]{1,0:T(8,128)(2,1)S(1)}, bf16[16,1152]{1,0:T(8,128)(2,1)S(1)}, u32[]{:S(2)}, u32[]{:S(2)}) collective-permute-start(bf16[16,1152]{1,0:T(8,128)(2,1)S(1)} %shard_map.144.refs_0_), channel_id=1, source_target_pairs={{0,8},{8,16},{16,24},{24,0},{1,9},{9,17},{17,25},{25,1},{2,10},{10... | collective-permute-start | bytes 110600 | tf_op jit(solution)/shard_map/ppermute | solution.py:64
  99.5 3.7 %collective-permute-start.15 = (bf16[16,1152]{1,0:T(8,128)(2,1)S(1)}, bf16[16,1152]{1,0:T(8,128)(2,1)S(1)}, u32[]{:S(2)}, u32[]{:S(2)}) collective-permute-start(bf16[16,1152]{1,0:T(8,128)(2,1)S(1)} %shard_map.144.refs_0_), channel_id=1, source_target_pairs={{0,16},{8,24},{16,0},{24,8},{1,17},{9,25},{17,1},{25,9},{2,18},{10... | collective-permute-start | bytes 110600 | tf_op jit(solution)/shard_map/ppermute | solution.py:64
  99.5 3.7 %collective-permute-start.16 = (bf16[16,1152]{1,0:T(8,128)(2,1)S(1)}, bf16[16,1152]{1,0:T(8,128)(2,1)S(1)}, u32[]{:S(2)}, u32[]{:S(2)}) collective-permute-start(bf16[16,1152]{1,0:T(8,128)(2,1)S(1)} %shard_map.144.refs_0_), channel_id=1, source_target_pairs={{0,24},{8,0},{16,8},{24,16},{1,25},{9,1},{17,9},{25,17},{2,26},{10... | collective-permute-start | bytes 110600 | tf_op jit(solution)/shard_map/ppermute | solution.py:64
  100.7 2.2 %copy-start = (bf16[2048,1024]{1,0:T(8,128)(2,1)S(1)}, bf16[2048,1024]{1,0:T(8,128)(2,1)}, u32[]{:S(2)}) copy-start(bf16[2048,1024]{1,0:T(8,128)(2,1)} %source) | copy-start | bytes 12582916
  103.2 8.8 %copy-start.1 = (bf16[1280,512]{1,0:T(8,128)(2,1)S(1)}, bf16[1280,512]{1,0:T(8,128)(2,1)}, u32[]{:S(2)}) copy-start(bf16[1280,512]{1,0:T(8,128)(2,1)} %all-gather.3.cloned.1.call-done) | copy-start | bytes 3932164
  105.6 5.5 %collective-permute-start.17 = (bf16[64,1024]{1,0:T(8,128)(2,1)S(1)}, bf16[64,1024]{1,0:T(8,128)(2,1)S(1)}, u32[]{:S(2)}, u32[]{:S(2)}) collective-permute-start(bf16[64,1024]{1,0:T(8,128)(2,1)S(1)} %get-tuple-element.95), channel_id=1, source_target_pairs={{0,1},{1,0},{2,3},{3,2},{4,5},{5,4},{6,7},{7,6},{8,9},{9,8},{10,11... | collective-permute-start | bytes 393224 | tf_op jit(solution)/shard_map/ppermute | solution.py:74
  111.2 4.8 %collective-permute-start.18 = (bf16[64,1024]{1,0:T(8,128)(2,1)S(1)}, bf16[64,1024]{1,0:T(8,128)(2,1)S(1)}, u32[]{:S(2)}, u32[]{:S(2)}) collective-permute-start(bf16[64,1024]{1,0:T(8,128)(2,1)S(1)} %shard_map.147.keep), channel_id=1, source_target_pairs={{0,2},{1,3},{2,0},{3,1},{4,6},{5,7},{6,4},{7,5},{8,10},{9,11},{10,... | collective-permute-start | bytes 393224 | tf_op jit(solution)/shard_map/ppermute | solution.py:69
  116.0 8.8 %collective-permute-start.19 = (bf16[64,1024]{1,0:T(8,128)(2,1)S(1)}, bf16[64,1024]{1,0:T(8,128)(2,1)S(1)}, u32[]{:S(2)}, u32[]{:S(2)}) collective-permute-start(bf16[64,1024]{1,0:T(8,128)(2,1)S(1)} %shard_map.149.keep), channel_id=1, source_target_pairs={{0,4},{1,5},{2,6},{3,7},{4,0},{5,1},{6,2},{7,3},{8,12},{9,13},{10,... | collective-permute-start | bytes 393224 | tf_op jit(solution)/shard_map/ppermute | solution.py:69
  124.9 2.0 %collective-permute-start.20 = (bf16[64,1024]{1,0:T(8,128)(2,1)S(1)}, bf16[64,1024]{1,0:T(8,128)(2,1)S(1)}, u32[]{:S(2)}, u32[]{:S(2)}) collective-permute-start(bf16[64,1024]{1,0:T(8,128)(2,1)S(1)} %shard_map.151.half), channel_id=1, source_target_pairs={{0,1},{1,0},{2,3},{3,2},{4,5},{5,4},{6,7},{7,6},{8,9},{9,8},{10,11... | collective-permute-start | bytes 393224 | tf_op jit(solution)/shard_map/ppermute | solution.py:74
  (4 other events, 3.3 us)
Sparse Core Ops, SparseCore 0:
  24.0 32.2 reduce-scatter.1
  58.0 25.1 all-gather.2
